TPU v7x, 256 devices: a whole 4x4x8 slice. The times are simulated.
256 devices in a mesh: dp: 32 (over z, y), fsdp: 8 (over x, core).
Axes of the slice: x: 4, y: 4, z: 8, core: 2. Of those that a mesh axis runs over, the one named last changes fastest.
Arguments:
- grads: bfloat16 [32, 2, 1792, 2048], P('dp', None, 'fsdp'), may hold values from -16.5 to 16.5
- errors: float32 [32, 2, 1792, 2048], P('dp', None, 'fsdp'), may hold values from -4 to 4
- q_prev: float32 [2, 32, 2048], replicated, may hold values from -0.125 to 0.125
- moment1: float32 [2, 28672, 128], P(None, ('fsdp', 'dp')), may hold values from -1.5 to 1.5
- moment2: float32 [2, 28672, 128], P(None, ('fsdp', 'dp')), may hold values from 0.001 to 0.1
Outputs:
- new_errors: float32 [32, 2, 1792, 2048], P('dp', None, 'fsdp')
- new_moment1: float32 [2, 28672, 128], P(None, ('fsdp', 'dp'))
- new_moment2: float32 [2, 28672, 128], P(None, ('fsdp', 'dp'))
- update: bfloat16 [2, 28672, 128], P(None, ('fsdp', 'dp'))
- q_next: float32 [2, 32, 2048], replicated
All inputs are finite; a program needn't handle non-finite values.
Results may differ from a plain program's by a relative error of at most 0.001.
Values sent between devices are 32-bit elements; how exact they have to be, the bound alone decides.
No kernel may reach another device: no remote copies, remote signals or barrier semaphores. Data moves between devices by JAX's collectives and lax.ppermute only.
A program may use at most 64 MiB of HBM per device.

v0:
```python
import jax
import jax.numpy as jnp
from jax import lax
from jax.sharding import PartitionSpec as P


def shards(grads, errors, q_prev, moment1, moment2):
    highest = lax.Precision.HIGHEST
    full = grads[0].astype(jnp.float32) + errors[0]
    replicas = lax.axis_size("dp")
    p_local = jnp.einsum("mdk,mrk->mrd", full, q_prev, precision=highest)
    p_mean = lax.psum(p_local, "dp") / replicas
    gram_local = jnp.einsum("mrd,msd->mrs", p_mean, p_mean, precision=highest)
    gram = lax.psum(gram_local, "fsdp")
    lower = jnp.linalg.cholesky(gram)
    p_hat = jax.scipy.linalg.solve_triangular(lower, p_mean, lower=True)
    q_local = jnp.einsum("mdk,mrd->mrk", full, p_hat, precision=highest)
    q_total = lax.psum(q_local, ("dp", "fsdp"))
    q_next = q_total / replicas
    approx = jnp.einsum("mrd,mrk->mdk", p_hat, q_next, precision=highest)
    new_errors = (full - approx)[None]
    flat = approx.reshape(2, -1, 128)
    state_rows = moment1.shape[1]
    start = lax.axis_index("dp") * state_rows
    mine = lax.dynamic_slice_in_dim(flat, start, state_rows, 1)
    new_moment1 = 0.9 * moment1 + 0.1 * mine
    new_moment2 = 0.95 * moment2 + 0.05 * mine * mine
    update = (new_moment1 / (jnp.sqrt(new_moment2) + 1e-08)).astype(jnp.bfloat16)
    return (new_errors, new_moment1, new_moment2, update, q_next)


def solution(mesh):
    in_specs = (
        P("dp", None, "fsdp", None),
        P("dp", None, "fsdp", None),
        P(),
        P(None, ("fsdp", "dp"), None),
        P(None, ("fsdp", "dp"), None),
    )
    out_specs = (
        P("dp", None, "fsdp", None),
        P(None, ("fsdp", "dp"), None),
        P(None, ("fsdp", "dp"), None),
        P(None, ("fsdp", "dp"), None),
        P(),
    )
    return jax.shard_map(shards, mesh=mesh, in_specs=in_specs, out_specs=out_specs, check_vma=False)
```

profile of v0, /device:TPU:1, one launch (start us, length us, event | category | flops | bytes accessed | tf_op | source)
XLA Modules:
  0.0 470.2 jit_solution(1589914747633269460)
XLA Ops:
  7.2 0.0 copy-start
  7.2 0.0 copy-start.1
  7.2 0.0 all-reduce.2.cloned.1.call-start
  7.3 0.9 copy-done
  8.2 6.3 %fusion.5 = f32[2,32,224]{2,1,0:T(8,128)S(1)} fusion(f32[2,32,2048]{2,1,0:T(8,128)S(1)} %copy-done, f32[1,2,224,2048]{3,2,1,0:T(8,128)} %param.6, bf16[1,2,224,2048]{3,2,1,0:T(8,128)(2,1)} %param.5), kind=kOutput, calls=%fused_computation.7 | convolution fusion | flops 354156544 | bytes 6086656 | tf_op jit(solution)/shard_map/mdk,mrk->mrd/dot_general | solution.py:11
  14.5 118.9 %psum.21 = f32[2,32,224]{2,1,0:T(8,128)S(1)} all-reduce(f32[2,32,224]{2,1,0:T(8,128)S(1)} %fusion.5), channel_id=1, replica_groups=mesh['dp'=32,'fsdp'=8] {'dp'}, use_global_device_ids=true, to_apply=%region_0.0 | all-reduce | flops 14336 | bytes 114688 | tf_op jit(solution)/shard_map/psum | solution.py:12
  133.4 0.2 fusion.11
  133.6 48.6 %psum.22 = f32[2,32,32]{1,2,0:T(8,128)S(1)} all-reduce(f32[2,32,32]{1,2,0:T(8,128)S(1)} %fusion.11), channel_id=1, replica_groups=mesh['dp'=32,'fsdp'=8] {'fsdp'}, use_global_device_ids=true, to_apply=%region_1.0 | all-reduce | flops 2048 | bytes 16384 | tf_op jit(solution)/shard_map/psum | solution.py:14
  182.2 0.1 copy.14
  182.3 5.9 %custom-call.8 = f32[2,32,32]{2,1,0:T(8,128)S(1)} custom-call(f32[2,32,32]{2,1,0:T(8,128)S(1)} %fusion.14), custom_call_target="Cholesky" | custom-call | tf_op jit(solution)/shard_map/jit(cholesky)/cholesky | solution.py:15
  188.2 0.1 compare_reduce_fusion
  188.3 0.1 select_bitcast_fusion
  188.4 4.9 %custom-call.9 = f32[2,1,32,32]{2,3,1,0:T(8,128)S(1)} custom-call(f32[2,1,32,32]{3,2,1,0:T(8,128)S(1)} %select_bitcast_fusion), custom_call_target="InvertDiagBlocksLowerTriangular" | custom-call | tf_op jit(solution)/shard_map/jit(_solve_triangular)/vmap()/triangular_solve | solution.py:16
  193.3 0.3 fusion.9
  193.6 0.0 copy-done.1
  193.6 5.3 %fusion = f32[2,32,2048]{2,1,0:T(8,128)} fusion(f32[2,32,224]{2,1,0:T(8,128)S(1)} %fusion.9, f32[1,2,224,2048]{3,2,1,0:T(8,128)} %param.6, bf16[1,2,224,2048]{3,2,1,0:T(8,128)(2,1)S(1)} %copy-done.1), kind=kOutput, calls=%fused_computation.1 | convolution fusion | flops 354156544 | bytes 6086656 | tf_op jit(solution)/shard_map/mdk,mrd->mrk/dot_general | solution.py:17
  198.9 0.0 all-reduce.2.cloned.1.call-update
  198.9 245.7 %all-reduce.2.cloned.1.call-done = f32[2,32,2048]{2,1,0:T(8,128)} async-done(((f32[2,32,2048]{2,1,0:T(8,128)}), f32[2,32,2048]{2,1,0:T(8,128)}) %all-reduce.2.cloned.1.call-update) | async-done | bytes 524304 | tf_op jit(solution)/shard_map/psum | solution.py:18
  444.6 1.1 broadcast_multiply_fusion
  445.7 0.0 copy-start.2
  445.7 4.9 %fusion.20 = f32[2,224,2048]{2,1,0:T(8,128)} fusion(f32[2,32,224]{2,1,0:T(8,128)S(1)} %fusion.9, f32[2,32,2048]{2,1,0:T(8,128)S(1)} %broadcast_multiply_fusion), kind=kOutput, calls=%fused_computation.29 | convolution fusion | flops 352321536 | bytes 4251648 | tf_op jit(solution)/shard_map/mrd,mrk->mdk/dot_general | solution.py:20
  450.6 4.7 %reshape.26 = f32[2,3584,128]{2,1,0:T(8,128)} reshape(f32[2,224,2048]{2,1,0:T(8,128)} %fusion.20) | data formatting | bytes 7340032 | tf_op jit(solution)/shard_map/reshape | solution.py:22
  455.4 0.0 copy-done.2
  455.4 0.0 copy-start.3
  455.4 0.0 copy-start.4
  455.4 6.3 %fusion.4 = f32[1,2,224,2048]{3,2,1,0:T(8,128)} fusion(f32[2,224,2048]{2,1,0:T(8,128)} %fusion.20, f32[1,2,224,2048]{3,2,1,0:T(8,128)} %param.6, bf16[1,2,224,2048]{3,2,1,0:T(8,128)(2,1)S(1)} %copy-done.1), kind=kLoop, calls=%fused_computation.5 | loop fusion | flops 2752512 | bytes 12845056 | tf_op jit(solution)/shard_map/broadcast_in_dim | solution.py:21
  461.7 0.0 copy-done.3
  461.7 0.0 copy-done.4
  461.7 1.6 divide_convert_fusion
  (4 shorter events, 0.1 us)
Async XLA Ops:
  7.2 1.0 copy-start
  7.2 186.4 %copy-start.1 = (bf16[1,2,224,2048]{3,2,1,0:T(8,128)(2,1)S(1)}, bf16[1,2,224,2048]{3,2,1,0:T(8,128)(2,1)}, u32[]{:S(2)}) copy-start(bf16[1,2,224,2048]{3,2,1,0:T(8,128)(2,1)} %param.5) | copy-start | bytes 5505028
  7.2 437.5 %all-reduce.2.cloned.1.call-start = ((), (), s32[]{:S(2)}) async-start(), calls=%async_computation | async-start | bytes 1048576 | tf_op jit(solution)/shard_map/psum | solution.py:18
  445.7 9.6 %copy-start.2 = (f32[2,32,2048]{2,1,0:T(8,128)}, f32[2,32,2048]{2,1,0:T(8,128)S(1)}, u32[]{:S(2)}) copy-start(f32[2,32,2048]{2,1,0:T(8,128)S(1)} %broadcast_multiply_fusion) | copy-start | bytes 1572868
  455.4 6.3 %copy-start.3 = (f32[2,112,128]{2,1,0:T(8,128)S(1)}, f32[2,112,128]{2,1,0:T(8,128)}, u32[]{:S(2)}) copy-start(f32[2,112,128]{2,1,0:T(8,128)} %param.9) | copy-start | bytes 344068
  455.4 6.3 %copy-start.4 = (f32[2,112,128]{2,1,0:T(8,128)S(1)}, f32[2,112,128]{2,1,0:T(8,128)}, u32[]{:S(2)}) copy-start(f32[2,112,128]{2,1,0:T(8,128)} %param.8) | copy-start | bytes 344068
Sparse Core Ops, SparseCore 0:
  199.0 245.5 all-reduce.1
where the time goes:
time: 471 us; the launch traced here: 470 us
  waiting for transfers between devices  246 us (52%)
  blocking collectives  168 us (36%)
  other arithmetic  20 us (4%)
  matrix products  16.9 us (4%)
  between operations  14.1 us (3%)
  local copies, waits for them, and re-layouts  5.78 us (1%)
    psum x1, waiting for transfers between devices, shards(): q_total = lax.psum(q_local, ('dp', 'fsdp'))  246 us
    psum x1, blocking collectives, shards(): p_mean = lax.psum(p_local, 'dp') / replicas  119 us
    psum x1, blocking collectives, shards(): gram = lax.psum(gram_local, 'fsdp')  48.6 us
  transfers between devices with their start and end apart: 1, of which 1 were waited for; matrix products, arithmetic and copies ran while one was open for 0% of the time, Pallas kernels for 0%

commit v1 on v0

v1 whole, which is shorter than its diff:
```python
import functools

import jax
import jax.numpy as jnp
from jax import lax
from jax.experimental import pallas as pl
from jax.experimental.pallas import tpu as pltpu
from jax.sharding import Mesh, PartitionSpec as P

F32 = jnp.float32
BF16 = jnp.bfloat16
RANK = 32
LANES = 128
VMEM_LIMIT = 24 * 2**20


def split(x):
    head = x.astype(BF16)
    return head, (x - head.astype(F32)).astype(BF16)


def dot(a, b, dims, precision=None):
    return lax.dot_general(a, b, (dims, ((), ())), precision=precision, preferred_element_type=F32)


def pack(square):
    return jnp.concatenate([square[8 * i : 8 * i + 8] for i in range(4)], axis=1)


def unpack(packed):
    return jnp.concatenate([packed[:, 32 * i : 32 * i + 32] for i in range(4)], axis=0)


def left_kernel(grads_ref, errors_ref, q_ref, full_ref, p_ref):
    m, step = pl.program_id(0), pl.program_id(1)
    full = grads_ref[0, 0].astype(F32) + errors_ref[0, 0]
    width = full.shape[1]
    full_ref[m, :, pl.ds(pl.multiple_of(step * width, width), width)] = full
    f_hi, f_lo = split(full)
    q_hi, q_lo = split(q_ref[0])
    wide = dot(jnp.concatenate([q_hi, q_lo], axis=0), f_hi, ((1,), (1,)))
    part = wide[:RANK] + wide[RANK:] + dot(q_hi, f_lo, ((1,), (1,)))

    @pl.when(step == 0)
    def _():
        p_ref[0] = part

    @pl.when(step > 0)
    def _():
        p_ref[0] += part


def left_factors(grads, errors, q_prev, blocks=2):
    _, projections, rows, columns = grads.shape
    width = columns // blocks
    return pl.pallas_call(
        left_kernel,
        grid=(projections, blocks),
        in_specs=[
            pl.BlockSpec((1, 1, rows, width), lambda m, k: (0, m, 0, k)),
            pl.BlockSpec((1, 1, rows, width), lambda m, k: (0, m, 0, k)),
            pl.BlockSpec((1, RANK, width), lambda m, k: (m, 0, k)),
        ],
        out_specs=[
            pl.BlockSpec(memory_space=pltpu.VMEM),
            pl.BlockSpec((1, RANK, rows), lambda m, k: (m, 0, 0)),
        ],
        out_shape=[
            jax.ShapeDtypeStruct((projections, rows, columns), F32),
            jax.ShapeDtypeStruct((projections, RANK, rows), F32),
        ],
        compiler_params=pltpu.CompilerParams(vmem_limit_bytes=VMEM_LIMIT),
        name="left_factors",
    )(grads, errors, q_prev)


def right_kernel(replicas, p_ref, full_ref, out_ref):
    projections, _, columns = full_ref.shape
    tiles = columns // LANES
    group = 4
    for m in range(projections):
        p = p_ref[m] * (1.0 / replicas)
        p_hi, p_lo = split(p)
        both = jnp.concatenate([p_hi, p_lo], axis=0)
        gram = pack(dot(p, p, ((1,), (1,)), lax.Precision.HIGHEST))
        for first in range(0, tiles, group):
            f_hi, f_lo = split(full_ref[m, :, first * LANES : (first + group) * LANES])
            wide = dot(both, f_hi, ((1,), (0,)))
            q = wide[:RANK] + wide[RANK:] + dot(p_hi, f_lo, ((1,), (0,)))
            for j in range(group):
                piece = m * tiles + first + j
                out_ref[piece, :RANK, :] = q[:, j * LANES : (j + 1) * LANES]
                out_ref[piece, RANK:, :] = gram


def right_terms(p_sum, full, replicas):
    projections, _, columns = full.shape
    return pl.pallas_call(
        functools.partial(right_kernel, replicas),
        in_specs=[pl.BlockSpec(memory_space=pltpu.VMEM)] * 2,
        out_specs=pl.BlockSpec(memory_space=pltpu.VMEM),
        out_shape=jax.ShapeDtypeStruct((projections * columns // LANES, RANK + 8, LANES), F32),
        compiler_params=pltpu.CompilerParams(vmem_limit_bytes=VMEM_LIMIT),
        name="right_terms",
    )(p_sum, full)


def factor_kernel(copies, sum_ref, out_ref):
    gram = unpack(sum_ref[RANK:, :]) * (1.0 / copies)
    row = lax.broadcasted_iota(jnp.int32, (RANK, RANK), 0)
    column = lax.broadcasted_iota(jnp.int32, (RANK, RANK), 1)
    work = jnp.concatenate([gram, (row == column).astype(F32)], axis=1)
    below = lax.broadcasted_iota(jnp.int32, (RANK, 2 * RANK), 0)
    scale = jnp.zeros((RANK, 1), F32)
    first = lax.broadcasted_iota(jnp.int32, (RANK, 1), 0)
    for k in range(RANK):
        top = work[k : k + 1, :]
        pivot = work[k : k + 1, k : k + 1]
        scale = jnp.where(first == k, lax.rsqrt(pivot), scale)
        if k < RANK - 1:
            ratio = work[:, k : k + 1] * (1.0 / pivot)
            work = jnp.where(below > k, work - ratio * top, work)
    out_ref[...] = pack(work[:, RANK:] * scale)


def inverse_factor(total, copies):
    return pl.pallas_call(
        functools.partial(factor_kernel, copies),
        in_specs=[pl.BlockSpec(memory_space=pltpu.VMEM)],
        out_specs=pl.BlockSpec(memory_space=pltpu.VMEM),
        out_shape=jax.ShapeDtypeStruct((8, LANES), F32),
        compiler_params=pltpu.CompilerParams(vmem_limit_bytes=VMEM_LIMIT),
        cost_estimate=pl.CostEstimate(flops=4_000_000, bytes_accessed=4_000_000, transcendentals=64),
        name="inverse_factor",
    )(total)


def piece_kernel(replicas, a_ref, b_ref, inverse_ref, out_ref):
    inverse = unpack(inverse_ref[...]) * (1.0 / replicas)
    q = dot(inverse, a_ref[...] + b_ref[...], ((1,), (0,)), lax.Precision.HIGHEST)
    both = jnp.concatenate([q, inverse_ref[...]], axis=0)
    out_ref[...] = jnp.broadcast_to(both[None], out_ref.shape)


def finished_piece(a, b, inverse, replicas, receivers):
    return pl.pallas_call(
        functools.partial(piece_kernel, replicas),
        in_specs=[pl.BlockSpec(memory_space=pltpu.VMEM)] * 3,
        out_specs=pl.BlockSpec(memory_space=pltpu.VMEM),
        out_shape=jax.ShapeDtypeStruct((receivers, RANK + 8, LANES), F32),
        compiler_params=pltpu.CompilerParams(vmem_limit_bytes=VMEM_LIMIT),
        name="finished_piece",
    )(a, b, inverse)


def update_kernel(replicas, place_ref, pieces_ref, p_ref, full_ref, m1_ref, m2_ref, err_ref, n1_ref, n2_ref, up_ref, q_ref, hat_ref, flat_ref):
    m, step = pl.program_id(0), pl.program_id(1)
    rows, width = err_ref.shape[2:]
    tiles = pieces_ref.shape[0]
    here = width // LANES

    @pl.when(step == 0)
    def _():
        inverse = unpack(pieces_ref[0, RANK:, :])
        p_hat = dot(inverse, p_ref[0] * (1.0 / replicas), ((1,), (0,)), lax.Precision.HIGHEST)
        hat = p_hat.T
        h_hi, h_lo = split(hat)
        hat_ref[...] = jnp.concatenate([h_hi, h_lo, h_hi], axis=1)
        mine = flat_ref.shape[0]
        at = lax.broadcasted_iota(jnp.int32, (8, rows), 0) + place_ref[0] * mine
        chosen = (lax.broadcasted_iota(jnp.int32, (8, rows), 1) == at).astype(F32)
        own = dot(chosen, hat, ((1,), (0,)), lax.Precision.HIGHEST)
        o_hi, o_lo = split(own)
        own3 = jnp.concatenate([o_hi, o_lo, o_hi], axis=1)
        q = jnp.concatenate([pieces_ref[j, :RANK, :] for j in range(tiles)], axis=1)
        q_ref[0] = q
        q_hi, q_lo = split(q)
        own_rows = dot(own3, jnp.concatenate([q_hi, q_hi, q_lo], axis=0), ((1,), (0,)))
        for j in range(tiles):
            flat_ref[:, j, :] = own_rows[:mine, j * LANES : (j + 1) * LANES]
        flat = flat_ref[...].reshape(mine * tiles, LANES)
        n1 = 0.9 * m1_ref[0] + 0.1 * flat
        n2 = 0.95 * m2_ref[0] + 0.05 * flat * flat
        n1_ref[0] = n1
        n2_ref[0] = n2
        up_ref[0] = (n1 / (jnp.sqrt(n2) + 1e-08)).astype(BF16)

    q = jnp.concatenate([pieces_ref[step * here + j, :RANK, :] for j in range(here)], axis=1)
    q_hi, q_lo = split(q)
    approx = dot(hat_ref[...], jnp.concatenate([q_hi, q_hi, q_lo], axis=0), ((1,), (0,)))
    err_ref[0, 0] = full_ref[m, :, pl.ds(pl.multiple_of(step * width, width), width)] - approx


def update(place, pieces, p_sum, full, moment1, moment2, replicas, blocks=2):
    projections, rows, columns = full.shape
    width, tiles = columns // blocks, columns // LANES
    state = moment1.shape[1]
    own = pl.BlockSpec((1, state, LANES), lambda m, k: (m, 0, 0))
    return pl.pallas_call(
        functools.partial(update_kernel, replicas),
        grid=(projections, blocks),
        in_specs=[
            pl.BlockSpec(memory_space=pltpu.SMEM),
            pl.BlockSpec((tiles, RANK + 8, LANES), lambda m, k: (m, 0, 0)),
            pl.BlockSpec((1, RANK, rows), lambda m, k: (m, 0, 0)),
            pl.BlockSpec(memory_space=pltpu.VMEM),
            own,
            own,
        ],
        out_specs=[
            pl.BlockSpec((1, 1, rows, width), lambda m, k: (0, m, 0, k)),
            own,
            own,
            own,
            pl.BlockSpec((1, RANK, columns), lambda m, k: (m, 0, 0)),
        ],
        out_shape=[
            jax.ShapeDtypeStruct((1, projections, rows, columns), F32),
            jax.ShapeDtypeStruct(moment1.shape, F32),
            jax.ShapeDtypeStruct(moment2.shape, F32),
            jax.ShapeDtypeStruct(moment1.shape, BF16),
            jax.ShapeDtypeStruct((projections, RANK, columns), F32),
        ],
        scratch_shapes=[
            pltpu.VMEM((rows, 3 * RANK), BF16),
            pltpu.VMEM((state // tiles, tiles, LANES), F32),
        ],
        compiler_params=pltpu.CompilerParams(vmem_limit_bytes=VMEM_LIMIT),
        name="update",
    )(place, pieces, p_sum, full, moment1, moment2)


def flip(axis, bit):
    return [(i, i ^ bit) for i in range(lax.axis_size(axis))]


def shards(grads, errors, q_prev, moment1, moment2):
    replicas = lax.axis_size(("z", "y"))
    full, p_sum = left_factors(grads, errors, q_prev)
    for axis, bit in (("y", 1), ("y", 2), ("z", 1), ("z", 2), ("z", 4)):
        p_sum = p_sum + lax.ppermute(p_sum, axis, flip(axis, bit))

    plane = ("y", "x", "c")
    owners = lax.axis_size(plane)
    terms = right_terms(p_sum, full, replicas)
    total = lax.all_to_all(terms, plane, 0, 0, tiled=True).sum(0)
    inverse = inverse_factor(total, lax.axis_size("y"))
    q = total[:RANK]
    q = q + lax.ppermute(q, "z", flip("z", 1))
    q = q + lax.ppermute(q, "z", flip("z", 2))
    piece = finished_piece(q, lax.ppermute(q, "z", flip("z", 4)), inverse, replicas, owners)
    pieces = lax.all_to_all(piece, plane, 0, 0, tiled=True)

    place = lax.axis_index(("z", "y"))[None]
    return tuple(update(place, pieces, p_sum, full, moment1, moment2, replicas))


def solution(mesh):
    mesh = Mesh(mesh.devices.reshape(8, 4, 4, 2), ("z", "y", "x", "c"))
    dp, fsdp = ("z", "y"), ("x", "c")
    blocks = P(dp, None, fsdp, None)
    states = P(None, fsdp + dp, None)
    return jax.shard_map(
        shards,
        mesh=mesh,
        in_specs=(blocks, blocks, P(), states, states),
        out_specs=(blocks, states, states, states, P()),
        check_vma=False,
    )
```

time: 471 us -> 105 us (0.22)
  waiting for transfers between devices: 246 us -> 26.4 us
  blocking collectives: 168 us -> 27 us
  starting transfers between devices: 0.04 us -> 30.1 us
  other arithmetic: 20 us -> 0.11 us
  matrix products: 16.9 us -> 0 us
  between operations: 14.1 us -> 0.73 us
  Pallas kernels: 0 us -> 11.5 us
    psum x1 -> x0, waiting for transfers between devices: 246 us -> none  [shards(): q_total = lax.psum(q_local, ('dp', 'fsdp'))]
    psum x2 -> x0, blocking collectives: 168 us -> none  [the longest x1 119 us: shards(): p_mean = lax.psum(p_local, 'dp') / replicas]
    all_to_all x0 -> x1, blocking collectives: none -> 27 us  [shards(): total = lax.all_to_all(terms, plane, 0, 0, tiled=True).sum(0)]
    ppermute x0 -> x8, starting transfers between devices: none -> 23.4 us  [the longest x5 16.3 us: shards(): p_sum = p_sum + lax.ppermute(p_sum, axis, flip(axis, bit))]
    dot_general x4 -> x0, matrix products: 16.6 us -> none  [the longest x1 6.27 us: shards(): p_local = jnp.einsum('mdk,mrk->mrd', full, q_prev, precision=highest)]
    ppermute x0 -> x8, waiting for transfers between devices: none -> 13.4 us  [the longest x5 8.66 us: shards(): p_sum = p_sum + lax.ppermute(p_sum, axis, flip(axis, bit))]
    all_to_all x0 -> x1, waiting for transfers between devices: none -> 13 us  [shards(): pieces = lax.all_to_all(piece, plane, 0, 0, tiled=True)]
    pallas_call x0 -> x5, Pallas kernels: none -> 11.5 us  [the longest x1 4.63 us: update(): pl.pallas_call(functools.partial(update_kernel, replicas), grid=(projecti...]
  transfers between devices with their start and end apart: 1 -> 9, of which waited for: 1 -> 8; matrix products, arithmetic and copies ran while one was open for 0% -> 0% of each run, Pallas kernels for 0% -> 3%
where the time goes in v1:
time: 105 us; the launch traced here: 104 us
  starting transfers between devices  30.1 us (29%)
  blocking collectives  27 us (26%)
  waiting for transfers between devices  26.4 us (25%)
  Pallas kernels  11.5 us (11%)
  local copies, waits for them, and re-layouts  8.46 us (8%)
    all_to_all x1, blocking collectives, shards(): total = lax.all_to_all(terms, plane, 0, 0, tiled=True).sum(0)  27 us
    ppermute x5, starting transfers between devices, shards(): p_sum = p_sum + lax.ppermute(p_sum, axis, flip(axis, bit))  16.3 us
    all_to_all x1, waiting for transfers between devices, shards(): pieces = lax.all_to_all(piece, plane, 0, 0, tiled=True)  13 us
    ppermute x5, waiting for transfers between devices, shards(): p_sum = p_sum + lax.ppermute(p_sum, axis, flip(axis, bit))  8.66 us
    unnamed x14, local copies, waits for them, and re-layouts  8.46 us
    all_to_all x1, starting transfers between devices, shards(): pieces = lax.all_to_all(piece, plane, 0, 0, tiled=True)  6.68 us
    ppermute x1, starting transfers between devices, shards(): lax.ppermute(q, 'z', flip('z', 4))  5.47 us
    pallas_call x1, Pallas kernels, update(): pl.pallas_call(functools.partial(update_kernel, replicas), grid=(projecti...  4.63 us
  transfers between devices with their start and end apart: 9, of which 8 were waited for; matrix products, arithmetic and copies ran while one was open for 0% of the time, Pallas kernels for 3%

profile of v1, /device:TPU:1, one launch (start us, length us, event | category | flops | bytes accessed | tf_op | source)
XLA Modules:
  0.0 104.3 jit_solution(3019655023661308828)
XLA Ops:
  0.6 2.0 %copy-done.2 = f32[1,2,224,2048]{3,2,1,0:T(8,128)S(1)} copy-done((f32[1,2,224,2048]{3,2,1,0:T(8,128)S(1)}, f32[1,2,224,2048]{3,2,1,0:T(8,128)}, u32[]{:S(2)}) %copy-start.2) | copy-done | bytes 3670040
  2.7 1.5 %copy-done.3 = bf16[1,2,224,2048]{3,2,1,0:T(8,128)(2,1)S(1)} copy-done((bf16[1,2,224,2048]{3,2,1,0:T(8,128)(2,1)S(1)}, bf16[1,2,224,2048]{3,2,1,0:T(8,128)(2,1)}, u32[]{:S(2)}) %copy-start.3) | copy-done | bytes 1835032
  4.2 1.0 copy-done.4
  5.2 2.1 %left_factors.1 = (f32[2,224,2048]{2,1,0:T(8,128)S(1)}, f32[2,32,224]{2,1,0:T(8,128)S(1)}) custom-call(bf16[1,2,224,2048]{3,2,1,0:T(8,128)(2,1)S(1)} %copy-done.3, f32[1,2,224,2048]{3,2,1,0:T(8,128)S(1)} %copy-done.2, f32[2,32,2048]{2,1,0:T(8,128)S(1)} %copy-done.4), custom_call_target="tpu_custom_call" | custom-call | tf_op jit(solution)/shard_map/left_factors/pallas_call | solution.py:56
  7.3 2.2 %collective-permute-start = (f32[2,32,224]{2,1,0:T(8,128)S(1)}, f32[2,32,224]{2,1,0:T(8,128)S(1)}, u32[]{:S(2)}, u32[]{:S(2)}) collective-permute-start(f32[2,32,224]{2,1,0:T(8,128)S(1)} %get-tuple-element.7), channel_id=1, source_target_pairs={{0,8},{8,0},{16,24},{24,16},{1,9},{9,1},{17,25},{25,17},{2,10},{10... | collective-permute-start | bytes 172040 | tf_op jit(solution)/shard_map/ppermute | solution.py:241
  9.5 1.7 %collective-permute-done = f32[2,32,224]{2,1,0:T(8,128)S(1)} collective-permute-done((f32[2,32,224]{2,1,0:T(8,128)S(1)}, f32[2,32,224]{2,1,0:T(8,128)S(1)}, u32[]{:S(2)}, u32[]{:S(2)}) %collective-permute-start) | collective-permute-done | bytes 57376 | tf_op jit(solution)/shard_map/ppermute | solution.py:241
  11.2 3.2 %collective-permute-start.1 = (f32[2,32,224]{2,1,0:T(8,128)S(1)}, f32[2,32,224]{2,1,0:T(8,128)S(1)}, u32[]{:S(2)}, u32[]{:S(2)}) collective-permute-start(f32[2,32,224]{2,1,0:T(8,128)S(1)} %add.25), channel_id=1, source_target_pairs={{0,16},{8,24},{16,0},{24,8},{1,17},{9,25},{17,1},{25,9},{2,18},{10... | collective-permute-start | bytes 172040 | tf_op jit(solution)/shard_map/ppermute | solution.py:241
  14.3 1.7 %collective-permute-done.1 = f32[2,32,224]{2,1,0:T(8,128)S(1)} collective-permute-done((f32[2,32,224]{2,1,0:T(8,128)S(1)}, f32[2,32,224]{2,1,0:T(8,128)S(1)}, u32[]{:S(2)}, u32[]{:S(2)}) %collective-permute-start.1) | collective-permute-done | bytes 57376 | tf_op jit(solution)/shard_map/ppermute | solution.py:241
  16.0 1.8 %collective-permute-start.2 = (f32[2,32,224]{2,1,0:T(8,128)S(1)}, f32[2,32,224]{2,1,0:T(8,128)S(1)}, u32[]{:S(2)}, u32[]{:S(2)}) collective-permute-start(f32[2,32,224]{2,1,0:T(8,128)S(1)} %add.26), channel_id=1, source_target_pairs={{0,32},{32,0},{64,96},{96,64},{128,160},{160,128},{192,224},{224,1... | collective-permute-start | bytes 172040 | tf_op jit(solution)/shard_map/ppermute | solution.py:241
  17.8 2.0 %collective-permute-done.2 = f32[2,32,224]{2,1,0:T(8,128)S(1)} collective-permute-done((f32[2,32,224]{2,1,0:T(8,128)S(1)}, f32[2,32,224]{2,1,0:T(8,128)S(1)}, u32[]{:S(2)}, u32[]{:S(2)}) %collective-permute-start.2) | collective-permute-done | bytes 57376 | tf_op jit(solution)/shard_map/ppermute | solution.py:241
  19.7 2.8 %collective-permute-start.3 = (f32[2,32,224]{2,1,0:T(8,128)S(1)}, f32[2,32,224]{2,1,0:T(8,128)S(1)}, u32[]{:S(2)}, u32[]{:S(2)}) collective-permute-start(f32[2,32,224]{2,1,0:T(8,128)S(1)} %add.27), channel_id=1, source_target_pairs={{0,64},{32,96},{64,0},{96,32},{128,192},{160,224},{192,128},{224,1... | collective-permute-start | bytes 172040 | tf_op jit(solution)/shard_map/ppermute | solution.py:241
  22.5 1.7 %collective-permute-done.3 = f32[2,32,224]{2,1,0:T(8,128)S(1)} collective-permute-done((f32[2,32,224]{2,1,0:T(8,128)S(1)}, f32[2,32,224]{2,1,0:T(8,128)S(1)}, u32[]{:S(2)}, u32[]{:S(2)}) %collective-permute-start.3) | collective-permute-done | bytes 57376 | tf_op jit(solution)/shard_map/ppermute | solution.py:241
  24.2 6.4 %collective-permute-start.4 = (f32[2,32,224]{2,1,0:T(8,128)S(1)}, f32[2,32,224]{2,1,0:T(8,128)S(1)}, u32[]{:S(2)}, u32[]{:S(2)}) collective-permute-start(f32[2,32,224]{2,1,0:T(8,128)S(1)} %add.28), channel_id=1, source_target_pairs={{0,128},{32,160},{64,192},{96,224},{128,0},{160,32},{192,64},{224,... | collective-permute-start | bytes 172040 | tf_op jit(solution)/shard_map/ppermute | solution.py:241
  30.6 1.7 %collective-permute-done.4 = f32[2,32,224]{2,1,0:T(8,128)S(1)} collective-permute-done((f32[2,32,224]{2,1,0:T(8,128)S(1)}, f32[2,32,224]{2,1,0:T(8,128)S(1)}, u32[]{:S(2)}, u32[]{:S(2)}) %collective-permute-start.4) | collective-permute-done | bytes 57376 | tf_op jit(solution)/shard_map/ppermute | solution.py:241
  32.3 0.0 copy-start.5
  32.3 0.0 copy-start.6
  32.4 0.8 right_terms.1
  33.2 0.0 copy-start
  33.2 1.8 %copy-done = f32[2,224,2048]{2,1,0:T(8,128)} copy-done((f32[2,224,2048]{2,1,0:T(8,128)}, f32[2,224,2048]{2,1,0:T(8,128)S(1)}, u32[]{:S(2)}) %copy-start) | copy-done | bytes 3670040
  35.0 27.0 %all_to_all.10 = f32[32,40,128]{2,1,0:T(8,128)S(1)} all-to-all(f32[32,40,128]{2,1,0:T(8,128)S(1)} %right_terms.1), channel_id=1, replica_groups=mesh['z'=8,'y'=4,'x'=4,'c'=2] {'y','x','c'}, dimensions={0} | all-to-all | bytes 1310720 | tf_op jit(solution)/shard_map/all_to_all | solution.py:246
  62.0 0.1 reduce_sum.9.sum_ref
  62.1 0.4 collective-permute-start.5
  62.5 2.2 %collective-permute-done.5 = f32[32,128]{1,0:T(8,128)S(1)} collective-permute-done((f32[32,128]{1,0:T(8,128)S(1)}, f32[32,128]{1,0:T(8,128)S(1)}, u32[]{:S(2)}, u32[]{:S(2)}) %collective-permute-start.5) | collective-permute-done | bytes 16416 | tf_op jit(solution)/shard_map/ppermute | solution.py:249
  64.8 1.2 %collective-permute-start.6 = (f32[32,128]{1,0:T(8,128)S(1)}, f32[32,128]{1,0:T(8,128)S(1)}, u32[]{:S(2)}, u32[]{:S(2)}) collective-permute-start(f32[32,128]{1,0:T(8,128)S(1)} %slice_add_fusion), channel_id=1, source_target_pairs={{0,64},{32,96},{64,0},{96,32},{128,192},{160,224},{192,128},{224,1... | collective-permute-start | bytes 49160 | tf_op jit(solution)/shard_map/ppermute | solution.py:250
  66.0 2.5 %collective-permute-done.6 = f32[32,128]{1,0:T(8,128)S(1)} collective-permute-done((f32[32,128]{1,0:T(8,128)S(1)}, f32[32,128]{1,0:T(8,128)S(1)}, u32[]{:S(2)}, u32[]{:S(2)}) %collective-permute-start.6) | collective-permute-done | bytes 16416 | tf_op jit(solution)/shard_map/ppermute | solution.py:250
  68.5 5.5 %collective-permute-start.7 = (f32[32,128]{1,0:T(8,128)S(1)}, f32[32,128]{1,0:T(8,128)S(1)}, u32[]{:S(2)}, u32[]{:S(2)}) collective-permute-start(f32[32,128]{1,0:T(8,128)S(1)} %add.31.a_ref), channel_id=1, source_target_pairs={{0,128},{32,160},{64,192},{96,224},{128,0},{160,32},{192,64},{224,... | collective-permute-start | bytes 49160 | tf_op jit(solution)/shard_map/ppermute | solution.py:251
  73.9 2.8 %inverse_factor.1.inverse_ref = f32[8,128]{1,0:T(8,128)S(1)} custom-call(f32[40,128]{1,0:T(8,128)S(1)} %reduce_sum.9.sum_ref), custom_call_target="tpu_custom_call" | custom-call | flops 4000000 | bytes 4000000 | tf_op jit(solution)/shard_map/inverse_factor/pallas_call | solution.py:127
  76.8 1.1 %finished_piece.1 = f32[32,40,128]{2,1,0:T(8,128)} custom-call(f32[32,128]{1,0:T(8,128)S(1)} %add.31.a_ref, f32[32,128]{1,0:T(8,128)S(1)} %collective-permute-done.7.b_ref, f32[8,128]{1,0:T(8,128)S(1)} %inverse_factor.1.inverse_ref), custom_call_target="tpu_custom_call" | custom-call | tf_op jit(solution)/shard_map/finished_piece/pallas_call | solution.py:146
  77.9 6.7 %all-to-all-start.1 = ((f32[32,40,128]{2,1,0:T(8,128)}), f32[32,40,128]{2,1,0:T(8,128)S(1)}, u32[]{:S(2)}, u32[]{:S(2)}) async-start(f32[32,40,128]{2,1,0:T(8,128)} %finished_piece.1), calls=%async_computation.1 | async-start | bytes 1310720 | tf_op jit(solution)/shard_map/all_to_all | solution.py:252
  84.6 13.0 %all-to-all-done.1.pieces_ref = f32[32,40,128]{2,1,0:T(8,128)S(1)} async-done(((f32[32,40,128]{2,1,0:T(8,128)}), f32[32,40,128]{2,1,0:T(8,128)S(1)}, u32[]{:S(2)}, u32[]{:S(2)}) %all-to-all-start.1) | async-done | bytes 655392 | tf_op jit(solution)/shard_map/all_to_all | solution.py:252
  97.6 2.0 %copy-done.1 = f32[2,224,2048]{2,1,0:T(8,128)S(1)} copy-done((f32[2,224,2048]{2,1,0:T(8,128)S(1)}, f32[2,224,2048]{2,1,0:T(8,128)}, u32[]{:S(2)}) %copy-start.1) | copy-done | bytes 3670040
  99.7 4.6 %update.1 = (f32[1,2,224,2048]{3,2,1,0:T(8,128)}, f32[2,112,128]{2,1,0:T(8,128)}, f32[2,112,128]{2,1,0:T(8,128)}, bf16[2,112,128]{2,1,0:T(8,128)(2,1)}, f32[2,32,2048]{2,1,0:T(8,128)}) custom-call(s32[1]{0:T(128)} %bitcast.place_ref, f32[32,40,128]{2,1,0:T(8,128)S(1)} %all-to-all-done.1.pieces_ref, f32[2,32,224]{2,1,0:T(8,128)S(1)} %add.29.p_ref, ...), custom_call_target="tpu_custom_call" | custom-call | tf_op jit(solution)/shard_map/update/pallas_call | solution.py:199
  (15 shorter events, 0.1 us)
Async XLA Ops:
  0.6 2.0 %copy-start.2 = (f32[1,2,224,2048]{3,2,1,0:T(8,128)S(1)}, f32[1,2,224,2048]{3,2,1,0:T(8,128)}, u32[]{:S(2)}) copy-start(f32[1,2,224,2048]{3,2,1,0:T(8,128)} %errors_ref.1) | copy-start | bytes 11010052
  2.7 1.5 %copy-start.3 = (bf16[1,2,224,2048]{3,2,1,0:T(8,128)(2,1)S(1)}, bf16[1,2,224,2048]{3,2,1,0:T(8,128)(2,1)}, u32[]{:S(2)}) copy-start(bf16[1,2,224,2048]{3,2,1,0:T(8,128)(2,1)} %grads_ref.1) | copy-start | bytes 5505028
  4.2 1.0 copy-start.4
  7.3 3.9 %collective-permute-start = (f32[2,32,224]{2,1,0:T(8,128)S(1)}, f32[2,32,224]{2,1,0:T(8,128)S(1)}, u32[]{:S(2)}, u32[]{:S(2)}) collective-permute-start(f32[2,32,224]{2,1,0:T(8,128)S(1)} %get-tuple-element.7), channel_id=1, source_target_pairs={{0,8},{8,0},{16,24},{24,16},{1,9},{9,1},{17,25},{25,17},{2,10},{10... | collective-permute-start | bytes 172040 | tf_op jit(solution)/shard_map/ppermute | solution.py:241
  11.2 4.8 %collective-permute-start.1 = (f32[2,32,224]{2,1,0:T(8,128)S(1)}, f32[2,32,224]{2,1,0:T(8,128)S(1)}, u32[]{:S(2)}, u32[]{:S(2)}) collective-permute-start(f32[2,32,224]{2,1,0:T(8,128)S(1)} %add.25), channel_id=1, source_target_pairs={{0,16},{8,24},{16,0},{24,8},{1,17},{9,25},{17,1},{25,9},{2,18},{10... | collective-permute-start | bytes 172040 | tf_op jit(solution)/shard_map/ppermute | solution.py:241
  16.0 3.7 %collective-permute-start.2 = (f32[2,32,224]{2,1,0:T(8,128)S(1)}, f32[2,32,224]{2,1,0:T(8,128)S(1)}, u32[]{:S(2)}, u32[]{:S(2)}) collective-permute-start(f32[2,32,224]{2,1,0:T(8,128)S(1)} %add.26), channel_id=1, source_target_pairs={{0,32},{32,0},{64,96},{96,64},{128,160},{160,128},{192,224},{224,1... | collective-permute-start | bytes 172040 | tf_op jit(solution)/shard_map/ppermute | solution.py:241
  19.7 4.5 %collective-permute-start.3 = (f32[2,32,224]{2,1,0:T(8,128)S(1)}, f32[2,32,224]{2,1,0:T(8,128)S(1)}, u32[]{:S(2)}, u32[]{:S(2)}) collective-permute-start(f32[2,32,224]{2,1,0:T(8,128)S(1)} %add.27), channel_id=1, source_target_pairs={{0,64},{32,96},{64,0},{96,32},{128,192},{160,224},{192,128},{224,1... | collective-permute-start | bytes 172040 | tf_op jit(solution)/shard_map/ppermute | solution.py:241
  24.2 8.1 %collective-permute-start.4 = (f32[2,32,224]{2,1,0:T(8,128)S(1)}, f32[2,32,224]{2,1,0:T(8,128)S(1)}, u32[]{:S(2)}, u32[]{:S(2)}) collective-permute-start(f32[2,32,224]{2,1,0:T(8,128)S(1)} %add.28), channel_id=1, source_target_pairs={{0,128},{32,160},{64,192},{96,224},{128,0},{160,32},{192,64},{224,... | collective-permute-start | bytes 172040 | tf_op jit(solution)/shard_map/ppermute | solution.py:241
  32.3 65.3 %copy-start.5 = (f32[2,112,128]{2,1,0:T(8,128)S(1)}, f32[2,112,128]{2,1,0:T(8,128)}, u32[]{:S(2)}) copy-start(f32[2,112,128]{2,1,0:T(8,128)} %m1_ref.1) | copy-start | bytes 344068
  32.3 65.3 %copy-start.6 = (f32[2,112,128]{2,1,0:T(8,128)S(1)}, f32[2,112,128]{2,1,0:T(8,128)}, u32[]{:S(2)}) copy-start(f32[2,112,128]{2,1,0:T(8,128)} %m2_ref.1) | copy-start | bytes 344068
  33.2 1.8 %copy-start = (f32[2,224,2048]{2,1,0:T(8,128)}, f32[2,224,2048]{2,1,0:T(8,128)S(1)}, u32[]{:S(2)}) copy-start(f32[2,224,2048]{2,1,0:T(8,128)S(1)} %get-tuple-element.8.full_ref) | copy-start | bytes 11010052
  62.1 2.7 %collective-permute-start.5 = (f32[32,128]{1,0:T(8,128)S(1)}, f32[32,128]{1,0:T(8,128)S(1)}, u32[]{:S(2)}, u32[]{:S(2)}) collective-permute-start(f32[32,128]{1,0:T(8,128)S(1)} %slice.4), channel_id=1, source_target_pairs={{0,32},{32,0},{64,96},{96,64},{128,160},{160,128},{192,224},{224,1... | collective-permute-start | bytes 49160 | tf_op jit(solution)/shard_map/ppermute | solution.py:249
  64.8 3.7 %collective-permute-start.6 = (f32[32,128]{1,0:T(8,128)S(1)}, f32[32,128]{1,0:T(8,128)S(1)}, u32[]{:S(2)}, u32[]{:S(2)}) collective-permute-start(f32[32,128]{1,0:T(8,128)S(1)} %slice_add_fusion), channel_id=1, source_target_pairs={{0,64},{32,96},{64,0},{96,32},{128,192},{160,224},{192,128},{224,1... | collective-permute-start | bytes 49160 | tf_op jit(solution)/shard_map/ppermute | solution.py:250
  68.5 8.3 %collective-permute-start.7 = (f32[32,128]{1,0:T(8,128)S(1)}, f32[32,128]{1,0:T(8,128)S(1)}, u32[]{:S(2)}, u32[]{:S(2)}) collective-permute-start(f32[32,128]{1,0:T(8,128)S(1)} %add.31.a_ref), channel_id=1, source_target_pairs={{0,128},{32,160},{64,192},{96,224},{128,0},{160,32},{192,64},{224,... | collective-permute-start | bytes 49160 | tf_op jit(solution)/shard_map/ppermute | solution.py:251
  77.9 19.7 %all-to-all-start.1 = ((f32[32,40,128]{2,1,0:T(8,128)}), f32[32,40,128]{2,1,0:T(8,128)S(1)}, u32[]{:S(2)}, u32[]{:S(2)}) async-start(f32[32,40,128]{2,1,0:T(8,128)} %finished_piece.1), calls=%async_computation.1 | async-start | bytes 1310720 | tf_op jit(solution)/shard_map/all_to_all | solution.py:252
  97.6 2.0 %copy-start.1 = (f32[2,224,2048]{2,1,0:T(8,128)S(1)}, f32[2,224,2048]{2,1,0:T(8,128)}, u32[]{:S(2)}) copy-start(f32[2,224,2048]{2,1,0:T(8,128)} %copy-done) | copy-start | bytes 11010052

commit v2 on v1

v2 whole, which is shorter than its diff:
```python
import functools

import jax
import jax.numpy as jnp
from jax import lax
from jax.experimental import pallas as pl
from jax.experimental.pallas import tpu as pltpu
from jax.sharding import Mesh, PartitionSpec as P

F32 = jnp.float32
BF16 = jnp.bfloat16
RANK = 32
LANES = 128
VMEM_LIMIT = 24 * 2**20


def split(x):
    head = x.astype(BF16)
    return head, (x - head.astype(F32)).astype(BF16)


def in_hbm(x):
    return pltpu.with_memory_space_constraint(x, pltpu.HBM)


def dot(a, b, dims, precision=None):
    return lax.dot_general(a, b, (dims, ((), ())), precision=precision, preferred_element_type=F32)


def pack(square):
    return jnp.concatenate([square[8 * i : 8 * i + 8] for i in range(4)], axis=1)


def unpack(packed):
    return jnp.concatenate([packed[:, 32 * i : 32 * i + 32] for i in range(4)], axis=0)


def left_kernel(grads_ref, errors_ref, q_ref, full_ref, p_ref):
    m, step = pl.program_id(0), pl.program_id(1)
    full = grads_ref[0, 0].astype(F32) + errors_ref[0, 0]
    width = full.shape[1]
    full_ref[m, :, pl.ds(pl.multiple_of(step * width, width), width)] = full
    f_hi, f_lo = split(full)
    q_hi, q_lo = split(q_ref[0])
    wide = dot(jnp.concatenate([q_hi, q_lo], axis=0), f_hi, ((1,), (1,)))
    part = wide[:RANK] + wide[RANK:] + dot(q_hi, f_lo, ((1,), (1,)))

    @pl.when(step == 0)
    def _():
        p_ref[0] = part

    @pl.when(step > 0)
    def _():
        p_ref[0] += part


def left_factors(grads, errors, q_prev, blocks=2):
    _, projections, rows, columns = grads.shape
    width = columns // blocks
    return pl.pallas_call(
        left_kernel,
        grid=(projections, blocks),
        in_specs=[
            pl.BlockSpec((1, 1, rows, width), lambda m, k: (0, m, 0, k)),
            pl.BlockSpec((1, 1, rows, width), lambda m, k: (0, m, 0, k)),
            pl.BlockSpec((1, RANK, width), lambda m, k: (m, 0, k)),
        ],
        out_specs=[
            pl.BlockSpec(memory_space=pltpu.VMEM),
            pl.BlockSpec((1, RANK, rows), lambda m, k: (m, 0, 0)),
        ],
        out_shape=[
            pltpu.VMEM((projections, rows, columns), F32),
            jax.ShapeDtypeStruct((projections, RANK, rows), F32),
        ],
        compiler_params=pltpu.CompilerParams(vmem_limit_bytes=VMEM_LIMIT),
        name="left_factors",
    )(in_hbm(grads), in_hbm(errors), in_hbm(q_prev))


def right_kernel(replicas, place_ref, p_ref, full_ref, keep_ref, send_ref):
    slots, height, _ = keep_ref.shape
    tiles = (height - 8) // RANK
    width = tiles * LANES
    x, core = place_ref[1], place_ref[2]
    for out_ref, m in ((send_ref, 1 - core), (keep_ref, core)):
        p = p_ref[m] * (1.0 / replicas)
        p_hi, p_lo = split(p)
        both = jnp.concatenate([p_hi, p_lo], axis=0)
        gram = pack(dot(p, p, ((1,), (1,)), lax.Precision.HIGHEST))
        for slot in range(slots):
            first = pl.multiple_of((x ^ slot) * width, width)
            f_hi, f_lo = split(full_ref[m, :, pl.ds(first, width)])
            wide = dot(both, f_hi, ((1,), (0,)))
            q = wide[:RANK] + wide[RANK:] + dot(p_hi, f_lo, ((1,), (0,)))
            for j in range(tiles):
                out_ref[slot, j * RANK : (j + 1) * RANK, :] = q[:, j * LANES : (j + 1) * LANES]
            out_ref[slot, tiles * RANK :, :] = gram


def right_terms(place, p_sum, full, replicas, slots):
    columns = full.shape[2]
    piece = jax.ShapeDtypeStruct((slots, columns // slots // LANES * RANK + 8, LANES), F32)
    return pl.pallas_call(
        functools.partial(right_kernel, replicas),
        in_specs=[pl.BlockSpec(memory_space=pltpu.SMEM)] + [pl.BlockSpec(memory_space=pltpu.VMEM)] * 2,
        out_specs=[pl.BlockSpec(memory_space=pltpu.VMEM)] * 2,
        out_shape=[piece, piece],
        compiler_params=pltpu.CompilerParams(vmem_limit_bytes=VMEM_LIMIT),
        name="right_terms",
    )(place, p_sum, full)


def factor_kernel(sum_ref, out_ref):
    gram = unpack(sum_ref[sum_ref.shape[0] - 8 :, :])
    row = lax.broadcasted_iota(jnp.int32, (RANK, RANK), 0)
    column = lax.broadcasted_iota(jnp.int32, (RANK, RANK), 1)
    work = jnp.concatenate([gram, (row == column).astype(F32)], axis=1)
    below = lax.broadcasted_iota(jnp.int32, (RANK, 2 * RANK), 0)
    scale = jnp.zeros((RANK, 1), F32)
    first = lax.broadcasted_iota(jnp.int32, (RANK, 1), 0)
    for k in range(RANK):
        top = work[k : k + 1, :]
        pivot = work[k : k + 1, k : k + 1]
        scale = jnp.where(first == k, lax.rsqrt(pivot), scale)
        if k < RANK - 1:
            ratio = work[:, k : k + 1] * (1.0 / pivot)
            work = jnp.where(below > k, work - ratio * top, work)
    out_ref[...] = pack(work[:, RANK:] * scale)


def inverse_factor(total):
    return pl.pallas_call(
        factor_kernel,
        in_specs=[pl.BlockSpec(memory_space=pltpu.VMEM)],
        out_specs=pl.BlockSpec(memory_space=pltpu.VMEM),
        out_shape=jax.ShapeDtypeStruct((8, LANES), F32),
        compiler_params=pltpu.CompilerParams(vmem_limit_bytes=VMEM_LIMIT),
        cost_estimate=pl.CostEstimate(flops=4_000_000, bytes_accessed=4_000_000, transcendentals=64),
        name="inverse_factor",
    )(total)


def piece_kernel(replicas, a_ref, b_ref, inverse_ref, out_ref):
    inverse = unpack(inverse_ref[...]) * (1.0 / replicas)
    tiles = a_ref.shape[0] // RANK
    rows = a_ref[...] + b_ref[...]
    wide = jnp.concatenate([rows[j * RANK : (j + 1) * RANK] for j in range(tiles)], axis=1)
    q = dot(inverse, wide, ((1,), (0,)), lax.Precision.HIGHEST)
    for j in range(tiles):
        out_ref[j * RANK : (j + 1) * RANK, :] = q[:, j * LANES : (j + 1) * LANES]
    out_ref[tiles * RANK :, :] = inverse_ref[...]


def finished_piece(a, b, inverse, replicas):
    return pl.pallas_call(
        functools.partial(piece_kernel, replicas),
        in_specs=[pl.BlockSpec(memory_space=pltpu.VMEM)] * 3,
        out_specs=pl.BlockSpec(memory_space=pltpu.VMEM),
        out_shape=jax.ShapeDtypeStruct((a.shape[0] + 8, LANES), F32),
        compiler_params=pltpu.CompilerParams(vmem_limit_bytes=VMEM_LIMIT),
        name="finished_piece",
    )(a, b, inverse)


def update_kernel(replicas, place_ref, own_ref, other_ref, p_ref, full_ref, m1_ref, m2_ref, err_ref, n1_ref, n2_ref, up_ref, q_ref, hat_ref, flat_ref):
    m, step = pl.program_id(0), pl.program_id(1)
    rows, width = err_ref.shape[2:]
    slots, height, _ = own_ref.shape
    tiles = (height - 8) // RANK
    x, mine_here = place_ref[1], m == place_ref[2]

    def piece(block):
        return jnp.where(mine_here, own_ref[block ^ x], other_ref[block ^ x])

    def wide(block):
        rows_of = piece(block)
        return [rows_of[j * RANK : (j + 1) * RANK] for j in range(tiles)]

    @pl.when(step == 0)
    def _():
        inverse = unpack(piece(0)[tiles * RANK :])
        p_hat = dot(inverse, p_ref[0] * (1.0 / replicas), ((1,), (0,)), lax.Precision.HIGHEST)
        hat = p_hat.T
        h_hi, h_lo = split(hat)
        hat_ref[...] = jnp.concatenate([h_hi, h_lo, h_hi], axis=1)
        mine = flat_ref.shape[0]
        at = lax.broadcasted_iota(jnp.int32, (8, rows), 0) + place_ref[0] * mine
        chosen = (lax.broadcasted_iota(jnp.int32, (8, rows), 1) == at).astype(F32)
        own = dot(chosen, hat, ((1,), (0,)), lax.Precision.HIGHEST)
        o_hi, o_lo = split(own)
        own3 = jnp.concatenate([o_hi, o_lo, o_hi], axis=1)
        q = jnp.concatenate([t for block in range(slots) for t in wide(block)], axis=1)
        q_ref[0] = q
        q_hi, q_lo = split(q)
        own_rows = dot(own3, jnp.concatenate([q_hi, q_hi, q_lo], axis=0), ((1,), (0,)))
        for j in range(slots * tiles):
            flat_ref[:, j, :] = own_rows[:mine, j * LANES : (j + 1) * LANES]
        flat = flat_ref[...].reshape(mine * slots * tiles, LANES)
        n1 = 0.9 * m1_ref[0] + 0.1 * flat
        n2 = 0.95 * m2_ref[0] + 0.05 * flat * flat
        n1_ref[0] = n1
        n2_ref[0] = n2
        up_ref[0] = (n1 / (jnp.sqrt(n2) + 1e-08)).astype(BF16)

    here = width // LANES // tiles
    q = jnp.concatenate([t for j in range(here) for t in wide(step * here + j)], axis=1)
    q_hi, q_lo = split(q)
    approx = dot(hat_ref[...], jnp.concatenate([q_hi, q_hi, q_lo], axis=0), ((1,), (0,)))
    err_ref[0, 0] = full_ref[m, :, pl.ds(pl.multiple_of(step * width, width), width)] - approx


def update(place, own, other, p_sum, full, moment1, moment2, replicas, blocks=2):
    projections, rows, columns = full.shape
    width, tiles = columns // blocks, columns // LANES
    state = moment1.shape[1]
    states = pl.BlockSpec((1, state, LANES), lambda m, k: (m, 0, 0))
    return pl.pallas_call(
        functools.partial(update_kernel, replicas),
        grid=(projections, blocks),
        in_specs=[
            pl.BlockSpec(memory_space=pltpu.SMEM),
            pl.BlockSpec(memory_space=pltpu.VMEM),
            pl.BlockSpec(memory_space=pltpu.VMEM),
            pl.BlockSpec((1, RANK, rows), lambda m, k: (m, 0, 0)),
            pl.BlockSpec(memory_space=pltpu.VMEM),
            states,
            states,
        ],
        out_specs=[
            pl.BlockSpec((1, 1, rows, width), lambda m, k: (0, m, 0, k)),
            states,
            states,
            states,
            pl.BlockSpec((1, RANK, columns), lambda m, k: (m, 0, 0)),
        ],
        out_shape=[
            jax.ShapeDtypeStruct((1, projections, rows, columns), F32),
            jax.ShapeDtypeStruct(moment1.shape, F32),
            jax.ShapeDtypeStruct(moment2.shape, F32),
            jax.ShapeDtypeStruct(moment1.shape, BF16),
            jax.ShapeDtypeStruct((projections, RANK, columns), F32),
        ],
        scratch_shapes=[
            pltpu.VMEM((rows, 3 * RANK), BF16),
            pltpu.VMEM((state // tiles, tiles, LANES), F32),
        ],
        compiler_params=pltpu.CompilerParams(vmem_limit_bytes=VMEM_LIMIT),
        name="update",
    )(place, own, other, p_sum, full, moment1, moment2)


def swap(value, axis, bit):
    return lax.ppermute(value, axis, [(i, i ^ bit) for i in range(lax.axis_size(axis))])


def four(values, axis):
    return (values[0] + swap(values[1], axis, 1)) + (swap(values[2], axis, 2) + swap(values[3], axis, 3))


def sum_replicas(value):
    value = four([value] * 4, "y")
    value = four([value] * 4, "z")
    return value, swap(value, "z", 4)


def shards(grads, errors, q_prev, moment1, moment2):
    replicas, slots = lax.axis_size(("z", "y")), lax.axis_size("x")
    place = jnp.stack([lax.axis_index(("z", "y")), lax.axis_index("x"), lax.axis_index("c")])
    full, p_local = left_factors(grads, errors, q_prev)
    p_low, p_high = sum_replicas(p_local)
    p_sum = p_low + p_high

    keep, send = right_terms(place, p_sum, full, replicas, slots)
    terms = keep + swap(send, "c", 1)
    total = four([terms[i] for i in range(slots)], "x")
    inverse = inverse_factor(total)
    piece = finished_piece(*sum_replicas(total[:-8]), inverse, replicas)
    own = jnp.stack([piece] + [swap(piece, "x", i) for i in range(1, slots)])
    other = swap(own, "c", 1)
    return tuple(update(place, own, other, p_sum, full, moment1, moment2, replicas))


def solution(mesh):
    mesh = Mesh(mesh.devices.reshape(8, 4, 4, 2), ("z", "y", "x", "c"))
    dp, fsdp = ("z", "y"), ("x", "c")
    blocks = P(dp, None, fsdp, None)
    states = P(None, fsdp + dp, None)
    return jax.shard_map(
        shards,
        mesh=mesh,
        in_specs=(blocks, blocks, P(), states, states),
        out_specs=(blocks, states, states, states, P()),
        check_vma=False,
    )
```

time: 105 us -> 88.6 us (0.84)
  blocking collectives: 27 us -> 0 us
  starting transfers between devices: 30.1 us -> 40.7 us
  local copies, waits for them, and re-layouts: 8.46 us -> 3.9 us
  waiting for transfers between devices: 26.4 us -> 29.2 us
  Pallas kernels: 11.5 us -> 13.7 us
    all_to_all x1 -> x0, blocking collectives: 27 us -> none  [shards(): total = lax.all_to_all(terms, plane, 0, 0, tiled=True).sum(0)]
    ppermute x8 -> x22, starting transfers between devices: 23.4 us -> 40.7 us  [swap(): lax.ppermute(value, axis, [(i, i ^ bit) for i in range(lax.axis_size(axis...]
    ppermute x8 -> x22, waiting for transfers between devices: 13.4 us -> 29.2 us  [swap(): lax.ppermute(value, axis, [(i, i ^ bit) for i in range(lax.axis_size(axis...]
    all_to_all x1 -> x0, waiting for transfers between devices: 13 us -> none  [shards(): pieces = lax.all_to_all(piece, plane, 0, 0, tiled=True)]
    all_to_all x1 -> x0, starting transfers between devices: 6.68 us -> none  [shards(): pieces = lax.all_to_all(piece, plane, 0, 0, tiled=True)]
    unnamed x14 -> x10, local copies, waits for them, and re-layouts: 8.46 us -> 3.88 us
    pallas_call x1, Pallas kernels: 2.05 us -> 4.05 us  [left_factors(): pl.pallas_call(left_kernel, grid=(projections, blocks), in_specs=[pl.Bloc...]
  transfers between devices with their start and end apart: 9 -> 22, of which waited for: 8 -> 16; matrix products, arithmetic and copies ran while one was open for 0% -> 0% of each run, Pallas kernels for 3% -> 3%
where the time goes in v2:
time: 88.6 us; the launch traced here: 88.4 us
  starting transfers between devices  40.7 us (46%)
  waiting for transfers between devices  29.2 us (33%)
  Pallas kernels  13.7 us (15%)
  local copies, waits for them, and re-layouts  3.9 us (4%)
    ppermute x22, starting transfers between devices, swap(): lax.ppermute(value, axis, [(i, i ^ bit) for i in range(lax.axis_size(axis...  40.7 us
    ppermute x22, waiting for transfers between devices, swap(): lax.ppermute(value, axis, [(i, i ^ bit) for i in range(lax.axis_size(axis...  29.2 us
    pallas_call x1, Pallas kernels, update(): pl.pallas_call(functools.partial(update_kernel, replicas), grid=(projecti...  5.27 us
    pallas_call x1, Pallas kernels, left_factors(): pl.pallas_call(left_kernel, grid=(projections, blocks), in_specs=[pl.Bloc...  4.05 us
    unnamed x10, local copies, waits for them, and re-layouts  3.88 us
    pallas_call x1, Pallas kernels, inverse_factor(): pl.pallas_call(factor_kernel, in_specs=[pl.BlockSpec(memory_space=pltpu.V...  2.85 us
  transfers between devices with their start and end apart: 22, of which 16 were waited for; matrix products, arithmetic and copies ran while one was open for 0% of the time, Pallas kernels for 3%

profile of v2, /device:TPU:1, one launch (start us, length us, event | category | flops | bytes accessed | tf_op | source)
XLA Modules:
  0.0 88.4 jit_solution(11340914742002317395)
XLA Ops:
  0.6 4.0 %left_factors.1 = (f32[2,224,2048]{2,1,0:T(8,128)S(1)}, f32[2,32,224]{2,1,0:T(8,128)S(1)}) custom-call(bf16[1,2,224,2048]{3,2,1,0:T(8,128)(2,1)} %grads_ref.1, f32[1,2,224,2048]{3,2,1,0:T(8,128)} %errors_ref.1, f32[2,32,2048]{2,1,0:T(8,128)} %q_ref.1), custom_call_target="tpu_custom_call" | custom-call | tf_op jit(solution)/shard_map/left_factors/pallas_call | solution.py:60
  4.7 1.8 %copy-done = f32[2,224,2048]{2,1,0:T(8,128)} copy-done((f32[2,224,2048]{2,1,0:T(8,128)}, f32[2,224,2048]{2,1,0:T(8,128)S(1)}, u32[]{:S(2)}) %copy-start) | copy-done | bytes 3670040
  6.5 3.6 %collective-permute-start.2 = (f32[2,32,224]{2,1,0:T(8,128)S(1)}, f32[2,32,224]{2,1,0:T(8,128)S(1)}, u32[]{:S(2)}, u32[]{:S(2)}) collective-permute-start(f32[2,32,224]{2,1,0:T(8,128)S(1)} %get-tuple-element.9), channel_id=1, source_target_pairs={{0,24},{8,16},{16,8},{24,0},{1,25},{9,17},{17,9},{25,1},{2,26},{10... | collective-permute-start | bytes 172040 | tf_op jit(solution)/shard_map/ppermute | solution.py:254
  10.7 1.4 %collective-permute-done.2 = f32[2,32,224]{2,1,0:T(8,128)S(1)} collective-permute-done((f32[2,32,224]{2,1,0:T(8,128)S(1)}, f32[2,32,224]{2,1,0:T(8,128)S(1)}, u32[]{:S(2)}, u32[]{:S(2)}) %collective-permute-start.2) | collective-permute-done | bytes 57376 | tf_op jit(solution)/shard_map/ppermute | solution.py:254
  12.1 2.7 %collective-permute-done.1 = f32[2,32,224]{2,1,0:T(8,128)S(1)} collective-permute-done((f32[2,32,224]{2,1,0:T(8,128)S(1)}, f32[2,32,224]{2,1,0:T(8,128)S(1)}, u32[]{:S(2)}, u32[]{:S(2)}) %collective-permute-start.1) | collective-permute-done | bytes 57376 | tf_op jit(solution)/shard_map/ppermute | solution.py:254
  14.8 4.3 %collective-permute-start.5 = (f32[2,32,224]{2,1,0:T(8,128)S(1)}, f32[2,32,224]{2,1,0:T(8,128)S(1)}, u32[]{:S(2)}, u32[]{:S(2)}) collective-permute-start(f32[2,32,224]{2,1,0:T(8,128)S(1)} %add_add_fusion.3), channel_id=1, source_target_pairs={{0,96},{32,64},{64,32},{96,0},{128,224},{160,192},{192,160},{224,1... | collective-permute-start | bytes 172040 | tf_op jit(solution)/shard_map/ppermute | solution.py:254
  19.6 1.3 %collective-permute-done.5 = f32[2,32,224]{2,1,0:T(8,128)S(1)} collective-permute-done((f32[2,32,224]{2,1,0:T(8,128)S(1)}, f32[2,32,224]{2,1,0:T(8,128)S(1)}, u32[]{:S(2)}, u32[]{:S(2)}) %collective-permute-start.5) | collective-permute-done | bytes 57376 | tf_op jit(solution)/shard_map/ppermute | solution.py:254
  20.8 3.1 %collective-permute-done.4 = f32[2,32,224]{2,1,0:T(8,128)S(1)} collective-permute-done((f32[2,32,224]{2,1,0:T(8,128)S(1)}, f32[2,32,224]{2,1,0:T(8,128)S(1)}, u32[]{:S(2)}, u32[]{:S(2)}) %collective-permute-start.4) | collective-permute-done | bytes 57376 | tf_op jit(solution)/shard_map/ppermute | solution.py:254
  24.0 6.3 %collective-permute-start.6 = (f32[2,32,224]{2,1,0:T(8,128)S(1)}, f32[2,32,224]{2,1,0:T(8,128)S(1)}, u32[]{:S(2)}, u32[]{:S(2)}) collective-permute-start(f32[2,32,224]{2,1,0:T(8,128)S(1)} %add_add_fusion.2), channel_id=1, source_target_pairs={{0,128},{32,160},{64,192},{96,224},{128,0},{160,32},{192,64},{224,... | collective-permute-start | bytes 172040 | tf_op jit(solution)/shard_map/ppermute | solution.py:254
  30.3 1.6 %collective-permute-done.6 = f32[2,32,224]{2,1,0:T(8,128)S(1)} collective-permute-done((f32[2,32,224]{2,1,0:T(8,128)S(1)}, f32[2,32,224]{2,1,0:T(8,128)S(1)}, u32[]{:S(2)}, u32[]{:S(2)}) %collective-permute-start.6) | collective-permute-done | bytes 57376 | tf_op jit(solution)/shard_map/ppermute | solution.py:254
  31.9 2.0 %copy-done.1 = f32[2,224,2048]{2,1,0:T(8,128)S(1)} copy-done((f32[2,224,2048]{2,1,0:T(8,128)S(1)}, f32[2,224,2048]{2,1,0:T(8,128)}, u32[]{:S(2)}) %copy-start.1) | copy-done | bytes 3670040
  34.0 1.3 %right_terms.1 = (f32[4,136,128]{2,1,0:T(8,128)S(1)}, f32[4,136,128]{2,1,0:T(8,128)S(1)}) custom-call(s32[3]{0:T(128)S(1)} %pad_add_fusion.place_ref, f32[2,32,224]{2,1,0:T(8,128)S(1)} %add.61.p_ref, f32[2,224,2048]{2,1,0:T(8,128)S(1)} %copy-done.1), custom_call_target="tpu_custom_call" | custom-call | tf_op jit(solution)/shard_map/right_terms/pallas_call | solution.py:104
  35.3 3.6 %collective-permute-start.7 = (f32[4,136,128]{2,1,0:T(8,128)S(1)}, f32[4,136,128]{2,1,0:T(8,128)S(1)}, u32[]{:S(2)}, u32[]{:S(2)}) collective-permute-start(f32[4,136,128]{2,1,0:T(8,128)S(1)} %get-tuple-element.12), channel_id=1, source_target_pairs={{0,1},{1,0},{2,3},{3,2},{4,5},{5,4},{6,7},{7,6},{8,9},{9,8},{10,11... | collective-permute-start | bytes 835592 | tf_op jit(solution)/shard_map/ppermute | solution.py:254
  38.9 1.2 %collective-permute-done.7 = f32[4,136,128]{2,1,0:T(8,128)S(1)} collective-permute-done((f32[4,136,128]{2,1,0:T(8,128)S(1)}, f32[4,136,128]{2,1,0:T(8,128)S(1)}, u32[]{:S(2)}, u32[]{:S(2)}) %collective-permute-start.7) | collective-permute-done | bytes 278560 | tf_op jit(solution)/shard_map/ppermute | solution.py:254
  40.2 2.6 %collective-permute-start.10 = (f32[136,128]{1,0:T(8,128)S(1)}, f32[136,128]{1,0:T(8,128)S(1)}, u32[]{:S(2)}, u32[]{:S(2)}) collective-permute-start(f32[136,128]{1,0:T(8,128)S(1)} %get-tuple-element.13), channel_id=1, source_target_pairs={{0,6},{2,4},{4,2},{6,0},{1,7},{3,5},{5,3},{7,1},{8,14},{10,12},{12... | collective-permute-start | bytes 208904 | tf_op jit(solution)/shard_map/ppermute | solution.py:254
  44.6 2.8 %collective-permute-done.9 = f32[136,128]{1,0:T(8,128)S(1)} collective-permute-done((f32[136,128]{1,0:T(8,128)S(1)}, f32[136,128]{1,0:T(8,128)S(1)}, u32[]{:S(2)}, u32[]{:S(2)}) %collective-permute-start.9) | collective-permute-done | bytes 69664 | tf_op jit(solution)/shard_map/ppermute | solution.py:254
  47.4 2.1 %collective-permute-start.12 = (f32[128,128]{1,0:T(8,128)S(1)}, f32[128,128]{1,0:T(8,128)S(1)}, u32[]{:S(2)}, u32[]{:S(2)}) collective-permute-start(f32[128,128]{1,0:T(8,128)S(1)} %slice.24), channel_id=1, source_target_pairs={{0,16},{8,24},{16,0},{24,8},{1,17},{9,25},{17,1},{25,9},{2,18},{10... | collective-permute-start | bytes 196616 | tf_op jit(solution)/shard_map/ppermute | solution.py:254
  50.2 2.0 %collective-permute-done.12 = f32[128,128]{1,0:T(8,128)S(1)} collective-permute-done((f32[128,128]{1,0:T(8,128)S(1)}, f32[128,128]{1,0:T(8,128)S(1)}, u32[]{:S(2)}, u32[]{:S(2)}) %collective-permute-start.12) | collective-permute-done | bytes 65568 | tf_op jit(solution)/shard_map/ppermute | solution.py:254
  52.1 1.7 %collective-permute-done.13 = f32[128,128]{1,0:T(8,128)S(1)} collective-permute-done((f32[128,128]{1,0:T(8,128)S(1)}, f32[128,128]{1,0:T(8,128)S(1)}, u32[]{:S(2)}, u32[]{:S(2)}) %collective-permute-start.13) | collective-permute-done | bytes 65568 | tf_op jit(solution)/shard_map/ppermute | solution.py:254
  53.9 2.2 %collective-permute-start.16 = (f32[128,128]{1,0:T(8,128)S(1)}, f32[128,128]{1,0:T(8,128)S(1)}, u32[]{:S(2)}, u32[]{:S(2)}) collective-permute-start(f32[128,128]{1,0:T(8,128)S(1)} %add_add_fusion.1), channel_id=1, source_target_pairs={{0,96},{32,64},{64,32},{96,0},{128,224},{160,192},{192,160},{224,1... | collective-permute-start | bytes 196616 | tf_op jit(solution)/shard_map/ppermute | solution.py:254
  56.3 1.2 %collective-permute-start.14 = (f32[128,128]{1,0:T(8,128)S(1)}, f32[128,128]{1,0:T(8,128)S(1)}, u32[]{:S(2)}, u32[]{:S(2)}) collective-permute-start(f32[128,128]{1,0:T(8,128)S(1)} %add_add_fusion.1), channel_id=1, source_target_pairs={{0,32},{32,0},{64,96},{96,64},{128,160},{160,128},{192,224},{224,1... | collective-permute-start | bytes 196616 | tf_op jit(solution)/shard_map/ppermute | solution.py:254
  57.5 1.4 %collective-permute-done.16 = f32[128,128]{1,0:T(8,128)S(1)} collective-permute-done((f32[128,128]{1,0:T(8,128)S(1)}, f32[128,128]{1,0:T(8,128)S(1)}, u32[]{:S(2)}, u32[]{:S(2)}) %collective-permute-start.16) | collective-permute-done | bytes 65568 | tf_op jit(solution)/shard_map/ppermute | solution.py:254
  58.9 2.5 %collective-permute-done.15 = f32[128,128]{1,0:T(8,128)S(1)} collective-permute-done((f32[128,128]{1,0:T(8,128)S(1)}, f32[128,128]{1,0:T(8,128)S(1)}, u32[]{:S(2)}, u32[]{:S(2)}) %collective-permute-start.15) | collective-permute-done | bytes 65568 | tf_op jit(solution)/shard_map/ppermute | solution.py:254
  61.4 3.7 %collective-permute-start.17 = (f32[128,128]{1,0:T(8,128)S(1)}, f32[128,128]{1,0:T(8,128)S(1)}, u32[]{:S(2)}, u32[]{:S(2)}) collective-permute-start(f32[128,128]{1,0:T(8,128)S(1)} %add_add_fusion.a_ref), channel_id=1, source_target_pairs={{0,128},{32,160},{64,192},{96,224},{128,0},{160,32},{192,64},{224,... | collective-permute-start | bytes 196616 | tf_op jit(solution)/shard_map/ppermute | solution.py:254
  65.2 2.8 %inverse_factor.1.inverse_ref = f32[8,128]{1,0:T(8,128)S(1)} custom-call(f32[136,128]{1,0:T(8,128)S(1)} %fusion.1.sum_ref), custom_call_target="tpu_custom_call" | custom-call | flops 4000000 | bytes 4000000 | tf_op jit(solution)/shard_map/inverse_factor/pallas_call | solution.py:133
  68.0 1.2 %collective-permute-done.17.b_ref = f32[128,128]{1,0:T(8,128)S(1)} collective-permute-done((f32[128,128]{1,0:T(8,128)S(1)}, f32[128,128]{1,0:T(8,128)S(1)}, u32[]{:S(2)}, u32[]{:S(2)}) %collective-permute-start.17) | collective-permute-done | bytes 65568 | tf_op jit(solution)/shard_map/ppermute | solution.py:254
  69.5 3.5 %collective-permute-start.20 = (f32[136,128]{1,0:T(8,128)S(1)}, f32[136,128]{1,0:T(8,128)S(1)}, u32[]{:S(2)}, u32[]{:S(2)}) collective-permute-start(f32[136,128]{1,0:T(8,128)S(1)} %finished_piece.1), channel_id=1, source_target_pairs={{0,6},{2,4},{4,2},{6,0},{1,7},{3,5},{5,3},{7,1},{8,14},{10,12},{12... | collective-permute-start | bytes 208904 | tf_op jit(solution)/shard_map/ppermute | solution.py:254
  73.6 1.3 %collective-permute-done.20 = f32[136,128]{1,0:T(8,128)S(1)} collective-permute-done((f32[136,128]{1,0:T(8,128)S(1)}, f32[136,128]{1,0:T(8,128)S(1)}, u32[]{:S(2)}, u32[]{:S(2)}) %collective-permute-start.20) | collective-permute-done | bytes 69664 | tf_op jit(solution)/shard_map/ppermute | solution.py:254
  75.0 2.7 %collective-permute-done.19 = f32[136,128]{1,0:T(8,128)S(1)} collective-permute-done((f32[136,128]{1,0:T(8,128)S(1)}, f32[136,128]{1,0:T(8,128)S(1)}, u32[]{:S(2)}, u32[]{:S(2)}) %collective-permute-start.19) | collective-permute-done | bytes 69664 | tf_op jit(solution)/shard_map/ppermute | solution.py:254
  77.7 4.3 %collective-permute-start.21 = (f32[4,136,128]{2,1,0:T(8,128)S(1)}, f32[4,136,128]{2,1,0:T(8,128)S(1)}, u32[]{:S(2)}, u32[]{:S(2)}) collective-permute-start(f32[4,136,128]{2,1,0:T(8,128)S(1)} %pad_maximum_fusion.own_ref), channel_id=1, source_target_pairs={{0,1},{1,0},{2,3},{3,2},{4,5},{5,4},{6,7},{7,6},{8,9},{9,8},{10,11... | collective-permute-start | bytes 835592 | tf_op jit(solution)/shard_map/ppermute | solution.py:254
  82.0 1.2 %collective-permute-done.21.other_ref = f32[4,136,128]{2,1,0:T(8,128)S(1)} collective-permute-done((f32[4,136,128]{2,1,0:T(8,128)S(1)}, f32[4,136,128]{2,1,0:T(8,128)S(1)}, u32[]{:S(2)}, u32[]{:S(2)}) %collective-permute-start.21) | collective-permute-done | bytes 278560 | tf_op jit(solution)/shard_map/ppermute | solution.py:254
  83.2 5.3 %update.1 = (f32[1,2,224,2048]{3,2,1,0:T(8,128)}, f32[2,112,128]{2,1,0:T(8,128)}, f32[2,112,128]{2,1,0:T(8,128)}, bf16[2,112,128]{2,1,0:T(8,128)(2,1)}, f32[2,32,2048]{2,1,0:T(8,128)}) custom-call(s32[3]{0:T(128)S(1)} %pad_add_fusion.place_ref, f32[4,136,128]{2,1,0:T(8,128)S(1)} %pad_maximum_fusion.own_ref, ...), custom_call_target="tpu_custom_call" | custom-call | tf_op jit(solution)/shard_map/update/pallas_call | solution.py:218
  (38 shorter events, 4.8 us)
Async XLA Ops:
  4.7 1.8 %copy-start = (f32[2,224,2048]{2,1,0:T(8,128)}, f32[2,224,2048]{2,1,0:T(8,128)S(1)}, u32[]{:S(2)}) copy-start(f32[2,224,2048]{2,1,0:T(8,128)S(1)} %get-tuple-element.10.full_ref) | copy-start | bytes 11010052
  6.5 5.6 %collective-permute-start.2 = (f32[2,32,224]{2,1,0:T(8,128)S(1)}, f32[2,32,224]{2,1,0:T(8,128)S(1)}, u32[]{:S(2)}, u32[]{:S(2)}) collective-permute-start(f32[2,32,224]{2,1,0:T(8,128)S(1)} %get-tuple-element.9), channel_id=1, source_target_pairs={{0,24},{8,16},{16,8},{24,0},{1,25},{9,17},{17,9},{25,1},{2,26},{10... | collective-permute-start | bytes 172040 | tf_op jit(solution)/shard_map/ppermute | solution.py:254
  10.1 4.7 %collective-permute-start.1 = (f32[2,32,224]{2,1,0:T(8,128)S(1)}, f32[2,32,224]{2,1,0:T(8,128)S(1)}, u32[]{:S(2)}, u32[]{:S(2)}) collective-permute-start(f32[2,32,224]{2,1,0:T(8,128)S(1)} %get-tuple-element.9), channel_id=1, source_target_pairs={{0,16},{8,24},{16,0},{24,8},{1,17},{9,25},{17,1},{25,9},{2,18},{10... | collective-permute-start | bytes 172040 | tf_op jit(solution)/shard_map/ppermute | solution.py:254
  10.4 4.4 %collective-permute-start = (f32[2,32,224]{2,1,0:T(8,128)S(1)}, f32[2,32,224]{2,1,0:T(8,128)S(1)}, u32[]{:S(2)}, u32[]{:S(2)}) collective-permute-start(f32[2,32,224]{2,1,0:T(8,128)S(1)} %get-tuple-element.9), channel_id=1, source_target_pairs={{0,8},{8,0},{16,24},{24,16},{1,9},{9,1},{17,25},{25,17},{2,10},{10... | collective-permute-start | bytes 172040 | tf_op jit(solution)/shard_map/ppermute | solution.py:254
  14.8 6.0 %collective-permute-start.5 = (f32[2,32,224]{2,1,0:T(8,128)S(1)}, f32[2,32,224]{2,1,0:T(8,128)S(1)}, u32[]{:S(2)}, u32[]{:S(2)}) collective-permute-start(f32[2,32,224]{2,1,0:T(8,128)S(1)} %add_add_fusion.3), channel_id=1, source_target_pairs={{0,96},{32,64},{64,32},{96,0},{128,224},{160,192},{192,160},{224,1... | collective-permute-start | bytes 172040 | tf_op jit(solution)/shard_map/ppermute | solution.py:254
  19.2 4.8 %collective-permute-start.4 = (f32[2,32,224]{2,1,0:T(8,128)S(1)}, f32[2,32,224]{2,1,0:T(8,128)S(1)}, u32[]{:S(2)}, u32[]{:S(2)}) collective-permute-start(f32[2,32,224]{2,1,0:T(8,128)S(1)} %add_add_fusion.3), channel_id=1, source_target_pairs={{0,64},{32,96},{64,0},{96,32},{128,192},{160,224},{192,128},{224,1... | collective-permute-start | bytes 172040 | tf_op jit(solution)/shard_map/ppermute | solution.py:254
  19.2 4.8 %collective-permute-start.3 = (f32[2,32,224]{2,1,0:T(8,128)S(1)}, f32[2,32,224]{2,1,0:T(8,128)S(1)}, u32[]{:S(2)}, u32[]{:S(2)}) collective-permute-start(f32[2,32,224]{2,1,0:T(8,128)S(1)} %add_add_fusion.3), channel_id=1, source_target_pairs={{0,32},{32,0},{64,96},{96,64},{128,160},{160,128},{192,224},{224,1... | collective-permute-start | bytes 172040 | tf_op jit(solution)/shard_map/ppermute | solution.py:254
  23.9 59.2 %copy-start.4 = (f32[2,112,128]{2,1,0:T(8,128)S(1)}, f32[2,112,128]{2,1,0:T(8,128)}, u32[]{:S(2)}) copy-start(f32[2,112,128]{2,1,0:T(8,128)} %m2_ref.1) | copy-start | bytes 344068
  24.0 59.2 %copy-start.3 = (f32[2,112,128]{2,1,0:T(8,128)S(1)}, f32[2,112,128]{2,1,0:T(8,128)}, u32[]{:S(2)}) copy-start(f32[2,112,128]{2,1,0:T(8,128)} %m1_ref.1) | copy-start | bytes 344068
  24.0 7.9 %collective-permute-start.6 = (f32[2,32,224]{2,1,0:T(8,128)S(1)}, f32[2,32,224]{2,1,0:T(8,128)S(1)}, u32[]{:S(2)}, u32[]{:S(2)}) collective-permute-start(f32[2,32,224]{2,1,0:T(8,128)S(1)} %add_add_fusion.2), channel_id=1, source_target_pairs={{0,128},{32,160},{64,192},{96,224},{128,0},{160,32},{192,64},{224,... | collective-permute-start | bytes 172040 | tf_op jit(solution)/shard_map/ppermute | solution.py:254
  31.9 2.0 %copy-start.1 = (f32[2,224,2048]{2,1,0:T(8,128)S(1)}, f32[2,224,2048]{2,1,0:T(8,128)}, u32[]{:S(2)}) copy-start(f32[2,224,2048]{2,1,0:T(8,128)} %copy-done) | copy-start | bytes 11010052
  34.0 49.2 %copy-start.2 = (f32[2,224,2048]{2,1,0:T(8,128)S(1)}, f32[2,224,2048]{2,1,0:T(8,128)}, u32[]{:S(2)}) copy-start(f32[2,224,2048]{2,1,0:T(8,128)} %copy-done) | copy-start | bytes 11010052
  35.3 4.8 %collective-permute-start.7 = (f32[4,136,128]{2,1,0:T(8,128)S(1)}, f32[4,136,128]{2,1,0:T(8,128)S(1)}, u32[]{:S(2)}, u32[]{:S(2)}) collective-permute-start(f32[4,136,128]{2,1,0:T(8,128)S(1)} %get-tuple-element.12), channel_id=1, source_target_pairs={{0,1},{1,0},{2,3},{3,2},{4,5},{5,4},{6,7},{7,6},{8,9},{9,8},{10,11... | collective-permute-start | bytes 835592 | tf_op jit(solution)/shard_map/ppermute | solution.py:254
  40.2 4.5 %collective-permute-start.10 = (f32[136,128]{1,0:T(8,128)S(1)}, f32[136,128]{1,0:T(8,128)S(1)}, u32[]{:S(2)}, u32[]{:S(2)}) collective-permute-start(f32[136,128]{1,0:T(8,128)S(1)} %get-tuple-element.13), channel_id=1, source_target_pairs={{0,6},{2,4},{4,2},{6,0},{1,7},{3,5},{5,3},{7,1},{8,14},{10,12},{12... | collective-permute-start | bytes 208904 | tf_op jit(solution)/shard_map/ppermute | solution.py:254
  42.7 4.7 %collective-permute-start.9 = (f32[136,128]{1,0:T(8,128)S(1)}, f32[136,128]{1,0:T(8,128)S(1)}, u32[]{:S(2)}, u32[]{:S(2)}) collective-permute-start(f32[136,128]{1,0:T(8,128)S(1)} %get-tuple-element.14), channel_id=1, source_target_pairs={{0,4},{2,6},{4,0},{6,2},{1,5},{3,7},{5,1},{7,3},{8,12},{10,14},{12... | collective-permute-start | bytes 208904 | tf_op jit(solution)/shard_map/ppermute | solution.py:254
  43.3 4.1 %collective-permute-start.8 = (f32[136,128]{1,0:T(8,128)S(1)}, f32[136,128]{1,0:T(8,128)S(1)}, u32[]{:S(2)}, u32[]{:S(2)}) collective-permute-start(f32[136,128]{1,0:T(8,128)S(1)} %get-tuple-element.15), channel_id=1, source_target_pairs={{0,2},{2,0},{4,6},{6,4},{1,3},{3,1},{5,7},{7,5},{8,10},{10,8},{12,... | collective-permute-start | bytes 208904 | tf_op jit(solution)/shard_map/ppermute | solution.py:254
  47.4 4.7 %collective-permute-start.12 = (f32[128,128]{1,0:T(8,128)S(1)}, f32[128,128]{1,0:T(8,128)S(1)}, u32[]{:S(2)}, u32[]{:S(2)}) collective-permute-start(f32[128,128]{1,0:T(8,128)S(1)} %slice.24), channel_id=1, source_target_pairs={{0,16},{8,24},{16,0},{24,8},{1,17},{9,25},{17,1},{25,9},{2,18},{10... | collective-permute-start | bytes 196616 | tf_op jit(solution)/shard_map/ppermute | solution.py:254
  49.6 4.3 %collective-permute-start.13 = (f32[128,128]{1,0:T(8,128)S(1)}, f32[128,128]{1,0:T(8,128)S(1)}, u32[]{:S(2)}, u32[]{:S(2)}) collective-permute-start(f32[128,128]{1,0:T(8,128)S(1)} %slice.24), channel_id=1, source_target_pairs={{0,24},{8,16},{16,8},{24,0},{1,25},{9,17},{17,9},{25,1},{2,26},{10... | collective-permute-start | bytes 196616 | tf_op jit(solution)/shard_map/ppermute | solution.py:254
  49.8 4.1 %collective-permute-start.11 = (f32[128,128]{1,0:T(8,128)S(1)}, f32[128,128]{1,0:T(8,128)S(1)}, u32[]{:S(2)}, u32[]{:S(2)}) collective-permute-start(f32[128,128]{1,0:T(8,128)S(1)} %slice.24), channel_id=1, source_target_pairs={{0,8},{8,0},{16,24},{24,16},{1,9},{9,1},{17,25},{25,17},{2,10},{10... | collective-permute-start | bytes 196616 | tf_op jit(solution)/shard_map/ppermute | solution.py:254
  53.9 5.0 %collective-permute-start.16 = (f32[128,128]{1,0:T(8,128)S(1)}, f32[128,128]{1,0:T(8,128)S(1)}, u32[]{:S(2)}, u32[]{:S(2)}) collective-permute-start(f32[128,128]{1,0:T(8,128)S(1)} %add_add_fusion.1), channel_id=1, source_target_pairs={{0,96},{32,64},{64,32},{96,0},{128,224},{160,192},{192,160},{224,1... | collective-permute-start | bytes 196616 | tf_op jit(solution)/shard_map/ppermute | solution.py:254
  56.2 5.3 %collective-permute-start.15 = (f32[128,128]{1,0:T(8,128)S(1)}, f32[128,128]{1,0:T(8,128)S(1)}, u32[]{:S(2)}, u32[]{:S(2)}) collective-permute-start(f32[128,128]{1,0:T(8,128)S(1)} %add_add_fusion.1), channel_id=1, source_target_pairs={{0,64},{32,96},{64,0},{96,32},{128,192},{160,224},{192,128},{224,1... | collective-permute-start | bytes 196616 | tf_op jit(solution)/shard_map/ppermute | solution.py:254
  56.3 5.1 %collective-permute-start.14 = (f32[128,128]{1,0:T(8,128)S(1)}, f32[128,128]{1,0:T(8,128)S(1)}, u32[]{:S(2)}, u32[]{:S(2)}) collective-permute-start(f32[128,128]{1,0:T(8,128)S(1)} %add_add_fusion.1), channel_id=1, source_target_pairs={{0,32},{32,0},{64,96},{96,64},{128,160},{160,128},{192,224},{224,1... | collective-permute-start | bytes 196616 | tf_op jit(solution)/shard_map/ppermute | solution.py:254
  61.4 7.8 %collective-permute-start.17 = (f32[128,128]{1,0:T(8,128)S(1)}, f32[128,128]{1,0:T(8,128)S(1)}, u32[]{:S(2)}, u32[]{:S(2)}) collective-permute-start(f32[128,128]{1,0:T(8,128)S(1)} %add_add_fusion.a_ref), channel_id=1, source_target_pairs={{0,128},{32,160},{64,192},{96,224},{128,0},{160,32},{192,64},{224,... | collective-permute-start | bytes 196616 | tf_op jit(solution)/shard_map/ppermute | solution.py:254
  69.5 5.5 %collective-permute-start.20 = (f32[136,128]{1,0:T(8,128)S(1)}, f32[136,128]{1,0:T(8,128)S(1)}, u32[]{:S(2)}, u32[]{:S(2)}) collective-permute-start(f32[136,128]{1,0:T(8,128)S(1)} %finished_piece.1), channel_id=1, source_target_pairs={{0,6},{2,4},{4,2},{6,0},{1,7},{3,5},{5,3},{7,1},{8,14},{10,12},{12... | collective-permute-start | bytes 208904 | tf_op jit(solution)/shard_map/ppermute | solution.py:254
  73.0 4.7 %collective-permute-start.19 = (f32[136,128]{1,0:T(8,128)S(1)}, f32[136,128]{1,0:T(8,128)S(1)}, u32[]{:S(2)}, u32[]{:S(2)}) collective-permute-start(f32[136,128]{1,0:T(8,128)S(1)} %finished_piece.1), channel_id=1, source_target_pairs={{0,4},{2,6},{4,0},{6,2},{1,5},{3,7},{5,1},{7,3},{8,12},{10,14},{12... | collective-permute-start | bytes 208904 | tf_op jit(solution)/shard_map/ppermute | solution.py:254
  73.5 4.1 %collective-permute-start.18 = (f32[136,128]{1,0:T(8,128)S(1)}, f32[136,128]{1,0:T(8,128)S(1)}, u32[]{:S(2)}, u32[]{:S(2)}) collective-permute-start(f32[136,128]{1,0:T(8,128)S(1)} %finished_piece.1), channel_id=1, source_target_pairs={{0,2},{2,0},{4,6},{6,4},{1,3},{3,1},{5,7},{7,5},{8,10},{10,8},{12,... | collective-permute-start | bytes 208904 | tf_op jit(solution)/shard_map/ppermute | solution.py:254
  77.7 5.5 %collective-permute-start.21 = (f32[4,136,128]{2,1,0:T(8,128)S(1)}, f32[4,136,128]{2,1,0:T(8,128)S(1)}, u32[]{:S(2)}, u32[]{:S(2)}) collective-permute-start(f32[4,136,128]{2,1,0:T(8,128)S(1)} %pad_maximum_fusion.own_ref), channel_id=1, source_target_pairs={{0,1},{1,0},{2,3},{3,2},{4,5},{5,4},{6,7},{7,6},{8,9},{9,8},{10,11... | collective-permute-start | bytes 835592 | tf_op jit(solution)/shard_map/ppermute | solution.py:254

commit v3 on v2

--- a/solution.py
+++ b/solution.py
@@ -78,11 +78,11 @@
     )(in_hbm(grads), in_hbm(errors), in_hbm(q_prev))
 
 
-def right_kernel(replicas, place_ref, p_ref, full_ref, keep_ref, send_ref):
+def right_kernel(replicas, p_ref, full_ref, keep_ref, send_ref):
     slots, height, _ = keep_ref.shape
     tiles = (height - 8) // RANK
     width = tiles * LANES
-    x, core = place_ref[1], place_ref[2]
+    x, core = lax.axis_index("x"), lax.axis_index("c")
     for out_ref, m in ((send_ref, 1 - core), (keep_ref, core)):
         p = p_ref[m] * (1.0 / replicas)
         p_hi, p_lo = split(p)
@@ -98,17 +98,17 @@
             out_ref[slot, tiles * RANK :, :] = gram
 
 
-def right_terms(place, p_sum, full, replicas, slots):
+def right_terms(p_sum, full, replicas, slots):
     columns = full.shape[2]
     piece = jax.ShapeDtypeStruct((slots, columns // slots // LANES * RANK + 8, LANES), F32)
     return pl.pallas_call(
         functools.partial(right_kernel, replicas),
-        in_specs=[pl.BlockSpec(memory_space=pltpu.SMEM)] + [pl.BlockSpec(memory_space=pltpu.VMEM)] * 2,
+        in_specs=[pl.BlockSpec(memory_space=pltpu.VMEM)] * 2,
         out_specs=[pl.BlockSpec(memory_space=pltpu.VMEM)] * 2,
         out_shape=[piece, piece],
         compiler_params=pltpu.CompilerParams(vmem_limit_bytes=VMEM_LIMIT),
         name="right_terms",
-    )(place, p_sum, full)
+    )(p_sum, full)
 
 
 def factor_kernel(sum_ref, out_ref):
@@ -163,12 +163,12 @@
     )(a, b, inverse)
 
 
-def update_kernel(replicas, place_ref, own_ref, other_ref, p_ref, full_ref, m1_ref, m2_ref, err_ref, n1_ref, n2_ref, up_ref, q_ref, hat_ref, flat_ref):
+def update_kernel(replicas, own_ref, other_ref, p_ref, full_ref, m1_ref, m2_ref, err_ref, n1_ref, n2_ref, up_ref, q_ref, hat_ref, flat_ref):
     m, step = pl.program_id(0), pl.program_id(1)
     rows, width = err_ref.shape[2:]
     slots, height, _ = own_ref.shape
     tiles = (height - 8) // RANK
-    x, mine_here = place_ref[1], m == place_ref[2]
+    x, mine_here = lax.axis_index("x"), m == lax.axis_index("c")
 
     def piece(block):
         return jnp.where(mine_here, own_ref[block ^ x], other_ref[block ^ x])
@@ -185,7 +185,7 @@
         h_hi, h_lo = split(hat)
         hat_ref[...] = jnp.concatenate([h_hi, h_lo, h_hi], axis=1)
         mine = flat_ref.shape[0]
-        at = lax.broadcasted_iota(jnp.int32, (8, rows), 0) + place_ref[0] * mine
+        at = lax.broadcasted_iota(jnp.int32, (8, rows), 0) + lax.axis_index(("z", "y")) * mine
         chosen = (lax.broadcasted_iota(jnp.int32, (8, rows), 1) == at).astype(F32)
         own = dot(chosen, hat, ((1,), (0,)), lax.Precision.HIGHEST)
         o_hi, o_lo = split(own)
@@ -210,7 +210,7 @@
     err_ref[0, 0] = full_ref[m, :, pl.ds(pl.multiple_of(step * width, width), width)] - approx
 
 
-def update(place, own, other, p_sum, full, moment1, moment2, replicas, blocks=2):
+def update(own, other, p_sum, full, moment1, moment2, replicas, blocks=2):
     projections, rows, columns = full.shape
     width, tiles = columns // blocks, columns // LANES
     state = moment1.shape[1]
@@ -219,7 +219,6 @@
         functools.partial(update_kernel, replicas),
         grid=(projections, blocks),
         in_specs=[
-            pl.BlockSpec(memory_space=pltpu.SMEM),
             pl.BlockSpec(memory_space=pltpu.VMEM),
             pl.BlockSpec(memory_space=pltpu.VMEM),
             pl.BlockSpec((1, RANK, rows), lambda m, k: (m, 0, 0)),
@@ -247,7 +246,7 @@
         ],
         compiler_params=pltpu.CompilerParams(vmem_limit_bytes=VMEM_LIMIT),
         name="update",
-    )(place, own, other, p_sum, full, moment1, moment2)
+    )(own, other, p_sum, full, moment1, moment2)
 
 
 def swap(value, axis, bit):
@@ -258,27 +257,27 @@
     return (values[0] + swap(values[1], axis, 1)) + (swap(values[2], axis, 2) + swap(values[3], axis, 3))
 
 
-def sum_replicas(value):
+def sum_replicas(value, other=None):
     value = four([value] * 4, "y")
+    if other is not None:
+        value, other = lax.optimization_barrier((value, other))
     value = four([value] * 4, "z")
-    return value, swap(value, "z", 4)
+    return value, swap(value, "z", 6), other
 
 
 def shards(grads, errors, q_prev, moment1, moment2):
     replicas, slots = lax.axis_size(("z", "y")), lax.axis_size("x")
-    place = jnp.stack([lax.axis_index(("z", "y")), lax.axis_index("x"), lax.axis_index("c")])
     full, p_local = left_factors(grads, errors, q_prev)
-    p_low, p_high = sum_replicas(p_local)
+    p_low, p_high, _ = sum_replicas(p_local)
     p_sum = p_low + p_high
 
-    keep, send = right_terms(place, p_sum, full, replicas, slots)
+    keep, send = right_terms(p_sum, full, replicas, slots)
     terms = keep + swap(send, "c", 1)
     total = four([terms[i] for i in range(slots)], "x")
-    inverse = inverse_factor(total)
-    piece = finished_piece(*sum_replicas(total[:-8]), inverse, replicas)
+    piece = finished_piece(*sum_replicas(total[:-8], inverse_factor(total)), replicas)
     own = jnp.stack([piece] + [swap(piece, "x", i) for i in range(1, slots)])
     other = swap(own, "c", 1)
-    return tuple(update(place, own, other, p_sum, full, moment1, moment2, replicas))
+    return tuple(update(own, other, p_sum, full, moment1, moment2, replicas))
 
 
 def solution(mesh):

time: 88.6 us -> 79 us (0.89)
  local copies, waits for them, and re-layouts: 3.9 us -> 0.04 us
  starting transfers between devices: 40.7 us -> 37.7 us
  waiting for transfers between devices: 29.2 us -> 27.6 us
  Pallas kernels: 13.7 us -> 12.6 us
    unnamed x10 -> x4, local copies, waits for them, and re-layouts: 3.88 us -> 0.01 us
    ppermute x22, starting transfers between devices: 40.7 us -> 37.7 us  [swap(): lax.ppermute(value, axis, [(i, i ^ bit) for i in range(lax.axis_size(axis...]
    ppermute x22, waiting for transfers between devices: 29.2 us -> 27.6 us  [swap(): lax.ppermute(value, axis, [(i, i ^ bit) for i in range(lax.axis_size(axis...]
  transfers between devices with their start and end apart: 22 -> 22, of which waited for: 16 -> 16; matrix products, arithmetic and copies ran while one was open for 0% -> 0% of each run, Pallas kernels for 3% -> 4%
where the time goes in v3:
time: 79 us; the launch traced here: 78.8 us
  starting transfers between devices  37.7 us (48%)
  waiting for transfers between devices  27.6 us (35%)
  Pallas kernels  12.6 us (16%)
    ppermute x22, starting transfers between devices, swap(): lax.ppermute(value, axis, [(i, i ^ bit) for i in range(lax.axis_size(axis...  37.7 us
    ppermute x22, waiting for transfers between devices, swap(): lax.ppermute(value, axis, [(i, i ^ bit) for i in range(lax.axis_size(axis...  27.6 us
    pallas_call x1, Pallas kernels, update(): pl.pallas_call(functools.partial(update_kernel, replicas), grid=(projecti...  4.72 us
    pallas_call x1, Pallas kernels, left_factors(): pl.pallas_call(left_kernel, grid=(projections, blocks), in_specs=[pl.Bloc...  4.05 us
    pallas_call x1, Pallas kernels, inverse_factor(): pl.pallas_call(factor_kernel, in_specs=[pl.BlockSpec(memory_space=pltpu.V...  2.85 us
  transfers between devices with their start and end apart: 22, of which 16 were waited for; matrix products, arithmetic and copies ran while one was open for 0% of the time, Pallas kernels for 4%

profile of v3, /device:TPU:1, one launch (start us, length us, event | category | flops | bytes accessed | tf_op | source)
XLA Modules:
  0.0 78.8 jit_solution(8036698319121488280)
XLA Ops:
  0.6 4.0 %left_factors.1 = (f32[2,224,2048]{2,1,0:T(8,128)S(1)}, f32[2,32,224]{2,1,0:T(8,128)S(1)}) custom-call(bf16[1,2,224,2048]{3,2,1,0:T(8,128)(2,1)} %grads_ref.1, f32[1,2,224,2048]{3,2,1,0:T(8,128)} %errors_ref.1, f32[2,32,2048]{2,1,0:T(8,128)} %q_ref.1), custom_call_target="tpu_custom_call" | custom-call | tf_op jit(solution)/shard_map/left_factors/pallas_call | solution.py:60
  4.7 3.6 %collective-permute-start.2 = (f32[2,32,224]{2,1,0:T(8,128)S(1)}, f32[2,32,224]{2,1,0:T(8,128)S(1)}, u32[]{:S(2)}, u32[]{:S(2)}) collective-permute-start(f32[2,32,224]{2,1,0:T(8,128)S(1)} %get-tuple-element.11), channel_id=1, source_target_pairs={{0,24},{8,16},{16,8},{24,0},{1,25},{9,17},{17,9},{25,1},{2,26},{10... | collective-permute-start | bytes 172040 | tf_op jit(solution)/shard_map/ppermute | solution.py:253
  9.0 1.0 %collective-permute-done.2 = f32[2,32,224]{2,1,0:T(8,128)S(1)} collective-permute-done((f32[2,32,224]{2,1,0:T(8,128)S(1)}, f32[2,32,224]{2,1,0:T(8,128)S(1)}, u32[]{:S(2)}, u32[]{:S(2)}) %collective-permute-start.2) | collective-permute-done | bytes 57376 | tf_op jit(solution)/shard_map/ppermute | solution.py:253
  10.0 3.1 %collective-permute-done.1 = f32[2,32,224]{2,1,0:T(8,128)S(1)} collective-permute-done((f32[2,32,224]{2,1,0:T(8,128)S(1)}, f32[2,32,224]{2,1,0:T(8,128)S(1)}, u32[]{:S(2)}, u32[]{:S(2)}) %collective-permute-start.1) | collective-permute-done | bytes 57376 | tf_op jit(solution)/shard_map/ppermute | solution.py:253
  13.1 4.3 %collective-permute-start.5 = (f32[2,32,224]{2,1,0:T(8,128)S(1)}, f32[2,32,224]{2,1,0:T(8,128)S(1)}, u32[]{:S(2)}, u32[]{:S(2)}) collective-permute-start(f32[2,32,224]{2,1,0:T(8,128)S(1)} %add_add_fusion.3), channel_id=1, source_target_pairs={{0,96},{32,64},{64,32},{96,0},{128,224},{160,192},{192,160},{224,1... | collective-permute-start | bytes 172040 | tf_op jit(solution)/shard_map/ppermute | solution.py:253
  17.8 1.3 %collective-permute-done.5 = f32[2,32,224]{2,1,0:T(8,128)S(1)} collective-permute-done((f32[2,32,224]{2,1,0:T(8,128)S(1)}, f32[2,32,224]{2,1,0:T(8,128)S(1)}, u32[]{:S(2)}, u32[]{:S(2)}) %collective-permute-start.5) | collective-permute-done | bytes 57376 | tf_op jit(solution)/shard_map/ppermute | solution.py:253
  19.1 3.1 %collective-permute-done.4 = f32[2,32,224]{2,1,0:T(8,128)S(1)} collective-permute-done((f32[2,32,224]{2,1,0:T(8,128)S(1)}, f32[2,32,224]{2,1,0:T(8,128)S(1)}, u32[]{:S(2)}, u32[]{:S(2)}) %collective-permute-start.4) | collective-permute-done | bytes 57376 | tf_op jit(solution)/shard_map/ppermute | solution.py:253
  22.2 3.3 %collective-permute-start.6 = (f32[2,32,224]{2,1,0:T(8,128)S(1)}, f32[2,32,224]{2,1,0:T(8,128)S(1)}, u32[]{:S(2)}, u32[]{:S(2)}) collective-permute-start(f32[2,32,224]{2,1,0:T(8,128)S(1)} %add_add_fusion.2), channel_id=1, source_target_pairs={{0,192},{32,224},{64,128},{96,160},{128,64},{160,96},{192,0},{224,... | collective-permute-start | bytes 172040 | tf_op jit(solution)/shard_map/ppermute | solution.py:253
  25.6 2.6 %collective-permute-done.6 = f32[2,32,224]{2,1,0:T(8,128)S(1)} collective-permute-done((f32[2,32,224]{2,1,0:T(8,128)S(1)}, f32[2,32,224]{2,1,0:T(8,128)S(1)}, u32[]{:S(2)}, u32[]{:S(2)}) %collective-permute-start.6) | collective-permute-done | bytes 57376 | tf_op jit(solution)/shard_map/ppermute | solution.py:253
  28.2 0.8 right_terms.1
  29.0 3.4 %collective-permute-start.7 = (f32[4,136,128]{2,1,0:T(8,128)S(1)}, f32[4,136,128]{2,1,0:T(8,128)S(1)}, u32[]{:S(2)}, u32[]{:S(2)}) collective-permute-start(f32[4,136,128]{2,1,0:T(8,128)S(1)} %get-tuple-element.14), channel_id=1, source_target_pairs={{0,1},{1,0},{2,3},{3,2},{4,5},{5,4},{6,7},{7,6},{8,9},{9,8},{10,11... | collective-permute-start | bytes 835592 | tf_op jit(solution)/shard_map/ppermute | solution.py:253
  32.4 1.2 %collective-permute-done.7 = f32[4,136,128]{2,1,0:T(8,128)S(1)} collective-permute-done((f32[4,136,128]{2,1,0:T(8,128)S(1)}, f32[4,136,128]{2,1,0:T(8,128)S(1)}, u32[]{:S(2)}, u32[]{:S(2)}) %collective-permute-start.7) | collective-permute-done | bytes 278560 | tf_op jit(solution)/shard_map/ppermute | solution.py:253
  33.7 2.6 %collective-permute-start.10 = (f32[136,128]{1,0:T(8,128)S(1)}, f32[136,128]{1,0:T(8,128)S(1)}, u32[]{:S(2)}, u32[]{:S(2)}) collective-permute-start(f32[136,128]{1,0:T(8,128)S(1)} %get-tuple-element.17), channel_id=1, source_target_pairs={{0,6},{2,4},{4,2},{6,0},{1,7},{3,5},{5,3},{7,1},{8,14},{10,12},{12... | collective-permute-start | bytes 208904 | tf_op jit(solution)/shard_map/ppermute | solution.py:253
  37.0 1.1 %collective-permute-done.10 = f32[136,128]{1,0:T(8,128)S(1)} collective-permute-done((f32[136,128]{1,0:T(8,128)S(1)}, f32[136,128]{1,0:T(8,128)S(1)}, u32[]{:S(2)}, u32[]{:S(2)}) %collective-permute-start.10) | collective-permute-done | bytes 69664 | tf_op jit(solution)/shard_map/ppermute | solution.py:253
  38.1 2.8 %collective-permute-done.9 = f32[136,128]{1,0:T(8,128)S(1)} collective-permute-done((f32[136,128]{1,0:T(8,128)S(1)}, f32[136,128]{1,0:T(8,128)S(1)}, u32[]{:S(2)}, u32[]{:S(2)}) %collective-permute-start.9) | collective-permute-done | bytes 69664 | tf_op jit(solution)/shard_map/ppermute | solution.py:253
  41.0 1.8 %collective-permute-start.12 = (f32[128,128]{1,0:T(8,128)S(1)}, f32[128,128]{1,0:T(8,128)S(1)}, u32[]{:S(2)}, u32[]{:S(2)}) collective-permute-start(f32[128,128]{1,0:T(8,128)S(1)} %slice.24), channel_id=1, source_target_pairs={{0,16},{8,24},{16,0},{24,8},{1,17},{9,25},{17,1},{25,9},{2,18},{10... | collective-permute-start | bytes 196616 | tf_op jit(solution)/shard_map/ppermute | solution.py:253
  42.8 1.0 %collective-permute-start.13 = (f32[128,128]{1,0:T(8,128)S(1)}, f32[128,128]{1,0:T(8,128)S(1)}, u32[]{:S(2)}, u32[]{:S(2)}) collective-permute-start(f32[128,128]{1,0:T(8,128)S(1)} %slice.24), channel_id=1, source_target_pairs={{0,24},{8,16},{16,8},{24,0},{1,25},{9,17},{17,9},{25,1},{2,26},{10... | collective-permute-start | bytes 196616 | tf_op jit(solution)/shard_map/ppermute | solution.py:253
  43.8 2.8 %inverse_factor.1.inverse_ref = f32[8,128]{1,0:T(8,128)S(1)} custom-call(f32[136,128]{1,0:T(8,128)S(1)} %fusion.1.sum_ref), custom_call_target="tpu_custom_call" | custom-call | flops 4000000 | bytes 4000000 | tf_op jit(solution)/shard_map/inverse_factor/pallas_call | solution.py:133
  47.5 1.5 %collective-permute-start.16 = (f32[128,128]{1,0:T(8,128)S(1)}, f32[128,128]{1,0:T(8,128)S(1)}, u32[]{:S(2)}, u32[]{:S(2)}) collective-permute-start(f32[128,128]{1,0:T(8,128)S(1)} %add_add_fusion.1), channel_id=1, source_target_pairs={{0,96},{32,64},{64,32},{96,0},{128,224},{160,192},{192,160},{224,1... | collective-permute-start | bytes 196616 | tf_op jit(solution)/shard_map/ppermute | solution.py:253
  49.1 1.1 %collective-permute-start.15 = (f32[128,128]{1,0:T(8,128)S(1)}, f32[128,128]{1,0:T(8,128)S(1)}, u32[]{:S(2)}, u32[]{:S(2)}) collective-permute-start(f32[128,128]{1,0:T(8,128)S(1)} %add_add_fusion.1), channel_id=1, source_target_pairs={{0,64},{32,96},{64,0},{96,32},{128,192},{160,224},{192,128},{224,1... | collective-permute-start | bytes 196616 | tf_op jit(solution)/shard_map/ppermute | solution.py:253
  50.2 1.0 %collective-permute-start.14 = (f32[128,128]{1,0:T(8,128)S(1)}, f32[128,128]{1,0:T(8,128)S(1)}, u32[]{:S(2)}, u32[]{:S(2)}) collective-permute-start(f32[128,128]{1,0:T(8,128)S(1)} %add_add_fusion.1), channel_id=1, source_target_pairs={{0,32},{32,0},{64,96},{96,64},{128,160},{160,128},{192,224},{224,1... | collective-permute-start | bytes 196616 | tf_op jit(solution)/shard_map/ppermute | solution.py:253
  51.2 1.4 %collective-permute-done.16 = f32[128,128]{1,0:T(8,128)S(1)} collective-permute-done((f32[128,128]{1,0:T(8,128)S(1)}, f32[128,128]{1,0:T(8,128)S(1)}, u32[]{:S(2)}, u32[]{:S(2)}) %collective-permute-start.16) | collective-permute-done | bytes 65568 | tf_op jit(solution)/shard_map/ppermute | solution.py:253
  52.6 1.4 %collective-permute-done.15 = f32[128,128]{1,0:T(8,128)S(1)} collective-permute-done((f32[128,128]{1,0:T(8,128)S(1)}, f32[128,128]{1,0:T(8,128)S(1)}, u32[]{:S(2)}, u32[]{:S(2)}) %collective-permute-start.15) | collective-permute-done | bytes 65568 | tf_op jit(solution)/shard_map/ppermute | solution.py:253
  54.0 3.5 %collective-permute-start.17 = (f32[128,128]{1,0:T(8,128)S(1)}, f32[128,128]{1,0:T(8,128)S(1)}, u32[]{:S(2)}, u32[]{:S(2)}) collective-permute-start(f32[128,128]{1,0:T(8,128)S(1)} %add_add_fusion.a_ref), channel_id=1, source_target_pairs={{0,192},{32,224},{64,128},{96,160},{128,64},{160,96},{192,0},{224,... | collective-permute-start | bytes 196616 | tf_op jit(solution)/shard_map/ppermute | solution.py:253
  57.5 2.7 %collective-permute-done.17.b_ref = f32[128,128]{1,0:T(8,128)S(1)} collective-permute-done((f32[128,128]{1,0:T(8,128)S(1)}, f32[128,128]{1,0:T(8,128)S(1)}, u32[]{:S(2)}, u32[]{:S(2)}) %collective-permute-start.17) | collective-permute-done | bytes 65568 | tf_op jit(solution)/shard_map/ppermute | solution.py:253
  60.4 2.8 %collective-permute-start.20 = (f32[136,128]{1,0:T(8,128)S(1)}, f32[136,128]{1,0:T(8,128)S(1)}, u32[]{:S(2)}, u32[]{:S(2)}) collective-permute-start(f32[136,128]{1,0:T(8,128)S(1)} %finished_piece.1), channel_id=1, source_target_pairs={{0,6},{2,4},{4,2},{6,0},{1,7},{3,5},{5,3},{7,1},{8,14},{10,12},{12... | collective-permute-start | bytes 208904 | tf_op jit(solution)/shard_map/ppermute | solution.py:253
  63.2 0.7 collective-permute-start.19
  63.9 1.3 %collective-permute-done.20 = f32[136,128]{1,0:T(8,128)S(1)} collective-permute-done((f32[136,128]{1,0:T(8,128)S(1)}, f32[136,128]{1,0:T(8,128)S(1)}, u32[]{:S(2)}, u32[]{:S(2)}) %collective-permute-start.20) | collective-permute-done | bytes 69664 | tf_op jit(solution)/shard_map/ppermute | solution.py:253
  65.2 2.7 %collective-permute-done.19 = f32[136,128]{1,0:T(8,128)S(1)} collective-permute-done((f32[136,128]{1,0:T(8,128)S(1)}, f32[136,128]{1,0:T(8,128)S(1)}, u32[]{:S(2)}, u32[]{:S(2)}) %collective-permute-start.19) | collective-permute-done | bytes 69664 | tf_op jit(solution)/shard_map/ppermute | solution.py:253
  67.9 5.0 %collective-permute-start.21 = (f32[4,136,128]{2,1,0:T(8,128)S(1)}, f32[4,136,128]{2,1,0:T(8,128)S(1)}, u32[]{:S(2)}, u32[]{:S(2)}) collective-permute-start(f32[4,136,128]{2,1,0:T(8,128)S(1)} %pad_maximum_fusion.own_ref), channel_id=1, source_target_pairs={{0,1},{1,0},{2,3},{3,2},{4,5},{5,4},{6,7},{7,6},{8,9},{9,8},{10,11... | collective-permute-start | bytes 835592 | tf_op jit(solution)/shard_map/ppermute | solution.py:253
  72.9 1.2 %collective-permute-done.21.other_ref = f32[4,136,128]{2,1,0:T(8,128)S(1)} collective-permute-done((f32[4,136,128]{2,1,0:T(8,128)S(1)}, f32[4,136,128]{2,1,0:T(8,128)S(1)}, u32[]{:S(2)}, u32[]{:S(2)}) %collective-permute-start.21) | collective-permute-done | bytes 278560 | tf_op jit(solution)/shard_map/ppermute | solution.py:253
  74.1 4.7 %update.1 = (f32[1,2,224,2048]{3,2,1,0:T(8,128)}, f32[2,112,128]{2,1,0:T(8,128)}, f32[2,112,128]{2,1,0:T(8,128)}, bf16[2,112,128]{2,1,0:T(8,128)(2,1)}, f32[2,32,2048]{2,1,0:T(8,128)}) custom-call(f32[4,136,128]{2,1,0:T(8,128)S(1)} %pad_maximum_fusion.own_ref, f32[4,136,128]{2,1,0:T(8,128)S(1)} %collective-permute-done.21.other_ref, ...), custom_call_target="tpu_custom_call" | custom-call | tf_op jit(solution)/shard_map/update/pallas_call | solution.py:218
  (31 shorter events, 3.2 us)
Async XLA Ops:
  4.7 5.3 %collective-permute-start.2 = (f32[2,32,224]{2,1,0:T(8,128)S(1)}, f32[2,32,224]{2,1,0:T(8,128)S(1)}, u32[]{:S(2)}, u32[]{:S(2)}) collective-permute-start(f32[2,32,224]{2,1,0:T(8,128)S(1)} %get-tuple-element.11), channel_id=1, source_target_pairs={{0,24},{8,16},{16,8},{24,0},{1,25},{9,17},{17,9},{25,1},{2,26},{10... | collective-permute-start | bytes 172040 | tf_op jit(solution)/shard_map/ppermute | solution.py:253
  8.3 4.7 %collective-permute-start.1 = (f32[2,32,224]{2,1,0:T(8,128)S(1)}, f32[2,32,224]{2,1,0:T(8,128)S(1)}, u32[]{:S(2)}, u32[]{:S(2)}) collective-permute-start(f32[2,32,224]{2,1,0:T(8,128)S(1)} %get-tuple-element.11), channel_id=1, source_target_pairs={{0,16},{8,24},{16,0},{24,8},{1,17},{9,25},{17,1},{25,9},{2,18},{10... | collective-permute-start | bytes 172040 | tf_op jit(solution)/shard_map/ppermute | solution.py:253
  8.7 4.4 %collective-permute-start = (f32[2,32,224]{2,1,0:T(8,128)S(1)}, f32[2,32,224]{2,1,0:T(8,128)S(1)}, u32[]{:S(2)}, u32[]{:S(2)}) collective-permute-start(f32[2,32,224]{2,1,0:T(8,128)S(1)} %get-tuple-element.11), channel_id=1, source_target_pairs={{0,8},{8,0},{16,24},{24,16},{1,9},{9,1},{17,25},{25,17},{2,10},{10... | collective-permute-start | bytes 172040 | tf_op jit(solution)/shard_map/ppermute | solution.py:253
  13.1 61.0 %copy-start = (f32[2,112,128]{2,1,0:T(8,128)S(1)}, f32[2,112,128]{2,1,0:T(8,128)}, u32[]{:S(2)}) copy-start(f32[2,112,128]{2,1,0:T(8,128)} %m1_ref.1) | copy-start | bytes 344068
  13.1 61.0 %copy-start.1 = (f32[2,112,128]{2,1,0:T(8,128)S(1)}, f32[2,112,128]{2,1,0:T(8,128)}, u32[]{:S(2)}) copy-start(f32[2,112,128]{2,1,0:T(8,128)} %m2_ref.1) | copy-start | bytes 344068
  13.1 6.0 %collective-permute-start.5 = (f32[2,32,224]{2,1,0:T(8,128)S(1)}, f32[2,32,224]{2,1,0:T(8,128)S(1)}, u32[]{:S(2)}, u32[]{:S(2)}) collective-permute-start(f32[2,32,224]{2,1,0:T(8,128)S(1)} %add_add_fusion.3), channel_id=1, source_target_pairs={{0,96},{32,64},{64,32},{96,0},{128,224},{160,192},{192,160},{224,1... | collective-permute-start | bytes 172040 | tf_op jit(solution)/shard_map/ppermute | solution.py:253
  17.4 4.8 %collective-permute-start.4 = (f32[2,32,224]{2,1,0:T(8,128)S(1)}, f32[2,32,224]{2,1,0:T(8,128)S(1)}, u32[]{:S(2)}, u32[]{:S(2)}) collective-permute-start(f32[2,32,224]{2,1,0:T(8,128)S(1)} %add_add_fusion.3), channel_id=1, source_target_pairs={{0,64},{32,96},{64,0},{96,32},{128,192},{160,224},{192,128},{224,1... | collective-permute-start | bytes 172040 | tf_op jit(solution)/shard_map/ppermute | solution.py:253
  17.4 4.8 %collective-permute-start.3 = (f32[2,32,224]{2,1,0:T(8,128)S(1)}, f32[2,32,224]{2,1,0:T(8,128)S(1)}, u32[]{:S(2)}, u32[]{:S(2)}) collective-permute-start(f32[2,32,224]{2,1,0:T(8,128)S(1)} %add_add_fusion.3), channel_id=1, source_target_pairs={{0,32},{32,0},{64,96},{96,64},{128,160},{160,128},{192,224},{224,1... | collective-permute-start | bytes 172040 | tf_op jit(solution)/shard_map/ppermute | solution.py:253
  22.2 6.0 %collective-permute-start.6 = (f32[2,32,224]{2,1,0:T(8,128)S(1)}, f32[2,32,224]{2,1,0:T(8,128)S(1)}, u32[]{:S(2)}, u32[]{:S(2)}) collective-permute-start(f32[2,32,224]{2,1,0:T(8,128)S(1)} %add_add_fusion.2), channel_id=1, source_target_pairs={{0,192},{32,224},{64,128},{96,160},{128,64},{160,96},{192,0},{224,... | collective-permute-start | bytes 172040 | tf_op jit(solution)/shard_map/ppermute | solution.py:253
  29.0 4.6 %collective-permute-start.7 = (f32[4,136,128]{2,1,0:T(8,128)S(1)}, f32[4,136,128]{2,1,0:T(8,128)S(1)}, u32[]{:S(2)}, u32[]{:S(2)}) collective-permute-start(f32[4,136,128]{2,1,0:T(8,128)S(1)} %get-tuple-element.14), channel_id=1, source_target_pairs={{0,1},{1,0},{2,3},{3,2},{4,5},{5,4},{6,7},{7,6},{8,9},{9,8},{10,11... | collective-permute-start | bytes 835592 | tf_op jit(solution)/shard_map/ppermute | solution.py:253
  33.7 4.5 %collective-permute-start.10 = (f32[136,128]{1,0:T(8,128)S(1)}, f32[136,128]{1,0:T(8,128)S(1)}, u32[]{:S(2)}, u32[]{:S(2)}) collective-permute-start(f32[136,128]{1,0:T(8,128)S(1)} %get-tuple-element.17), channel_id=1, source_target_pairs={{0,6},{2,4},{4,2},{6,0},{1,7},{3,5},{5,3},{7,1},{8,14},{10,12},{12... | collective-permute-start | bytes 208904 | tf_op jit(solution)/shard_map/ppermute | solution.py:253
  36.3 4.7 %collective-permute-start.9 = (f32[136,128]{1,0:T(8,128)S(1)}, f32[136,128]{1,0:T(8,128)S(1)}, u32[]{:S(2)}, u32[]{:S(2)}) collective-permute-start(f32[136,128]{1,0:T(8,128)S(1)} %get-tuple-element.18), channel_id=1, source_target_pairs={{0,4},{2,6},{4,0},{6,2},{1,5},{3,7},{5,1},{7,3},{8,12},{10,14},{12... | collective-permute-start | bytes 208904 | tf_op jit(solution)/shard_map/ppermute | solution.py:253
  36.8 4.1 %collective-permute-start.8 = (f32[136,128]{1,0:T(8,128)S(1)}, f32[136,128]{1,0:T(8,128)S(1)}, u32[]{:S(2)}, u32[]{:S(2)}) collective-permute-start(f32[136,128]{1,0:T(8,128)S(1)} %get-tuple-element.19), channel_id=1, source_target_pairs={{0,2},{2,0},{4,6},{6,4},{1,3},{3,1},{5,7},{7,5},{8,10},{10,8},{12,... | collective-permute-start | bytes 208904 | tf_op jit(solution)/shard_map/ppermute | solution.py:253
  41.0 5.7 %collective-permute-start.12 = (f32[128,128]{1,0:T(8,128)S(1)}, f32[128,128]{1,0:T(8,128)S(1)}, u32[]{:S(2)}, u32[]{:S(2)}) collective-permute-start(f32[128,128]{1,0:T(8,128)S(1)} %slice.24), channel_id=1, source_target_pairs={{0,16},{8,24},{16,0},{24,8},{1,17},{9,25},{17,1},{25,9},{2,18},{10... | collective-permute-start | bytes 196616 | tf_op jit(solution)/shard_map/ppermute | solution.py:253
  42.8 4.3 %collective-permute-start.13 = (f32[128,128]{1,0:T(8,128)S(1)}, f32[128,128]{1,0:T(8,128)S(1)}, u32[]{:S(2)}, u32[]{:S(2)}) collective-permute-start(f32[128,128]{1,0:T(8,128)S(1)} %slice.24), channel_id=1, source_target_pairs={{0,24},{8,16},{16,8},{24,0},{1,25},{9,17},{17,9},{25,1},{2,26},{10... | collective-permute-start | bytes 196616 | tf_op jit(solution)/shard_map/ppermute | solution.py:253
  43.8 3.8 %collective-permute-start.11 = (f32[128,128]{1,0:T(8,128)S(1)}, f32[128,128]{1,0:T(8,128)S(1)}, u32[]{:S(2)}, u32[]{:S(2)}) collective-permute-start(f32[128,128]{1,0:T(8,128)S(1)} %slice.24), channel_id=1, source_target_pairs={{0,8},{8,0},{16,24},{24,16},{1,9},{9,1},{17,25},{25,17},{2,10},{10... | collective-permute-start | bytes 196616 | tf_op jit(solution)/shard_map/ppermute | solution.py:253
  47.5 5.0 %collective-permute-start.16 = (f32[128,128]{1,0:T(8,128)S(1)}, f32[128,128]{1,0:T(8,128)S(1)}, u32[]{:S(2)}, u32[]{:S(2)}) collective-permute-start(f32[128,128]{1,0:T(8,128)S(1)} %add_add_fusion.1), channel_id=1, source_target_pairs={{0,96},{32,64},{64,32},{96,0},{128,224},{160,192},{192,160},{224,1... | collective-permute-start | bytes 196616 | tf_op jit(solution)/shard_map/ppermute | solution.py:253
  49.1 4.9 %collective-permute-start.15 = (f32[128,128]{1,0:T(8,128)S(1)}, f32[128,128]{1,0:T(8,128)S(1)}, u32[]{:S(2)}, u32[]{:S(2)}) collective-permute-start(f32[128,128]{1,0:T(8,128)S(1)} %add_add_fusion.1), channel_id=1, source_target_pairs={{0,64},{32,96},{64,0},{96,32},{128,192},{160,224},{192,128},{224,1... | collective-permute-start | bytes 196616 | tf_op jit(solution)/shard_map/ppermute | solution.py:253
  50.2 3.8 %collective-permute-start.14 = (f32[128,128]{1,0:T(8,128)S(1)}, f32[128,128]{1,0:T(8,128)S(1)}, u32[]{:S(2)}, u32[]{:S(2)}) collective-permute-start(f32[128,128]{1,0:T(8,128)S(1)} %add_add_fusion.1), channel_id=1, source_target_pairs={{0,32},{32,0},{64,96},{96,64},{128,160},{160,128},{192,224},{224,1... | collective-permute-start | bytes 196616 | tf_op jit(solution)/shard_map/ppermute | solution.py:253
  54.0 6.2 %collective-permute-start.17 = (f32[128,128]{1,0:T(8,128)S(1)}, f32[128,128]{1,0:T(8,128)S(1)}, u32[]{:S(2)}, u32[]{:S(2)}) collective-permute-start(f32[128,128]{1,0:T(8,128)S(1)} %add_add_fusion.a_ref), channel_id=1, source_target_pairs={{0,192},{32,224},{64,128},{96,160},{128,64},{160,96},{192,0},{224,... | collective-permute-start | bytes 196616 | tf_op jit(solution)/shard_map/ppermute | solution.py:253
  60.4 4.8 %collective-permute-start.20 = (f32[136,128]{1,0:T(8,128)S(1)}, f32[136,128]{1,0:T(8,128)S(1)}, u32[]{:S(2)}, u32[]{:S(2)}) collective-permute-start(f32[136,128]{1,0:T(8,128)S(1)} %finished_piece.1), channel_id=1, source_target_pairs={{0,6},{2,4},{4,2},{6,0},{1,7},{3,5},{5,3},{7,1},{8,14},{10,12},{12... | collective-permute-start | bytes 208904 | tf_op jit(solution)/shard_map/ppermute | solution.py:253
  63.2 4.7 %collective-permute-start.19 = (f32[136,128]{1,0:T(8,128)S(1)}, f32[136,128]{1,0:T(8,128)S(1)}, u32[]{:S(2)}, u32[]{:S(2)}) collective-permute-start(f32[136,128]{1,0:T(8,128)S(1)} %finished_piece.1), channel_id=1, source_target_pairs={{0,4},{2,6},{4,0},{6,2},{1,5},{3,7},{5,1},{7,3},{8,12},{10,14},{12... | collective-permute-start | bytes 208904 | tf_op jit(solution)/shard_map/ppermute | solution.py:253
  63.9 4.0 %collective-permute-start.18 = (f32[136,128]{1,0:T(8,128)S(1)}, f32[136,128]{1,0:T(8,128)S(1)}, u32[]{:S(2)}, u32[]{:S(2)}) collective-permute-start(f32[136,128]{1,0:T(8,128)S(1)} %finished_piece.1), channel_id=1, source_target_pairs={{0,2},{2,0},{4,6},{6,4},{1,3},{3,1},{5,7},{7,5},{8,10},{10,8},{12,... | collective-permute-start | bytes 208904 | tf_op jit(solution)/shard_map/ppermute | solution.py:253
  67.9 6.2 %collective-permute-start.21 = (f32[4,136,128]{2,1,0:T(8,128)S(1)}, f32[4,136,128]{2,1,0:T(8,128)S(1)}, u32[]{:S(2)}, u32[]{:S(2)}) collective-permute-start(f32[4,136,128]{2,1,0:T(8,128)S(1)} %pad_maximum_fusion.own_ref), channel_id=1, source_target_pairs={{0,1},{1,0},{2,3},{3,2},{4,5},{5,4},{6,7},{7,6},{8,9},{9,8},{10,11... | collective-permute-start | bytes 835592 | tf_op jit(solution)/shard_map/ppermute | solution.py:253

commit v4 on v0

v4 whole, which is shorter than its diff:
```python
import functools

import jax
import jax.numpy as jnp
from jax import lax
from jax.experimental import pallas as pl
from jax.experimental.pallas import tpu as pltpu
from jax.sharding import Mesh, PartitionSpec as P

F32 = jnp.float32
BF16 = jnp.bfloat16
RANK = 32
LANES = 128
VMEM_LIMIT = 24 * 2**20
PARAMS = pltpu.CompilerParams(vmem_limit_bytes=VMEM_LIMIT)
WHOLE = pl.BlockSpec(memory_space=pltpu.VMEM)
AWAY = pl.BlockSpec(memory_space=pl.ANY)


def in_hbm(x):
    return pltpu.with_memory_space_constraint(x, pltpu.HBM)


def split(x):
    head = x.astype(BF16)
    return head, (x - head.astype(F32)).astype(BF16)


def left_three(x):
    hi, lo = split(x)
    return jnp.concatenate([hi, lo, hi], axis=1)


def right_three(x):
    hi, lo = split(x)
    return jnp.concatenate([hi, hi, lo], axis=0)


def dot(a, b, a_dim, b_dim, precision=None):
    return lax.dot_general(a, b, (((a_dim,), (b_dim,)), ((), ())), precision=precision, preferred_element_type=F32)


def pack(square):
    return jnp.concatenate([square[8 * i : 8 * i + 8] for i in range(4)], axis=1)


def unpack(packed):
    return jnp.concatenate([packed[:, 32 * i : 32 * i + 32] for i in range(4)], axis=0)


def left_columns(packed, m):
    columns = [packed[:, RANK * i : RANK * i + RANK] for i in range(4)]
    return jnp.concatenate([jnp.where(m == 0, columns[0], columns[1]), jnp.where(m == 0, columns[2], columns[3])], axis=0)


def left_kernel(grads_hbm, errors_hbm, q_hbm, full_ref, p_ref, grads_ref, q_ref, grads_sem, errors_sem, q_sem):
    projections, rows, _ = full_ref.shape
    q_copy = pltpu.make_async_copy(q_hbm, q_ref, q_sem)
    copies = [
        (
            pltpu.make_async_copy(grads_hbm.at[0, m], grads_ref.at[m], grads_sem.at[m]),
            pltpu.make_async_copy(errors_hbm.at[0, m], full_ref.at[m], errors_sem.at[m]),
        )
        for m in range(projections)
    ]
    q_copy.start()
    for pair in copies:
        for copy in pair:
            copy.start()
    q_copy.wait()
    for m, pair in enumerate(copies):
        q_hi, q_lo = split(q_ref[m])
        both = jnp.concatenate([q_hi, q_lo], axis=0)
        for copy in pair:
            copy.wait()
        full = grads_ref[m].astype(F32) + full_ref[m]
        full_ref[m] = full
        f_hi, f_lo = split(full)
        wide = dot(f_hi, both, 1, 1)
        p = wide[:, :RANK] + wide[:, RANK:] + dot(f_lo, q_hi, 1, 1)
        p_ref[:, RANK * m : RANK * (m + 1)] = p[: rows // 2]
        p_ref[:, RANK * (2 + m) : RANK * (3 + m)] = p[rows // 2 :]


def left_factors(grads, errors, q_prev):
    _, projections, rows, columns = grads.shape
    return pl.pallas_call(
        left_kernel,
        in_specs=[AWAY] * 3,
        out_specs=[WHOLE] * 2,
        out_shape=[pltpu.VMEM((projections, rows, columns), F32), pltpu.VMEM((rows // 2, LANES), F32)],
        scratch_shapes=[
            pltpu.VMEM((projections, rows, columns), BF16),
            pltpu.VMEM(q_prev.shape, F32),
            pltpu.SemaphoreType.DMA((projections,)),
            pltpu.SemaphoreType.DMA((projections,)),
            pltpu.SemaphoreType.DMA,
        ],
        compiler_params=PARAMS,
        name="left_factors",
    )(in_hbm(grads), in_hbm(errors), in_hbm(q_prev))


def right_kernel(replicas, mine, p_ref, full_ref, out_ref):
    slots, height, _ = out_ref.shape
    tiles = (height - 8) // RANK
    width = tiles * LANES
    x, core = lax.axis_index("x"), lax.axis_index("c")
    m = core if mine else 1 - core
    p = (left_columns(p_ref[...], m) * (1.0 / replicas)).T
    p_hi, p_lo = split(p)
    both = jnp.concatenate([p_hi, p_lo], axis=0)
    gram = pack(dot(p, p, 1, 1, lax.Precision.HIGHEST))
    for slot in range(slots):
        first = pl.multiple_of((x ^ slot) * width, width)
        f_hi, f_lo = split(full_ref[m, :, pl.ds(first, width)])
        wide = dot(both, f_hi, 1, 0)
        q = wide[:RANK] + wide[RANK:] + dot(p_hi, f_lo, 1, 0)
        for j in range(tiles):
            out_ref[slot, j * RANK : (j + 1) * RANK, :] = q[:, j * LANES : (j + 1) * LANES]
        out_ref[slot, tiles * RANK :, :] = gram


def right_terms(p_sum, full, replicas, slots, mine):
    height = full.shape[2] // slots // LANES * RANK + 8
    return pl.pallas_call(
        functools.partial(right_kernel, replicas, mine),
        in_specs=[WHOLE] * 2,
        out_specs=WHOLE,
        out_shape=jax.ShapeDtypeStruct((slots, height, LANES), F32),
        compiler_params=PARAMS,
        name="right_terms_own" if mine else "right_terms_other",
    )(p_sum, full)


def factor_kernel(sum_ref, out_ref):
    gram = unpack(sum_ref[sum_ref.shape[0] - 8 :, :])
    row = lax.broadcasted_iota(jnp.int32, (RANK, RANK), 0)
    column = lax.broadcasted_iota(jnp.int32, (RANK, RANK), 1)
    work = jnp.concatenate([gram, (row == column).astype(F32)], axis=1)
    below = lax.broadcasted_iota(jnp.int32, (RANK, 2 * RANK), 0)
    scale = jnp.zeros((RANK, 1), F32)
    first = lax.broadcasted_iota(jnp.int32, (RANK, 1), 0)
    for k in range(RANK):
        top = work[k : k + 1, :]
        pivot = work[k : k + 1, k : k + 1]
        scale = jnp.where(first == k, lax.rsqrt(pivot), scale)
        if k < RANK - 1:
            ratio = work[:, k : k + 1] * (1.0 / pivot)
            work = jnp.where(below > k, work - ratio * top, work)
    out_ref[...] = pack(work[:, RANK:] * scale)


def inverse_factor(total):
    return pl.pallas_call(
        factor_kernel,
        in_specs=[WHOLE],
        out_specs=WHOLE,
        out_shape=jax.ShapeDtypeStruct((8, LANES), F32),
        compiler_params=PARAMS,
        cost_estimate=pl.CostEstimate(flops=4_000_000, bytes_accessed=4_000_000, transcendentals=64),
        name="inverse_factor",
    )(total)


def hat_kernel(replicas, p_ref, own_ref, other_ref, hat_ref, rows_ref):
    rows = hat_ref.shape[1]
    share = rows // replicas
    core = lax.axis_index("c")
    at = lax.broadcasted_iota(jnp.int32, (16, rows), 0) + lax.axis_index(("z", "y")) * share
    chosen = (lax.broadcasted_iota(jnp.int32, (16, rows), 1) == at).astype(F32)
    for i, (inverse_ref, m) in enumerate(((own_ref, core), (other_ref, 1 - core))):
        p = left_columns(p_ref[...], m) * (1.0 / replicas)
        hat = dot(p, unpack(inverse_ref[...]), 1, 1, lax.Precision.HIGHEST)
        hat_ref[i] = left_three(hat)
        rows_ref[i] = left_three(dot(chosen, hat, 1, 0, lax.Precision.HIGHEST))


def orthonormal(p_sum, own, other, replicas):
    rows = 2 * p_sum.shape[0]
    return pl.pallas_call(
        functools.partial(hat_kernel, replicas),
        in_specs=[WHOLE] * 3,
        out_specs=[WHOLE] * 2,
        out_shape=[jax.ShapeDtypeStruct((2, rows, 3 * RANK), BF16), jax.ShapeDtypeStruct((2, 16, 3 * RANK), BF16)],
        compiler_params=PARAMS,
        cost_estimate=pl.CostEstimate(flops=4_000_000, bytes_accessed=3_000_000, transcendentals=64),
        name="orthonormal",
    )(p_sum, own, other)


def piece_kernel(replicas, a_ref, b_ref, inverse_ref, out_ref):
    inverse = unpack(inverse_ref[...]) * (1.0 / replicas)
    tiles = a_ref.shape[0] // RANK
    rows = a_ref[...] + b_ref[...]
    wide = jnp.concatenate([rows[j * RANK : (j + 1) * RANK] for j in range(tiles)], axis=1)
    q = dot(inverse, wide, 1, 0, lax.Precision.HIGHEST)
    for j in range(tiles):
        out_ref[j * RANK : (j + 1) * RANK, :] = q[:, j * LANES : (j + 1) * LANES]


def finished_piece(a, b, inverse, replicas):
    return pl.pallas_call(
        functools.partial(piece_kernel, replicas),
        in_specs=[WHOLE] * 3,
        out_specs=WHOLE,
        out_shape=jax.ShapeDtypeStruct(a.shape, F32),
        compiler_params=PARAMS,
        name="finished_piece",
    )(a, b, inverse)


def update_kernel(mine, pieces_ref, hat_ref, rows_ref, full_ref, m1_ref, m2_ref, *refs):
    err_hbm, n1_hbm, n2_hbm, up_hbm, q_hbm, err_ref, n1_ref, n2_ref, up_ref, q_ref, tile_ref, flat_ref, err_sem, sem = refs[-14:]
    slots, height, _ = pieces_ref.shape
    tiles = height // RANK
    width = tiles * LANES
    x, core = lax.axis_index("x"), lax.axis_index("c")
    i, m = (0, core) if mine else (1, 1 - core)
    copies = []
    for slot in range(slots):
        block = x ^ slot
        here = pl.ds(pl.multiple_of(block * width, width), width)
        q = jnp.concatenate([pieces_ref[slot, j * RANK : (j + 1) * RANK, :] for j in range(tiles)], axis=1)
        right = right_three(q)
        err_ref[slot] = full_ref[m, :, here] - dot(hat_ref[i], right, 1, 0)
        copies.append(pltpu.make_async_copy(err_ref.at[slot], err_hbm.at[0, m, :, here], err_sem.at[slot]))
        copies[-1].start()
        q_ref[:, here] = q
        state = dot(rows_ref[i], right, 1, 0)
        for j in range(tiles):
            tile_ref[block * tiles + j] = state[:8, j * LANES : (j + 1) * LANES]
    share = flat_ref.shape[0]
    for j in range(slots * tiles):
        flat_ref[:, j, :] = tile_ref[j, :share, :]
    flat = flat_ref[...].reshape(share * slots * tiles, LANES)
    n1 = 0.9 * m1_ref[m] + 0.1 * flat
    n2 = 0.95 * m2_ref[m] + 0.05 * flat * flat
    n1_ref[...] = n1
    n2_ref[...] = n2
    up_ref[...] = (n1 / (jnp.sqrt(n2) + 1e-08)).astype(BF16)
    for k, (here, there) in enumerate(((n1_ref, n1_hbm), (n2_ref, n2_hbm), (up_ref, up_hbm), (q_ref, q_hbm))):
        copies.append(pltpu.make_async_copy(here, there.at[m], sem.at[k]))
        copies[-1].start()
    for copy in copies:
        copy.wait()


def update(pieces, hat, rows, full, moment1, moment2, mine, before=()):
    projections, depth, columns = full.shape
    slots, height, _ = pieces.shape
    state, tiles = moment1.shape[1], columns // LANES
    return pl.pallas_call(
        functools.partial(update_kernel, mine),
        in_specs=[WHOLE] * 6 + [AWAY] * len(before),
        out_specs=[AWAY] * 5,
        out_shape=[
            pltpu.HBM((1, projections, depth, columns), F32),
            pltpu.HBM(moment1.shape, F32),
            pltpu.HBM(moment2.shape, F32),
            pltpu.HBM(moment1.shape, BF16),
            pltpu.HBM((projections, RANK, columns), F32),
        ],
        scratch_shapes=[
            pltpu.VMEM((slots, depth, columns // slots), F32),
            pltpu.VMEM((state, LANES), F32),
            pltpu.VMEM((state, LANES), F32),
            pltpu.VMEM((state, LANES), BF16),
            pltpu.VMEM((RANK, columns), F32),
            pltpu.VMEM((tiles, 8, LANES), F32),
            pltpu.VMEM((state // tiles, tiles, LANES), F32),
            pltpu.SemaphoreType.DMA((slots,)),
            pltpu.SemaphoreType.DMA((4,)),
        ],
        input_output_aliases={6 + k: k for k in range(len(before))},
        compiler_params=PARAMS,
        cost_estimate=pl.CostEstimate(flops=100_000_000, bytes_accessed=4_000_000, transcendentals=30_000),
        name="update_own" if mine else "update_other",
    )(pieces, hat, rows, full, moment1, moment2, *before)


def swap(value, axis, bit):
    return lax.ppermute(value, axis, [(i, i ^ bit) for i in range(lax.axis_size(axis))])


def four(values, axis):
    return (values[0] + swap(values[1], axis, 1)) + (swap(values[2], axis, 2) + swap(values[3], axis, 3))


def shards(grads, errors, q_prev, moment1, moment2):
    replicas, slots = lax.axis_size(("z", "y")), lax.axis_size("x")
    full, p = left_factors(grads, errors, q_prev)
    p = four([p] * 4, "y")
    p = four([p] * 4, "z")
    p = p + swap(p, "z", 6)

    terms = swap(right_terms(p, full, replicas, slots, False), "c", 1) + right_terms(p, full, replicas, slots, True)
    total = four([terms[i] for i in range(slots)], "x")
    inverse = inverse_factor(total)
    q = four([total[:-8]] * 4, "y")
    q, inverse = lax.optimization_barrier((q, inverse))
    hat, rows = orthonormal(p, inverse, swap(inverse, "c", 1), replicas)
    q = four([q] * 4, "z")
    q, hat, rows = lax.optimization_barrier((q, hat, rows))
    piece = finished_piece(q, swap(q, "z", 6), inverse, replicas)
    own = jnp.stack([piece] + [swap(piece, "x", i) for i in range(1, slots)])
    other = swap(own, "c", 1)
    done = update(own, hat, rows, full, moment1, moment2, True)
    return tuple(update(other, hat, rows, full, moment1, moment2, False, done))


def solution(mesh):
    mesh = Mesh(mesh.devices.reshape(8, 4, 4, 2), ("z", "y", "x", "c"))
    dp, fsdp = ("z", "y"), ("x", "c")
    blocks = P(dp, None, fsdp, None)
    states = P(None, fsdp + dp, None)
    return jax.shard_map(
        shards,
        mesh=mesh,
        in_specs=(blocks, blocks, P(), states, states),
        out_specs=(blocks, states, states, states, P()),
        check_vma=False,
    )
```

time: 471 us -> 75.4 us (0.16)
  waiting for transfers between devices: 246 us -> 20.4 us
  blocking collectives: 168 us -> 0 us
  starting transfers between devices: 0.04 us -> 41.6 us
  other arithmetic: 20 us -> 0.15 us
  matrix products: 16.9 us -> 0 us
  between operations: 14.1 us -> 0.91 us
  Pallas kernels: 0 us -> 12.2 us
  local copies, waits for them, and re-layouts: 5.78 us -> 0.03 us
    psum x1 -> x0, waiting for transfers between devices: 246 us -> none  [shards(): q_total = lax.psum(q_local, ('dp', 'fsdp'))]
    psum x2 -> x0, blocking collectives: 168 us -> none  [the longest x1 119 us: shards(): p_mean = lax.psum(p_local, 'dp') / replicas]
    ppermute x0 -> x23, starting transfers between devices: none -> 41.6 us  [swap(): lax.ppermute(value, axis, [(i, i ^ bit) for i in range(lax.axis_size(axis...]
    ppermute x0 -> x23, waiting for transfers between devices: none -> 20.4 us  [swap(): lax.ppermute(value, axis, [(i, i ^ bit) for i in range(lax.axis_size(axis...]
    dot_general x4 -> x0, matrix products: 16.6 us -> none  [the longest x1 6.27 us: shards(): p_local = jnp.einsum('mdk,mrk->mrd', full, q_prev, precision=highest)]
    pallas_call x0 -> x8, Pallas kernels: none -> 12.2 us  [the longest x1 3.63 us: left_factors(): pl.pallas_call(left_kernel, in_specs=[AWAY] * 3, out_specs=[WHOLE] * 2, o...]
    another operation x7 -> x1, other arithmetic: 11 us -> 0.02 us  [shards(): own = jnp.stack([piece] + [swap(piece, 'x', i) for i in range(1, slots)])]
    broadcast_in_dim x1 -> x0, other arithmetic: 6.3 us -> none  [shards(): new_errors = (full - approx)[None]]
  transfers between devices with their start and end apart: 1 -> 23, of which waited for: 1 -> 13; matrix products, arithmetic and copies ran while one was open for 0% -> 0% of each run, Pallas kernels for 0% -> 8%
where the time goes in v4:
time: 75.4 us; the launch traced here: 75.3 us
  starting transfers between devices  41.6 us (55%)
  waiting for transfers between devices  20.4 us (27%)
  Pallas kernels  12.2 us (16%)
  between operations  0.91 us (1%)
    ppermute x23, starting transfers between devices, swap(): lax.ppermute(value, axis, [(i, i ^ bit) for i in range(lax.axis_size(axis...  41.6 us
    ppermute x23, waiting for transfers between devices, swap(): lax.ppermute(value, axis, [(i, i ^ bit) for i in range(lax.axis_size(axis...  20.4 us
    pallas_call x1, Pallas kernels, left_factors(): pl.pallas_call(left_kernel, in_specs=[AWAY] * 3, out_specs=[WHOLE] * 2, o...  3.63 us
    pallas_call x2, Pallas kernels, update(): pl.pallas_call(functools.partial(update_kernel, mine), in_specs=[WHOLE] *...  3.3 us
    pallas_call x1, Pallas kernels, inverse_factor(): pl.pallas_call(factor_kernel, in_specs=[WHOLE], out_specs=WHOLE, out_shap...  2.85 us
  transfers between devices with their start and end apart: 23, of which 13 were waited for; matrix products, arithmetic and copies ran while one was open for 0% of the time, Pallas kernels for 8%

profile of v4, /device:TPU:1, one launch (start us, length us, event | category | flops | bytes accessed | tf_op | source)
XLA Modules:
  0.0 75.3 jit_solution(18119624985780233314)
XLA Ops:
  0.6 3.6 %left_factors.1 = (f32[2,224,2048]{2,1,0:T(8,128)S(1)}, f32[112,128]{1,0:T(8,128)S(1)}) custom-call(bf16[1,2,224,2048]{3,2,1,0:T(8,128)(2,1)} %grads_hbm.1, f32[1,2,224,2048]{3,2,1,0:T(8,128)} %errors_hbm.1, f32[2,32,2048]{2,1,0:T(8,128)} %q_hbm.1), custom_call_target="tpu_custom_call" | custom-call | tf_op jit(solution)/shard_map/left_factors/pallas_call | solution.py:87
  4.3 3.6 %collective-permute-start.2 = (f32[112,128]{1,0:T(8,128)S(1)}, f32[112,128]{1,0:T(8,128)S(1)}, u32[]{:S(2)}, u32[]{:S(2)}) collective-permute-start(f32[112,128]{1,0:T(8,128)S(1)} %get-tuple-element.19), channel_id=1, source_target_pairs={{0,24},{8,16},{16,8},{24,0},{1,25},{9,17},{17,9},{25,1},{2,26},{10... | collective-permute-start | bytes 172040 | tf_op jit(solution)/shard_map/ppermute | solution.py:283
  8.6 0.9 %collective-permute-done.2 = f32[112,128]{1,0:T(8,128)S(1)} collective-permute-done((f32[112,128]{1,0:T(8,128)S(1)}, f32[112,128]{1,0:T(8,128)S(1)}, u32[]{:S(2)}, u32[]{:S(2)}) %collective-permute-start.2) | collective-permute-done | bytes 57376 | tf_op jit(solution)/shard_map/ppermute | solution.py:283
  9.5 3.1 %collective-permute-done.1 = f32[112,128]{1,0:T(8,128)S(1)} collective-permute-done((f32[112,128]{1,0:T(8,128)S(1)}, f32[112,128]{1,0:T(8,128)S(1)}, u32[]{:S(2)}, u32[]{:S(2)}) %collective-permute-start.1) | collective-permute-done | bytes 57376 | tf_op jit(solution)/shard_map/ppermute | solution.py:283
  12.6 4.3 %collective-permute-start.5 = (f32[112,128]{1,0:T(8,128)S(1)}, f32[112,128]{1,0:T(8,128)S(1)}, u32[]{:S(2)}, u32[]{:S(2)}) collective-permute-start(f32[112,128]{1,0:T(8,128)S(1)} %add_add_fusion.3), channel_id=1, source_target_pairs={{0,96},{32,64},{64,32},{96,0},{128,224},{160,192},{192,160},{224,1... | collective-permute-start | bytes 172040 | tf_op jit(solution)/shard_map/ppermute | solution.py:283
  17.3 1.2 %collective-permute-done.5 = f32[112,128]{1,0:T(8,128)S(1)} collective-permute-done((f32[112,128]{1,0:T(8,128)S(1)}, f32[112,128]{1,0:T(8,128)S(1)}, u32[]{:S(2)}, u32[]{:S(2)}) %collective-permute-start.5) | collective-permute-done | bytes 57376 | tf_op jit(solution)/shard_map/ppermute | solution.py:283
  18.5 2.9 %collective-permute-done.4 = f32[112,128]{1,0:T(8,128)S(1)} collective-permute-done((f32[112,128]{1,0:T(8,128)S(1)}, f32[112,128]{1,0:T(8,128)S(1)}, u32[]{:S(2)}, u32[]{:S(2)}) %collective-permute-start.4) | collective-permute-done | bytes 57376 | tf_op jit(solution)/shard_map/ppermute | solution.py:283
  21.4 3.4 %collective-permute-start.6 = (f32[112,128]{1,0:T(8,128)S(1)}, f32[112,128]{1,0:T(8,128)S(1)}, u32[]{:S(2)}, u32[]{:S(2)}) collective-permute-start(f32[112,128]{1,0:T(8,128)S(1)} %add_add_fusion.2), channel_id=1, source_target_pairs={{0,192},{32,224},{64,128},{96,160},{128,64},{160,96},{192,0},{224,... | collective-permute-start | bytes 172040 | tf_op jit(solution)/shard_map/ppermute | solution.py:283
  24.8 2.3 %collective-permute-done.6 = f32[112,128]{1,0:T(8,128)S(1)} collective-permute-done((f32[112,128]{1,0:T(8,128)S(1)}, f32[112,128]{1,0:T(8,128)S(1)}, u32[]{:S(2)}, u32[]{:S(2)}) %collective-permute-start.6) | collective-permute-done | bytes 57376 | tf_op jit(solution)/shard_map/ppermute | solution.py:283
  27.2 0.7 right_terms_other.1
  27.8 3.9 %collective-permute-start.7 = (f32[4,136,128]{2,1,0:T(8,128)S(1)}, f32[4,136,128]{2,1,0:T(8,128)S(1)}, u32[]{:S(2)}, u32[]{:S(2)}) collective-permute-start(f32[4,136,128]{2,1,0:T(8,128)S(1)} %right_terms_other.1), channel_id=1, source_target_pairs={{0,1},{1,0},{2,3},{3,2},{4,5},{5,4},{6,7},{7,6},{8,9},{9,8},{10,11... | collective-permute-start | bytes 835592 | tf_op jit(solution)/shard_map/ppermute | solution.py:283
  33.0 2.6 %collective-permute-start.10 = (f32[136,128]{1,0:T(8,128)S(1)}, f32[136,128]{1,0:T(8,128)S(1)}, u32[]{:S(2)}, u32[]{:S(2)}) collective-permute-start(f32[136,128]{1,0:T(8,128)S(1)} %get-tuple-element.33), channel_id=1, source_target_pairs={{0,6},{2,4},{4,2},{6,0},{1,7},{3,5},{5,3},{7,1},{8,14},{10,12},{12... | collective-permute-start | bytes 208904 | tf_op jit(solution)/shard_map/ppermute | solution.py:283
  36.3 1.1 %collective-permute-done.10 = f32[136,128]{1,0:T(8,128)S(1)} collective-permute-done((f32[136,128]{1,0:T(8,128)S(1)}, f32[136,128]{1,0:T(8,128)S(1)}, u32[]{:S(2)}, u32[]{:S(2)}) %collective-permute-start.10) | collective-permute-done | bytes 69664 | tf_op jit(solution)/shard_map/ppermute | solution.py:283
  37.5 2.8 %collective-permute-done.9 = f32[136,128]{1,0:T(8,128)S(1)} collective-permute-done((f32[136,128]{1,0:T(8,128)S(1)}, f32[136,128]{1,0:T(8,128)S(1)}, u32[]{:S(2)}, u32[]{:S(2)}) %collective-permute-start.9) | collective-permute-done | bytes 69664 | tf_op jit(solution)/shard_map/ppermute | solution.py:283
  40.3 1.7 %collective-permute-start.12 = (f32[128,128]{1,0:T(8,128)S(1)}, f32[128,128]{1,0:T(8,128)S(1)}, u32[]{:S(2)}, u32[]{:S(2)}) collective-permute-start(f32[128,128]{1,0:T(8,128)S(1)} %slice.24), channel_id=1, source_target_pairs={{0,16},{8,24},{16,0},{24,8},{1,17},{9,25},{17,1},{25,9},{2,18},{10... | collective-permute-start | bytes 196616 | tf_op jit(solution)/shard_map/ppermute | solution.py:283
  42.0 0.8 %collective-permute-start.13 = (f32[128,128]{1,0:T(8,128)S(1)}, f32[128,128]{1,0:T(8,128)S(1)}, u32[]{:S(2)}, u32[]{:S(2)}) collective-permute-start(f32[128,128]{1,0:T(8,128)S(1)} %slice.24), channel_id=1, source_target_pairs={{0,24},{8,16},{16,8},{24,0},{1,25},{9,17},{17,9},{25,1},{2,26},{10... | collective-permute-start | bytes 196616 | tf_op jit(solution)/shard_map/ppermute | solution.py:283
  43.0 2.8 %inverse_factor.1.own_ref.inverse_ref = f32[8,128]{1,0:T(8,128)S(1)} custom-call(f32[136,128]{1,0:T(8,128)S(1)} %fusion.1.sum_ref), custom_call_target="tpu_custom_call" | custom-call | flops 4000000 | bytes 4000000 | tf_op jit(solution)/shard_map/inverse_factor/pallas_call | solution.py:155
  46.4 1.7 %collective-permute-start.16 = (f32[128,128]{1,0:T(8,128)S(1)}, f32[128,128]{1,0:T(8,128)S(1)}, u32[]{:S(2)}, u32[]{:S(2)}) collective-permute-start(f32[128,128]{1,0:T(8,128)S(1)} %add_add_fusion.1), channel_id=1, source_target_pairs={{0,96},{32,64},{64,32},{96,0},{128,224},{160,192},{192,160},{224,1... | collective-permute-start | bytes 196616 | tf_op jit(solution)/shard_map/ppermute | solution.py:283
  48.0 1.5 %collective-permute-start.15 = (f32[128,128]{1,0:T(8,128)S(1)}, f32[128,128]{1,0:T(8,128)S(1)}, u32[]{:S(2)}, u32[]{:S(2)}) collective-permute-start(f32[128,128]{1,0:T(8,128)S(1)} %add_add_fusion.1), channel_id=1, source_target_pairs={{0,64},{32,96},{64,0},{96,32},{128,192},{160,224},{192,128},{224,1... | collective-permute-start | bytes 196616 | tf_op jit(solution)/shard_map/ppermute | solution.py:283
  50.0 4.5 %collective-permute-start.17 = (f32[8,128]{1,0:T(8,128)S(1)}, f32[8,128]{1,0:T(8,128)S(1)}, u32[]{:S(2)}, u32[]{:S(2)}) collective-permute-start(f32[8,128]{1,0:T(8,128)S(1)} %inverse_factor.1.own_ref.inverse_ref), channel_id=1, source_target_pairs={{0,1},{1,0},{2,3},{3,2},{4,5},{5,4},{6,7},{7,6},{8,9},{9,8},{10,11... | collective-permute-start | bytes 12296 | tf_op jit(solution)/shard_map/ppermute | solution.py:283
  54.4 0.8 %collective-permute-done.17.other_ref = f32[8,128]{1,0:T(8,128)S(1)} collective-permute-done((f32[8,128]{1,0:T(8,128)S(1)}, f32[8,128]{1,0:T(8,128)S(1)}, u32[]{:S(2)}, u32[]{:S(2)}) %collective-permute-start.17) | collective-permute-done | bytes 4128 | tf_op jit(solution)/shard_map/ppermute | solution.py:283
  55.3 0.9 %orthonormal.1 = (bf16[2,224,96]{2,1,0:T(8,128)(2,1)S(1)}, bf16[2,16,96]{2,1,0:T(8,128)(2,1)S(1)}) custom-call(f32[112,128]{1,0:T(8,128)S(1)} %add.57.p_ref, f32[8,128]{1,0:T(8,128)S(1)} %inverse_factor.1.own_ref.inverse_ref, f32[8,128]{1,0:T(8,128)S(1)} %collective-permute-done.17.other_ref), custom_call_target="tpu_custom_call" | custom-call | flops 4000000 | bytes 3000000 | tf_op jit(solution)/shard_map/orthonormal/pallas_call | solution.py:181
  56.3 3.5 %collective-permute-start.18 = (f32[128,128]{1,0:T(8,128)S(1)}, f32[128,128]{1,0:T(8,128)S(1)}, u32[]{:S(2)}, u32[]{:S(2)}) collective-permute-start(f32[128,128]{1,0:T(8,128)S(1)} %add_add_fusion.a_ref), channel_id=1, source_target_pairs={{0,192},{32,224},{64,128},{96,160},{128,64},{160,96},{192,0},{224,... | collective-permute-start | bytes 196616 | tf_op jit(solution)/shard_map/ppermute | solution.py:283
  59.8 1.9 %collective-permute-done.18.b_ref = f32[128,128]{1,0:T(8,128)S(1)} collective-permute-done((f32[128,128]{1,0:T(8,128)S(1)}, f32[128,128]{1,0:T(8,128)S(1)}, u32[]{:S(2)}, u32[]{:S(2)}) %collective-permute-start.18) | collective-permute-done | bytes 65568 | tf_op jit(solution)/shard_map/ppermute | solution.py:283
  61.9 1.0 %collective-permute-start.21 = (f32[128,128]{1,0:T(8,128)S(1)}, f32[128,128]{1,0:T(8,128)S(1)}, u32[]{:S(2)}, u32[]{:S(2)}) collective-permute-start(f32[128,128]{1,0:T(8,128)S(1)} %finished_piece.1), channel_id=1, source_target_pairs={{0,6},{2,4},{4,2},{6,0},{1,7},{3,5},{5,3},{7,1},{8,14},{10,12},{12... | collective-permute-start | bytes 196616 | tf_op jit(solution)/shard_map/ppermute | solution.py:283
  62.9 0.9 %collective-permute-start.20 = (f32[128,128]{1,0:T(8,128)S(1)}, f32[128,128]{1,0:T(8,128)S(1)}, u32[]{:S(2)}, u32[]{:S(2)}) collective-permute-start(f32[128,128]{1,0:T(8,128)S(1)} %finished_piece.1), channel_id=1, source_target_pairs={{0,4},{2,6},{4,0},{6,2},{1,5},{3,7},{5,1},{7,3},{8,12},{10,14},{12... | collective-permute-start | bytes 196616 | tf_op jit(solution)/shard_map/ppermute | solution.py:283
  63.8 1.4 %collective-permute-start.19 = (f32[128,128]{1,0:T(8,128)S(1)}, f32[128,128]{1,0:T(8,128)S(1)}, u32[]{:S(2)}, u32[]{:S(2)}) collective-permute-start(f32[128,128]{1,0:T(8,128)S(1)} %finished_piece.1), channel_id=1, source_target_pairs={{0,2},{2,0},{4,6},{6,4},{1,3},{3,1},{5,7},{7,5},{8,10},{10,8},{12,... | collective-permute-start | bytes 196616 | tf_op jit(solution)/shard_map/ppermute | solution.py:283
  65.2 1.1 %collective-permute-done.21 = f32[128,128]{1,0:T(8,128)S(1)} collective-permute-done((f32[128,128]{1,0:T(8,128)S(1)}, f32[128,128]{1,0:T(8,128)S(1)}, u32[]{:S(2)}, u32[]{:S(2)}) %collective-permute-start.21) | collective-permute-done | bytes 65568 | tf_op jit(solution)/shard_map/ppermute | solution.py:283
  66.3 1.3 %collective-permute-done.20 = f32[128,128]{1,0:T(8,128)S(1)} collective-permute-done((f32[128,128]{1,0:T(8,128)S(1)}, f32[128,128]{1,0:T(8,128)S(1)}, u32[]{:S(2)}, u32[]{:S(2)}) %collective-permute-start.20) | collective-permute-done | bytes 65568 | tf_op jit(solution)/shard_map/ppermute | solution.py:283
  67.6 4.3 %collective-permute-start.22 = (f32[4,128,128]{2,1,0:T(8,128)S(1)}, f32[4,128,128]{2,1,0:T(8,128)S(1)}, u32[]{:S(2)}, u32[]{:S(2)}) collective-permute-start(f32[4,128,128]{2,1,0:T(8,128)S(1)} %pad_maximum_fusion.pieces_ref), channel_id=1, source_target_pairs={{0,1},{1,0},{2,3},{3,2},{4,5},{5,4},{6,7},{7,6},{8,9},{9,8},{10,11... | collective-permute-start | bytes 786440 | tf_op jit(solution)/shard_map/ppermute | solution.py:283
  71.9 1.6 %update_own.1 = (f32[1,2,224,2048]{3,2,1,0:T(8,128)}, f32[2,112,128]{2,1,0:T(8,128)}, f32[2,112,128]{2,1,0:T(8,128)}, bf16[2,112,128]{2,1,0:T(8,128)(2,1)}, f32[2,32,2048]{2,1,0:T(8,128)}) custom-call(f32[4,128,128]{2,1,0:T(8,128)S(1)} %pad_maximum_fusion.pieces_ref, bf16[2,224,96]{2,1,0:T(8,128)(2,1)S(1)} %get-tuple-element.26.hat_ref, ...), custom_call_target="tpu_custom_call" | custom-call | flops 100000000 | bytes 4000000 | tf_op jit(solution)/shard_map/update_own/pallas_call | solution.py:253
  73.5 1.6 %update_other.1 = (f32[1,2,224,2048]{3,2,1,0:T(8,128)}, f32[2,112,128]{2,1,0:T(8,128)}, f32[2,112,128]{2,1,0:T(8,128)}, bf16[2,112,128]{2,1,0:T(8,128)(2,1)}, f32[2,32,2048]{2,1,0:T(8,128)}) custom-call(f32[4,128,128]{2,1,0:T(8,128)S(1)} %collective-permute-done.22.pieces_ref, ...), custom_call_target="tpu_custom_call", output_to_operand_aliasing={{0}: (6, {}), {1}: (7, {}), {2}: (8, {}), {3}: (9, {}), {4}... | custom-call | flops 100000000 | bytes 4000000 | tf_op jit(solution)/shard_map/update_other/pallas_call | solution.py:253
  (36 shorter events, 4.6 us)
Async XLA Ops:
  4.3 5.2 %collective-permute-start.2 = (f32[112,128]{1,0:T(8,128)S(1)}, f32[112,128]{1,0:T(8,128)S(1)}, u32[]{:S(2)}, u32[]{:S(2)}) collective-permute-start(f32[112,128]{1,0:T(8,128)S(1)} %get-tuple-element.19), channel_id=1, source_target_pairs={{0,24},{8,16},{16,8},{24,0},{1,25},{9,17},{17,9},{25,1},{2,26},{10... | collective-permute-start | bytes 172040 | tf_op jit(solution)/shard_map/ppermute | solution.py:283
  7.9 4.6 %collective-permute-start.1 = (f32[112,128]{1,0:T(8,128)S(1)}, f32[112,128]{1,0:T(8,128)S(1)}, u32[]{:S(2)}, u32[]{:S(2)}) collective-permute-start(f32[112,128]{1,0:T(8,128)S(1)} %get-tuple-element.19), channel_id=1, source_target_pairs={{0,16},{8,24},{16,0},{24,8},{1,17},{9,25},{17,1},{25,9},{2,18},{10... | collective-permute-start | bytes 172040 | tf_op jit(solution)/shard_map/ppermute | solution.py:283
  8.3 4.3 %collective-permute-start = (f32[112,128]{1,0:T(8,128)S(1)}, f32[112,128]{1,0:T(8,128)S(1)}, u32[]{:S(2)}, u32[]{:S(2)}) collective-permute-start(f32[112,128]{1,0:T(8,128)S(1)} %get-tuple-element.19), channel_id=1, source_target_pairs={{0,8},{8,0},{16,24},{24,16},{1,9},{9,1},{17,25},{25,17},{2,10},{10... | collective-permute-start | bytes 172040 | tf_op jit(solution)/shard_map/ppermute | solution.py:283
  12.6 5.9 %collective-permute-start.5 = (f32[112,128]{1,0:T(8,128)S(1)}, f32[112,128]{1,0:T(8,128)S(1)}, u32[]{:S(2)}, u32[]{:S(2)}) collective-permute-start(f32[112,128]{1,0:T(8,128)S(1)} %add_add_fusion.3), channel_id=1, source_target_pairs={{0,96},{32,64},{64,32},{96,0},{128,224},{160,192},{192,160},{224,1... | collective-permute-start | bytes 172040 | tf_op jit(solution)/shard_map/ppermute | solution.py:283
  16.9 4.5 %collective-permute-start.4 = (f32[112,128]{1,0:T(8,128)S(1)}, f32[112,128]{1,0:T(8,128)S(1)}, u32[]{:S(2)}, u32[]{:S(2)}) collective-permute-start(f32[112,128]{1,0:T(8,128)S(1)} %add_add_fusion.3), channel_id=1, source_target_pairs={{0,64},{32,96},{64,0},{96,32},{128,192},{160,224},{192,128},{224,1... | collective-permute-start | bytes 172040 | tf_op jit(solution)/shard_map/ppermute | solution.py:283
  16.9 4.5 %collective-permute-start.3 = (f32[112,128]{1,0:T(8,128)S(1)}, f32[112,128]{1,0:T(8,128)S(1)}, u32[]{:S(2)}, u32[]{:S(2)}) collective-permute-start(f32[112,128]{1,0:T(8,128)S(1)} %add_add_fusion.3), channel_id=1, source_target_pairs={{0,32},{32,0},{64,96},{96,64},{128,160},{160,128},{192,224},{224,1... | collective-permute-start | bytes 172040 | tf_op jit(solution)/shard_map/ppermute | solution.py:283
  21.4 5.8 %collective-permute-start.6 = (f32[112,128]{1,0:T(8,128)S(1)}, f32[112,128]{1,0:T(8,128)S(1)}, u32[]{:S(2)}, u32[]{:S(2)}) collective-permute-start(f32[112,128]{1,0:T(8,128)S(1)} %add_add_fusion.2), channel_id=1, source_target_pairs={{0,192},{32,224},{64,128},{96,160},{128,64},{160,96},{192,0},{224,... | collective-permute-start | bytes 172040 | tf_op jit(solution)/shard_map/ppermute | solution.py:283
  27.8 44.0 %copy-start = (f32[2,112,128]{2,1,0:T(8,128)S(1)}, f32[2,112,128]{2,1,0:T(8,128)}, u32[]{:S(2)}) copy-start(f32[2,112,128]{2,1,0:T(8,128)} %m1_ref.3) | copy-start | bytes 344068
  27.8 44.0 %copy-start.1 = (f32[2,112,128]{2,1,0:T(8,128)S(1)}, f32[2,112,128]{2,1,0:T(8,128)}, u32[]{:S(2)}) copy-start(f32[2,112,128]{2,1,0:T(8,128)} %m2_ref.3) | copy-start | bytes 344068
  27.8 5.1 %collective-permute-start.7 = (f32[4,136,128]{2,1,0:T(8,128)S(1)}, f32[4,136,128]{2,1,0:T(8,128)S(1)}, u32[]{:S(2)}, u32[]{:S(2)}) collective-permute-start(f32[4,136,128]{2,1,0:T(8,128)S(1)} %right_terms_other.1), channel_id=1, source_target_pairs={{0,1},{1,0},{2,3},{3,2},{4,5},{5,4},{6,7},{7,6},{8,9},{9,8},{10,11... | collective-permute-start | bytes 835592 | tf_op jit(solution)/shard_map/ppermute | solution.py:283
  33.0 4.5 %collective-permute-start.10 = (f32[136,128]{1,0:T(8,128)S(1)}, f32[136,128]{1,0:T(8,128)S(1)}, u32[]{:S(2)}, u32[]{:S(2)}) collective-permute-start(f32[136,128]{1,0:T(8,128)S(1)} %get-tuple-element.33), channel_id=1, source_target_pairs={{0,6},{2,4},{4,2},{6,0},{1,7},{3,5},{5,3},{7,1},{8,14},{10,12},{12... | collective-permute-start | bytes 208904 | tf_op jit(solution)/shard_map/ppermute | solution.py:283
  35.6 4.7 %collective-permute-start.9 = (f32[136,128]{1,0:T(8,128)S(1)}, f32[136,128]{1,0:T(8,128)S(1)}, u32[]{:S(2)}, u32[]{:S(2)}) collective-permute-start(f32[136,128]{1,0:T(8,128)S(1)} %get-tuple-element.34), channel_id=1, source_target_pairs={{0,4},{2,6},{4,0},{6,2},{1,5},{3,7},{5,1},{7,3},{8,12},{10,14},{12... | collective-permute-start | bytes 208904 | tf_op jit(solution)/shard_map/ppermute | solution.py:283
  36.1 4.1 %collective-permute-start.8 = (f32[136,128]{1,0:T(8,128)S(1)}, f32[136,128]{1,0:T(8,128)S(1)}, u32[]{:S(2)}, u32[]{:S(2)}) collective-permute-start(f32[136,128]{1,0:T(8,128)S(1)} %get-tuple-element.35), channel_id=1, source_target_pairs={{0,2},{2,0},{4,6},{6,4},{1,3},{3,1},{5,7},{7,5},{8,10},{10,8},{12,... | collective-permute-start | bytes 208904 | tf_op jit(solution)/shard_map/ppermute | solution.py:283
  40.3 5.6 %collective-permute-start.12 = (f32[128,128]{1,0:T(8,128)S(1)}, f32[128,128]{1,0:T(8,128)S(1)}, u32[]{:S(2)}, u32[]{:S(2)}) collective-permute-start(f32[128,128]{1,0:T(8,128)S(1)} %slice.24), channel_id=1, source_target_pairs={{0,16},{8,24},{16,0},{24,8},{1,17},{9,25},{17,1},{25,9},{2,18},{10... | collective-permute-start | bytes 196616 | tf_op jit(solution)/shard_map/ppermute | solution.py:283
  42.0 4.3 %collective-permute-start.13 = (f32[128,128]{1,0:T(8,128)S(1)}, f32[128,128]{1,0:T(8,128)S(1)}, u32[]{:S(2)}, u32[]{:S(2)}) collective-permute-start(f32[128,128]{1,0:T(8,128)S(1)} %slice.24), channel_id=1, source_target_pairs={{0,24},{8,16},{16,8},{24,0},{1,25},{9,17},{17,9},{25,1},{2,26},{10... | collective-permute-start | bytes 196616 | tf_op jit(solution)/shard_map/ppermute | solution.py:283
  42.8 3.5 %collective-permute-start.11 = (f32[128,128]{1,0:T(8,128)S(1)}, f32[128,128]{1,0:T(8,128)S(1)}, u32[]{:S(2)}, u32[]{:S(2)}) collective-permute-start(f32[128,128]{1,0:T(8,128)S(1)} %slice.24), channel_id=1, source_target_pairs={{0,8},{8,0},{16,24},{24,16},{1,9},{9,1},{17,25},{25,17},{2,10},{10... | collective-permute-start | bytes 196616 | tf_op jit(solution)/shard_map/ppermute | solution.py:283
  46.4 9.8 %collective-permute-start.16 = (f32[128,128]{1,0:T(8,128)S(1)}, f32[128,128]{1,0:T(8,128)S(1)}, u32[]{:S(2)}, u32[]{:S(2)}) collective-permute-start(f32[128,128]{1,0:T(8,128)S(1)} %add_add_fusion.1), channel_id=1, source_target_pairs={{0,96},{32,64},{64,32},{96,0},{128,224},{160,192},{192,160},{224,1... | collective-permute-start | bytes 196616 | tf_op jit(solution)/shard_map/ppermute | solution.py:283
  48.0 8.2 %collective-permute-start.15 = (f32[128,128]{1,0:T(8,128)S(1)}, f32[128,128]{1,0:T(8,128)S(1)}, u32[]{:S(2)}, u32[]{:S(2)}) collective-permute-start(f32[128,128]{1,0:T(8,128)S(1)} %add_add_fusion.1), channel_id=1, source_target_pairs={{0,64},{32,96},{64,0},{96,32},{128,192},{160,224},{192,128},{224,1... | collective-permute-start | bytes 196616 | tf_op jit(solution)/shard_map/ppermute | solution.py:283
  49.5 6.7 %collective-permute-start.14 = (f32[128,128]{1,0:T(8,128)S(1)}, f32[128,128]{1,0:T(8,128)S(1)}, u32[]{:S(2)}, u32[]{:S(2)}) collective-permute-start(f32[128,128]{1,0:T(8,128)S(1)} %add_add_fusion.1), channel_id=1, source_target_pairs={{0,32},{32,0},{64,96},{96,64},{128,160},{160,128},{192,224},{224,1... | collective-permute-start | bytes 196616 | tf_op jit(solution)/shard_map/ppermute | solution.py:283
  50.0 5.3 %collective-permute-start.17 = (f32[8,128]{1,0:T(8,128)S(1)}, f32[8,128]{1,0:T(8,128)S(1)}, u32[]{:S(2)}, u32[]{:S(2)}) collective-permute-start(f32[8,128]{1,0:T(8,128)S(1)} %inverse_factor.1.own_ref.inverse_ref), channel_id=1, source_target_pairs={{0,1},{1,0},{2,3},{3,2},{4,5},{5,4},{6,7},{7,6},{8,9},{9,8},{10,11... | collective-permute-start | bytes 12296 | tf_op jit(solution)/shard_map/ppermute | solution.py:283
  56.3 5.4 %collective-permute-start.18 = (f32[128,128]{1,0:T(8,128)S(1)}, f32[128,128]{1,0:T(8,128)S(1)}, u32[]{:S(2)}, u32[]{:S(2)}) collective-permute-start(f32[128,128]{1,0:T(8,128)S(1)} %add_add_fusion.a_ref), channel_id=1, source_target_pairs={{0,192},{32,224},{64,128},{96,160},{128,64},{160,96},{192,0},{224,... | collective-permute-start | bytes 196616 | tf_op jit(solution)/shard_map/ppermute | solution.py:283
  61.9 4.3 %collective-permute-start.21 = (f32[128,128]{1,0:T(8,128)S(1)}, f32[128,128]{1,0:T(8,128)S(1)}, u32[]{:S(2)}, u32[]{:S(2)}) collective-permute-start(f32[128,128]{1,0:T(8,128)S(1)} %finished_piece.1), channel_id=1, source_target_pairs={{0,6},{2,4},{4,2},{6,0},{1,7},{3,5},{5,3},{7,1},{8,14},{10,12},{12... | collective-permute-start | bytes 196616 | tf_op jit(solution)/shard_map/ppermute | solution.py:283
  62.9 4.6 %collective-permute-start.20 = (f32[128,128]{1,0:T(8,128)S(1)}, f32[128,128]{1,0:T(8,128)S(1)}, u32[]{:S(2)}, u32[]{:S(2)}) collective-permute-start(f32[128,128]{1,0:T(8,128)S(1)} %finished_piece.1), channel_id=1, source_target_pairs={{0,4},{2,6},{4,0},{6,2},{1,5},{3,7},{5,1},{7,3},{8,12},{10,14},{12... | collective-permute-start | bytes 196616 | tf_op jit(solution)/shard_map/ppermute | solution.py:283
  63.8 3.7 %collective-permute-start.19 = (f32[128,128]{1,0:T(8,128)S(1)}, f32[128,128]{1,0:T(8,128)S(1)}, u32[]{:S(2)}, u32[]{:S(2)}) collective-permute-start(f32[128,128]{1,0:T(8,128)S(1)} %finished_piece.1), channel_id=1, source_target_pairs={{0,2},{2,0},{4,6},{6,4},{1,3},{3,1},{5,7},{7,5},{8,10},{10,8},{12,... | collective-permute-start | bytes 196616 | tf_op jit(solution)/shard_map/ppermute | solution.py:283
  67.6 5.9 %collective-permute-start.22 = (f32[4,128,128]{2,1,0:T(8,128)S(1)}, f32[4,128,128]{2,1,0:T(8,128)S(1)}, u32[]{:S(2)}, u32[]{:S(2)}) collective-permute-start(f32[4,128,128]{2,1,0:T(8,128)S(1)} %pad_maximum_fusion.pieces_ref), channel_id=1, source_target_pairs={{0,1},{1,0},{2,3},{3,2},{4,5},{5,4},{6,7},{7,6},{8,9},{9,8},{10,11... | collective-permute-start | bytes 786440 | tf_op jit(solution)/shard_map/ppermute | solution.py:283

commit v5 on v4

--- a/solution.py
+++ b/solution.py
@@ -48,47 +48,51 @@
     return jnp.concatenate([packed[:, 32 * i : 32 * i + 32] for i in range(4)], axis=0)
 
 
-def left_columns(packed, m):
-    columns = [packed[:, RANK * i : RANK * i + RANK] for i in range(4)]
-    return jnp.concatenate([jnp.where(m == 0, columns[0], columns[1]), jnp.where(m == 0, columns[2], columns[3])], axis=0)
-
-
-def left_kernel(grads_hbm, errors_hbm, q_hbm, full_ref, p_ref, grads_ref, q_ref, grads_sem, errors_sem, q_sem):
-    projections, rows, _ = full_ref.shape
+def pack_rows(columns):
+    rows = columns.shape[0] // 4
+    return jnp.concatenate([columns[rows * i : rows * (i + 1)] for i in range(4)], axis=1)
+
+
+def unpack_rows(packed):
+    return jnp.concatenate([packed[:, RANK * i : RANK * (i + 1)] for i in range(4)], axis=0)
+
+
+def left_kernel(grads_hbm, errors_hbm, q_hbm, other_ref, own_ref, p_other_ref, p_own_ref, grads_ref, q_ref, grads_sem, errors_sem, q_sem):
+    core = lax.axis_index("c")
+    parts = ((1 - core, other_ref, p_other_ref), (core, own_ref, p_own_ref))
     q_copy = pltpu.make_async_copy(q_hbm, q_ref, q_sem)
     copies = [
         (
-            pltpu.make_async_copy(grads_hbm.at[0, m], grads_ref.at[m], grads_sem.at[m]),
-            pltpu.make_async_copy(errors_hbm.at[0, m], full_ref.at[m], errors_sem.at[m]),
+            pltpu.make_async_copy(grads_hbm.at[0, m], grads_ref.at[i], grads_sem.at[i]),
+            pltpu.make_async_copy(errors_hbm.at[0, m], full_ref, errors_sem.at[i]),
         )
-        for m in range(projections)
+        for i, (m, full_ref, _) in enumerate(parts)
     ]
     q_copy.start()
     for pair in copies:
         for copy in pair:
             copy.start()
     q_copy.wait()
-    for m, pair in enumerate(copies):
+    for i, (m, full_ref, p_ref) in enumerate(parts):
         q_hi, q_lo = split(q_ref[m])
         both = jnp.concatenate([q_hi, q_lo], axis=0)
-        for copy in pair:
+        for copy in copies[i]:
             copy.wait()
-        full = grads_ref[m].astype(F32) + full_ref[m]
-        full_ref[m] = full
+        full = grads_ref[i].astype(F32) + full_ref[...]
+        full_ref[...] = full
         f_hi, f_lo = split(full)
         wide = dot(f_hi, both, 1, 1)
-        p = wide[:, :RANK] + wide[:, RANK:] + dot(f_lo, q_hi, 1, 1)
-        p_ref[:, RANK * m : RANK * (m + 1)] = p[: rows // 2]
-        p_ref[:, RANK * (2 + m) : RANK * (3 + m)] = p[rows // 2 :]
+        p_ref[...] = pack_rows(wide[:, :RANK] + wide[:, RANK:] + dot(f_lo, q_hi, 1, 1))
 
 
 def left_factors(grads, errors, q_prev):
     _, projections, rows, columns = grads.shape
+    full, p = pltpu.VMEM((rows, columns), F32), pltpu.VMEM((rows // 4, LANES), F32)
     return pl.pallas_call(
         left_kernel,
         in_specs=[AWAY] * 3,
-        out_specs=[WHOLE] * 2,
-        out_shape=[pltpu.VMEM((projections, rows, columns), F32), pltpu.VMEM((rows // 2, LANES), F32)],
+        out_specs=[WHOLE] * 4,
+        out_shape=[full, full, p, p],
         scratch_shapes=[
             pltpu.VMEM((projections, rows, columns), BF16),
             pltpu.VMEM(q_prev.shape, F32),
@@ -101,19 +105,20 @@
     )(in_hbm(grads), in_hbm(errors), in_hbm(q_prev))
 
 
-def right_kernel(replicas, mine, p_ref, full_ref, out_ref):
+def right_kernel(replicas, p_ref, own_ref, gift_ref, out_ref):
     slots, height, _ = out_ref.shape
     tiles = (height - 8) // RANK
     width = tiles * LANES
-    x, core = lax.axis_index("x"), lax.axis_index("c")
-    m = core if mine else 1 - core
-    p = (left_columns(p_ref[...], m) * (1.0 / replicas)).T
+    x = lax.axis_index("x")
+    half = p_ref.shape[0] // 2
+    columns = jnp.concatenate([unpack_rows(p_ref[:half]), unpack_rows(p_ref[half:])], axis=0)
+    p = (columns * (1.0 / replicas)).T
     p_hi, p_lo = split(p)
     both = jnp.concatenate([p_hi, p_lo], axis=0)
     gram = pack(dot(p, p, 1, 1, lax.Precision.HIGHEST))
     for slot in range(slots):
-        first = pl.multiple_of((x ^ slot) * width, width)
-        f_hi, f_lo = split(full_ref[m, :, pl.ds(first, width)])
+        here = pl.ds(pl.multiple_of((x ^ slot) * width, width), width)
+        f_hi, f_lo = split(jnp.concatenate([own_ref[:, here], gift_ref[:, here]], axis=0))
         wide = dot(both, f_hi, 1, 0)
         q = wide[:RANK] + wide[RANK:] + dot(p_hi, f_lo, 1, 0)
         for j in range(tiles):
@@ -121,16 +126,16 @@
         out_ref[slot, tiles * RANK :, :] = gram
 
 
-def right_terms(p_sum, full, replicas, slots, mine):
-    height = full.shape[2] // slots // LANES * RANK + 8
-    return pl.pallas_call(
-        functools.partial(right_kernel, replicas, mine),
-        in_specs=[WHOLE] * 2,
+def right_terms(p_sum, own, gift, replicas, slots):
+    height = own.shape[1] // slots // LANES * RANK + 8
+    return pl.pallas_call(
+        functools.partial(right_kernel, replicas),
+        in_specs=[WHOLE] * 3,
         out_specs=WHOLE,
         out_shape=jax.ShapeDtypeStruct((slots, height, LANES), F32),
         compiler_params=PARAMS,
-        name="right_terms_own" if mine else "right_terms_other",
-    )(p_sum, full)
+        name="right_terms",
+    )(p_sum, own, gift)
 
 
 def factor_kernel(sum_ref, out_ref):
@@ -163,30 +168,48 @@
     )(total)
 
 
-def hat_kernel(replicas, p_ref, own_ref, other_ref, hat_ref, rows_ref):
+def hat_kernel(replicas, p_ref, inverse_ref, own_ref, other_ref):
+    half = p_ref.shape[0] // 2
+    inverse = unpack(inverse_ref[...])
+    for i, out_ref in enumerate((own_ref, other_ref)):
+        p = unpack_rows(p_ref[half * i : half * (i + 1)]) * (1.0 / replicas)
+        out_ref[...] = pack_rows(dot(p, inverse, 1, 1, lax.Precision.HIGHEST))
+
+
+def orthonormal(p_sum, inverse, replicas):
+    half = jax.ShapeDtypeStruct((p_sum.shape[0] // 2, LANES), F32)
+    return pl.pallas_call(
+        functools.partial(hat_kernel, replicas),
+        in_specs=[WHOLE] * 2,
+        out_specs=[WHOLE] * 2,
+        out_shape=[half, half],
+        compiler_params=PARAMS,
+        cost_estimate=pl.CostEstimate(flops=4_000_000, bytes_accessed=1_000_000, transcendentals=64),
+        name="orthonormal",
+    )(p_sum, inverse)
+
+
+def side_kernel(replicas, own_ref, other_ref, hat_ref, rows_ref):
     rows = hat_ref.shape[1]
-    share = rows // replicas
-    core = lax.axis_index("c")
-    at = lax.broadcasted_iota(jnp.int32, (16, rows), 0) + lax.axis_index(("z", "y")) * share
+    at = lax.broadcasted_iota(jnp.int32, (16, rows), 0) + lax.axis_index(("z", "y")) * (rows // replicas)
     chosen = (lax.broadcasted_iota(jnp.int32, (16, rows), 1) == at).astype(F32)
-    for i, (inverse_ref, m) in enumerate(((own_ref, core), (other_ref, 1 - core))):
-        p = left_columns(p_ref[...], m) * (1.0 / replicas)
-        hat = dot(p, unpack(inverse_ref[...]), 1, 1, lax.Precision.HIGHEST)
+    for i, ref in enumerate((own_ref, other_ref)):
+        hat = unpack_rows(ref[...])
         hat_ref[i] = left_three(hat)
         rows_ref[i] = left_three(dot(chosen, hat, 1, 0, lax.Precision.HIGHEST))
 
 
-def orthonormal(p_sum, own, other, replicas):
-    rows = 2 * p_sum.shape[0]
-    return pl.pallas_call(
-        functools.partial(hat_kernel, replicas),
-        in_specs=[WHOLE] * 3,
+def left_sides(own, other, replicas):
+    rows = 4 * own.shape[0]
+    return pl.pallas_call(
+        functools.partial(side_kernel, replicas),
+        in_specs=[WHOLE] * 2,
         out_specs=[WHOLE] * 2,
         out_shape=[jax.ShapeDtypeStruct((2, rows, 3 * RANK), BF16), jax.ShapeDtypeStruct((2, 16, 3 * RANK), BF16)],
         compiler_params=PARAMS,
-        cost_estimate=pl.CostEstimate(flops=4_000_000, bytes_accessed=3_000_000, transcendentals=64),
-        name="orthonormal",
-    )(p_sum, own, other)
+        cost_estimate=pl.CostEstimate(flops=4_000_000, bytes_accessed=1_000_000, transcendentals=64),
+        name="left_sides",
+    )(own, other)
 
 
 def piece_kernel(replicas, a_ref, b_ref, inverse_ref, out_ref):
@@ -223,7 +246,7 @@
         here = pl.ds(pl.multiple_of(block * width, width), width)
         q = jnp.concatenate([pieces_ref[slot, j * RANK : (j + 1) * RANK, :] for j in range(tiles)], axis=1)
         right = right_three(q)
-        err_ref[slot] = full_ref[m, :, here] - dot(hat_ref[i], right, 1, 0)
+        err_ref[slot] = full_ref[:, here] - dot(hat_ref[i], right, 1, 0)
         copies.append(pltpu.make_async_copy(err_ref.at[slot], err_hbm.at[0, m, :, here], err_sem.at[slot]))
         copies[-1].start()
         q_ref[:, here] = q
@@ -247,8 +270,8 @@
 
 
 def update(pieces, hat, rows, full, moment1, moment2, mine, before=()):
-    projections, depth, columns = full.shape
-    slots, height, _ = pieces.shape
+    depth, columns = full.shape
+    projections, slots = hat.shape[0], pieces.shape[0]
     state, tiles = moment1.shape[1], columns // LANES
     return pl.pallas_call(
         functools.partial(update_kernel, mine),
@@ -289,24 +312,30 @@
 
 def shards(grads, errors, q_prev, moment1, moment2):
     replicas, slots = lax.axis_size(("z", "y")), lax.axis_size("x")
-    full, p = left_factors(grads, errors, q_prev)
+    other_full, own_full, p_other, p_own = left_factors(grads, errors, q_prev)
+    p = jnp.concatenate([p_own, swap(p_other, "c", 1)])
+    p, other_full = lax.optimization_barrier((p, other_full))
+    gift = swap(other_full, "c", 1)
     p = four([p] * 4, "y")
     p = four([p] * 4, "z")
     p = p + swap(p, "z", 6)
 
-    terms = swap(right_terms(p, full, replicas, slots, False), "c", 1) + right_terms(p, full, replicas, slots, True)
+    terms = right_terms(p, own_full, gift, replicas, slots)
     total = four([terms[i] for i in range(slots)], "x")
     inverse = inverse_factor(total)
     q = four([total[:-8]] * 4, "y")
     q, inverse = lax.optimization_barrier((q, inverse))
-    hat, rows = orthonormal(p, inverse, swap(inverse, "c", 1), replicas)
+    hat_own, hat_other = orthonormal(p, inverse, replicas)
+    hat_gift = swap(hat_other, "c", 1)
     q = four([q] * 4, "z")
-    q, hat, rows = lax.optimization_barrier((q, hat, rows))
-    piece = finished_piece(q, swap(q, "z", 6), inverse, replicas)
+    q, hat_own, hat_gift = lax.optimization_barrier((q, hat_own, hat_gift))
+    hat, rows = left_sides(hat_own, hat_gift, replicas)
+    far, hat, rows = lax.optimization_barrier((swap(q, "z", 6), hat, rows))
+    piece = finished_piece(q, far, inverse, replicas)
     own = jnp.stack([piece] + [swap(piece, "x", i) for i in range(1, slots)])
     other = swap(own, "c", 1)
-    done = update(own, hat, rows, full, moment1, moment2, True)
-    return tuple(update(other, hat, rows, full, moment1, moment2, False, done))
+    done = update(own, hat, rows, own_full, moment1, moment2, True)
+    return tuple(update(other, hat, rows, other_full, moment1, moment2, False, done))
 
 
 def solution(mesh):

time: 75.4 us -> 75.3 us (level)
  starting transfers between devices: 41.6 us -> 43.1 us
  waiting for transfers between devices: 20.4 us -> 19 us
    ppermute x23 -> x24, starting transfers between devices: 41.6 us -> 43.1 us  [swap(): lax.ppermute(value, axis, [(i, i ^ bit) for i in range(lax.axis_size(axis...]
    ppermute x23 -> x24, waiting for transfers between devices: 20.4 us -> 19 us  [swap(): lax.ppermute(value, axis, [(i, i ^ bit) for i in range(lax.axis_size(axis...]
  transfers between devices with their start and end apart: 23 -> 24, of which waited for: 13 -> 14; matrix products, arithmetic and copies ran while one was open for 0% -> 0% of each run, Pallas kernels for 8% -> 7%
where the time goes in v5:
time: 75.3 us; the launch traced here: 75.2 us
  starting transfers between devices  43.1 us (57%)
  waiting for transfers between devices  19 us (25%)
  Pallas kernels  12 us (16%)
  between operations  0.91 us (1%)
    ppermute x24, starting transfers between devices, swap(): lax.ppermute(value, axis, [(i, i ^ bit) for i in range(lax.axis_size(axis...  43.1 us
    ppermute x24, waiting for transfers between devices, swap(): lax.ppermute(value, axis, [(i, i ^ bit) for i in range(lax.axis_size(axis...  19 us
    pallas_call x1, Pallas kernels, left_factors(): pl.pallas_call(left_kernel, in_specs=[AWAY] * 3, out_specs=[WHOLE] * 4, o...  3.64 us
    pallas_call x2, Pallas kernels, update(): pl.pallas_call(functools.partial(update_kernel, mine), in_specs=[WHOLE] *...  3.3 us
    pallas_call x1, Pallas kernels, inverse_factor(): pl.pallas_call(factor_kernel, in_specs=[WHOLE], out_specs=WHOLE, out_shap...  2.85 us
  transfers between devices with their start and end apart: 24, of which 14 were waited for; matrix products, arithmetic and copies ran while one was open for 0% of the time, Pallas kernels for 7%

profile of v5, /device:TPU:1, one launch (start us, length us, event | category | flops | bytes accessed | tf_op | source)
XLA Modules:
  0.0 75.2 jit_solution(16007306001417317972)
XLA Ops:
  0.6 3.6 %left_factors.1 = (f32[224,2048]{1,0:T(8,128)S(1)}, f32[224,2048]{1,0:T(8,128)S(1)}, f32[56,128]{1,0:T(8,128)S(1)}, f32[56,128]{1,0:T(8,128)S(1)}) custom-call(bf16[1,2,224,2048]{3,2,1,0:T(8,128)(2,1)} %grads_hbm.1, f32[1,2,224,2048]{3,2,1,0:T(8,128)} %errors_hbm.1, f32[2,32,2048]{2,1,0:T(8,128)} %q_hbm.1), custom_call_target="tpu_custom_call" | custom-call | tf_op jit(solution)/shard_map/left_factors/pallas_call | solution.py:91
  4.3 3.3 %collective-permute-start = (f32[56,128]{1,0:T(8,128)S(1)}, f32[56,128]{1,0:T(8,128)S(1)}, u32[]{:S(2)}, u32[]{:S(2)}) collective-permute-start(f32[56,128]{1,0:T(8,128)S(1)} %get-tuple-element.29), channel_id=1, source_target_pairs={{0,1},{1,0},{2,3},{3,2},{4,5},{5,4},{6,7},{7,6},{8,9},{9,8},{10,11... | collective-permute-start | bytes 86024 | tf_op jit(solution)/shard_map/ppermute | solution.py:306
  7.6 0.9 %collective-permute-done = f32[56,128]{1,0:T(8,128)S(1)} collective-permute-done((f32[56,128]{1,0:T(8,128)S(1)}, f32[56,128]{1,0:T(8,128)S(1)}, u32[]{:S(2)}, u32[]{:S(2)}) %collective-permute-start) | collective-permute-done | bytes 28704 | tf_op jit(solution)/shard_map/ppermute | solution.py:306
  8.8 1.0 %collective-permute-start.3 = (f32[112,128]{1,0:T(8,128)S(1)}, f32[112,128]{1,0:T(8,128)S(1)}, u32[]{:S(2)}, u32[]{:S(2)}) collective-permute-start(f32[112,128]{1,0:T(8,128)S(1)} %pad_maximum_fusion.1), channel_id=1, source_target_pairs={{0,24},{8,16},{16,8},{24,0},{1,25},{9,17},{17,9},{25,1},{2,26},{10... | collective-permute-start | bytes 172040 | tf_op jit(solution)/shard_map/ppermute | solution.py:306
  10.2 1.9 %collective-permute-start.1 = (f32[112,128]{1,0:T(8,128)S(1)}, f32[112,128]{1,0:T(8,128)S(1)}, u32[]{:S(2)}, u32[]{:S(2)}) collective-permute-start(f32[112,128]{1,0:T(8,128)S(1)} %pad_maximum_fusion.1), channel_id=1, source_target_pairs={{0,8},{8,0},{16,24},{24,16},{1,9},{9,1},{17,25},{25,17},{2,10},{10... | collective-permute-start | bytes 172040 | tf_op jit(solution)/shard_map/ppermute | solution.py:306
  12.1 1.0 %collective-permute-done.3 = f32[112,128]{1,0:T(8,128)S(1)} collective-permute-done((f32[112,128]{1,0:T(8,128)S(1)}, f32[112,128]{1,0:T(8,128)S(1)}, u32[]{:S(2)}, u32[]{:S(2)}) %collective-permute-start.3) | collective-permute-done | bytes 57376 | tf_op jit(solution)/shard_map/ppermute | solution.py:306
  13.1 1.3 %collective-permute-done.2 = f32[112,128]{1,0:T(8,128)S(1)} collective-permute-done((f32[112,128]{1,0:T(8,128)S(1)}, f32[112,128]{1,0:T(8,128)S(1)}, u32[]{:S(2)}, u32[]{:S(2)}) %collective-permute-start.2) | collective-permute-done | bytes 57376 | tf_op jit(solution)/shard_map/ppermute | solution.py:306
  14.9 3.9 %collective-permute-start.6 = (f32[112,128]{1,0:T(8,128)S(1)}, f32[112,128]{1,0:T(8,128)S(1)}, u32[]{:S(2)}, u32[]{:S(2)}) collective-permute-start(f32[112,128]{1,0:T(8,128)S(1)} %add_add_fusion.3), channel_id=1, source_target_pairs={{0,96},{32,64},{64,32},{96,0},{128,224},{160,192},{192,160},{224,1... | collective-permute-start | bytes 172040 | tf_op jit(solution)/shard_map/ppermute | solution.py:306
  19.2 1.2 %collective-permute-done.6 = f32[112,128]{1,0:T(8,128)S(1)} collective-permute-done((f32[112,128]{1,0:T(8,128)S(1)}, f32[112,128]{1,0:T(8,128)S(1)}, u32[]{:S(2)}, u32[]{:S(2)}) %collective-permute-start.6) | collective-permute-done | bytes 57376 | tf_op jit(solution)/shard_map/ppermute | solution.py:306
  20.4 2.7 %collective-permute-done.5 = f32[112,128]{1,0:T(8,128)S(1)} collective-permute-done((f32[112,128]{1,0:T(8,128)S(1)}, f32[112,128]{1,0:T(8,128)S(1)}, u32[]{:S(2)}, u32[]{:S(2)}) %collective-permute-start.5) | collective-permute-done | bytes 57376 | tf_op jit(solution)/shard_map/ppermute | solution.py:306
  23.1 3.9 %collective-permute-start.7 = (f32[112,128]{1,0:T(8,128)S(1)}, f32[112,128]{1,0:T(8,128)S(1)}, u32[]{:S(2)}, u32[]{:S(2)}) collective-permute-start(f32[112,128]{1,0:T(8,128)S(1)} %add_add_fusion.2), channel_id=1, source_target_pairs={{0,192},{32,224},{64,128},{96,160},{128,64},{160,96},{192,0},{224,... | collective-permute-start | bytes 172040 | tf_op jit(solution)/shard_map/ppermute | solution.py:306
  27.0 2.1 %collective-permute-done.7 = f32[112,128]{1,0:T(8,128)S(1)} collective-permute-done((f32[112,128]{1,0:T(8,128)S(1)}, f32[112,128]{1,0:T(8,128)S(1)}, u32[]{:S(2)}, u32[]{:S(2)}) %collective-permute-start.7) | collective-permute-done | bytes 57376 | tf_op jit(solution)/shard_map/ppermute | solution.py:306
  29.1 1.1 %right_terms.1 = f32[4,136,128]{2,1,0:T(8,128)S(1)} custom-call(f32[112,128]{1,0:T(8,128)S(1)} %add.54.p_ref, f32[224,2048]{1,0:T(8,128)S(1)} %get-tuple-element.32.own_ref.full_ref, f32[224,2048]{1,0:T(8,128)S(1)} %collective-permute-done.8.gift_ref), custom_call_target="tpu_custom_call" | custom-call | tf_op jit(solution)/shard_map/right_terms/pallas_call | solution.py:131
  30.2 2.6 %collective-permute-start.11 = (f32[136,128]{1,0:T(8,128)S(1)}, f32[136,128]{1,0:T(8,128)S(1)}, u32[]{:S(2)}, u32[]{:S(2)}) collective-permute-start(f32[136,128]{1,0:T(8,128)S(1)} %get-tuple-element.51), channel_id=1, source_target_pairs={{0,6},{2,4},{4,2},{6,0},{1,7},{3,5},{5,3},{7,1},{8,14},{10,12},{12... | collective-permute-start | bytes 208904 | tf_op jit(solution)/shard_map/ppermute | solution.py:306
  33.5 1.1 %collective-permute-done.11 = f32[136,128]{1,0:T(8,128)S(1)} collective-permute-done((f32[136,128]{1,0:T(8,128)S(1)}, f32[136,128]{1,0:T(8,128)S(1)}, u32[]{:S(2)}, u32[]{:S(2)}) %collective-permute-start.11) | collective-permute-done | bytes 69664 | tf_op jit(solution)/shard_map/ppermute | solution.py:306
  34.6 2.8 %collective-permute-done.10 = f32[136,128]{1,0:T(8,128)S(1)} collective-permute-done((f32[136,128]{1,0:T(8,128)S(1)}, f32[136,128]{1,0:T(8,128)S(1)}, u32[]{:S(2)}, u32[]{:S(2)}) %collective-permute-start.10) | collective-permute-done | bytes 69664 | tf_op jit(solution)/shard_map/ppermute | solution.py:306
  37.5 1.9 %collective-permute-start.13 = (f32[128,128]{1,0:T(8,128)S(1)}, f32[128,128]{1,0:T(8,128)S(1)}, u32[]{:S(2)}, u32[]{:S(2)}) collective-permute-start(f32[128,128]{1,0:T(8,128)S(1)} %slice.24), channel_id=1, source_target_pairs={{0,16},{8,24},{16,0},{24,8},{1,17},{9,25},{17,1},{25,9},{2,18},{10... | collective-permute-start | bytes 196616 | tf_op jit(solution)/shard_map/ppermute | solution.py:306
  40.2 2.8 %inverse_factor.1.inverse_ref = f32[8,128]{1,0:T(8,128)S(1)} custom-call(f32[136,128]{1,0:T(8,128)S(1)} %fusion.1.sum_ref), custom_call_target="tpu_custom_call" | custom-call | flops 4000000 | bytes 4000000 | tf_op jit(solution)/shard_map/inverse_factor/pallas_call | solution.py:160
  43.7 1.7 %collective-permute-start.17 = (f32[128,128]{1,0:T(8,128)S(1)}, f32[128,128]{1,0:T(8,128)S(1)}, u32[]{:S(2)}, u32[]{:S(2)}) collective-permute-start(f32[128,128]{1,0:T(8,128)S(1)} %add_add_fusion.1), channel_id=1, source_target_pairs={{0,96},{32,64},{64,32},{96,0},{128,224},{160,192},{192,160},{224,1... | collective-permute-start | bytes 196616 | tf_op jit(solution)/shard_map/ppermute | solution.py:306
  45.4 1.8 %collective-permute-start.16 = (f32[128,128]{1,0:T(8,128)S(1)}, f32[128,128]{1,0:T(8,128)S(1)}, u32[]{:S(2)}, u32[]{:S(2)}) collective-permute-start(f32[128,128]{1,0:T(8,128)S(1)} %add_add_fusion.1), channel_id=1, source_target_pairs={{0,64},{32,96},{64,0},{96,32},{128,192},{160,224},{192,128},{224,1... | collective-permute-start | bytes 196616 | tf_op jit(solution)/shard_map/ppermute | solution.py:306
  47.9 7.1 %collective-permute-start.18 = (f32[56,128]{1,0:T(8,128)S(1)}, f32[56,128]{1,0:T(8,128)S(1)}, u32[]{:S(2)}, u32[]{:S(2)}) collective-permute-start(f32[56,128]{1,0:T(8,128)S(1)} %get-tuple-element.37), channel_id=1, source_target_pairs={{0,1},{1,0},{2,3},{3,2},{4,5},{5,4},{6,7},{7,6},{8,9},{9,8},{10,11... | collective-permute-start | bytes 86024 | tf_op jit(solution)/shard_map/ppermute | solution.py:306
  55.0 0.8 %collective-permute-done.18.other_ref = f32[56,128]{1,0:T(8,128)S(1)} collective-permute-done((f32[56,128]{1,0:T(8,128)S(1)}, f32[56,128]{1,0:T(8,128)S(1)}, u32[]{:S(2)}, u32[]{:S(2)}) %collective-permute-start.18) | collective-permute-done | bytes 28704 | tf_op jit(solution)/shard_map/ppermute | solution.py:306
  55.8 3.4 %collective-permute-start.19 = (f32[128,128]{1,0:T(8,128)S(1)}, f32[128,128]{1,0:T(8,128)S(1)}, u32[]{:S(2)}, u32[]{:S(2)}) collective-permute-start(f32[128,128]{1,0:T(8,128)S(1)} %add_add_fusion.a_ref), channel_id=1, source_target_pairs={{0,192},{32,224},{64,128},{96,160},{128,64},{160,96},{192,0},{224,... | collective-permute-start | bytes 196616 | tf_op jit(solution)/shard_map/ppermute | solution.py:306
  59.6 1.5 %collective-permute-done.19.b_ref = f32[128,128]{1,0:T(8,128)S(1)} collective-permute-done((f32[128,128]{1,0:T(8,128)S(1)}, f32[128,128]{1,0:T(8,128)S(1)}, u32[]{:S(2)}, u32[]{:S(2)}) %collective-permute-start.19) | collective-permute-done | bytes 65568 | tf_op jit(solution)/shard_map/ppermute | solution.py:306
  61.4 1.1 %collective-permute-start.22 = (f32[128,128]{1,0:T(8,128)S(1)}, f32[128,128]{1,0:T(8,128)S(1)}, u32[]{:S(2)}, u32[]{:S(2)}) collective-permute-start(f32[128,128]{1,0:T(8,128)S(1)} %finished_piece.1), channel_id=1, source_target_pairs={{0,6},{2,4},{4,2},{6,0},{1,7},{3,5},{5,3},{7,1},{8,14},{10,12},{12... | collective-permute-start | bytes 196616 | tf_op jit(solution)/shard_map/ppermute | solution.py:306
  62.5 0.7 collective-permute-start.21
  63.2 1.4 %collective-permute-start.20 = (f32[128,128]{1,0:T(8,128)S(1)}, f32[128,128]{1,0:T(8,128)S(1)}, u32[]{:S(2)}, u32[]{:S(2)}) collective-permute-start(f32[128,128]{1,0:T(8,128)S(1)} %finished_piece.1), channel_id=1, source_target_pairs={{0,2},{2,0},{4,6},{6,4},{1,3},{3,1},{5,7},{7,5},{8,10},{10,8},{12,... | collective-permute-start | bytes 196616 | tf_op jit(solution)/shard_map/ppermute | solution.py:306
  64.6 1.1 %collective-permute-done.22 = f32[128,128]{1,0:T(8,128)S(1)} collective-permute-done((f32[128,128]{1,0:T(8,128)S(1)}, f32[128,128]{1,0:T(8,128)S(1)}, u32[]{:S(2)}, u32[]{:S(2)}) %collective-permute-start.22) | collective-permute-done | bytes 65568 | tf_op jit(solution)/shard_map/ppermute | solution.py:306
  65.7 1.4 %collective-permute-done.21 = f32[128,128]{1,0:T(8,128)S(1)} collective-permute-done((f32[128,128]{1,0:T(8,128)S(1)}, f32[128,128]{1,0:T(8,128)S(1)}, u32[]{:S(2)}, u32[]{:S(2)}) %collective-permute-start.21) | collective-permute-done | bytes 65568 | tf_op jit(solution)/shard_map/ppermute | solution.py:306
  67.1 4.6 %collective-permute-start.23 = (f32[4,128,128]{2,1,0:T(8,128)S(1)}, f32[4,128,128]{2,1,0:T(8,128)S(1)}, u32[]{:S(2)}, u32[]{:S(2)}) collective-permute-start(f32[4,128,128]{2,1,0:T(8,128)S(1)} %pad_maximum_fusion.pieces_ref), channel_id=1, source_target_pairs={{0,1},{1,0},{2,3},{3,2},{4,5},{5,4},{6,7},{7,6},{8,9},{9,8},{10,11... | collective-permute-start | bytes 786440 | tf_op jit(solution)/shard_map/ppermute | solution.py:306
  71.8 1.6 %update_own.1 = (f32[1,2,224,2048]{3,2,1,0:T(8,128)}, f32[2,112,128]{2,1,0:T(8,128)}, f32[2,112,128]{2,1,0:T(8,128)}, bf16[2,112,128]{2,1,0:T(8,128)(2,1)}, f32[2,32,2048]{2,1,0:T(8,128)}) custom-call(f32[4,128,128]{2,1,0:T(8,128)S(1)} %pad_maximum_fusion.pieces_ref, bf16[2,224,96]{2,1,0:T(8,128)(2,1)S(1)} %get-tuple-element.44.hat_ref, ...), custom_call_target="tpu_custom_call" | custom-call | flops 100000000 | bytes 4000000 | tf_op jit(solution)/shard_map/update_own/pallas_call | solution.py:276
  73.4 1.6 %update_other.1 = (f32[1,2,224,2048]{3,2,1,0:T(8,128)}, f32[2,112,128]{2,1,0:T(8,128)}, f32[2,112,128]{2,1,0:T(8,128)}, bf16[2,112,128]{2,1,0:T(8,128)(2,1)}, f32[2,32,2048]{2,1,0:T(8,128)}) custom-call(f32[4,128,128]{2,1,0:T(8,128)S(1)} %collective-permute-done.23.pieces_ref, ...), custom_call_target="tpu_custom_call", output_to_operand_aliasing={{0}: (6, {}), {1}: (7, {}), {2}: (8, {}), {3}: (9, {}), {4}... | custom-call | flops 100000000 | bytes 4000000 | tf_op jit(solution)/shard_map/update_other/pallas_call | solution.py:276
  (38 shorter events, 5.3 us)
Async XLA Ops:
  4.3 4.2 %collective-permute-start = (f32[56,128]{1,0:T(8,128)S(1)}, f32[56,128]{1,0:T(8,128)S(1)}, u32[]{:S(2)}, u32[]{:S(2)}) collective-permute-start(f32[56,128]{1,0:T(8,128)S(1)} %get-tuple-element.29), channel_id=1, source_target_pairs={{0,1},{1,0},{2,3},{3,2},{4,5},{5,4},{6,7},{7,6},{8,9},{9,8},{10,11... | collective-permute-start | bytes 86024 | tf_op jit(solution)/shard_map/ppermute | solution.py:306
  8.5 20.6 %collective-permute-start.8 = (f32[224,2048]{1,0:T(8,128)S(1)}, f32[224,2048]{1,0:T(8,128)S(1)}, u32[]{:S(2)}, u32[]{:S(2)}) collective-permute-start(f32[224,2048]{1,0:T(8,128)S(1)} %get-tuple-element.33.full_ref), channel_id=1, source_target_pairs={{0,1},{1,0},{2,3},{3,2},{4,5},{5,4},{6,7},{7,6},{8,9},{9,8},{10,11... | collective-permute-start | bytes 5505032 | tf_op jit(solution)/shard_map/ppermute | solution.py:306
  8.8 4.2 %collective-permute-start.3 = (f32[112,128]{1,0:T(8,128)S(1)}, f32[112,128]{1,0:T(8,128)S(1)}, u32[]{:S(2)}, u32[]{:S(2)}) collective-permute-start(f32[112,128]{1,0:T(8,128)S(1)} %pad_maximum_fusion.1), channel_id=1, source_target_pairs={{0,24},{8,16},{16,8},{24,0},{1,25},{9,17},{17,9},{25,1},{2,26},{10... | collective-permute-start | bytes 172040 | tf_op jit(solution)/shard_map/ppermute | solution.py:306
  9.8 4.5 %collective-permute-start.2 = (f32[112,128]{1,0:T(8,128)S(1)}, f32[112,128]{1,0:T(8,128)S(1)}, u32[]{:S(2)}, u32[]{:S(2)}) collective-permute-start(f32[112,128]{1,0:T(8,128)S(1)} %pad_maximum_fusion.1), channel_id=1, source_target_pairs={{0,16},{8,24},{16,0},{24,8},{1,17},{9,25},{17,1},{25,9},{2,18},{10... | collective-permute-start | bytes 172040 | tf_op jit(solution)/shard_map/ppermute | solution.py:306
  10.2 4.7 %collective-permute-start.1 = (f32[112,128]{1,0:T(8,128)S(1)}, f32[112,128]{1,0:T(8,128)S(1)}, u32[]{:S(2)}, u32[]{:S(2)}) collective-permute-start(f32[112,128]{1,0:T(8,128)S(1)} %pad_maximum_fusion.1), channel_id=1, source_target_pairs={{0,8},{8,0},{16,24},{24,16},{1,9},{9,1},{17,25},{25,17},{2,10},{10... | collective-permute-start | bytes 172040 | tf_op jit(solution)/shard_map/ppermute | solution.py:306
  14.9 5.5 %collective-permute-start.6 = (f32[112,128]{1,0:T(8,128)S(1)}, f32[112,128]{1,0:T(8,128)S(1)}, u32[]{:S(2)}, u32[]{:S(2)}) collective-permute-start(f32[112,128]{1,0:T(8,128)S(1)} %add_add_fusion.3), channel_id=1, source_target_pairs={{0,96},{32,64},{64,32},{96,0},{128,224},{160,192},{192,160},{224,1... | collective-permute-start | bytes 172040 | tf_op jit(solution)/shard_map/ppermute | solution.py:306
  18.8 4.3 %collective-permute-start.5 = (f32[112,128]{1,0:T(8,128)S(1)}, f32[112,128]{1,0:T(8,128)S(1)}, u32[]{:S(2)}, u32[]{:S(2)}) collective-permute-start(f32[112,128]{1,0:T(8,128)S(1)} %add_add_fusion.3), channel_id=1, source_target_pairs={{0,64},{32,96},{64,0},{96,32},{128,192},{160,224},{192,128},{224,1... | collective-permute-start | bytes 172040 | tf_op jit(solution)/shard_map/ppermute | solution.py:306
  18.8 4.3 %collective-permute-start.4 = (f32[112,128]{1,0:T(8,128)S(1)}, f32[112,128]{1,0:T(8,128)S(1)}, u32[]{:S(2)}, u32[]{:S(2)}) collective-permute-start(f32[112,128]{1,0:T(8,128)S(1)} %add_add_fusion.3), channel_id=1, source_target_pairs={{0,32},{32,0},{64,96},{96,64},{128,160},{160,128},{192,224},{224,1... | collective-permute-start | bytes 172040 | tf_op jit(solution)/shard_map/ppermute | solution.py:306
  23.1 5.9 %collective-permute-start.7 = (f32[112,128]{1,0:T(8,128)S(1)}, f32[112,128]{1,0:T(8,128)S(1)}, u32[]{:S(2)}, u32[]{:S(2)}) collective-permute-start(f32[112,128]{1,0:T(8,128)S(1)} %add_add_fusion.2), channel_id=1, source_target_pairs={{0,192},{32,224},{64,128},{96,160},{128,64},{160,96},{192,0},{224,... | collective-permute-start | bytes 172040 | tf_op jit(solution)/shard_map/ppermute | solution.py:306
  30.1 41.6 %copy-start = (f32[2,112,128]{2,1,0:T(8,128)S(1)}, f32[2,112,128]{2,1,0:T(8,128)}, u32[]{:S(2)}) copy-start(f32[2,112,128]{2,1,0:T(8,128)} %m1_ref.3) | copy-start | bytes 344068
  30.2 41.6 %copy-start.1 = (f32[2,112,128]{2,1,0:T(8,128)S(1)}, f32[2,112,128]{2,1,0:T(8,128)}, u32[]{:S(2)}) copy-start(f32[2,112,128]{2,1,0:T(8,128)} %m2_ref.3) | copy-start | bytes 344068
  30.2 4.5 %collective-permute-start.11 = (f32[136,128]{1,0:T(8,128)S(1)}, f32[136,128]{1,0:T(8,128)S(1)}, u32[]{:S(2)}, u32[]{:S(2)}) collective-permute-start(f32[136,128]{1,0:T(8,128)S(1)} %get-tuple-element.51), channel_id=1, source_target_pairs={{0,6},{2,4},{4,2},{6,0},{1,7},{3,5},{5,3},{7,1},{8,14},{10,12},{12... | collective-permute-start | bytes 208904 | tf_op jit(solution)/shard_map/ppermute | solution.py:306
  32.8 4.7 %collective-permute-start.10 = (f32[136,128]{1,0:T(8,128)S(1)}, f32[136,128]{1,0:T(8,128)S(1)}, u32[]{:S(2)}, u32[]{:S(2)}) collective-permute-start(f32[136,128]{1,0:T(8,128)S(1)} %get-tuple-element.52), channel_id=1, source_target_pairs={{0,4},{2,6},{4,0},{6,2},{1,5},{3,7},{5,1},{7,3},{8,12},{10,14},{12... | collective-permute-start | bytes 208904 | tf_op jit(solution)/shard_map/ppermute | solution.py:306
  33.3 4.2 %collective-permute-start.9 = (f32[136,128]{1,0:T(8,128)S(1)}, f32[136,128]{1,0:T(8,128)S(1)}, u32[]{:S(2)}, u32[]{:S(2)}) collective-permute-start(f32[136,128]{1,0:T(8,128)S(1)} %get-tuple-element.53), channel_id=1, source_target_pairs={{0,2},{2,0},{4,6},{6,4},{1,3},{3,1},{5,7},{7,5},{8,10},{10,8},{12,... | collective-permute-start | bytes 208904 | tf_op jit(solution)/shard_map/ppermute | solution.py:306
  37.5 5.6 %collective-permute-start.13 = (f32[128,128]{1,0:T(8,128)S(1)}, f32[128,128]{1,0:T(8,128)S(1)}, u32[]{:S(2)}, u32[]{:S(2)}) collective-permute-start(f32[128,128]{1,0:T(8,128)S(1)} %slice.24), channel_id=1, source_target_pairs={{0,16},{8,24},{16,0},{24,8},{1,17},{9,25},{17,1},{25,9},{2,18},{10... | collective-permute-start | bytes 196616 | tf_op jit(solution)/shard_map/ppermute | solution.py:306
  39.4 4.3 %collective-permute-start.14 = (f32[128,128]{1,0:T(8,128)S(1)}, f32[128,128]{1,0:T(8,128)S(1)}, u32[]{:S(2)}, u32[]{:S(2)}) collective-permute-start(f32[128,128]{1,0:T(8,128)S(1)} %slice.24), channel_id=1, source_target_pairs={{0,24},{8,16},{16,8},{24,0},{1,25},{9,17},{17,9},{25,1},{2,26},{10... | collective-permute-start | bytes 196616 | tf_op jit(solution)/shard_map/ppermute | solution.py:306
  39.8 3.9 %collective-permute-start.12 = (f32[128,128]{1,0:T(8,128)S(1)}, f32[128,128]{1,0:T(8,128)S(1)}, u32[]{:S(2)}, u32[]{:S(2)}) collective-permute-start(f32[128,128]{1,0:T(8,128)S(1)} %slice.24), channel_id=1, source_target_pairs={{0,8},{8,0},{16,24},{24,16},{1,9},{9,1},{17,25},{25,17},{2,10},{10... | collective-permute-start | bytes 196616 | tf_op jit(solution)/shard_map/ppermute | solution.py:306
  43.7 11.2 %collective-permute-start.17 = (f32[128,128]{1,0:T(8,128)S(1)}, f32[128,128]{1,0:T(8,128)S(1)}, u32[]{:S(2)}, u32[]{:S(2)}) collective-permute-start(f32[128,128]{1,0:T(8,128)S(1)} %add_add_fusion.1), channel_id=1, source_target_pairs={{0,96},{32,64},{64,32},{96,0},{128,224},{160,192},{192,160},{224,1... | collective-permute-start | bytes 196616 | tf_op jit(solution)/shard_map/ppermute | solution.py:306
  45.4 9.5 %collective-permute-start.16 = (f32[128,128]{1,0:T(8,128)S(1)}, f32[128,128]{1,0:T(8,128)S(1)}, u32[]{:S(2)}, u32[]{:S(2)}) collective-permute-start(f32[128,128]{1,0:T(8,128)S(1)} %add_add_fusion.1), channel_id=1, source_target_pairs={{0,64},{32,96},{64,0},{96,32},{128,192},{160,224},{192,128},{224,1... | collective-permute-start | bytes 196616 | tf_op jit(solution)/shard_map/ppermute | solution.py:306
  47.3 7.7 %collective-permute-start.15 = (f32[128,128]{1,0:T(8,128)S(1)}, f32[128,128]{1,0:T(8,128)S(1)}, u32[]{:S(2)}, u32[]{:S(2)}) collective-permute-start(f32[128,128]{1,0:T(8,128)S(1)} %add_add_fusion.1), channel_id=1, source_target_pairs={{0,32},{32,0},{64,96},{96,64},{128,160},{160,128},{192,224},{224,1... | collective-permute-start | bytes 196616 | tf_op jit(solution)/shard_map/ppermute | solution.py:306
  47.9 7.9 %collective-permute-start.18 = (f32[56,128]{1,0:T(8,128)S(1)}, f32[56,128]{1,0:T(8,128)S(1)}, u32[]{:S(2)}, u32[]{:S(2)}) collective-permute-start(f32[56,128]{1,0:T(8,128)S(1)} %get-tuple-element.37), channel_id=1, source_target_pairs={{0,1},{1,0},{2,3},{3,2},{4,5},{5,4},{6,7},{7,6},{8,9},{9,8},{10,11... | collective-permute-start | bytes 86024 | tf_op jit(solution)/shard_map/ppermute | solution.py:306
  55.8 5.3 %collective-permute-start.19 = (f32[128,128]{1,0:T(8,128)S(1)}, f32[128,128]{1,0:T(8,128)S(1)}, u32[]{:S(2)}, u32[]{:S(2)}) collective-permute-start(f32[128,128]{1,0:T(8,128)S(1)} %add_add_fusion.a_ref), channel_id=1, source_target_pairs={{0,192},{32,224},{64,128},{96,160},{128,64},{160,96},{192,0},{224,... | collective-permute-start | bytes 196616 | tf_op jit(solution)/shard_map/ppermute | solution.py:306
  61.4 4.3 %collective-permute-start.22 = (f32[128,128]{1,0:T(8,128)S(1)}, f32[128,128]{1,0:T(8,128)S(1)}, u32[]{:S(2)}, u32[]{:S(2)}) collective-permute-start(f32[128,128]{1,0:T(8,128)S(1)} %finished_piece.1), channel_id=1, source_target_pairs={{0,6},{2,4},{4,2},{6,0},{1,7},{3,5},{5,3},{7,1},{8,14},{10,12},{12... | collective-permute-start | bytes 196616 | tf_op jit(solution)/shard_map/ppermute | solution.py:306
  62.5 4.6 %collective-permute-start.21 = (f32[128,128]{1,0:T(8,128)S(1)}, f32[128,128]{1,0:T(8,128)S(1)}, u32[]{:S(2)}, u32[]{:S(2)}) collective-permute-start(f32[128,128]{1,0:T(8,128)S(1)} %finished_piece.1), channel_id=1, source_target_pairs={{0,4},{2,6},{4,0},{6,2},{1,5},{3,7},{5,1},{7,3},{8,12},{10,14},{12... | collective-permute-start | bytes 196616 | tf_op jit(solution)/shard_map/ppermute | solution.py:306
  63.2 3.9 %collective-permute-start.20 = (f32[128,128]{1,0:T(8,128)S(1)}, f32[128,128]{1,0:T(8,128)S(1)}, u32[]{:S(2)}, u32[]{:S(2)}) collective-permute-start(f32[128,128]{1,0:T(8,128)S(1)} %finished_piece.1), channel_id=1, source_target_pairs={{0,2},{2,0},{4,6},{6,4},{1,3},{3,1},{5,7},{7,5},{8,10},{10,8},{12,... | collective-permute-start | bytes 196616 | tf_op jit(solution)/shard_map/ppermute | solution.py:306
  67.1 6.3 %collective-permute-start.23 = (f32[4,128,128]{2,1,0:T(8,128)S(1)}, f32[4,128,128]{2,1,0:T(8,128)S(1)}, u32[]{:S(2)}, u32[]{:S(2)}) collective-permute-start(f32[4,128,128]{2,1,0:T(8,128)S(1)} %pad_maximum_fusion.pieces_ref), channel_id=1, source_target_pairs={{0,1},{1,0},{2,3},{3,2},{4,5},{5,4},{6,7},{7,6},{8,9},{9,8},{10,11... | collective-permute-start | bytes 786440 | tf_op jit(solution)/shard_map/ppermute | solution.py:306

commit v6 on v5

--- a/solution.py
+++ b/solution.py
@@ -2,6 +2,7 @@
 
 import jax
 import jax.numpy as jnp
+import numpy as np
 from jax import lax
 from jax.experimental import pallas as pl
 from jax.experimental.pallas import tpu as pltpu
@@ -105,11 +106,15 @@
     )(in_hbm(grads), in_hbm(errors), in_hbm(q_prev))
 
 
+def block_place(core):
+    return jnp.where(core == 0, lax.axis_index("x"), lax.axis_index("y"))
+
+
 def right_kernel(replicas, p_ref, own_ref, gift_ref, out_ref):
     slots, height, _ = out_ref.shape
     tiles = (height - 8) // RANK
     width = tiles * LANES
-    x = lax.axis_index("x")
+    place = block_place(lax.axis_index("c"))
     half = p_ref.shape[0] // 2
     columns = jnp.concatenate([unpack_rows(p_ref[:half]), unpack_rows(p_ref[half:])], axis=0)
     p = (columns * (1.0 / replicas)).T
@@ -117,7 +122,7 @@
     both = jnp.concatenate([p_hi, p_lo], axis=0)
     gram = pack(dot(p, p, 1, 1, lax.Precision.HIGHEST))
     for slot in range(slots):
-        here = pl.ds(pl.multiple_of((x ^ slot) * width, width), width)
+        here = pl.ds(pl.multiple_of((place ^ slot) * width, width), width)
         f_hi, f_lo = split(jnp.concatenate([own_ref[:, here], gift_ref[:, here]], axis=0))
         wide = dot(both, f_hi, 1, 0)
         q = wide[:RANK] + wide[RANK:] + dot(p_hi, f_lo, 1, 0)
@@ -138,8 +143,8 @@
     )(p_sum, own, gift)
 
 
-def factor_kernel(sum_ref, out_ref):
-    gram = unpack(sum_ref[sum_ref.shape[0] - 8 :, :])
+def factor_kernel(copies, sum_ref, out_ref):
+    gram = unpack(sum_ref[sum_ref.shape[0] - 8 :, :]) * (1.0 / copies)
     row = lax.broadcasted_iota(jnp.int32, (RANK, RANK), 0)
     column = lax.broadcasted_iota(jnp.int32, (RANK, RANK), 1)
     work = jnp.concatenate([gram, (row == column).astype(F32)], axis=1)
@@ -156,9 +161,9 @@
     out_ref[...] = pack(work[:, RANK:] * scale)
 
 
-def inverse_factor(total):
-    return pl.pallas_call(
-        factor_kernel,
+def inverse_factor(total, copies):
+    return pl.pallas_call(
+        functools.partial(factor_kernel, copies),
         in_specs=[WHOLE],
         out_specs=WHOLE,
         out_shape=jax.ShapeDtypeStruct((8, LANES), F32),
@@ -238,11 +243,12 @@
     slots, height, _ = pieces_ref.shape
     tiles = height // RANK
     width = tiles * LANES
-    x, core = lax.axis_index("x"), lax.axis_index("c")
+    core = lax.axis_index("c")
     i, m = (0, core) if mine else (1, 1 - core)
+    place = block_place(m)
     copies = []
     for slot in range(slots):
-        block = x ^ slot
+        block = place ^ slot
         here = pl.ds(pl.multiple_of(block * width, width), width)
         q = jnp.concatenate([pieces_ref[slot, j * RANK : (j + 1) * RANK, :] for j in range(tiles)], axis=1)
         right = right_three(q)
@@ -302,38 +308,43 @@
     )(pieces, hat, rows, full, moment1, moment2, *before)
 
 
-def swap(value, axis, bit):
-    return lax.ppermute(value, axis, [(i, i ^ bit) for i in range(lax.axis_size(axis))])
-
-
-def four(values, axis):
-    return (values[0] + swap(values[1], axis, 1)) + (swap(values[2], axis, 2) + swap(values[3], axis, 3))
+def swap(value, axes, bit):
+    names = ("z", "y", "x", "c")
+    sizes = tuple(lax.axis_size(name) for name in names)
+    pairs = []
+    for here in np.ndindex(*sizes):
+        there = list(here)
+        there[names.index(axes[here[-1]])] ^= bit
+        pairs.append((int(np.ravel_multi_index(here, sizes)), int(np.ravel_multi_index(there, sizes))))
+    return lax.ppermute(value, names, pairs)
+
+
+def four(values, axes):
+    return (values[0] + swap(values[1], axes, 1)) + (swap(values[2], axes, 2) + swap(values[3], axes, 3))
 
 
 def shards(grads, errors, q_prev, moment1, moment2):
     replicas, slots = lax.axis_size(("z", "y")), lax.axis_size("x")
     other_full, own_full, p_other, p_own = left_factors(grads, errors, q_prev)
-    p = jnp.concatenate([p_own, swap(p_other, "c", 1)])
+    p = jnp.concatenate([p_own, swap(p_other, "cc", 1)])
     p, other_full = lax.optimization_barrier((p, other_full))
-    gift = swap(other_full, "c", 1)
-    p = four([p] * 4, "y")
-    p = four([p] * 4, "z")
-    p = p + swap(p, "z", 6)
+    gift = swap(other_full, "cc", 1)
+    p = four([p] * 4, "yz")
+    p = four([p] * 4, "zy")
+    p = p + swap(p, "zz", 6)
 
     terms = right_terms(p, own_full, gift, replicas, slots)
-    total = four([terms[i] for i in range(slots)], "x")
-    inverse = inverse_factor(total)
-    q = four([total[:-8]] * 4, "y")
+    total = four([terms[i] for i in range(slots)], "xy")
+    total = four([total] * 4, "zx")
+    inverse = inverse_factor(total, slots)
+    q = four([total[:-8]] * 4, "yz")
     q, inverse = lax.optimization_barrier((q, inverse))
     hat_own, hat_other = orthonormal(p, inverse, replicas)
-    hat_gift = swap(hat_other, "c", 1)
-    q = four([q] * 4, "z")
-    q, hat_own, hat_gift = lax.optimization_barrier((q, hat_own, hat_gift))
-    hat, rows = left_sides(hat_own, hat_gift, replicas)
-    far, hat, rows = lax.optimization_barrier((swap(q, "z", 6), hat, rows))
+    hat, rows = left_sides(hat_own, swap(hat_other, "cc", 1), replicas)
+    far, hat, rows = lax.optimization_barrier((swap(q, "zz", 6), hat, rows))
     piece = finished_piece(q, far, inverse, replicas)
-    own = jnp.stack([piece] + [swap(piece, "x", i) for i in range(1, slots)])
-    other = swap(own, "c", 1)
+    own = jnp.stack([piece] + [swap(piece, "xy", i) for i in range(1, slots)])
+    other = swap(own, "cc", 1)
     done = update(own, hat, rows, own_full, moment1, moment2, True)
     return tuple(update(other, hat, rows, other_full, moment1, moment2, False, done))
 

time: 75.3 us -> 78.1 us (1.037)
  waiting for transfers between devices: 19 us -> 23.5 us
  starting transfers between devices: 43.1 us -> 41.4 us
    ppermute x24, waiting for transfers between devices: 19 us -> 23.5 us  [swap(): return lax.ppermute(value, names, pairs)]
    ppermute x24, starting transfers between devices: 43.1 us -> 41.4 us  [swap(): return lax.ppermute(value, names, pairs)]
  transfers between devices with their start and end apart: 24 -> 24, of which waited for: 14 -> 15; matrix products, arithmetic and copies ran while one was open for 0% -> 0% of each run, Pallas kernels for 7% -> 7%
where the time goes in v6:
time: 78.1 us; the launch traced here: 78 us
  starting transfers between devices  41.4 us (53%)
  waiting for transfers between devices  23.5 us (30%)
  Pallas kernels  12 us (15%)
  between operations  0.9 us (1%)
    ppermute x24, starting transfers between devices, swap(): return lax.ppermute(value, names, pairs)  41.4 us
    ppermute x24, waiting for transfers between devices, swap(): return lax.ppermute(value, names, pairs)  23.5 us
    pallas_call x1, Pallas kernels, left_factors(): pl.pallas_call(left_kernel, in_specs=[AWAY] * 3, out_specs=[WHOLE] * 4, o...  3.64 us
    pallas_call x2, Pallas kernels, update(): pl.pallas_call(functools.partial(update_kernel, mine), in_specs=[WHOLE] *...  3.29 us
    pallas_call x1, Pallas kernels, inverse_factor(): pl.pallas_call(functools.partial(factor_kernel, copies), in_specs=[WHOLE]...  2.85 us
  transfers between devices with their start and end apart: 24, of which 15 were waited for; matrix products, arithmetic and copies ran while one was open for 0% of the time, Pallas kernels for 7%

profile of v6, /device:TPU:1, one launch (start us, length us, event | category | flops | bytes accessed | tf_op | source)
XLA Modules:
  0.0 78.0 jit_solution(5134893117931222637)
XLA Ops:
  0.6 3.6 %left_factors.1 = (f32[224,2048]{1,0:T(8,128)S(1)}, f32[224,2048]{1,0:T(8,128)S(1)}, f32[56,128]{1,0:T(8,128)S(1)}, f32[56,128]{1,0:T(8,128)S(1)}) custom-call(bf16[1,2,224,2048]{3,2,1,0:T(8,128)(2,1)} %grads_hbm.1, f32[1,2,224,2048]{3,2,1,0:T(8,128)} %errors_hbm.1, f32[2,32,2048]{2,1,0:T(8,128)} %q_hbm.1), custom_call_target="tpu_custom_call" | custom-call | tf_op jit(solution)/shard_map/left_factors/pallas_call | solution.py:92
  4.3 3.3 %collective-permute-start = (f32[56,128]{1,0:T(8,128)S(1)}, f32[56,128]{1,0:T(8,128)S(1)}, u32[]{:S(2)}, u32[]{:S(2)}) collective-permute-start(f32[56,128]{1,0:T(8,128)S(1)} %get-tuple-element.26), channel_id=1, source_target_pairs={{0,1},{1,0},{2,3},{3,2},{4,5},{5,4},{6,7},{7,6},{8,9},{9,8},{10,11... | collective-permute-start | bytes 86024 | tf_op jit(solution)/shard_map/ppermute | solution.py:319
  8.8 2.6 %collective-permute-start.3 = (f32[112,128]{1,0:T(8,128)S(1)}, f32[112,128]{1,0:T(8,128)S(1)}, u32[]{:S(2)}, u32[]{:S(2)}) collective-permute-start(f32[112,128]{1,0:T(8,128)S(1)} %pad_maximum_fusion.1), channel_id=1, source_target_pairs={{0,24},{1,97},{2,26},{3,99},{4,28},{5,101},{6,30},{7,103},{8,16},{... | collective-permute-start | bytes 172040 | tf_op jit(solution)/shard_map/ppermute | solution.py:319
  11.4 0.9 %collective-permute-start.1 = (f32[112,128]{1,0:T(8,128)S(1)}, f32[112,128]{1,0:T(8,128)S(1)}, u32[]{:S(2)}, u32[]{:S(2)}) collective-permute-start(f32[112,128]{1,0:T(8,128)S(1)} %pad_maximum_fusion.1), channel_id=1, source_target_pairs={{0,8},{1,33},{2,10},{3,35},{4,12},{5,37},{6,14},{7,39},{8,0},{9,41... | collective-permute-start | bytes 172040 | tf_op jit(solution)/shard_map/ppermute | solution.py:319
  12.4 1.3 %collective-permute-done.3 = f32[112,128]{1,0:T(8,128)S(1)} collective-permute-done((f32[112,128]{1,0:T(8,128)S(1)}, f32[112,128]{1,0:T(8,128)S(1)}, u32[]{:S(2)}, u32[]{:S(2)}) %collective-permute-start.3) | collective-permute-done | bytes 57376 | tf_op jit(solution)/shard_map/ppermute | solution.py:319
  13.6 1.9 %collective-permute-done.2 = f32[112,128]{1,0:T(8,128)S(1)} collective-permute-done((f32[112,128]{1,0:T(8,128)S(1)}, f32[112,128]{1,0:T(8,128)S(1)}, u32[]{:S(2)}, u32[]{:S(2)}) %collective-permute-start.2) | collective-permute-done | bytes 57376 | tf_op jit(solution)/shard_map/ppermute | solution.py:319
  15.6 2.6 %collective-permute-start.6 = (f32[112,128]{1,0:T(8,128)S(1)}, f32[112,128]{1,0:T(8,128)S(1)}, u32[]{:S(2)}, u32[]{:S(2)}) collective-permute-start(f32[112,128]{1,0:T(8,128)S(1)} %add_add_fusion.3), channel_id=1, source_target_pairs={{0,96},{1,25},{2,98},{3,27},{4,100},{5,29},{6,102},{7,31},{8,104},... | collective-permute-start | bytes 172040 | tf_op jit(solution)/shard_map/ppermute | solution.py:319
  18.9 1.0 %collective-permute-done.6 = f32[112,128]{1,0:T(8,128)S(1)} collective-permute-done((f32[112,128]{1,0:T(8,128)S(1)}, f32[112,128]{1,0:T(8,128)S(1)}, u32[]{:S(2)}, u32[]{:S(2)}) %collective-permute-start.6) | collective-permute-done | bytes 57376 | tf_op jit(solution)/shard_map/ppermute | solution.py:319
  19.9 2.8 %collective-permute-done.5 = f32[112,128]{1,0:T(8,128)S(1)} collective-permute-done((f32[112,128]{1,0:T(8,128)S(1)}, f32[112,128]{1,0:T(8,128)S(1)}, u32[]{:S(2)}, u32[]{:S(2)}) %collective-permute-start.5) | collective-permute-done | bytes 57376 | tf_op jit(solution)/shard_map/ppermute | solution.py:319
  22.7 3.7 %collective-permute-start.7 = (f32[112,128]{1,0:T(8,128)S(1)}, f32[112,128]{1,0:T(8,128)S(1)}, u32[]{:S(2)}, u32[]{:S(2)}) collective-permute-start(f32[112,128]{1,0:T(8,128)S(1)} %add_add_fusion.2), channel_id=1, source_target_pairs={{0,192},{1,193},{2,194},{3,195},{4,196},{5,197},{6,198},{7,199},{8... | collective-permute-start | bytes 172040 | tf_op jit(solution)/shard_map/ppermute | solution.py:319
  26.4 2.1 %collective-permute-done.7 = f32[112,128]{1,0:T(8,128)S(1)} collective-permute-done((f32[112,128]{1,0:T(8,128)S(1)}, f32[112,128]{1,0:T(8,128)S(1)}, u32[]{:S(2)}, u32[]{:S(2)}) %collective-permute-start.7) | collective-permute-done | bytes 57376 | tf_op jit(solution)/shard_map/ppermute | solution.py:319
  28.5 1.1 %right_terms.1 = f32[4,136,128]{2,1,0:T(8,128)S(1)} custom-call(f32[112,128]{1,0:T(8,128)S(1)} %add.54.p_ref, f32[224,2048]{1,0:T(8,128)S(1)} %get-tuple-element.29.own_ref.full_ref, f32[224,2048]{1,0:T(8,128)S(1)} %collective-permute-done.8.gift_ref), custom_call_target="tpu_custom_call" | custom-call | tf_op jit(solution)/shard_map/right_terms/pallas_call | solution.py:136
  29.7 1.1 %collective-permute-start.11 = (f32[136,128]{1,0:T(8,128)S(1)}, f32[136,128]{1,0:T(8,128)S(1)}, u32[]{:S(2)}, u32[]{:S(2)}) collective-permute-start(f32[136,128]{1,0:T(8,128)S(1)} %get-tuple-element.45), channel_id=1, source_target_pairs={{0,6},{1,25},{2,4},{3,27},{4,2},{5,29},{6,0},{7,31},{8,14},{9,17},... | collective-permute-start | bytes 208904 | tf_op jit(solution)/shard_map/ppermute | solution.py:319
  31.6 1.4 %collective-permute-start.9 = (f32[136,128]{1,0:T(8,128)S(1)}, f32[136,128]{1,0:T(8,128)S(1)}, u32[]{:S(2)}, u32[]{:S(2)}) collective-permute-start(f32[136,128]{1,0:T(8,128)S(1)} %get-tuple-element.47), channel_id=1, source_target_pairs={{0,2},{1,9},{2,0},{3,11},{4,6},{5,13},{6,4},{7,15},{8,10},{9,1},{1... | collective-permute-start | bytes 208904 | tf_op jit(solution)/shard_map/ppermute | solution.py:319
  33.0 1.1 %collective-permute-done.11 = f32[136,128]{1,0:T(8,128)S(1)} collective-permute-done((f32[136,128]{1,0:T(8,128)S(1)}, f32[136,128]{1,0:T(8,128)S(1)}, u32[]{:S(2)}, u32[]{:S(2)}) %collective-permute-start.11) | collective-permute-done | bytes 69664 | tf_op jit(solution)/shard_map/ppermute | solution.py:319
  34.1 1.3 %collective-permute-done.10 = f32[136,128]{1,0:T(8,128)S(1)} collective-permute-done((f32[136,128]{1,0:T(8,128)S(1)}, f32[136,128]{1,0:T(8,128)S(1)}, u32[]{:S(2)}, u32[]{:S(2)}) %collective-permute-start.10) | collective-permute-done | bytes 69664 | tf_op jit(solution)/shard_map/ppermute | solution.py:319
  35.5 2.6 %collective-permute-start.14 = (f32[136,128]{1,0:T(8,128)S(1)}, f32[136,128]{1,0:T(8,128)S(1)}, u32[]{:S(2)}, u32[]{:S(2)}) collective-permute-start(f32[136,128]{1,0:T(8,128)S(1)} %fusion.1), channel_id=1, source_target_pairs={{0,96},{1,7},{2,98},{3,5},{4,100},{5,3},{6,102},{7,1},{8,104},{9,1... | collective-permute-start | bytes 208904 | tf_op jit(solution)/shard_map/ppermute | solution.py:319
  38.8 1.1 %collective-permute-done.14 = f32[136,128]{1,0:T(8,128)S(1)} collective-permute-done((f32[136,128]{1,0:T(8,128)S(1)}, f32[136,128]{1,0:T(8,128)S(1)}, u32[]{:S(2)}, u32[]{:S(2)}) %collective-permute-start.14) | collective-permute-done | bytes 69664 | tf_op jit(solution)/shard_map/ppermute | solution.py:319
  39.9 3.1 %collective-permute-done.13 = f32[136,128]{1,0:T(8,128)S(1)} collective-permute-done((f32[136,128]{1,0:T(8,128)S(1)}, f32[136,128]{1,0:T(8,128)S(1)}, u32[]{:S(2)}, u32[]{:S(2)}) %collective-permute-start.13) | collective-permute-done | bytes 69664 | tf_op jit(solution)/shard_map/ppermute | solution.py:319
  43.1 1.5 %collective-permute-start.16 = (f32[128,128]{1,0:T(8,128)S(1)}, f32[128,128]{1,0:T(8,128)S(1)}, u32[]{:S(2)}, u32[]{:S(2)}) collective-permute-start(f32[128,128]{1,0:T(8,128)S(1)} %slice.24), channel_id=1, source_target_pairs={{0,16},{1,65},{2,18},{3,67},{4,20},{5,69},{6,22},{7,71},{8,24},{9,... | collective-permute-start | bytes 196616 | tf_op jit(solution)/shard_map/ppermute | solution.py:319
  44.5 1.0 %collective-permute-start.17 = (f32[128,128]{1,0:T(8,128)S(1)}, f32[128,128]{1,0:T(8,128)S(1)}, u32[]{:S(2)}, u32[]{:S(2)}) collective-permute-start(f32[128,128]{1,0:T(8,128)S(1)} %slice.24), channel_id=1, source_target_pairs={{0,24},{1,97},{2,26},{3,99},{4,28},{5,101},{6,30},{7,103},{8,16},{... | collective-permute-start | bytes 196616 | tf_op jit(solution)/shard_map/ppermute | solution.py:319
  45.8 2.8 %inverse_factor.1.inverse_ref = f32[8,128]{1,0:T(8,128)S(1)} custom-call(f32[136,128]{1,0:T(8,128)S(1)} %add_add_fusion.sum_ref), custom_call_target="tpu_custom_call" | custom-call | flops 4000000 | bytes 4000000 | tf_op jit(solution)/shard_map/inverse_factor/pallas_call | solution.py:165
  48.7 2.3 %collective-permute-done.16 = f32[128,128]{1,0:T(8,128)S(1)} collective-permute-done((f32[128,128]{1,0:T(8,128)S(1)}, f32[128,128]{1,0:T(8,128)S(1)}, u32[]{:S(2)}, u32[]{:S(2)}) %collective-permute-start.16) | collective-permute-done | bytes 65568 | tf_op jit(solution)/shard_map/ppermute | solution.py:319
  51.6 3.3 %collective-permute-start.18 = (f32[128,128]{1,0:T(8,128)S(1)}, f32[128,128]{1,0:T(8,128)S(1)}, u32[]{:S(2)}, u32[]{:S(2)}) collective-permute-start(f32[128,128]{1,0:T(8,128)S(1)} %add_add_fusion.1.a_ref), channel_id=1, source_target_pairs={{0,192},{1,193},{2,194},{3,195},{4,196},{5,197},{6,198},{7,199},{8... | collective-permute-start | bytes 196616 | tf_op jit(solution)/shard_map/ppermute | solution.py:319
  55.4 8.0 %collective-permute-start.19 = (f32[56,128]{1,0:T(8,128)S(1)}, f32[56,128]{1,0:T(8,128)S(1)}, u32[]{:S(2)}, u32[]{:S(2)}) collective-permute-start(f32[56,128]{1,0:T(8,128)S(1)} %get-tuple-element.34), channel_id=1, source_target_pairs={{0,1},{1,0},{2,3},{3,2},{4,5},{5,4},{6,7},{7,6},{8,9},{9,8},{10,11... | collective-permute-start | bytes 86024 | tf_op jit(solution)/shard_map/ppermute | solution.py:319
  65.0 1.8 %collective-permute-start.22 = (f32[128,128]{1,0:T(8,128)S(1)}, f32[128,128]{1,0:T(8,128)S(1)}, u32[]{:S(2)}, u32[]{:S(2)}) collective-permute-start(f32[128,128]{1,0:T(8,128)S(1)} %finished_piece.1), channel_id=1, source_target_pairs={{0,6},{1,25},{2,4},{3,27},{4,2},{5,29},{6,0},{7,31},{8,14},{9,17},... | collective-permute-start | bytes 196616 | tf_op jit(solution)/shard_map/ppermute | solution.py:319
  67.1 1.2 %collective-permute-start.20 = (f32[128,128]{1,0:T(8,128)S(1)}, f32[128,128]{1,0:T(8,128)S(1)}, u32[]{:S(2)}, u32[]{:S(2)}) collective-permute-start(f32[128,128]{1,0:T(8,128)S(1)} %finished_piece.1), channel_id=1, source_target_pairs={{0,2},{1,9},{2,0},{3,11},{4,6},{5,13},{6,4},{7,15},{8,10},{9,1},{1... | collective-permute-start | bytes 196616 | tf_op jit(solution)/shard_map/ppermute | solution.py:319
  68.2 1.1 %collective-permute-done.22 = f32[128,128]{1,0:T(8,128)S(1)} collective-permute-done((f32[128,128]{1,0:T(8,128)S(1)}, f32[128,128]{1,0:T(8,128)S(1)}, u32[]{:S(2)}, u32[]{:S(2)}) %collective-permute-start.22) | collective-permute-done | bytes 65568 | tf_op jit(solution)/shard_map/ppermute | solution.py:319
  69.3 2.0 %collective-permute-done.21 = f32[128,128]{1,0:T(8,128)S(1)} collective-permute-done((f32[128,128]{1,0:T(8,128)S(1)}, f32[128,128]{1,0:T(8,128)S(1)}, u32[]{:S(2)}, u32[]{:S(2)}) %collective-permute-start.21) | collective-permute-done | bytes 65568 | tf_op jit(solution)/shard_map/ppermute | solution.py:319
  71.4 3.2 %collective-permute-start.23 = (f32[4,128,128]{2,1,0:T(8,128)S(1)}, f32[4,128,128]{2,1,0:T(8,128)S(1)}, u32[]{:S(2)}, u32[]{:S(2)}) collective-permute-start(f32[4,128,128]{2,1,0:T(8,128)S(1)} %pad_maximum_fusion.pieces_ref), channel_id=1, source_target_pairs={{0,1},{1,0},{2,3},{3,2},{4,5},{5,4},{6,7},{7,6},{8,9},{9,8},{10,11... | collective-permute-start | bytes 786440 | tf_op jit(solution)/shard_map/ppermute | solution.py:319
  74.5 1.6 %update_own.1 = (f32[1,2,224,2048]{3,2,1,0:T(8,128)}, f32[2,112,128]{2,1,0:T(8,128)}, f32[2,112,128]{2,1,0:T(8,128)}, bf16[2,112,128]{2,1,0:T(8,128)(2,1)}, f32[2,32,2048]{2,1,0:T(8,128)}) custom-call(f32[4,128,128]{2,1,0:T(8,128)S(1)} %pad_maximum_fusion.pieces_ref, bf16[2,224,96]{2,1,0:T(8,128)(2,1)S(1)} %get-tuple-element.38.hat_ref, ...), custom_call_target="tpu_custom_call" | custom-call | flops 100000000 | bytes 4000000 | tf_op jit(solution)/shard_map/update_own/pallas_call | solution.py:282
  76.2 1.6 %update_other.1 = (f32[1,2,224,2048]{3,2,1,0:T(8,128)}, f32[2,112,128]{2,1,0:T(8,128)}, f32[2,112,128]{2,1,0:T(8,128)}, bf16[2,112,128]{2,1,0:T(8,128)(2,1)}, f32[2,32,2048]{2,1,0:T(8,128)}) custom-call(f32[4,128,128]{2,1,0:T(8,128)S(1)} %collective-permute-done.23.pieces_ref, ...), custom_call_target="tpu_custom_call", output_to_operand_aliasing={{0}: (6, {}), {1}: (7, {}), {2}: (8, {}), {3}: (9, {}), {4}... | custom-call | flops 100000000 | bytes 4000000 | tf_op jit(solution)/shard_map/update_other/pallas_call | solution.py:282
  (38 shorter events, 6.9 us)
Async XLA Ops:
  4.3 4.2 %collective-permute-start = (f32[56,128]{1,0:T(8,128)S(1)}, f32[56,128]{1,0:T(8,128)S(1)}, u32[]{:S(2)}, u32[]{:S(2)}) collective-permute-start(f32[56,128]{1,0:T(8,128)S(1)} %get-tuple-element.26), channel_id=1, source_target_pairs={{0,1},{1,0},{2,3},{3,2},{4,5},{5,4},{6,7},{7,6},{8,9},{9,8},{10,11... | collective-permute-start | bytes 86024 | tf_op jit(solution)/shard_map/ppermute | solution.py:319
  8.5 20.1 %collective-permute-start.8 = (f32[224,2048]{1,0:T(8,128)S(1)}, f32[224,2048]{1,0:T(8,128)S(1)}, u32[]{:S(2)}, u32[]{:S(2)}) collective-permute-start(f32[224,2048]{1,0:T(8,128)S(1)} %get-tuple-element.30.full_ref), channel_id=1, source_target_pairs={{0,1},{1,0},{2,3},{3,2},{4,5},{5,4},{6,7},{7,6},{8,9},{9,8},{10,11... | collective-permute-start | bytes 5505032 | tf_op jit(solution)/shard_map/ppermute | solution.py:319
  8.8 4.8 %collective-permute-start.3 = (f32[112,128]{1,0:T(8,128)S(1)}, f32[112,128]{1,0:T(8,128)S(1)}, u32[]{:S(2)}, u32[]{:S(2)}) collective-permute-start(f32[112,128]{1,0:T(8,128)S(1)} %pad_maximum_fusion.1), channel_id=1, source_target_pairs={{0,24},{1,97},{2,26},{3,99},{4,28},{5,101},{6,30},{7,103},{8,16},{... | collective-permute-start | bytes 172040 | tf_op jit(solution)/shard_map/ppermute | solution.py:319
  11.4 4.1 %collective-permute-start.2 = (f32[112,128]{1,0:T(8,128)S(1)}, f32[112,128]{1,0:T(8,128)S(1)}, u32[]{:S(2)}, u32[]{:S(2)}) collective-permute-start(f32[112,128]{1,0:T(8,128)S(1)} %pad_maximum_fusion.1), channel_id=1, source_target_pairs={{0,16},{1,65},{2,18},{3,67},{4,20},{5,69},{6,22},{7,71},{8,24},{9,... | collective-permute-start | bytes 172040 | tf_op jit(solution)/shard_map/ppermute | solution.py:319
  11.4 4.1 %collective-permute-start.1 = (f32[112,128]{1,0:T(8,128)S(1)}, f32[112,128]{1,0:T(8,128)S(1)}, u32[]{:S(2)}, u32[]{:S(2)}) collective-permute-start(f32[112,128]{1,0:T(8,128)S(1)} %pad_maximum_fusion.1), channel_id=1, source_target_pairs={{0,8},{1,33},{2,10},{3,35},{4,12},{5,37},{6,14},{7,39},{8,0},{9,41... | collective-permute-start | bytes 172040 | tf_op jit(solution)/shard_map/ppermute | solution.py:319
  15.6 4.3 %collective-permute-start.6 = (f32[112,128]{1,0:T(8,128)S(1)}, f32[112,128]{1,0:T(8,128)S(1)}, u32[]{:S(2)}, u32[]{:S(2)}) collective-permute-start(f32[112,128]{1,0:T(8,128)S(1)} %add_add_fusion.3), channel_id=1, source_target_pairs={{0,96},{1,25},{2,98},{3,27},{4,100},{5,29},{6,102},{7,31},{8,104},... | collective-permute-start | bytes 172040 | tf_op jit(solution)/shard_map/ppermute | solution.py:319
  18.2 4.5 %collective-permute-start.5 = (f32[112,128]{1,0:T(8,128)S(1)}, f32[112,128]{1,0:T(8,128)S(1)}, u32[]{:S(2)}, u32[]{:S(2)}) collective-permute-start(f32[112,128]{1,0:T(8,128)S(1)} %add_add_fusion.3), channel_id=1, source_target_pairs={{0,64},{1,17},{2,66},{3,19},{4,68},{5,21},{6,70},{7,23},{8,72},{9,... | collective-permute-start | bytes 172040 | tf_op jit(solution)/shard_map/ppermute | solution.py:319
  18.5 4.2 %collective-permute-start.4 = (f32[112,128]{1,0:T(8,128)S(1)}, f32[112,128]{1,0:T(8,128)S(1)}, u32[]{:S(2)}, u32[]{:S(2)}) collective-permute-start(f32[112,128]{1,0:T(8,128)S(1)} %add_add_fusion.3), channel_id=1, source_target_pairs={{0,32},{1,9},{2,34},{3,11},{4,36},{5,13},{6,38},{7,15},{8,40},{9,1... | collective-permute-start | bytes 172040 | tf_op jit(solution)/shard_map/ppermute | solution.py:319
  22.7 5.8 %collective-permute-start.7 = (f32[112,128]{1,0:T(8,128)S(1)}, f32[112,128]{1,0:T(8,128)S(1)}, u32[]{:S(2)}, u32[]{:S(2)}) collective-permute-start(f32[112,128]{1,0:T(8,128)S(1)} %add_add_fusion.2), channel_id=1, source_target_pairs={{0,192},{1,193},{2,194},{3,195},{4,196},{5,197},{6,198},{7,199},{8... | collective-permute-start | bytes 172040 | tf_op jit(solution)/shard_map/ppermute | solution.py:319
  29.6 44.9 %copy-start = (f32[2,112,128]{2,1,0:T(8,128)S(1)}, f32[2,112,128]{2,1,0:T(8,128)}, u32[]{:S(2)}) copy-start(f32[2,112,128]{2,1,0:T(8,128)} %m1_ref.3) | copy-start | bytes 344068
  29.6 44.9 %copy-start.1 = (f32[2,112,128]{2,1,0:T(8,128)S(1)}, f32[2,112,128]{2,1,0:T(8,128)}, u32[]{:S(2)}) copy-start(f32[2,112,128]{2,1,0:T(8,128)} %m2_ref.3) | copy-start | bytes 344068
  29.7 4.5 %collective-permute-start.11 = (f32[136,128]{1,0:T(8,128)S(1)}, f32[136,128]{1,0:T(8,128)S(1)}, u32[]{:S(2)}, u32[]{:S(2)}) collective-permute-start(f32[136,128]{1,0:T(8,128)S(1)} %get-tuple-element.45), channel_id=1, source_target_pairs={{0,6},{1,25},{2,4},{3,27},{4,2},{5,29},{6,0},{7,31},{8,14},{9,17},... | collective-permute-start | bytes 208904 | tf_op jit(solution)/shard_map/ppermute | solution.py:319
  30.8 4.7 %collective-permute-start.10 = (f32[136,128]{1,0:T(8,128)S(1)}, f32[136,128]{1,0:T(8,128)S(1)}, u32[]{:S(2)}, u32[]{:S(2)}) collective-permute-start(f32[136,128]{1,0:T(8,128)S(1)} %get-tuple-element.46), channel_id=1, source_target_pairs={{0,4},{1,17},{2,6},{3,19},{4,0},{5,21},{6,2},{7,23},{8,12},{9,25},... | collective-permute-start | bytes 208904 | tf_op jit(solution)/shard_map/ppermute | solution.py:319
  31.6 3.9 %collective-permute-start.9 = (f32[136,128]{1,0:T(8,128)S(1)}, f32[136,128]{1,0:T(8,128)S(1)}, u32[]{:S(2)}, u32[]{:S(2)}) collective-permute-start(f32[136,128]{1,0:T(8,128)S(1)} %get-tuple-element.47), channel_id=1, source_target_pairs={{0,2},{1,9},{2,0},{3,11},{4,6},{5,13},{6,4},{7,15},{8,10},{9,1},{1... | collective-permute-start | bytes 208904 | tf_op jit(solution)/shard_map/ppermute | solution.py:319
  35.5 4.5 %collective-permute-start.14 = (f32[136,128]{1,0:T(8,128)S(1)}, f32[136,128]{1,0:T(8,128)S(1)}, u32[]{:S(2)}, u32[]{:S(2)}) collective-permute-start(f32[136,128]{1,0:T(8,128)S(1)} %fusion.1), channel_id=1, source_target_pairs={{0,96},{1,7},{2,98},{3,5},{4,100},{5,3},{6,102},{7,1},{8,104},{9,1... | collective-permute-start | bytes 208904 | tf_op jit(solution)/shard_map/ppermute | solution.py:319
  38.1 5.0 %collective-permute-start.13 = (f32[136,128]{1,0:T(8,128)S(1)}, f32[136,128]{1,0:T(8,128)S(1)}, u32[]{:S(2)}, u32[]{:S(2)}) collective-permute-start(f32[136,128]{1,0:T(8,128)S(1)} %fusion.1), channel_id=1, source_target_pairs={{0,64},{1,5},{2,66},{3,7},{4,68},{5,1},{6,70},{7,3},{8,72},{9,13},... | collective-permute-start | bytes 208904 | tf_op jit(solution)/shard_map/ppermute | solution.py:319
  38.6 4.5 %collective-permute-start.12 = (f32[136,128]{1,0:T(8,128)S(1)}, f32[136,128]{1,0:T(8,128)S(1)}, u32[]{:S(2)}, u32[]{:S(2)}) collective-permute-start(f32[136,128]{1,0:T(8,128)S(1)} %fusion.1), channel_id=1, source_target_pairs={{0,32},{1,3},{2,34},{3,1},{4,36},{5,7},{6,38},{7,5},{8,40},{9,11},... | collective-permute-start | bytes 208904 | tf_op jit(solution)/shard_map/ppermute | solution.py:319
  43.1 7.9 %collective-permute-start.16 = (f32[128,128]{1,0:T(8,128)S(1)}, f32[128,128]{1,0:T(8,128)S(1)}, u32[]{:S(2)}, u32[]{:S(2)}) collective-permute-start(f32[128,128]{1,0:T(8,128)S(1)} %slice.24), channel_id=1, source_target_pairs={{0,16},{1,65},{2,18},{3,67},{4,20},{5,69},{6,22},{7,71},{8,24},{9,... | collective-permute-start | bytes 196616 | tf_op jit(solution)/shard_map/ppermute | solution.py:319
  44.5 6.5 %collective-permute-start.17 = (f32[128,128]{1,0:T(8,128)S(1)}, f32[128,128]{1,0:T(8,128)S(1)}, u32[]{:S(2)}, u32[]{:S(2)}) collective-permute-start(f32[128,128]{1,0:T(8,128)S(1)} %slice.24), channel_id=1, source_target_pairs={{0,24},{1,97},{2,26},{3,99},{4,28},{5,101},{6,30},{7,103},{8,16},{... | collective-permute-start | bytes 196616 | tf_op jit(solution)/shard_map/ppermute | solution.py:319
  45.6 6.0 %collective-permute-start.15 = (f32[128,128]{1,0:T(8,128)S(1)}, f32[128,128]{1,0:T(8,128)S(1)}, u32[]{:S(2)}, u32[]{:S(2)}) collective-permute-start(f32[128,128]{1,0:T(8,128)S(1)} %slice.24), channel_id=1, source_target_pairs={{0,8},{1,33},{2,10},{3,35},{4,12},{5,37},{6,14},{7,39},{8,0},{9,41... | collective-permute-start | bytes 196616 | tf_op jit(solution)/shard_map/ppermute | solution.py:319
  51.6 13.1 %collective-permute-start.18 = (f32[128,128]{1,0:T(8,128)S(1)}, f32[128,128]{1,0:T(8,128)S(1)}, u32[]{:S(2)}, u32[]{:S(2)}) collective-permute-start(f32[128,128]{1,0:T(8,128)S(1)} %add_add_fusion.1.a_ref), channel_id=1, source_target_pairs={{0,192},{1,193},{2,194},{3,195},{4,196},{5,197},{6,198},{7,199},{8... | collective-permute-start | bytes 196616 | tf_op jit(solution)/shard_map/ppermute | solution.py:319
  55.4 8.9 %collective-permute-start.19 = (f32[56,128]{1,0:T(8,128)S(1)}, f32[56,128]{1,0:T(8,128)S(1)}, u32[]{:S(2)}, u32[]{:S(2)}) collective-permute-start(f32[56,128]{1,0:T(8,128)S(1)} %get-tuple-element.34), channel_id=1, source_target_pairs={{0,1},{1,0},{2,3},{3,2},{4,5},{5,4},{6,7},{7,6},{8,9},{9,8},{10,11... | collective-permute-start | bytes 86024 | tf_op jit(solution)/shard_map/ppermute | solution.py:319
  65.0 4.3 %collective-permute-start.22 = (f32[128,128]{1,0:T(8,128)S(1)}, f32[128,128]{1,0:T(8,128)S(1)}, u32[]{:S(2)}, u32[]{:S(2)}) collective-permute-start(f32[128,128]{1,0:T(8,128)S(1)} %finished_piece.1), channel_id=1, source_target_pairs={{0,6},{1,25},{2,4},{3,27},{4,2},{5,29},{6,0},{7,31},{8,14},{9,17},... | collective-permute-start | bytes 196616 | tf_op jit(solution)/shard_map/ppermute | solution.py:319
  66.7 4.6 %collective-permute-start.21 = (f32[128,128]{1,0:T(8,128)S(1)}, f32[128,128]{1,0:T(8,128)S(1)}, u32[]{:S(2)}, u32[]{:S(2)}) collective-permute-start(f32[128,128]{1,0:T(8,128)S(1)} %finished_piece.1), channel_id=1, source_target_pairs={{0,4},{1,17},{2,6},{3,19},{4,0},{5,21},{6,2},{7,23},{8,12},{9,25},... | collective-permute-start | bytes 196616 | tf_op jit(solution)/shard_map/ppermute | solution.py:319
  67.1 4.3 %collective-permute-start.20 = (f32[128,128]{1,0:T(8,128)S(1)}, f32[128,128]{1,0:T(8,128)S(1)}, u32[]{:S(2)}, u32[]{:S(2)}) collective-permute-start(f32[128,128]{1,0:T(8,128)S(1)} %finished_piece.1), channel_id=1, source_target_pairs={{0,2},{1,9},{2,0},{3,11},{4,6},{5,13},{6,4},{7,15},{8,10},{9,1},{1... | collective-permute-start | bytes 196616 | tf_op jit(solution)/shard_map/ppermute | solution.py:319
  71.4 4.8 %collective-permute-start.23 = (f32[4,128,128]{2,1,0:T(8,128)S(1)}, f32[4,128,128]{2,1,0:T(8,128)S(1)}, u32[]{:S(2)}, u32[]{:S(2)}) collective-permute-start(f32[4,128,128]{2,1,0:T(8,128)S(1)} %pad_maximum_fusion.pieces_ref), channel_id=1, source_target_pairs={{0,1},{1,0},{2,3},{3,2},{4,5},{5,4},{6,7},{7,6},{8,9},{9,8},{10,11... | collective-permute-start | bytes 786440 | tf_op jit(solution)/shard_map/ppermute | solution.py:319

commit v7 on v5

--- a/solution.py
+++ b/solution.py
@@ -2,6 +2,7 @@
 
 import jax
 import jax.numpy as jnp
+import numpy as np
 from jax import lax
 from jax.experimental import pallas as pl
 from jax.experimental.pallas import tpu as pltpu
@@ -57,9 +58,13 @@
     return jnp.concatenate([packed[:, RANK * i : RANK * (i + 1)] for i in range(4)], axis=0)
 
 
-def left_kernel(grads_hbm, errors_hbm, q_hbm, other_ref, own_ref, p_other_ref, p_own_ref, grads_ref, q_ref, grads_sem, errors_sem, q_sem):
-    core = lax.axis_index("c")
-    parts = ((1 - core, other_ref, p_other_ref), (core, own_ref, p_own_ref))
+def lane():
+    return (lax.axis_index("c") + sum(lax.axis_index(name) // 2 for name in ("x", "y", "z"))) % 2
+
+
+def left_kernel(grads_hbm, errors_hbm, q_hbm, other_ref, own_ref, p_send_ref, p_keep_ref, grads_ref, q_ref, grads_sem, errors_sem, q_sem):
+    core, mine = lax.axis_index("c"), lane()
+    parts = ((1 - mine, other_ref, p_send_ref), (mine, own_ref, p_keep_ref))
     q_copy = pltpu.make_async_copy(q_hbm, q_ref, q_sem)
     copies = [
         (
@@ -82,12 +87,13 @@
         full_ref[...] = full
         f_hi, f_lo = split(full)
         wide = dot(f_hi, both, 1, 1)
-        p_ref[...] = pack_rows(wide[:, :RANK] + wide[:, RANK:] + dot(f_lo, q_hi, 1, 1))
+        p_ref[core] = pack_rows(wide[:, :RANK] + wide[:, RANK:] + dot(f_lo, q_hi, 1, 1))
+        p_ref[1 - core] = jnp.zeros(p_ref.shape[1:], F32)
 
 
 def left_factors(grads, errors, q_prev):
     _, projections, rows, columns = grads.shape
-    full, p = pltpu.VMEM((rows, columns), F32), pltpu.VMEM((rows // 4, LANES), F32)
+    full, p = pltpu.VMEM((rows, columns), F32), pltpu.VMEM((2, rows // 4, LANES), F32)
     return pl.pallas_call(
         left_kernel,
         in_specs=[AWAY] * 3,
@@ -109,13 +115,16 @@
     slots, height, _ = out_ref.shape
     tiles = (height - 8) // RANK
     width = tiles * LANES
-    x = lax.axis_index("x")
-    half = p_ref.shape[0] // 2
-    columns = jnp.concatenate([unpack_rows(p_ref[:half]), unpack_rows(p_ref[half:])], axis=0)
-    p = (columns * (1.0 / replicas)).T
-    p_hi, p_lo = split(p)
+    x, core = lax.axis_index("x"), lax.axis_index("c")
+
+    def factors(first, second):
+        columns = jnp.concatenate([unpack_rows(p_ref[first]), unpack_rows(p_ref[second])], axis=0)
+        return (columns * (1.0 / replicas)).T
+
+    p = factors(0, 1)
+    gram = pack(dot(p, p, 1, 1, lax.Precision.HIGHEST))
+    p_hi, p_lo = split(factors(core, 1 - core))
     both = jnp.concatenate([p_hi, p_lo], axis=0)
-    gram = pack(dot(p, p, 1, 1, lax.Precision.HIGHEST))
     for slot in range(slots):
         here = pl.ds(pl.multiple_of((x ^ slot) * width, width), width)
         f_hi, f_lo = split(jnp.concatenate([own_ref[:, here], gift_ref[:, here]], axis=0))
@@ -169,15 +178,15 @@
 
 
 def hat_kernel(replicas, p_ref, inverse_ref, own_ref, other_ref):
-    half = p_ref.shape[0] // 2
+    core = lax.axis_index("c")
     inverse = unpack(inverse_ref[...])
-    for i, out_ref in enumerate((own_ref, other_ref)):
-        p = unpack_rows(p_ref[half * i : half * (i + 1)]) * (1.0 / replicas)
+    for place, out_ref in ((core, own_ref), (1 - core, other_ref)):
+        p = unpack_rows(p_ref[place]) * (1.0 / replicas)
         out_ref[...] = pack_rows(dot(p, inverse, 1, 1, lax.Precision.HIGHEST))
 
 
 def orthonormal(p_sum, inverse, replicas):
-    half = jax.ShapeDtypeStruct((p_sum.shape[0] // 2, LANES), F32)
+    half = jax.ShapeDtypeStruct(p_sum.shape[1:], F32)
     return pl.pallas_call(
         functools.partial(hat_kernel, replicas),
         in_specs=[WHOLE] * 2,
@@ -238,8 +247,8 @@
     slots, height, _ = pieces_ref.shape
     tiles = height // RANK
     width = tiles * LANES
-    x, core = lax.axis_index("x"), lax.axis_index("c")
-    i, m = (0, core) if mine else (1, 1 - core)
+    x = lax.axis_index("x")
+    i, m = (0, lane()) if mine else (1, 1 - lane())
     copies = []
     for slot in range(slots):
         block = x ^ slot
@@ -303,7 +312,16 @@
 
 
 def swap(value, axis, bit):
-    return lax.ppermute(value, axis, [(i, i ^ bit) for i in range(lax.axis_size(axis))])
+    names = ("z", "y", "x", "c")
+    sizes = tuple(lax.axis_size(name) for name in names)
+    pairs = []
+    for here in np.ndindex(*sizes):
+        there = list(here)
+        there[names.index(axis)] ^= bit
+        if axis != "c":
+            there[-1] ^= bit // 2 % 2
+        pairs.append((int(np.ravel_multi_index(here, sizes)), int(np.ravel_multi_index(there, sizes))))
+    return lax.ppermute(value, names, pairs)
 
 
 def four(values, axis):
@@ -312,8 +330,8 @@
 
 def shards(grads, errors, q_prev, moment1, moment2):
     replicas, slots = lax.axis_size(("z", "y")), lax.axis_size("x")
-    other_full, own_full, p_other, p_own = left_factors(grads, errors, q_prev)
-    p = jnp.concatenate([p_own, swap(p_other, "c", 1)])
+    other_full, own_full, p_send, p_keep = left_factors(grads, errors, q_prev)
+    p = p_keep + swap(p_send, "c", 1)
     p, other_full = lax.optimization_barrier((p, other_full))
     gift = swap(other_full, "c", 1)
     p = four([p] * 4, "y")

time: 75.3 us -> 77.6 us (1.031)
  waiting for transfers between devices: 19 us -> 29.6 us
  starting transfers between devices: 43.1 us -> 34.7 us
    ppermute x24, waiting for transfers between devices: 19 us -> 29.6 us  [swap(): return lax.ppermute(value, names, pairs)]
    ppermute x24, starting transfers between devices: 43.1 us -> 34.7 us  [swap(): return lax.ppermute(value, names, pairs)]
  transfers between devices with their start and end apart: 24 -> 24, of which waited for: 14 -> 15; matrix products, arithmetic and copies ran while one was open for 0% -> 0% of each run, Pallas kernels for 7% -> 7%
where the time goes in v7:
time: 77.6 us; the launch traced here: 77.5 us
  starting transfers between devices  34.7 us (45%)
  waiting for transfers between devices  29.6 us (38%)
  Pallas kernels  12.1 us (16%)
  between operations  0.91 us (1%)
    ppermute x24, starting transfers between devices, swap(): return lax.ppermute(value, names, pairs)  34.7 us
    ppermute x24, waiting for transfers between devices, swap(): return lax.ppermute(value, names, pairs)  29.6 us
    pallas_call x1, Pallas kernels, left_factors(): pl.pallas_call(left_kernel, in_specs=[AWAY] * 3, out_specs=[WHOLE] * 4, o...  3.64 us
    pallas_call x2, Pallas kernels, update(): pl.pallas_call(functools.partial(update_kernel, mine), in_specs=[WHOLE] *...  3.29 us
    pallas_call x1, Pallas kernels, inverse_factor(): pl.pallas_call(factor_kernel, in_specs=[WHOLE], out_specs=WHOLE, out_shap...  2.85 us
  transfers between devices with their start and end apart: 24, of which 15 were waited for; matrix products, arithmetic and copies ran while one was open for 0% of the time, Pallas kernels for 7%

profile of v7, /device:TPU:1, one launch (start us, length us, event | category | flops | bytes accessed | tf_op | source)
XLA Modules:
  0.0 77.5 jit_solution(14365494024292721259)
XLA Ops:
  0.6 3.6 %left_factors.1 = (f32[224,2048]{1,0:T(8,128)S(1)}, f32[224,2048]{1,0:T(8,128)S(1)}, f32[2,56,128]{2,1,0:T(8,128)S(1)}, f32[2,56,128]{2,1,0:T(8,128)S(1)}) custom-call(bf16[1,2,224,2048]{3,2,1,0:T(8,128)(2,1)} %grads_hbm.1, f32[1,2,224,2048]{3,2,1,0:T(8,128)} %errors_hbm.1, f32[2,32,2048]{2,1,0:T(8,128)} %q_hbm.1), custom_call_target="tpu_custom_call" | custom-call | tf_op jit(solution)/shard_map/left_factors/pallas_call | solution.py:97
  4.3 3.3 %collective-permute-start = (f32[2,56,128]{2,1,0:T(8,128)S(1)}, f32[2,56,128]{2,1,0:T(8,128)S(1)}, u32[]{:S(2)}, u32[]{:S(2)}) collective-permute-start(f32[2,56,128]{2,1,0:T(8,128)S(1)} %get-tuple-element.29), channel_id=1, source_target_pairs={{0,1},{1,0},{2,3},{3,2},{4,5},{5,4},{6,7},{7,6},{8,9},{9,8},{10,11... | collective-permute-start | bytes 172040 | tf_op jit(solution)/shard_map/ppermute | solution.py:324
  7.6 0.9 %collective-permute-done = f32[2,56,128]{2,1,0:T(8,128)S(1)} collective-permute-done((f32[2,56,128]{2,1,0:T(8,128)S(1)}, f32[2,56,128]{2,1,0:T(8,128)S(1)}, u32[]{:S(2)}, u32[]{:S(2)}) %collective-permute-start) | collective-permute-done | bytes 57376 | tf_op jit(solution)/shard_map/ppermute | solution.py:324
  8.9 1.0 %collective-permute-start.3 = (f32[2,56,128]{2,1,0:T(8,128)S(1)}, f32[2,56,128]{2,1,0:T(8,128)S(1)}, u32[]{:S(2)}, u32[]{:S(2)}) collective-permute-start(f32[2,56,128]{2,1,0:T(8,128)S(1)} %add.51), channel_id=1, source_target_pairs={{0,25},{1,24},{2,27},{3,26},{4,29},{5,28},{6,31},{7,30},{8,17},{9,... | collective-permute-start | bytes 172040 | tf_op jit(solution)/shard_map/ppermute | solution.py:324
  10.6 1.9 %collective-permute-start.1 = (f32[2,56,128]{2,1,0:T(8,128)S(1)}, f32[2,56,128]{2,1,0:T(8,128)S(1)}, u32[]{:S(2)}, u32[]{:S(2)}) collective-permute-start(f32[2,56,128]{2,1,0:T(8,128)S(1)} %add.51), channel_id=1, source_target_pairs={{0,8},{1,9},{2,10},{3,11},{4,12},{5,13},{6,14},{7,15},{8,0},{9,1},... | collective-permute-start | bytes 172040 | tf_op jit(solution)/shard_map/ppermute | solution.py:324
  12.5 1.3 %collective-permute-done.3 = f32[2,56,128]{2,1,0:T(8,128)S(1)} collective-permute-done((f32[2,56,128]{2,1,0:T(8,128)S(1)}, f32[2,56,128]{2,1,0:T(8,128)S(1)}, u32[]{:S(2)}, u32[]{:S(2)}) %collective-permute-start.3) | collective-permute-done | bytes 57376 | tf_op jit(solution)/shard_map/ppermute | solution.py:324
  13.8 1.9 %collective-permute-done.2 = f32[2,56,128]{2,1,0:T(8,128)S(1)} collective-permute-done((f32[2,56,128]{2,1,0:T(8,128)S(1)}, f32[2,56,128]{2,1,0:T(8,128)S(1)}, u32[]{:S(2)}, u32[]{:S(2)}) %collective-permute-start.2) | collective-permute-done | bytes 57376 | tf_op jit(solution)/shard_map/ppermute | solution.py:324
  16.0 4.2 %collective-permute-start.6 = (f32[2,56,128]{2,1,0:T(8,128)S(1)}, f32[2,56,128]{2,1,0:T(8,128)S(1)}, u32[]{:S(2)}, u32[]{:S(2)}) collective-permute-start(f32[2,56,128]{2,1,0:T(8,128)S(1)} %add_add_fusion.3), channel_id=1, source_target_pairs={{0,97},{1,96},{2,99},{3,98},{4,101},{5,100},{6,103},{7,102},{8,105... | collective-permute-start | bytes 172040 | tf_op jit(solution)/shard_map/ppermute | solution.py:324
  20.6 1.8 %collective-permute-done.6 = f32[2,56,128]{2,1,0:T(8,128)S(1)} collective-permute-done((f32[2,56,128]{2,1,0:T(8,128)S(1)}, f32[2,56,128]{2,1,0:T(8,128)S(1)}, u32[]{:S(2)}, u32[]{:S(2)}) %collective-permute-start.6) | collective-permute-done | bytes 57376 | tf_op jit(solution)/shard_map/ppermute | solution.py:324
  22.3 2.7 %collective-permute-done.5 = f32[2,56,128]{2,1,0:T(8,128)S(1)} collective-permute-done((f32[2,56,128]{2,1,0:T(8,128)S(1)}, f32[2,56,128]{2,1,0:T(8,128)S(1)}, u32[]{:S(2)}, u32[]{:S(2)}) %collective-permute-start.5) | collective-permute-done | bytes 57376 | tf_op jit(solution)/shard_map/ppermute | solution.py:324
  25.1 4.4 %collective-permute-start.7 = (f32[2,56,128]{2,1,0:T(8,128)S(1)}, f32[2,56,128]{2,1,0:T(8,128)S(1)}, u32[]{:S(2)}, u32[]{:S(2)}) collective-permute-start(f32[2,56,128]{2,1,0:T(8,128)S(1)} %add_add_fusion.2), channel_id=1, source_target_pairs={{0,193},{1,192},{2,195},{3,194},{4,197},{5,196},{6,199},{7,198},{8... | collective-permute-start | bytes 172040 | tf_op jit(solution)/shard_map/ppermute | solution.py:324
  29.5 2.2 %collective-permute-done.7 = f32[2,56,128]{2,1,0:T(8,128)S(1)} collective-permute-done((f32[2,56,128]{2,1,0:T(8,128)S(1)}, f32[2,56,128]{2,1,0:T(8,128)S(1)}, u32[]{:S(2)}, u32[]{:S(2)}) %collective-permute-start.7) | collective-permute-done | bytes 57376 | tf_op jit(solution)/shard_map/ppermute | solution.py:324
  31.8 1.2 %right_terms.1 = f32[4,136,128]{2,1,0:T(8,128)S(1)} custom-call(f32[2,56,128]{2,1,0:T(8,128)S(1)} %add.58.p_ref, f32[224,2048]{1,0:T(8,128)S(1)} %get-tuple-element.32.own_ref.full_ref, f32[224,2048]{1,0:T(8,128)S(1)} %collective-permute-done.8.gift_ref), custom_call_target="tpu_custom_call" | custom-call | tf_op jit(solution)/shard_map/right_terms/pallas_call | solution.py:140
  33.0 2.8 %collective-permute-start.11 = (f32[136,128]{1,0:T(8,128)S(1)}, f32[136,128]{1,0:T(8,128)S(1)}, u32[]{:S(2)}, u32[]{:S(2)}) collective-permute-start(f32[136,128]{1,0:T(8,128)S(1)} %get-tuple-element.51), channel_id=1, source_target_pairs={{0,7},{1,6},{2,5},{3,4},{4,3},{5,2},{6,1},{7,0},{8,15},{9,14},{10,... | collective-permute-start | bytes 208904 | tf_op jit(solution)/shard_map/ppermute | solution.py:324
  36.6 2.2 %collective-permute-done.11 = f32[136,128]{1,0:T(8,128)S(1)} collective-permute-done((f32[136,128]{1,0:T(8,128)S(1)}, f32[136,128]{1,0:T(8,128)S(1)}, u32[]{:S(2)}, u32[]{:S(2)}) %collective-permute-start.11) | collective-permute-done | bytes 69664 | tf_op jit(solution)/shard_map/ppermute | solution.py:324
  38.8 2.9 %collective-permute-done.10 = f32[136,128]{1,0:T(8,128)S(1)} collective-permute-done((f32[136,128]{1,0:T(8,128)S(1)}, f32[136,128]{1,0:T(8,128)S(1)}, u32[]{:S(2)}, u32[]{:S(2)}) %collective-permute-start.10) | collective-permute-done | bytes 69664 | tf_op jit(solution)/shard_map/ppermute | solution.py:324
  41.7 1.7 %collective-permute-start.13 = (f32[128,128]{1,0:T(8,128)S(1)}, f32[128,128]{1,0:T(8,128)S(1)}, u32[]{:S(2)}, u32[]{:S(2)}) collective-permute-start(f32[128,128]{1,0:T(8,128)S(1)} %slice.24), channel_id=1, source_target_pairs={{0,17},{1,16},{2,19},{3,18},{4,21},{5,20},{6,23},{7,22},{8,25},{9,... | collective-permute-start | bytes 196616 | tf_op jit(solution)/shard_map/ppermute | solution.py:324
  43.5 1.1 %collective-permute-start.14 = (f32[128,128]{1,0:T(8,128)S(1)}, f32[128,128]{1,0:T(8,128)S(1)}, u32[]{:S(2)}, u32[]{:S(2)}) collective-permute-start(f32[128,128]{1,0:T(8,128)S(1)} %slice.24), channel_id=1, source_target_pairs={{0,25},{1,24},{2,27},{3,26},{4,29},{5,28},{6,31},{7,30},{8,17},{9,... | collective-permute-start | bytes 196616 | tf_op jit(solution)/shard_map/ppermute | solution.py:324
  44.7 2.8 %inverse_factor.1.inverse_ref = f32[8,128]{1,0:T(8,128)S(1)} custom-call(f32[136,128]{1,0:T(8,128)S(1)} %fusion.1.sum_ref), custom_call_target="tpu_custom_call" | custom-call | flops 4000000 | bytes 4000000 | tf_op jit(solution)/shard_map/inverse_factor/pallas_call | solution.py:169
  47.6 1.2 %collective-permute-done.14 = f32[128,128]{1,0:T(8,128)S(1)} collective-permute-done((f32[128,128]{1,0:T(8,128)S(1)}, f32[128,128]{1,0:T(8,128)S(1)}, u32[]{:S(2)}, u32[]{:S(2)}) %collective-permute-start.14) | collective-permute-done | bytes 65568 | tf_op jit(solution)/shard_map/ppermute | solution.py:324
  48.8 2.9 %collective-permute-start.17 = (f32[128,128]{1,0:T(8,128)S(1)}, f32[128,128]{1,0:T(8,128)S(1)}, u32[]{:S(2)}, u32[]{:S(2)}) collective-permute-start(f32[128,128]{1,0:T(8,128)S(1)} %add_add_fusion.1), channel_id=1, source_target_pairs={{0,97},{1,96},{2,99},{3,98},{4,101},{5,100},{6,103},{7,102},{8,105... | collective-permute-start | bytes 196616 | tf_op jit(solution)/shard_map/ppermute | solution.py:324
  51.6 1.3 %collective-permute-start.16 = (f32[128,128]{1,0:T(8,128)S(1)}, f32[128,128]{1,0:T(8,128)S(1)}, u32[]{:S(2)}, u32[]{:S(2)}) collective-permute-start(f32[128,128]{1,0:T(8,128)S(1)} %add_add_fusion.1), channel_id=1, source_target_pairs={{0,65},{1,64},{2,67},{3,66},{4,69},{5,68},{6,71},{7,70},{8,73},{9,... | collective-permute-start | bytes 196616 | tf_op jit(solution)/shard_map/ppermute | solution.py:324
  53.4 0.7 collective-permute-start.18
  54.8 4.4 %collective-permute-done.16 = f32[128,128]{1,0:T(8,128)S(1)} collective-permute-done((f32[128,128]{1,0:T(8,128)S(1)}, f32[128,128]{1,0:T(8,128)S(1)}, u32[]{:S(2)}, u32[]{:S(2)}) %collective-permute-start.16) | collective-permute-done | bytes 65568 | tf_op jit(solution)/shard_map/ppermute | solution.py:324
  59.3 3.1 %collective-permute-start.19 = (f32[128,128]{1,0:T(8,128)S(1)}, f32[128,128]{1,0:T(8,128)S(1)}, u32[]{:S(2)}, u32[]{:S(2)}) collective-permute-start(f32[128,128]{1,0:T(8,128)S(1)} %add_add_fusion.a_ref), channel_id=1, source_target_pairs={{0,193},{1,192},{2,195},{3,194},{4,197},{5,196},{6,199},{7,198},{8... | collective-permute-start | bytes 196616 | tf_op jit(solution)/shard_map/ppermute | solution.py:324
  62.8 2.9 %collective-permute-done.19.b_ref = f32[128,128]{1,0:T(8,128)S(1)} collective-permute-done((f32[128,128]{1,0:T(8,128)S(1)}, f32[128,128]{1,0:T(8,128)S(1)}, u32[]{:S(2)}, u32[]{:S(2)}) %collective-permute-start.19) | collective-permute-done | bytes 65568 | tf_op jit(solution)/shard_map/ppermute | solution.py:324
  65.9 2.1 %collective-permute-start.22 = (f32[128,128]{1,0:T(8,128)S(1)}, f32[128,128]{1,0:T(8,128)S(1)}, u32[]{:S(2)}, u32[]{:S(2)}) collective-permute-start(f32[128,128]{1,0:T(8,128)S(1)} %finished_piece.1), channel_id=1, source_target_pairs={{0,7},{1,6},{2,5},{3,4},{4,3},{5,2},{6,1},{7,0},{8,15},{9,14},{10,... | collective-permute-start | bytes 196616 | tf_op jit(solution)/shard_map/ppermute | solution.py:324
  68.5 0.9 %collective-permute-start.20 = (f32[128,128]{1,0:T(8,128)S(1)}, f32[128,128]{1,0:T(8,128)S(1)}, u32[]{:S(2)}, u32[]{:S(2)}) collective-permute-start(f32[128,128]{1,0:T(8,128)S(1)} %finished_piece.1), channel_id=1, source_target_pairs={{0,2},{1,3},{2,0},{3,1},{4,6},{5,7},{6,4},{7,5},{8,10},{9,11},{10,... | collective-permute-start | bytes 196616 | tf_op jit(solution)/shard_map/ppermute | solution.py:324
  69.5 1.8 %collective-permute-done.22 = f32[128,128]{1,0:T(8,128)S(1)} collective-permute-done((f32[128,128]{1,0:T(8,128)S(1)}, f32[128,128]{1,0:T(8,128)S(1)}, u32[]{:S(2)}, u32[]{:S(2)}) %collective-permute-start.22) | collective-permute-done | bytes 65568 | tf_op jit(solution)/shard_map/ppermute | solution.py:324
  71.3 2.6 %collective-permute-done.21 = f32[128,128]{1,0:T(8,128)S(1)} collective-permute-done((f32[128,128]{1,0:T(8,128)S(1)}, f32[128,128]{1,0:T(8,128)S(1)}, u32[]{:S(2)}, u32[]{:S(2)}) %collective-permute-start.21) | collective-permute-done | bytes 65568 | tf_op jit(solution)/shard_map/ppermute | solution.py:324
  74.0 1.6 %update_own.1 = (f32[1,2,224,2048]{3,2,1,0:T(8,128)}, f32[2,112,128]{2,1,0:T(8,128)}, f32[2,112,128]{2,1,0:T(8,128)}, bf16[2,112,128]{2,1,0:T(8,128)(2,1)}, f32[2,32,2048]{2,1,0:T(8,128)}) custom-call(f32[4,128,128]{2,1,0:T(8,128)S(1)} %pad_maximum_fusion.pieces_ref, bf16[2,224,96]{2,1,0:T(8,128)(2,1)S(1)} %get-tuple-element.44.hat_ref, ...), custom_call_target="tpu_custom_call" | custom-call | flops 100000000 | bytes 4000000 | tf_op jit(solution)/shard_map/update_own/pallas_call | solution.py:285
  75.7 1.6 %update_other.1 = (f32[1,2,224,2048]{3,2,1,0:T(8,128)}, f32[2,112,128]{2,1,0:T(8,128)}, f32[2,112,128]{2,1,0:T(8,128)}, bf16[2,112,128]{2,1,0:T(8,128)(2,1)}, f32[2,32,2048]{2,1,0:T(8,128)}) custom-call(f32[4,128,128]{2,1,0:T(8,128)S(1)} %collective-permute-done.23.pieces_ref, ...), custom_call_target="tpu_custom_call", output_to_operand_aliasing={{0}: (6, {}), {1}: (7, {}), {2}: (8, {}), {3}: (9, {}), {4}... | custom-call | flops 100000000 | bytes 4000000 | tf_op jit(solution)/shard_map/update_other/pallas_call | solution.py:285
  (38 shorter events, 5.6 us)
Async XLA Ops:
  4.3 4.2 %collective-permute-start = (f32[2,56,128]{2,1,0:T(8,128)S(1)}, f32[2,56,128]{2,1,0:T(8,128)S(1)}, u32[]{:S(2)}, u32[]{:S(2)}) collective-permute-start(f32[2,56,128]{2,1,0:T(8,128)S(1)} %get-tuple-element.29), channel_id=1, source_target_pairs={{0,1},{1,0},{2,3},{3,2},{4,5},{5,4},{6,7},{7,6},{8,9},{9,8},{10,11... | collective-permute-start | bytes 172040 | tf_op jit(solution)/shard_map/ppermute | solution.py:324
  8.5 23.3 %collective-permute-start.8 = (f32[224,2048]{1,0:T(8,128)S(1)}, f32[224,2048]{1,0:T(8,128)S(1)}, u32[]{:S(2)}, u32[]{:S(2)}) collective-permute-start(f32[224,2048]{1,0:T(8,128)S(1)} %get-tuple-element.33.full_ref), channel_id=1, source_target_pairs={{0,1},{1,0},{2,3},{3,2},{4,5},{5,4},{6,7},{7,6},{8,9},{9,8},{10,11... | collective-permute-start | bytes 5505032 | tf_op jit(solution)/shard_map/ppermute | solution.py:324
  8.9 4.9 %collective-permute-start.3 = (f32[2,56,128]{2,1,0:T(8,128)S(1)}, f32[2,56,128]{2,1,0:T(8,128)S(1)}, u32[]{:S(2)}, u32[]{:S(2)}) collective-permute-start(f32[2,56,128]{2,1,0:T(8,128)S(1)} %add.51), channel_id=1, source_target_pairs={{0,25},{1,24},{2,27},{3,26},{4,29},{5,28},{6,31},{7,30},{8,17},{9,... | collective-permute-start | bytes 172040 | tf_op jit(solution)/shard_map/ppermute | solution.py:324
  9.9 5.7 %collective-permute-start.2 = (f32[2,56,128]{2,1,0:T(8,128)S(1)}, f32[2,56,128]{2,1,0:T(8,128)S(1)}, u32[]{:S(2)}, u32[]{:S(2)}) collective-permute-start(f32[2,56,128]{2,1,0:T(8,128)S(1)} %add.51), channel_id=1, source_target_pairs={{0,17},{1,16},{2,19},{3,18},{4,21},{5,20},{6,23},{7,22},{8,25},{9,... | collective-permute-start | bytes 172040 | tf_op jit(solution)/shard_map/ppermute | solution.py:324
  10.6 5.3 %collective-permute-start.1 = (f32[2,56,128]{2,1,0:T(8,128)S(1)}, f32[2,56,128]{2,1,0:T(8,128)S(1)}, u32[]{:S(2)}, u32[]{:S(2)}) collective-permute-start(f32[2,56,128]{2,1,0:T(8,128)S(1)} %add.51), channel_id=1, source_target_pairs={{0,8},{1,9},{2,10},{3,11},{4,12},{5,13},{6,14},{7,15},{8,0},{9,1},... | collective-permute-start | bytes 172040 | tf_op jit(solution)/shard_map/ppermute | solution.py:324
  16.0 6.4 %collective-permute-start.6 = (f32[2,56,128]{2,1,0:T(8,128)S(1)}, f32[2,56,128]{2,1,0:T(8,128)S(1)}, u32[]{:S(2)}, u32[]{:S(2)}) collective-permute-start(f32[2,56,128]{2,1,0:T(8,128)S(1)} %add_add_fusion.3), channel_id=1, source_target_pairs={{0,97},{1,96},{2,99},{3,98},{4,101},{5,100},{6,103},{7,102},{8,105... | collective-permute-start | bytes 172040 | tf_op jit(solution)/shard_map/ppermute | solution.py:324
  20.2 4.9 %collective-permute-start.5 = (f32[2,56,128]{2,1,0:T(8,128)S(1)}, f32[2,56,128]{2,1,0:T(8,128)S(1)}, u32[]{:S(2)}, u32[]{:S(2)}) collective-permute-start(f32[2,56,128]{2,1,0:T(8,128)S(1)} %add_add_fusion.3), channel_id=1, source_target_pairs={{0,65},{1,64},{2,67},{3,66},{4,69},{5,68},{6,71},{7,70},{8,73},{9,... | collective-permute-start | bytes 172040 | tf_op jit(solution)/shard_map/ppermute | solution.py:324
  20.2 4.9 %collective-permute-start.4 = (f32[2,56,128]{2,1,0:T(8,128)S(1)}, f32[2,56,128]{2,1,0:T(8,128)S(1)}, u32[]{:S(2)}, u32[]{:S(2)}) collective-permute-start(f32[2,56,128]{2,1,0:T(8,128)S(1)} %add_add_fusion.3), channel_id=1, source_target_pairs={{0,32},{1,33},{2,34},{3,35},{4,36},{5,37},{6,38},{7,39},{8,40},{9,... | collective-permute-start | bytes 172040 | tf_op jit(solution)/shard_map/ppermute | solution.py:324
  25.1 6.7 %collective-permute-start.7 = (f32[2,56,128]{2,1,0:T(8,128)S(1)}, f32[2,56,128]{2,1,0:T(8,128)S(1)}, u32[]{:S(2)}, u32[]{:S(2)}) collective-permute-start(f32[2,56,128]{2,1,0:T(8,128)S(1)} %add_add_fusion.2), channel_id=1, source_target_pairs={{0,193},{1,192},{2,195},{3,194},{4,197},{5,196},{6,199},{7,198},{8... | collective-permute-start | bytes 172040 | tf_op jit(solution)/shard_map/ppermute | solution.py:324
  32.9 41.1 %copy-start = (f32[2,112,128]{2,1,0:T(8,128)S(1)}, f32[2,112,128]{2,1,0:T(8,128)}, u32[]{:S(2)}) copy-start(f32[2,112,128]{2,1,0:T(8,128)} %m1_ref.3) | copy-start | bytes 344068
  33.0 41.1 %copy-start.1 = (f32[2,112,128]{2,1,0:T(8,128)S(1)}, f32[2,112,128]{2,1,0:T(8,128)}, u32[]{:S(2)}) copy-start(f32[2,112,128]{2,1,0:T(8,128)} %m2_ref.3) | copy-start | bytes 344068
  33.0 5.8 %collective-permute-start.11 = (f32[136,128]{1,0:T(8,128)S(1)}, f32[136,128]{1,0:T(8,128)S(1)}, u32[]{:S(2)}, u32[]{:S(2)}) collective-permute-start(f32[136,128]{1,0:T(8,128)S(1)} %get-tuple-element.51), channel_id=1, source_target_pairs={{0,7},{1,6},{2,5},{3,4},{4,3},{5,2},{6,1},{7,0},{8,15},{9,14},{10,... | collective-permute-start | bytes 208904 | tf_op jit(solution)/shard_map/ppermute | solution.py:324
  35.8 5.9 %collective-permute-start.10 = (f32[136,128]{1,0:T(8,128)S(1)}, f32[136,128]{1,0:T(8,128)S(1)}, u32[]{:S(2)}, u32[]{:S(2)}) collective-permute-start(f32[136,128]{1,0:T(8,128)S(1)} %get-tuple-element.52), channel_id=1, source_target_pairs={{0,5},{1,4},{2,7},{3,6},{4,1},{5,0},{6,3},{7,2},{8,13},{9,12},{10,... | collective-permute-start | bytes 208904 | tf_op jit(solution)/shard_map/ppermute | solution.py:324
  36.4 5.3 %collective-permute-start.9 = (f32[136,128]{1,0:T(8,128)S(1)}, f32[136,128]{1,0:T(8,128)S(1)}, u32[]{:S(2)}, u32[]{:S(2)}) collective-permute-start(f32[136,128]{1,0:T(8,128)S(1)} %get-tuple-element.53), channel_id=1, source_target_pairs={{0,2},{1,3},{2,0},{3,1},{4,6},{5,7},{6,4},{7,5},{8,10},{9,11},{10,... | collective-permute-start | bytes 208904 | tf_op jit(solution)/shard_map/ppermute | solution.py:324
  41.7 5.9 %collective-permute-start.13 = (f32[128,128]{1,0:T(8,128)S(1)}, f32[128,128]{1,0:T(8,128)S(1)}, u32[]{:S(2)}, u32[]{:S(2)}) collective-permute-start(f32[128,128]{1,0:T(8,128)S(1)} %slice.24), channel_id=1, source_target_pairs={{0,17},{1,16},{2,19},{3,18},{4,21},{5,20},{6,23},{7,22},{8,25},{9,... | collective-permute-start | bytes 196616 | tf_op jit(solution)/shard_map/ppermute | solution.py:324
  43.5 5.3 %collective-permute-start.14 = (f32[128,128]{1,0:T(8,128)S(1)}, f32[128,128]{1,0:T(8,128)S(1)}, u32[]{:S(2)}, u32[]{:S(2)}) collective-permute-start(f32[128,128]{1,0:T(8,128)S(1)} %slice.24), channel_id=1, source_target_pairs={{0,25},{1,24},{2,27},{3,26},{4,29},{5,28},{6,31},{7,30},{8,17},{9,... | collective-permute-start | bytes 196616 | tf_op jit(solution)/shard_map/ppermute | solution.py:324
  44.5 4.2 %collective-permute-start.12 = (f32[128,128]{1,0:T(8,128)S(1)}, f32[128,128]{1,0:T(8,128)S(1)}, u32[]{:S(2)}, u32[]{:S(2)}) collective-permute-start(f32[128,128]{1,0:T(8,128)S(1)} %slice.24), channel_id=1, source_target_pairs={{0,8},{1,9},{2,10},{3,11},{4,12},{5,13},{6,14},{7,15},{8,0},{9,1},... | collective-permute-start | bytes 196616 | tf_op jit(solution)/shard_map/ppermute | solution.py:324
  48.8 6.0 %collective-permute-start.17 = (f32[128,128]{1,0:T(8,128)S(1)}, f32[128,128]{1,0:T(8,128)S(1)}, u32[]{:S(2)}, u32[]{:S(2)}) collective-permute-start(f32[128,128]{1,0:T(8,128)S(1)} %add_add_fusion.1), channel_id=1, source_target_pairs={{0,97},{1,96},{2,99},{3,98},{4,101},{5,100},{6,103},{7,102},{8,105... | collective-permute-start | bytes 196616 | tf_op jit(solution)/shard_map/ppermute | solution.py:324
  51.6 7.6 %collective-permute-start.16 = (f32[128,128]{1,0:T(8,128)S(1)}, f32[128,128]{1,0:T(8,128)S(1)}, u32[]{:S(2)}, u32[]{:S(2)}) collective-permute-start(f32[128,128]{1,0:T(8,128)S(1)} %add_add_fusion.1), channel_id=1, source_target_pairs={{0,65},{1,64},{2,67},{3,66},{4,69},{5,68},{6,71},{7,70},{8,73},{9,... | collective-permute-start | bytes 196616 | tf_op jit(solution)/shard_map/ppermute | solution.py:324
  52.9 6.3 %collective-permute-start.15 = (f32[128,128]{1,0:T(8,128)S(1)}, f32[128,128]{1,0:T(8,128)S(1)}, u32[]{:S(2)}, u32[]{:S(2)}) collective-permute-start(f32[128,128]{1,0:T(8,128)S(1)} %add_add_fusion.1), channel_id=1, source_target_pairs={{0,32},{1,33},{2,34},{3,35},{4,36},{5,37},{6,38},{7,39},{8,40},{9,... | collective-permute-start | bytes 196616 | tf_op jit(solution)/shard_map/ppermute | solution.py:324
  53.4 5.8 %collective-permute-start.18 = (f32[56,128]{1,0:T(8,128)S(1)}, f32[56,128]{1,0:T(8,128)S(1)}, u32[]{:S(2)}, u32[]{:S(2)}) collective-permute-start(f32[56,128]{1,0:T(8,128)S(1)} %get-tuple-element.37), channel_id=1, source_target_pairs={{0,1},{1,0},{2,3},{3,2},{4,5},{5,4},{6,7},{7,6},{8,9},{9,8},{10,11... | collective-permute-start | bytes 86024 | tf_op jit(solution)/shard_map/ppermute | solution.py:324
  59.3 6.4 %collective-permute-start.19 = (f32[128,128]{1,0:T(8,128)S(1)}, f32[128,128]{1,0:T(8,128)S(1)}, u32[]{:S(2)}, u32[]{:S(2)}) collective-permute-start(f32[128,128]{1,0:T(8,128)S(1)} %add_add_fusion.a_ref), channel_id=1, source_target_pairs={{0,193},{1,192},{2,195},{3,194},{4,197},{5,196},{6,199},{7,198},{8... | collective-permute-start | bytes 196616 | tf_op jit(solution)/shard_map/ppermute | solution.py:324
  65.9 5.3 %collective-permute-start.22 = (f32[128,128]{1,0:T(8,128)S(1)}, f32[128,128]{1,0:T(8,128)S(1)}, u32[]{:S(2)}, u32[]{:S(2)}) collective-permute-start(f32[128,128]{1,0:T(8,128)S(1)} %finished_piece.1), channel_id=1, source_target_pairs={{0,7},{1,6},{2,5},{3,4},{4,3},{5,2},{6,1},{7,0},{8,15},{9,14},{10,... | collective-permute-start | bytes 196616 | tf_op jit(solution)/shard_map/ppermute | solution.py:324
  68.0 5.8 %collective-permute-start.21 = (f32[128,128]{1,0:T(8,128)S(1)}, f32[128,128]{1,0:T(8,128)S(1)}, u32[]{:S(2)}, u32[]{:S(2)}) collective-permute-start(f32[128,128]{1,0:T(8,128)S(1)} %finished_piece.1), channel_id=1, source_target_pairs={{0,5},{1,4},{2,7},{3,6},{4,1},{5,0},{6,3},{7,2},{8,13},{9,12},{10,... | collective-permute-start | bytes 196616 | tf_op jit(solution)/shard_map/ppermute | solution.py:324
  68.5 5.3 %collective-permute-start.20 = (f32[128,128]{1,0:T(8,128)S(1)}, f32[128,128]{1,0:T(8,128)S(1)}, u32[]{:S(2)}, u32[]{:S(2)}) collective-permute-start(f32[128,128]{1,0:T(8,128)S(1)} %finished_piece.1), channel_id=1, source_target_pairs={{0,2},{1,3},{2,0},{3,1},{4,6},{5,7},{6,4},{7,5},{8,10},{9,11},{10,... | collective-permute-start | bytes 196616 | tf_op jit(solution)/shard_map/ppermute | solution.py:324
  73.8 1.9 %collective-permute-start.23 = (f32[4,128,128]{2,1,0:T(8,128)S(1)}, f32[4,128,128]{2,1,0:T(8,128)S(1)}, u32[]{:S(2)}, u32[]{:S(2)}) collective-permute-start(f32[4,128,128]{2,1,0:T(8,128)S(1)} %pad_maximum_fusion.pieces_ref), channel_id=1, source_target_pairs={{0,1},{1,0},{2,3},{3,2},{4,5},{5,4},{6,7},{7,6},{8,9},{9,8},{10,11... | collective-permute-start | bytes 786440 | tf_op jit(solution)/shard_map/ppermute | solution.py:324

commit v8 on v5

--- a/solution.py
+++ b/solution.py
@@ -57,55 +57,99 @@
     return jnp.concatenate([packed[:, RANK * i : RANK * (i + 1)] for i in range(4)], axis=0)
 
 
-def left_kernel(grads_hbm, errors_hbm, q_hbm, other_ref, own_ref, p_other_ref, p_own_ref, grads_ref, q_ref, grads_sem, errors_sem, q_sem):
+def left_terms(full, q):
+    q_hi, q_lo = split(q)
+    f_hi, f_lo = split(full)
+    wide = dot(f_hi, jnp.concatenate([q_hi, q_lo], axis=0), 1, 1)
+    return pack_rows(wide[:, :RANK] + wide[:, RANK:] + dot(f_lo, q_hi, 1, 1))
+
+
+def load_kernel(grads_hbm, errors_hbm, q_hbm, other_ref, p_ref, grads_ref, errors_ref, q_ref, other_grads_ref, other_q_ref, grads_sem, errors_sem, q_sem):
     core = lax.axis_index("c")
-    parts = ((1 - core, other_ref, p_other_ref), (core, own_ref, p_own_ref))
-    q_copy = pltpu.make_async_copy(q_hbm, q_ref, q_sem)
-    copies = [
-        (
-            pltpu.make_async_copy(grads_hbm.at[0, m], grads_ref.at[i], grads_sem.at[i]),
-            pltpu.make_async_copy(errors_hbm.at[0, m], full_ref, errors_sem.at[i]),
-        )
-        for i, (m, full_ref, _) in enumerate(parts)
-    ]
-    q_copy.start()
-    for pair in copies:
-        for copy in pair:
-            copy.start()
-    q_copy.wait()
-    for i, (m, full_ref, p_ref) in enumerate(parts):
-        q_hi, q_lo = split(q_ref[m])
-        both = jnp.concatenate([q_hi, q_lo], axis=0)
-        for copy in copies[i]:
-            copy.wait()
-        full = grads_ref[i].astype(F32) + full_ref[...]
-        full_ref[...] = full
-        f_hi, f_lo = split(full)
-        wide = dot(f_hi, both, 1, 1)
-        p_ref[...] = pack_rows(wide[:, :RANK] + wide[:, RANK:] + dot(f_lo, q_hi, 1, 1))
-
-
-def left_factors(grads, errors, q_prev):
+    copies = []
+    for i, (m, q, grads, errors) in enumerate(((1 - core, other_q_ref, other_grads_ref, other_ref), (core, q_ref, grads_ref, errors_ref))):
+        copies += [
+            pltpu.make_async_copy(q_hbm.at[m], q, q_sem.at[i]),
+            pltpu.make_async_copy(grads_hbm.at[0, m], grads, grads_sem.at[i]),
+            pltpu.make_async_copy(errors_hbm.at[0, m], errors, errors_sem.at[i]),
+        ]
+    for copy in copies:
+        copy.start()
+    for copy in copies[:3]:
+        copy.wait()
+    full = other_grads_ref[...].astype(F32) + other_ref[...]
+    other_ref[...] = full
+    p_ref[...] = left_terms(full, other_q_ref[...])
+    for copy in copies[3:]:
+        copy.wait()
+
+
+def load(grads, errors, q_prev):
     _, projections, rows, columns = grads.shape
-    full, p = pltpu.VMEM((rows, columns), F32), pltpu.VMEM((rows // 4, LANES), F32)
-    return pl.pallas_call(
-        left_kernel,
+    return pl.pallas_call(
+        load_kernel,
         in_specs=[AWAY] * 3,
-        out_specs=[WHOLE] * 4,
-        out_shape=[full, full, p, p],
+        out_specs=[WHOLE] * 5,
+        out_shape=[
+            pltpu.VMEM((rows, columns), F32),
+            pltpu.VMEM((rows // 4, LANES), F32),
+            pltpu.VMEM((rows, columns), BF16),
+            pltpu.VMEM((rows, columns), F32),
+            pltpu.VMEM(q_prev.shape[1:], F32),
+        ],
         scratch_shapes=[
-            pltpu.VMEM((projections, rows, columns), BF16),
-            pltpu.VMEM(q_prev.shape, F32),
+            pltpu.VMEM((rows, columns), BF16),
+            pltpu.VMEM(q_prev.shape[1:], F32),
             pltpu.SemaphoreType.DMA((projections,)),
             pltpu.SemaphoreType.DMA((projections,)),
-            pltpu.SemaphoreType.DMA,
+            pltpu.SemaphoreType.DMA((projections,)),
         ],
         compiler_params=PARAMS,
-        name="left_factors",
+        name="load",
     )(in_hbm(grads), in_hbm(errors), in_hbm(q_prev))
 
 
-def right_kernel(replicas, p_ref, own_ref, gift_ref, out_ref):
+def left_kernel(grads_ref, errors_ref, q_ref, full_ref, p_ref):
+    full = grads_ref[...].astype(F32) + errors_ref[...]
+    full_ref[...] = full
+    p_ref[...] = left_terms(full, q_ref[...])
+
+
+def left_own(grads, errors, q):
+    rows, columns = grads.shape
+    return pl.pallas_call(
+        left_kernel,
+        in_specs=[WHOLE] * 3,
+        out_specs=[WHOLE] * 2,
+        out_shape=[pltpu.VMEM((rows, columns), F32), pltpu.VMEM((rows // 4, LANES), F32)],
+        compiler_params=PARAMS,
+        cost_estimate=pl.CostEstimate(flops=100_000_000, bytes_accessed=3_000_000, transcendentals=0),
+        name="left_own",
+    )(grads, errors, q)
+
+
+def halves_kernel(own_ref, gift_ref, hi_ref, lo_ref):
+    rows = own_ref.shape[0]
+    for i, ref in enumerate((own_ref, gift_ref)):
+        hi, lo = split(ref[...])
+        hi_ref[rows * i : rows * (i + 1)] = hi
+        lo_ref[rows * i : rows * (i + 1)] = lo
+
+
+def halves(own, gift):
+    both = pltpu.VMEM((2 * own.shape[0], own.shape[1]), BF16)
+    return pl.pallas_call(
+        halves_kernel,
+        in_specs=[WHOLE] * 2,
+        out_specs=[WHOLE] * 2,
+        out_shape=[both, both],
+        compiler_params=PARAMS,
+        cost_estimate=pl.CostEstimate(flops=4_000_000, bytes_accessed=3_000_000, transcendentals=0),
+        name="halves",
+    )(own, gift)
+
+
+def right_kernel(replicas, p_ref, hi_ref, lo_ref, out_ref):
     slots, height, _ = out_ref.shape
     tiles = (height - 8) // RANK
     width = tiles * LANES
@@ -118,16 +162,15 @@
     gram = pack(dot(p, p, 1, 1, lax.Precision.HIGHEST))
     for slot in range(slots):
         here = pl.ds(pl.multiple_of((x ^ slot) * width, width), width)
-        f_hi, f_lo = split(jnp.concatenate([own_ref[:, here], gift_ref[:, here]], axis=0))
-        wide = dot(both, f_hi, 1, 0)
-        q = wide[:RANK] + wide[RANK:] + dot(p_hi, f_lo, 1, 0)
+        wide = dot(both, hi_ref[:, here], 1, 0)
+        q = wide[:RANK] + wide[RANK:] + dot(p_hi, lo_ref[:, here], 1, 0)
         for j in range(tiles):
             out_ref[slot, j * RANK : (j + 1) * RANK, :] = q[:, j * LANES : (j + 1) * LANES]
         out_ref[slot, tiles * RANK :, :] = gram
 
 
-def right_terms(p_sum, own, gift, replicas, slots):
-    height = own.shape[1] // slots // LANES * RANK + 8
+def right_terms(p_sum, hi, lo, replicas, slots):
+    height = hi.shape[1] // slots // LANES * RANK + 8
     return pl.pallas_call(
         functools.partial(right_kernel, replicas),
         in_specs=[WHOLE] * 3,
@@ -135,7 +178,7 @@
         out_shape=jax.ShapeDtypeStruct((slots, height, LANES), F32),
         compiler_params=PARAMS,
         name="right_terms",
-    )(p_sum, own, gift)
+    )(p_sum, hi, lo)
 
 
 def factor_kernel(sum_ref, out_ref):
@@ -312,15 +355,17 @@
 
 def shards(grads, errors, q_prev, moment1, moment2):
     replicas, slots = lax.axis_size(("z", "y")), lax.axis_size("x")
-    other_full, own_full, p_other, p_own = left_factors(grads, errors, q_prev)
+    other_full, p_other, own_grads, own_errors, own_q = load(grads, errors, q_prev)
+    own_full, p_own = left_own(own_grads, own_errors, own_q)
     p = jnp.concatenate([p_own, swap(p_other, "c", 1)])
-    p, other_full = lax.optimization_barrier((p, other_full))
-    gift = swap(other_full, "c", 1)
+    p, gift = lax.optimization_barrier((p, other_full))
+    gift = swap(gift, "c", 1)
     p = four([p] * 4, "y")
     p = four([p] * 4, "z")
-    p = p + swap(p, "z", 6)
-
-    terms = right_terms(p, own_full, gift, replicas, slots)
+    far, hi, lo = lax.optimization_barrier((swap(p, "z", 6), *halves(own_full, gift)))
+    p = p + far
+
+    terms = right_terms(p, hi, lo, replicas, slots)
     total = four([terms[i] for i in range(slots)], "x")
     inverse = inverse_factor(total)
     q = four([total[:-8]] * 4, "y")

time: 75.3 us -> 74.4 us (0.988)
  waiting for transfers between devices: 19 us -> 17.4 us
    ppermute x24, waiting for transfers between devices: 19 us -> 17.4 us  [swap(): lax.ppermute(value, axis, [(i, i ^ bit) for i in range(lax.axis_size(axis...]
    pallas_call x1 -> x3, Pallas kernels: 3.64 us -> 4.16 us  [the longest x1 2.84 us: load(): pl.pallas_call(load_kernel, in_specs=[AWAY] * 3, out_specs=[WHOLE] * 5, o...]
  transfers between devices with their start and end apart: 24 -> 24, of which waited for: 14 -> 13; matrix products, arithmetic and copies ran while one was open for 0% -> 0% of each run, Pallas kernels for 7% -> 9%
where the time goes in v8:
time: 74.4 us
  starting transfers between devices  43.6 us (59%)
  waiting for transfers between devices  17.4 us (23%)
  Pallas kernels  12.4 us (17%)
  between operations  0.9 us (1%)
    ppermute x24, starting transfers between devices, swap(): lax.ppermute(value, axis, [(i, i ^ bit) for i in range(lax.axis_size(axis...  43.6 us
    ppermute x24, waiting for transfers between devices, swap(): lax.ppermute(value, axis, [(i, i ^ bit) for i in range(lax.axis_size(axis...  17.4 us
    pallas_call x2, Pallas kernels, update(): pl.pallas_call(functools.partial(update_kernel, mine), in_specs=[WHOLE] *...  3.29 us
    pallas_call x1, Pallas kernels, inverse_factor(): pl.pallas_call(factor_kernel, in_specs=[WHOLE], out_specs=WHOLE, out_shap...  2.85 us
    pallas_call x1, Pallas kernels, load(): pl.pallas_call(load_kernel, in_specs=[AWAY] * 3, out_specs=[WHOLE] * 5, o...  2.84 us
  transfers between devices with their start and end apart: 24, of which 13 were waited for; matrix products, arithmetic and copies ran while one was open for 0% of the time, Pallas kernels for 9%

profile of v8, /device:TPU:1, one launch (start us, length us, event | category | flops | bytes accessed | tf_op | source)
XLA Modules:
  0.0 74.4 jit_solution(2408996641089026549)
XLA Ops:
  0.6 2.8 %load.1 = (f32[224,2048]{1,0:T(8,128)S(1)}, f32[56,128]{1,0:T(8,128)S(1)}, bf16[224,2048]{1,0:T(8,128)(2,1)S(1)}, f32[224,2048]{1,0:T(8,128)S(1)}, f32[32,2048]{1,0:T(8,128)S(1)}) custom-call(bf16[1,2,224,2048]{3,2,1,0:T(8,128)(2,1)} %grads_hbm.1, f32[1,2,224,2048]{3,2,1,0:T(8,128)} %errors_hbm.1, f32[2,32,2048]{2,1,0:T(8,128)} %q_hbm.1), custom_call_target="tpu_custom_call" | custom-call | tf_op jit(solution)/shard_map/load/pallas_call | solution.py:89
  3.5 3.3 %collective-permute-start = (f32[56,128]{1,0:T(8,128)S(1)}, f32[56,128]{1,0:T(8,128)S(1)}, u32[]{:S(2)}, u32[]{:S(2)}) collective-permute-start(f32[56,128]{1,0:T(8,128)S(1)} %get-tuple-element.40), channel_id=1, source_target_pairs={{0,1},{1,0},{2,3},{3,2},{4,5},{5,4},{6,7},{7,6},{8,9},{9,8},{10,11... | collective-permute-start | bytes 86024 | tf_op jit(solution)/shard_map/ppermute | solution.py:349
  6.8 0.8 %left_own.1 = (f32[224,2048]{1,0:T(8,128)S(1)}, f32[56,128]{1,0:T(8,128)S(1)}) custom-call(bf16[224,2048]{1,0:T(8,128)(2,1)S(1)} %get-tuple-element.36.grads_ref, f32[224,2048]{1,0:T(8,128)S(1)} %get-tuple-element.37.errors_ref, f32[32,2048]{1,0:T(8,128)S(1)} %get-tuple-element.38.q_ref), custom_call_target="tpu_custom_call" | custom-call | flops 100000000 | bytes 3000000 | tf_op jit(solution)/shard_map/left_own/pallas_call | solution.py:120
  8.0 1.0 %collective-permute-start.3 = (f32[112,128]{1,0:T(8,128)S(1)}, f32[112,128]{1,0:T(8,128)S(1)}, u32[]{:S(2)}, u32[]{:S(2)}) collective-permute-start(f32[112,128]{1,0:T(8,128)S(1)} %pad_maximum_fusion.1), channel_id=1, source_target_pairs={{0,24},{8,16},{16,8},{24,0},{1,25},{9,17},{17,9},{25,1},{2,26},{10... | collective-permute-start | bytes 172040 | tf_op jit(solution)/shard_map/ppermute | solution.py:349
  9.4 1.9 %collective-permute-start.1 = (f32[112,128]{1,0:T(8,128)S(1)}, f32[112,128]{1,0:T(8,128)S(1)}, u32[]{:S(2)}, u32[]{:S(2)}) collective-permute-start(f32[112,128]{1,0:T(8,128)S(1)} %pad_maximum_fusion.1), channel_id=1, source_target_pairs={{0,8},{8,0},{16,24},{24,16},{1,9},{9,1},{17,25},{25,17},{2,10},{10... | collective-permute-start | bytes 172040 | tf_op jit(solution)/shard_map/ppermute | solution.py:349
  11.3 1.0 %collective-permute-done.3 = f32[112,128]{1,0:T(8,128)S(1)} collective-permute-done((f32[112,128]{1,0:T(8,128)S(1)}, f32[112,128]{1,0:T(8,128)S(1)}, u32[]{:S(2)}, u32[]{:S(2)}) %collective-permute-start.3) | collective-permute-done | bytes 57376 | tf_op jit(solution)/shard_map/ppermute | solution.py:349
  12.3 1.3 %collective-permute-done.2 = f32[112,128]{1,0:T(8,128)S(1)} collective-permute-done((f32[112,128]{1,0:T(8,128)S(1)}, f32[112,128]{1,0:T(8,128)S(1)}, u32[]{:S(2)}, u32[]{:S(2)}) %collective-permute-start.2) | collective-permute-done | bytes 57376 | tf_op jit(solution)/shard_map/ppermute | solution.py:349
  13.7 4.3 %collective-permute-start.6 = (f32[112,128]{1,0:T(8,128)S(1)}, f32[112,128]{1,0:T(8,128)S(1)}, u32[]{:S(2)}, u32[]{:S(2)}) collective-permute-start(f32[112,128]{1,0:T(8,128)S(1)} %add_add_fusion.3), channel_id=1, source_target_pairs={{0,96},{32,64},{64,32},{96,0},{128,224},{160,192},{192,160},{224,1... | collective-permute-start | bytes 172040 | tf_op jit(solution)/shard_map/ppermute | solution.py:349
  18.4 1.2 %collective-permute-done.6 = f32[112,128]{1,0:T(8,128)S(1)} collective-permute-done((f32[112,128]{1,0:T(8,128)S(1)}, f32[112,128]{1,0:T(8,128)S(1)}, u32[]{:S(2)}, u32[]{:S(2)}) %collective-permute-start.6) | collective-permute-done | bytes 57376 | tf_op jit(solution)/shard_map/ppermute | solution.py:349
  19.6 2.7 %collective-permute-done.5 = f32[112,128]{1,0:T(8,128)S(1)} collective-permute-done((f32[112,128]{1,0:T(8,128)S(1)}, f32[112,128]{1,0:T(8,128)S(1)}, u32[]{:S(2)}, u32[]{:S(2)}) %collective-permute-start.5) | collective-permute-done | bytes 57376 | tf_op jit(solution)/shard_map/ppermute | solution.py:349
  22.3 3.9 %collective-permute-start.7 = (f32[112,128]{1,0:T(8,128)S(1)}, f32[112,128]{1,0:T(8,128)S(1)}, u32[]{:S(2)}, u32[]{:S(2)}) collective-permute-start(f32[112,128]{1,0:T(8,128)S(1)} %add_add_fusion.2), channel_id=1, source_target_pairs={{0,192},{32,224},{64,128},{96,160},{128,64},{160,96},{192,0},{224,... | collective-permute-start | bytes 172040 | tf_op jit(solution)/shard_map/ppermute | solution.py:349
  26.7 1.6 %collective-permute-done.7 = f32[112,128]{1,0:T(8,128)S(1)} collective-permute-done((f32[112,128]{1,0:T(8,128)S(1)}, f32[112,128]{1,0:T(8,128)S(1)}, u32[]{:S(2)}, u32[]{:S(2)}) %collective-permute-start.7) | collective-permute-done | bytes 57376 | tf_op jit(solution)/shard_map/ppermute | solution.py:349
  28.2 0.9 %right_terms.1 = f32[4,136,128]{2,1,0:T(8,128)S(1)} custom-call(f32[112,128]{1,0:T(8,128)S(1)} %add.54.p_ref, bf16[448,2048]{1,0:T(8,128)(2,1)S(1)} %get-tuple-element.48.hi_ref, bf16[448,2048]{1,0:T(8,128)(2,1)S(1)} %get-tuple-element.49.lo_ref), custom_call_target="tpu_custom_call" | custom-call | tf_op jit(solution)/shard_map/right_terms/pallas_call | solution.py:174
  29.2 2.6 %collective-permute-start.11 = (f32[136,128]{1,0:T(8,128)S(1)}, f32[136,128]{1,0:T(8,128)S(1)}, u32[]{:S(2)}, u32[]{:S(2)}) collective-permute-start(f32[136,128]{1,0:T(8,128)S(1)} %get-tuple-element.67), channel_id=1, source_target_pairs={{0,6},{2,4},{4,2},{6,0},{1,7},{3,5},{5,3},{7,1},{8,14},{10,12},{12... | collective-permute-start | bytes 208904 | tf_op jit(solution)/shard_map/ppermute | solution.py:349
  32.5 1.1 %collective-permute-done.11 = f32[136,128]{1,0:T(8,128)S(1)} collective-permute-done((f32[136,128]{1,0:T(8,128)S(1)}, f32[136,128]{1,0:T(8,128)S(1)}, u32[]{:S(2)}, u32[]{:S(2)}) %collective-permute-start.11) | collective-permute-done | bytes 69664 | tf_op jit(solution)/shard_map/ppermute | solution.py:349
  33.7 2.8 %collective-permute-done.10 = f32[136,128]{1,0:T(8,128)S(1)} collective-permute-done((f32[136,128]{1,0:T(8,128)S(1)}, f32[136,128]{1,0:T(8,128)S(1)}, u32[]{:S(2)}, u32[]{:S(2)}) %collective-permute-start.10) | collective-permute-done | bytes 69664 | tf_op jit(solution)/shard_map/ppermute | solution.py:349
  36.5 2.0 %collective-permute-start.13 = (f32[128,128]{1,0:T(8,128)S(1)}, f32[128,128]{1,0:T(8,128)S(1)}, u32[]{:S(2)}, u32[]{:S(2)}) collective-permute-start(f32[128,128]{1,0:T(8,128)S(1)} %slice.24), channel_id=1, source_target_pairs={{0,16},{8,24},{16,0},{24,8},{1,17},{9,25},{17,1},{25,9},{2,18},{10... | collective-permute-start | bytes 196616 | tf_op jit(solution)/shard_map/ppermute | solution.py:349
  39.2 2.8 %inverse_factor.1.inverse_ref = f32[8,128]{1,0:T(8,128)S(1)} custom-call(f32[136,128]{1,0:T(8,128)S(1)} %fusion.1.sum_ref), custom_call_target="tpu_custom_call" | custom-call | flops 4000000 | bytes 4000000 | tf_op jit(solution)/shard_map/inverse_factor/pallas_call | solution.py:203
  42.0 0.7 collective-permute-done.14
  42.8 1.7 %collective-permute-start.17 = (f32[128,128]{1,0:T(8,128)S(1)}, f32[128,128]{1,0:T(8,128)S(1)}, u32[]{:S(2)}, u32[]{:S(2)}) collective-permute-start(f32[128,128]{1,0:T(8,128)S(1)} %add_add_fusion.1), channel_id=1, source_target_pairs={{0,96},{32,64},{64,32},{96,0},{128,224},{160,192},{192,160},{224,1... | collective-permute-start | bytes 196616 | tf_op jit(solution)/shard_map/ppermute | solution.py:349
  44.5 1.8 %collective-permute-start.16 = (f32[128,128]{1,0:T(8,128)S(1)}, f32[128,128]{1,0:T(8,128)S(1)}, u32[]{:S(2)}, u32[]{:S(2)}) collective-permute-start(f32[128,128]{1,0:T(8,128)S(1)} %add_add_fusion.1), channel_id=1, source_target_pairs={{0,64},{32,96},{64,0},{96,32},{128,192},{160,224},{192,128},{224,1... | collective-permute-start | bytes 196616 | tf_op jit(solution)/shard_map/ppermute | solution.py:349
  46.9 7.2 %collective-permute-start.18 = (f32[56,128]{1,0:T(8,128)S(1)}, f32[56,128]{1,0:T(8,128)S(1)}, u32[]{:S(2)}, u32[]{:S(2)}) collective-permute-start(f32[56,128]{1,0:T(8,128)S(1)} %get-tuple-element.53), channel_id=1, source_target_pairs={{0,1},{1,0},{2,3},{3,2},{4,5},{5,4},{6,7},{7,6},{8,9},{9,8},{10,11... | collective-permute-start | bytes 86024 | tf_op jit(solution)/shard_map/ppermute | solution.py:349
  54.1 0.8 %collective-permute-done.18.other_ref = f32[56,128]{1,0:T(8,128)S(1)} collective-permute-done((f32[56,128]{1,0:T(8,128)S(1)}, f32[56,128]{1,0:T(8,128)S(1)}, u32[]{:S(2)}, u32[]{:S(2)}) %collective-permute-start.18) | collective-permute-done | bytes 28704 | tf_op jit(solution)/shard_map/ppermute | solution.py:349
  54.9 3.4 %collective-permute-start.19 = (f32[128,128]{1,0:T(8,128)S(1)}, f32[128,128]{1,0:T(8,128)S(1)}, u32[]{:S(2)}, u32[]{:S(2)}) collective-permute-start(f32[128,128]{1,0:T(8,128)S(1)} %add_add_fusion.a_ref), channel_id=1, source_target_pairs={{0,192},{32,224},{64,128},{96,160},{128,64},{160,96},{192,0},{224,... | collective-permute-start | bytes 196616 | tf_op jit(solution)/shard_map/ppermute | solution.py:349
  58.8 1.5 %collective-permute-done.19.b_ref = f32[128,128]{1,0:T(8,128)S(1)} collective-permute-done((f32[128,128]{1,0:T(8,128)S(1)}, f32[128,128]{1,0:T(8,128)S(1)}, u32[]{:S(2)}, u32[]{:S(2)}) %collective-permute-start.19) | collective-permute-done | bytes 65568 | tf_op jit(solution)/shard_map/ppermute | solution.py:349
  60.5 1.1 %collective-permute-start.22 = (f32[128,128]{1,0:T(8,128)S(1)}, f32[128,128]{1,0:T(8,128)S(1)}, u32[]{:S(2)}, u32[]{:S(2)}) collective-permute-start(f32[128,128]{1,0:T(8,128)S(1)} %finished_piece.1), channel_id=1, source_target_pairs={{0,6},{2,4},{4,2},{6,0},{1,7},{3,5},{5,3},{7,1},{8,14},{10,12},{12... | collective-permute-start | bytes 196616 | tf_op jit(solution)/shard_map/ppermute | solution.py:349
  62.4 1.4 %collective-permute-start.20 = (f32[128,128]{1,0:T(8,128)S(1)}, f32[128,128]{1,0:T(8,128)S(1)}, u32[]{:S(2)}, u32[]{:S(2)}) collective-permute-start(f32[128,128]{1,0:T(8,128)S(1)} %finished_piece.1), channel_id=1, source_target_pairs={{0,2},{2,0},{4,6},{6,4},{1,3},{3,1},{5,7},{7,5},{8,10},{10,8},{12,... | collective-permute-start | bytes 196616 | tf_op jit(solution)/shard_map/ppermute | solution.py:349
  63.8 1.1 %collective-permute-done.22 = f32[128,128]{1,0:T(8,128)S(1)} collective-permute-done((f32[128,128]{1,0:T(8,128)S(1)}, f32[128,128]{1,0:T(8,128)S(1)}, u32[]{:S(2)}, u32[]{:S(2)}) %collective-permute-start.22) | collective-permute-done | bytes 65568 | tf_op jit(solution)/shard_map/ppermute | solution.py:349
  64.9 1.4 %collective-permute-done.21 = f32[128,128]{1,0:T(8,128)S(1)} collective-permute-done((f32[128,128]{1,0:T(8,128)S(1)}, f32[128,128]{1,0:T(8,128)S(1)}, u32[]{:S(2)}, u32[]{:S(2)}) %collective-permute-start.21) | collective-permute-done | bytes 65568 | tf_op jit(solution)/shard_map/ppermute | solution.py:349
  66.3 4.6 %collective-permute-start.23 = (f32[4,128,128]{2,1,0:T(8,128)S(1)}, f32[4,128,128]{2,1,0:T(8,128)S(1)}, u32[]{:S(2)}, u32[]{:S(2)}) collective-permute-start(f32[4,128,128]{2,1,0:T(8,128)S(1)} %pad_maximum_fusion.pieces_ref), channel_id=1, source_target_pairs={{0,1},{1,0},{2,3},{3,2},{4,5},{5,4},{6,7},{7,6},{8,9},{9,8},{10,11... | collective-permute-start | bytes 786440 | tf_op jit(solution)/shard_map/ppermute | solution.py:349
  70.9 1.6 %update_own.1 = (f32[1,2,224,2048]{3,2,1,0:T(8,128)}, f32[2,112,128]{2,1,0:T(8,128)}, f32[2,112,128]{2,1,0:T(8,128)}, bf16[2,112,128]{2,1,0:T(8,128)(2,1)}, f32[2,32,2048]{2,1,0:T(8,128)}) custom-call(f32[4,128,128]{2,1,0:T(8,128)S(1)} %pad_maximum_fusion.pieces_ref, bf16[2,224,96]{2,1,0:T(8,128)(2,1)S(1)} %get-tuple-element.60.hat_ref, ...), custom_call_target="tpu_custom_call" | custom-call | flops 100000000 | bytes 4000000 | tf_op jit(solution)/shard_map/update_own/pallas_call | solution.py:319
  72.6 1.7 %update_other.1 = (f32[1,2,224,2048]{3,2,1,0:T(8,128)}, f32[2,112,128]{2,1,0:T(8,128)}, f32[2,112,128]{2,1,0:T(8,128)}, bf16[2,112,128]{2,1,0:T(8,128)(2,1)}, f32[2,32,2048]{2,1,0:T(8,128)}) custom-call(f32[4,128,128]{2,1,0:T(8,128)S(1)} %collective-permute-done.23.pieces_ref, ...), custom_call_target="tpu_custom_call", output_to_operand_aliasing={{0}: (6, {}), {1}: (7, {}), {2}: (8, {}), {3}: (9, {}), {4}... | custom-call | flops 100000000 | bytes 4000000 | tf_op jit(solution)/shard_map/update_other/pallas_call | solution.py:319
  (40 shorter events, 5.5 us)
Async XLA Ops:
  3.5 4.2 %collective-permute-start = (f32[56,128]{1,0:T(8,128)S(1)}, f32[56,128]{1,0:T(8,128)S(1)}, u32[]{:S(2)}, u32[]{:S(2)}) collective-permute-start(f32[56,128]{1,0:T(8,128)S(1)} %get-tuple-element.40), channel_id=1, source_target_pairs={{0,1},{1,0},{2,3},{3,2},{4,5},{5,4},{6,7},{7,6},{8,9},{9,8},{10,11... | collective-permute-start | bytes 86024 | tf_op jit(solution)/shard_map/ppermute | solution.py:349
  7.7 18.5 %collective-permute-start.8 = (f32[224,2048]{1,0:T(8,128)S(1)}, f32[224,2048]{1,0:T(8,128)S(1)}, u32[]{:S(2)}, u32[]{:S(2)}) collective-permute-start(f32[224,2048]{1,0:T(8,128)S(1)} %get-tuple-element.44.full_ref), channel_id=1, source_target_pairs={{0,1},{1,0},{2,3},{3,2},{4,5},{5,4},{6,7},{7,6},{8,9},{9,8},{10,11... | collective-permute-start | bytes 5505032 | tf_op jit(solution)/shard_map/ppermute | solution.py:349
  8.0 4.2 %collective-permute-start.3 = (f32[112,128]{1,0:T(8,128)S(1)}, f32[112,128]{1,0:T(8,128)S(1)}, u32[]{:S(2)}, u32[]{:S(2)}) collective-permute-start(f32[112,128]{1,0:T(8,128)S(1)} %pad_maximum_fusion.1), channel_id=1, source_target_pairs={{0,24},{8,16},{16,8},{24,0},{1,25},{9,17},{17,9},{25,1},{2,26},{10... | collective-permute-start | bytes 172040 | tf_op jit(solution)/shard_map/ppermute | solution.py:349
  9.0 4.5 %collective-permute-start.2 = (f32[112,128]{1,0:T(8,128)S(1)}, f32[112,128]{1,0:T(8,128)S(1)}, u32[]{:S(2)}, u32[]{:S(2)}) collective-permute-start(f32[112,128]{1,0:T(8,128)S(1)} %pad_maximum_fusion.1), channel_id=1, source_target_pairs={{0,16},{8,24},{16,0},{24,8},{1,17},{9,25},{17,1},{25,9},{2,18},{10... | collective-permute-start | bytes 172040 | tf_op jit(solution)/shard_map/ppermute | solution.py:349
  9.4 4.3 %collective-permute-start.1 = (f32[112,128]{1,0:T(8,128)S(1)}, f32[112,128]{1,0:T(8,128)S(1)}, u32[]{:S(2)}, u32[]{:S(2)}) collective-permute-start(f32[112,128]{1,0:T(8,128)S(1)} %pad_maximum_fusion.1), channel_id=1, source_target_pairs={{0,8},{8,0},{16,24},{24,16},{1,9},{9,1},{17,25},{25,17},{2,10},{10... | collective-permute-start | bytes 172040 | tf_op jit(solution)/shard_map/ppermute | solution.py:349
  13.7 5.8 %collective-permute-start.6 = (f32[112,128]{1,0:T(8,128)S(1)}, f32[112,128]{1,0:T(8,128)S(1)}, u32[]{:S(2)}, u32[]{:S(2)}) collective-permute-start(f32[112,128]{1,0:T(8,128)S(1)} %add_add_fusion.3), channel_id=1, source_target_pairs={{0,96},{32,64},{64,32},{96,0},{128,224},{160,192},{192,160},{224,1... | collective-permute-start | bytes 172040 | tf_op jit(solution)/shard_map/ppermute | solution.py:349
  18.0 4.3 %collective-permute-start.5 = (f32[112,128]{1,0:T(8,128)S(1)}, f32[112,128]{1,0:T(8,128)S(1)}, u32[]{:S(2)}, u32[]{:S(2)}) collective-permute-start(f32[112,128]{1,0:T(8,128)S(1)} %add_add_fusion.3), channel_id=1, source_target_pairs={{0,64},{32,96},{64,0},{96,32},{128,192},{160,224},{192,128},{224,1... | collective-permute-start | bytes 172040 | tf_op jit(solution)/shard_map/ppermute | solution.py:349
  18.0 4.3 %collective-permute-start.4 = (f32[112,128]{1,0:T(8,128)S(1)}, f32[112,128]{1,0:T(8,128)S(1)}, u32[]{:S(2)}, u32[]{:S(2)}) collective-permute-start(f32[112,128]{1,0:T(8,128)S(1)} %add_add_fusion.3), channel_id=1, source_target_pairs={{0,32},{32,0},{64,96},{96,64},{128,160},{160,128},{192,224},{224,1... | collective-permute-start | bytes 172040 | tf_op jit(solution)/shard_map/ppermute | solution.py:349
  22.3 5.9 %collective-permute-start.7 = (f32[112,128]{1,0:T(8,128)S(1)}, f32[112,128]{1,0:T(8,128)S(1)}, u32[]{:S(2)}, u32[]{:S(2)}) collective-permute-start(f32[112,128]{1,0:T(8,128)S(1)} %add_add_fusion.2), channel_id=1, source_target_pairs={{0,192},{32,224},{64,128},{96,160},{128,64},{160,96},{192,0},{224,... | collective-permute-start | bytes 172040 | tf_op jit(solution)/shard_map/ppermute | solution.py:349
  29.2 41.7 %copy-start = (f32[2,112,128]{2,1,0:T(8,128)S(1)}, f32[2,112,128]{2,1,0:T(8,128)}, u32[]{:S(2)}) copy-start(f32[2,112,128]{2,1,0:T(8,128)} %m1_ref.3) | copy-start | bytes 344068
  29.2 41.7 %copy-start.1 = (f32[2,112,128]{2,1,0:T(8,128)S(1)}, f32[2,112,128]{2,1,0:T(8,128)}, u32[]{:S(2)}) copy-start(f32[2,112,128]{2,1,0:T(8,128)} %m2_ref.3) | copy-start | bytes 344068
  29.2 4.5 %collective-permute-start.11 = (f32[136,128]{1,0:T(8,128)S(1)}, f32[136,128]{1,0:T(8,128)S(1)}, u32[]{:S(2)}, u32[]{:S(2)}) collective-permute-start(f32[136,128]{1,0:T(8,128)S(1)} %get-tuple-element.67), channel_id=1, source_target_pairs={{0,6},{2,4},{4,2},{6,0},{1,7},{3,5},{5,3},{7,1},{8,14},{10,12},{12... | collective-permute-start | bytes 208904 | tf_op jit(solution)/shard_map/ppermute | solution.py:349
  31.8 4.7 %collective-permute-start.10 = (f32[136,128]{1,0:T(8,128)S(1)}, f32[136,128]{1,0:T(8,128)S(1)}, u32[]{:S(2)}, u32[]{:S(2)}) collective-permute-start(f32[136,128]{1,0:T(8,128)S(1)} %get-tuple-element.68), channel_id=1, source_target_pairs={{0,4},{2,6},{4,0},{6,2},{1,5},{3,7},{5,1},{7,3},{8,12},{10,14},{12... | collective-permute-start | bytes 208904 | tf_op jit(solution)/shard_map/ppermute | solution.py:349
  32.3 4.1 %collective-permute-start.9 = (f32[136,128]{1,0:T(8,128)S(1)}, f32[136,128]{1,0:T(8,128)S(1)}, u32[]{:S(2)}, u32[]{:S(2)}) collective-permute-start(f32[136,128]{1,0:T(8,128)S(1)} %get-tuple-element.69), channel_id=1, source_target_pairs={{0,2},{2,0},{4,6},{6,4},{1,3},{3,1},{5,7},{7,5},{8,10},{10,8},{12,... | collective-permute-start | bytes 208904 | tf_op jit(solution)/shard_map/ppermute | solution.py:349
  36.5 5.6 %collective-permute-start.13 = (f32[128,128]{1,0:T(8,128)S(1)}, f32[128,128]{1,0:T(8,128)S(1)}, u32[]{:S(2)}, u32[]{:S(2)}) collective-permute-start(f32[128,128]{1,0:T(8,128)S(1)} %slice.24), channel_id=1, source_target_pairs={{0,16},{8,24},{16,0},{24,8},{1,17},{9,25},{17,1},{25,9},{2,18},{10... | collective-permute-start | bytes 196616 | tf_op jit(solution)/shard_map/ppermute | solution.py:349
  38.5 4.3 %collective-permute-start.14 = (f32[128,128]{1,0:T(8,128)S(1)}, f32[128,128]{1,0:T(8,128)S(1)}, u32[]{:S(2)}, u32[]{:S(2)}) collective-permute-start(f32[128,128]{1,0:T(8,128)S(1)} %slice.24), channel_id=1, source_target_pairs={{0,24},{8,16},{16,8},{24,0},{1,25},{9,17},{17,9},{25,1},{2,26},{10... | collective-permute-start | bytes 196616 | tf_op jit(solution)/shard_map/ppermute | solution.py:349
  38.9 3.8 %collective-permute-start.12 = (f32[128,128]{1,0:T(8,128)S(1)}, f32[128,128]{1,0:T(8,128)S(1)}, u32[]{:S(2)}, u32[]{:S(2)}) collective-permute-start(f32[128,128]{1,0:T(8,128)S(1)} %slice.24), channel_id=1, source_target_pairs={{0,8},{8,0},{16,24},{24,16},{1,9},{9,1},{17,25},{25,17},{2,10},{10... | collective-permute-start | bytes 196616 | tf_op jit(solution)/shard_map/ppermute | solution.py:349
  42.8 11.3 %collective-permute-start.17 = (f32[128,128]{1,0:T(8,128)S(1)}, f32[128,128]{1,0:T(8,128)S(1)}, u32[]{:S(2)}, u32[]{:S(2)}) collective-permute-start(f32[128,128]{1,0:T(8,128)S(1)} %add_add_fusion.1), channel_id=1, source_target_pairs={{0,96},{32,64},{64,32},{96,0},{128,224},{160,192},{192,160},{224,1... | collective-permute-start | bytes 196616 | tf_op jit(solution)/shard_map/ppermute | solution.py:349
  44.5 9.6 %collective-permute-start.16 = (f32[128,128]{1,0:T(8,128)S(1)}, f32[128,128]{1,0:T(8,128)S(1)}, u32[]{:S(2)}, u32[]{:S(2)}) collective-permute-start(f32[128,128]{1,0:T(8,128)S(1)} %add_add_fusion.1), channel_id=1, source_target_pairs={{0,64},{32,96},{64,0},{96,32},{128,192},{160,224},{192,128},{224,1... | collective-permute-start | bytes 196616 | tf_op jit(solution)/shard_map/ppermute | solution.py:349
  46.3 7.8 %collective-permute-start.15 = (f32[128,128]{1,0:T(8,128)S(1)}, f32[128,128]{1,0:T(8,128)S(1)}, u32[]{:S(2)}, u32[]{:S(2)}) collective-permute-start(f32[128,128]{1,0:T(8,128)S(1)} %add_add_fusion.1), channel_id=1, source_target_pairs={{0,32},{32,0},{64,96},{96,64},{128,160},{160,128},{192,224},{224,1... | collective-permute-start | bytes 196616 | tf_op jit(solution)/shard_map/ppermute | solution.py:349
  46.9 8.0 %collective-permute-start.18 = (f32[56,128]{1,0:T(8,128)S(1)}, f32[56,128]{1,0:T(8,128)S(1)}, u32[]{:S(2)}, u32[]{:S(2)}) collective-permute-start(f32[56,128]{1,0:T(8,128)S(1)} %get-tuple-element.53), channel_id=1, source_target_pairs={{0,1},{1,0},{2,3},{3,2},{4,5},{5,4},{6,7},{7,6},{8,9},{9,8},{10,11... | collective-permute-start | bytes 86024 | tf_op jit(solution)/shard_map/ppermute | solution.py:349
  54.9 5.3 %collective-permute-start.19 = (f32[128,128]{1,0:T(8,128)S(1)}, f32[128,128]{1,0:T(8,128)S(1)}, u32[]{:S(2)}, u32[]{:S(2)}) collective-permute-start(f32[128,128]{1,0:T(8,128)S(1)} %add_add_fusion.a_ref), channel_id=1, source_target_pairs={{0,192},{32,224},{64,128},{96,160},{128,64},{160,96},{192,0},{224,... | collective-permute-start | bytes 196616 | tf_op jit(solution)/shard_map/ppermute | solution.py:349
  60.5 4.3 %collective-permute-start.22 = (f32[128,128]{1,0:T(8,128)S(1)}, f32[128,128]{1,0:T(8,128)S(1)}, u32[]{:S(2)}, u32[]{:S(2)}) collective-permute-start(f32[128,128]{1,0:T(8,128)S(1)} %finished_piece.1), channel_id=1, source_target_pairs={{0,6},{2,4},{4,2},{6,0},{1,7},{3,5},{5,3},{7,1},{8,14},{10,12},{12... | collective-permute-start | bytes 196616 | tf_op jit(solution)/shard_map/ppermute | solution.py:349
  61.6 4.6 %collective-permute-start.21 = (f32[128,128]{1,0:T(8,128)S(1)}, f32[128,128]{1,0:T(8,128)S(1)}, u32[]{:S(2)}, u32[]{:S(2)}) collective-permute-start(f32[128,128]{1,0:T(8,128)S(1)} %finished_piece.1), channel_id=1, source_target_pairs={{0,4},{2,6},{4,0},{6,2},{1,5},{3,7},{5,1},{7,3},{8,12},{10,14},{12... | collective-permute-start | bytes 196616 | tf_op jit(solution)/shard_map/ppermute | solution.py:349
  62.4 3.9 %collective-permute-start.20 = (f32[128,128]{1,0:T(8,128)S(1)}, f32[128,128]{1,0:T(8,128)S(1)}, u32[]{:S(2)}, u32[]{:S(2)}) collective-permute-start(f32[128,128]{1,0:T(8,128)S(1)} %finished_piece.1), channel_id=1, source_target_pairs={{0,2},{2,0},{4,6},{6,4},{1,3},{3,1},{5,7},{7,5},{8,10},{10,8},{12,... | collective-permute-start | bytes 196616 | tf_op jit(solution)/shard_map/ppermute | solution.py:349
  66.3 6.3 %collective-permute-start.23 = (f32[4,128,128]{2,1,0:T(8,128)S(1)}, f32[4,128,128]{2,1,0:T(8,128)S(1)}, u32[]{:S(2)}, u32[]{:S(2)}) collective-permute-start(f32[4,128,128]{2,1,0:T(8,128)S(1)} %pad_maximum_fusion.pieces_ref), channel_id=1, source_target_pairs={{0,1},{1,0},{2,3},{3,2},{4,5},{5,4},{6,7},{7,6},{8,9},{9,8},{10,11... | collective-permute-start | bytes 786440 | tf_op jit(solution)/shard_map/ppermute | solution.py:349

commit v9 on v8

--- a/solution.py
+++ b/solution.py
@@ -276,73 +276,106 @@
     )(a, b, inverse)
 
 
-def update_kernel(mine, pieces_ref, hat_ref, rows_ref, full_ref, m1_ref, m2_ref, *refs):
-    err_hbm, n1_hbm, n2_hbm, up_hbm, q_hbm, err_ref, n1_ref, n2_ref, up_ref, q_ref, tile_ref, flat_ref, err_sem, sem = refs[-14:]
-    slots, height, _ = pieces_ref.shape
-    tiles = height // RANK
-    width = tiles * LANES
-    x, core = lax.axis_index("x"), lax.axis_index("c")
-    i, m = (0, core) if mine else (1, 1 - core)
+def update_kernel(counts, blocks, adam, *refs):
+    names = ("pieces", "hat", "rows", "full", "moments", "before", "out", "scratch")
+    groups = {}
+    for name, count in zip(names, counts, strict=True):
+        groups[name], refs = refs[:count], refs[count:]
+    (hat_ref,), (rows_ref,) = groups["hat"], groups["rows"]
+    err_hbm = groups["out"][0]
+    err_ref, err_sem = groups["scratch"][:2]
+    x, own = lax.axis_index("x"), lax.axis_index("c")
+    depth, width = err_ref.shape[1:]
+    tiles = width // LANES
+
+    def piece(array, index):
+        ref = groups["pieces"][array]
+        return jnp.concatenate([ref[index, j * RANK : (j + 1) * RANK, :] for j in range(tiles)], axis=1)
+
+    def place(slot):
+        return pl.ds(pl.multiple_of((x ^ slot) * width, width), width)
+
     copies = []
-    for slot in range(slots):
-        block = x ^ slot
-        here = pl.ds(pl.multiple_of(block * width, width), width)
-        q = jnp.concatenate([pieces_ref[slot, j * RANK : (j + 1) * RANK, :] for j in range(tiles)], axis=1)
-        right = right_three(q)
-        err_ref[slot] = full_ref[:, here] - dot(hat_ref[i], right, 1, 0)
-        copies.append(pltpu.make_async_copy(err_ref.at[slot], err_hbm.at[0, m, :, here], err_sem.at[slot]))
+
+    def send(here, there, sem):
+        copies.append(pltpu.make_async_copy(here, there, sem))
         copies[-1].start()
-        q_ref[:, here] = q
-        state = dot(rows_ref[i], right, 1, 0)
-        for j in range(tiles):
-            tile_ref[block * tiles + j] = state[:8, j * LANES : (j + 1) * LANES]
-    share = flat_ref.shape[0]
-    for j in range(slots * tiles):
-        flat_ref[:, j, :] = tile_ref[j, :share, :]
-    flat = flat_ref[...].reshape(share * slots * tiles, LANES)
-    n1 = 0.9 * m1_ref[m] + 0.1 * flat
-    n2 = 0.95 * m2_ref[m] + 0.05 * flat * flat
-    n1_ref[...] = n1
-    n2_ref[...] = n2
-    up_ref[...] = (n1 / (jnp.sqrt(n2) + 1e-08)).astype(BF16)
-    for k, (here, there) in enumerate(((n1_ref, n1_hbm), (n2_ref, n2_hbm), (up_ref, up_hbm), (q_ref, q_hbm))):
-        copies.append(pltpu.make_async_copy(here, there.at[m], sem.at[k]))
-        copies[-1].start()
+
+    for k, (i, slot, array, index) in enumerate(blocks):
+        right = right_three(piece(array, index))
+        err_ref[k] = groups["full"][i][:, place(slot)] - dot(hat_ref[i], right, 1, 0)
+        send(err_ref.at[k], err_hbm.at[0, (own + i) % 2, :, place(slot)], err_sem.at[k])
+    if adam is not None:
+        i, sources = adam
+        m = (own + i) % 2
+        m1_ref, m2_ref = groups["moments"]
+        n1_ref, n2_ref, up_ref, q_ref, tile_ref, flat_ref, sem = groups["scratch"][2:]
+        for slot, (array, index) in enumerate(sources):
+            q = piece(array, index)
+            q_ref[:, place(slot)] = q
+            state = dot(rows_ref[i], right_three(q), 1, 0)
+            for j in range(tiles):
+                tile_ref[(x ^ slot) * tiles + j] = state[:8, j * LANES : (j + 1) * LANES]
+        share, total = flat_ref.shape[:2]
+        for j in range(total):
+            flat_ref[:, j, :] = tile_ref[j, :share, :]
+        flat = flat_ref[...].reshape(share * total, LANES)
+        n1 = 0.9 * m1_ref[m] + 0.1 * flat
+        n2 = 0.95 * m2_ref[m] + 0.05 * flat * flat
+        n1_ref[...] = n1
+        n2_ref[...] = n2
+        up_ref[...] = (n1 / (jnp.sqrt(n2) + 1e-08)).astype(BF16)
+        for k, (here, there) in enumerate(zip((n1_ref, n2_ref, up_ref, q_ref), groups["out"][1:], strict=True)):
+            send(here, there.at[m], sem.at[k])
     for copy in copies:
         copy.wait()
 
 
-def update(pieces, hat, rows, full, moment1, moment2, mine, before=()):
-    depth, columns = full.shape
-    projections, slots = hat.shape[0], pieces.shape[0]
-    state, tiles = moment1.shape[1], columns // LANES
-    return pl.pallas_call(
-        functools.partial(update_kernel, mine),
-        in_specs=[WHOLE] * 6 + [AWAY] * len(before),
-        out_specs=[AWAY] * 5,
-        out_shape=[
-            pltpu.HBM((1, projections, depth, columns), F32),
-            pltpu.HBM(moment1.shape, F32),
-            pltpu.HBM(moment2.shape, F32),
-            pltpu.HBM(moment1.shape, BF16),
-            pltpu.HBM((projections, RANK, columns), F32),
-        ],
-        scratch_shapes=[
-            pltpu.VMEM((slots, depth, columns // slots), F32),
+def update(blocks, adam, hat, rows, fulls, moments, name, before=()):
+    arrays = []
+
+    def at(pieces):
+        for k, array in enumerate(arrays):
+            if array is pieces:
+                return k
+        arrays.append(pieces)
+        return len(arrays) - 1
+
+    blocks = tuple((i, slot, at(pieces), index) for i, slot, pieces, index in blocks)
+    if adam is not None:
+        adam = (adam[0], tuple((at(pieces), index) for pieces, index in adam[1]))
+    depth, columns = fulls[0].shape
+    state, tiles = moments[0].shape[1], columns // LANES
+    width = arrays[0].shape[1] // RANK * LANES
+    out = [pltpu.HBM((1, 2, depth, columns), F32)]
+    scratch = [pltpu.VMEM((len(blocks), depth, width), F32), pltpu.SemaphoreType.DMA((len(blocks),))]
+    if adam is None:
+        moments = ()
+    else:
+        shape = moments[0].shape
+        out += [pltpu.HBM(shape, F32), pltpu.HBM(shape, F32), pltpu.HBM(shape, BF16), pltpu.HBM((2, RANK, columns), F32)]
+        scratch += [
             pltpu.VMEM((state, LANES), F32),
             pltpu.VMEM((state, LANES), F32),
             pltpu.VMEM((state, LANES), BF16),
             pltpu.VMEM((RANK, columns), F32),
             pltpu.VMEM((tiles, 8, LANES), F32),
             pltpu.VMEM((state // tiles, tiles, LANES), F32),
-            pltpu.SemaphoreType.DMA((slots,)),
             pltpu.SemaphoreType.DMA((4,)),
-        ],
-        input_output_aliases={6 + k: k for k in range(len(before))},
-        compiler_params=PARAMS,
-        cost_estimate=pl.CostEstimate(flops=100_000_000, bytes_accessed=4_000_000, transcendentals=30_000),
-        name="update_own" if mine else "update_other",
-    )(pieces, hat, rows, full, moment1, moment2, *before)
+        ]
+    given = (*arrays, hat, rows, *fulls, *moments)
+    counts = (len(arrays), 1, 1, len(fulls), len(moments), len(before), len(out), len(scratch))
+    return pl.pallas_call(
+        functools.partial(update_kernel, counts, blocks, adam),
+        in_specs=[WHOLE] * len(given) + [AWAY] * len(before),
+        out_specs=[AWAY] * len(out),
+        out_shape=out,
+        scratch_shapes=scratch,
+        input_output_aliases={len(given) + k: k for k in range(len(before))},
+        compiler_params=PARAMS,
+        cost_estimate=pl.CostEstimate(flops=20_000_000 * len(blocks), bytes_accessed=1_000_000 * len(blocks), transcendentals=30_000),
+        name=name,
+    )(*given, *before)
 
 
 def swap(value, axis, bit):
@@ -377,10 +410,19 @@
     hat, rows = left_sides(hat_own, hat_gift, replicas)
     far, hat, rows = lax.optimization_barrier((swap(q, "z", 6), hat, rows))
     piece = finished_piece(q, far, inverse, replicas)
-    own = jnp.stack([piece] + [swap(piece, "x", i) for i in range(1, slots)])
-    other = swap(own, "c", 1)
-    done = update(own, hat, rows, own_full, moment1, moment2, True)
-    return tuple(update(other, hat, rows, other_full, moment1, moment2, False, done))
+    side = (hat, rows, (own_full, other_full), (moment1, moment2))
+    own0 = piece[None]
+    other0 = swap(own0, "c", 1)
+    own3, own2, own1 = (swap(own0, "x", i) for i in (3, 2, 1))
+    other3 = swap(own3, "c", 1)
+    err = update([(0, 0, own0, 0), (1, 0, other0, 0)], None, *side, "update_first")
+    err = update([(0, 3, own3, 0)], None, *side, "update_second", err)
+    own1, own2, other3, err = lax.optimization_barrier((own1, own2, other3, err))
+    last = swap(jnp.concatenate([own1, own2]), "c", 1)
+    sources = [(own0, 0), (own1, 0), (own2, 0), (own3, 0)]
+    done = update([(0, 1, own1, 0), (0, 2, own2, 0), (1, 3, other3, 0)], (0, sources), *side, "update_third", err)
+    sources = [(other0, 0), (last, 0), (last, 1), (other3, 0)]
+    return tuple(update([(1, 1, last, 0), (1, 2, last, 1)], (1, sources), *side, "update_fourth", done))
 
 
 def solution(mesh):

time: 74.4 us -> 74.7 us (level)
  waiting for transfers between devices: 17.4 us -> 14.9 us
  Pallas kernels: 12.4 us -> 14 us
  starting transfers between devices: 43.6 us -> 44.7 us
    ppermute x24 -> x26, waiting for transfers between devices: 17.4 us -> 14.9 us  [swap(): lax.ppermute(value, axis, [(i, i ^ bit) for i in range(lax.axis_size(axis...]
    pallas_call x2 -> x4, Pallas kernels: 3.29 us -> 4.92 us  [update(): pl.pallas_call(functools.partial(update_kernel, counts, blocks, adam), in...]
    ppermute x24 -> x26, starting transfers between devices: 43.6 us -> 44.7 us  [swap(): lax.ppermute(value, axis, [(i, i ^ bit) for i in range(lax.axis_size(axis...]
  transfers between devices with their start and end apart: 24 -> 26, of which waited for: 13 -> 11; matrix products, arithmetic and copies ran while one was open for 0% -> 0% of each run, Pallas kernels for 9% -> 12%
where the time goes in v9:
time: 74.7 us
  starting transfers between devices  44.7 us (60%)
  waiting for transfers between devices  14.9 us (20%)
  Pallas kernels  14 us (19%)
  between operations  0.96 us (1%)
    ppermute x26, starting transfers between devices, swap(): lax.ppermute(value, axis, [(i, i ^ bit) for i in range(lax.axis_size(axis...  44.7 us
    ppermute x26, waiting for transfers between devices, swap(): lax.ppermute(value, axis, [(i, i ^ bit) for i in range(lax.axis_size(axis...  14.9 us
    pallas_call x4, Pallas kernels, update(): pl.pallas_call(functools.partial(update_kernel, counts, blocks, adam), in...  4.92 us
    pallas_call x1, Pallas kernels, inverse_factor(): pl.pallas_call(factor_kernel, in_specs=[WHOLE], out_specs=WHOLE, out_shap...  2.85 us
    pallas_call x1, Pallas kernels, load(): pl.pallas_call(load_kernel, in_specs=[AWAY] * 3, out_specs=[WHOLE] * 5, o...  2.84 us
  transfers between devices with their start and end apart: 26, of which 11 were waited for; matrix products, arithmetic and copies ran while one was open for 0% of the time, Pallas kernels for 12%

profile of v9, /device:TPU:1, one launch (start us, length us, event | category | flops | bytes accessed | tf_op | source)
XLA Modules:
  0.0 74.7 jit_solution(17733721046413047238)
XLA Ops:
  0.6 2.8 %load.1 = (f32[224,2048]{1,0:T(8,128)S(1)}, f32[56,128]{1,0:T(8,128)S(1)}, bf16[224,2048]{1,0:T(8,128)(2,1)S(1)}, f32[224,2048]{1,0:T(8,128)S(1)}, f32[32,2048]{1,0:T(8,128)S(1)}) custom-call(bf16[1,2,224,2048]{3,2,1,0:T(8,128)(2,1)} %grads_hbm.1, f32[1,2,224,2048]{3,2,1,0:T(8,128)} %errors_hbm.1, f32[2,32,2048]{2,1,0:T(8,128)} %q_hbm.1), custom_call_target="tpu_custom_call" | custom-call | tf_op jit(solution)/shard_map/load/pallas_call | solution.py:89
  3.5 3.3 %collective-permute-start = (f32[56,128]{1,0:T(8,128)S(1)}, f32[56,128]{1,0:T(8,128)S(1)}, u32[]{:S(2)}, u32[]{:S(2)}) collective-permute-start(f32[56,128]{1,0:T(8,128)S(1)} %get-tuple-element.44), channel_id=1, source_target_pairs={{0,1},{1,0},{2,3},{3,2},{4,5},{5,4},{6,7},{7,6},{8,9},{9,8},{10,11... | collective-permute-start | bytes 86024 | tf_op jit(solution)/shard_map/ppermute | solution.py:382
  6.8 0.8 %left_own.1 = (f32[224,2048]{1,0:T(8,128)S(1)}, f32[56,128]{1,0:T(8,128)S(1)}) custom-call(bf16[224,2048]{1,0:T(8,128)(2,1)S(1)} %get-tuple-element.40.grads_ref, f32[224,2048]{1,0:T(8,128)S(1)} %get-tuple-element.41.errors_ref, f32[32,2048]{1,0:T(8,128)S(1)} %get-tuple-element.42.q_ref), custom_call_target="tpu_custom_call" | custom-call | flops 100000000 | bytes 3000000 | tf_op jit(solution)/shard_map/left_own/pallas_call | solution.py:120
  8.0 1.0 %collective-permute-start.3 = (f32[112,128]{1,0:T(8,128)S(1)}, f32[112,128]{1,0:T(8,128)S(1)}, u32[]{:S(2)}, u32[]{:S(2)}) collective-permute-start(f32[112,128]{1,0:T(8,128)S(1)} %pad_maximum_fusion.1), channel_id=1, source_target_pairs={{0,24},{8,16},{16,8},{24,0},{1,25},{9,17},{17,9},{25,1},{2,26},{10... | collective-permute-start | bytes 172040 | tf_op jit(solution)/shard_map/ppermute | solution.py:382
  9.4 1.9 %collective-permute-start.1 = (f32[112,128]{1,0:T(8,128)S(1)}, f32[112,128]{1,0:T(8,128)S(1)}, u32[]{:S(2)}, u32[]{:S(2)}) collective-permute-start(f32[112,128]{1,0:T(8,128)S(1)} %pad_maximum_fusion.1), channel_id=1, source_target_pairs={{0,8},{8,0},{16,24},{24,16},{1,9},{9,1},{17,25},{25,17},{2,10},{10... | collective-permute-start | bytes 172040 | tf_op jit(solution)/shard_map/ppermute | solution.py:382
  11.3 1.0 %collective-permute-done.3 = f32[112,128]{1,0:T(8,128)S(1)} collective-permute-done((f32[112,128]{1,0:T(8,128)S(1)}, f32[112,128]{1,0:T(8,128)S(1)}, u32[]{:S(2)}, u32[]{:S(2)}) %collective-permute-start.3) | collective-permute-done | bytes 57376 | tf_op jit(solution)/shard_map/ppermute | solution.py:382
  12.3 1.3 %collective-permute-done.2 = f32[112,128]{1,0:T(8,128)S(1)} collective-permute-done((f32[112,128]{1,0:T(8,128)S(1)}, f32[112,128]{1,0:T(8,128)S(1)}, u32[]{:S(2)}, u32[]{:S(2)}) %collective-permute-start.2) | collective-permute-done | bytes 57376 | tf_op jit(solution)/shard_map/ppermute | solution.py:382
  13.7 4.3 %collective-permute-start.6 = (f32[112,128]{1,0:T(8,128)S(1)}, f32[112,128]{1,0:T(8,128)S(1)}, u32[]{:S(2)}, u32[]{:S(2)}) collective-permute-start(f32[112,128]{1,0:T(8,128)S(1)} %add_add_fusion.3), channel_id=1, source_target_pairs={{0,96},{32,64},{64,32},{96,0},{128,224},{160,192},{192,160},{224,1... | collective-permute-start | bytes 172040 | tf_op jit(solution)/shard_map/ppermute | solution.py:382
  18.4 1.2 %collective-permute-done.6 = f32[112,128]{1,0:T(8,128)S(1)} collective-permute-done((f32[112,128]{1,0:T(8,128)S(1)}, f32[112,128]{1,0:T(8,128)S(1)}, u32[]{:S(2)}, u32[]{:S(2)}) %collective-permute-start.6) | collective-permute-done | bytes 57376 | tf_op jit(solution)/shard_map/ppermute | solution.py:382
  19.6 2.7 %collective-permute-done.5 = f32[112,128]{1,0:T(8,128)S(1)} collective-permute-done((f32[112,128]{1,0:T(8,128)S(1)}, f32[112,128]{1,0:T(8,128)S(1)}, u32[]{:S(2)}, u32[]{:S(2)}) %collective-permute-start.5) | collective-permute-done | bytes 57376 | tf_op jit(solution)/shard_map/ppermute | solution.py:382
  22.3 3.9 %collective-permute-start.7 = (f32[112,128]{1,0:T(8,128)S(1)}, f32[112,128]{1,0:T(8,128)S(1)}, u32[]{:S(2)}, u32[]{:S(2)}) collective-permute-start(f32[112,128]{1,0:T(8,128)S(1)} %add_add_fusion.2), channel_id=1, source_target_pairs={{0,192},{32,224},{64,128},{96,160},{128,64},{160,96},{192,0},{224,... | collective-permute-start | bytes 172040 | tf_op jit(solution)/shard_map/ppermute | solution.py:382
  26.7 1.6 %collective-permute-done.7 = f32[112,128]{1,0:T(8,128)S(1)} collective-permute-done((f32[112,128]{1,0:T(8,128)S(1)}, f32[112,128]{1,0:T(8,128)S(1)}, u32[]{:S(2)}, u32[]{:S(2)}) %collective-permute-start.7) | collective-permute-done | bytes 57376 | tf_op jit(solution)/shard_map/ppermute | solution.py:382
  28.2 0.9 %right_terms.1 = f32[4,136,128]{2,1,0:T(8,128)S(1)} custom-call(f32[112,128]{1,0:T(8,128)S(1)} %add.54.p_ref, bf16[448,2048]{1,0:T(8,128)(2,1)S(1)} %get-tuple-element.52.hi_ref, bf16[448,2048]{1,0:T(8,128)(2,1)S(1)} %get-tuple-element.53.lo_ref), custom_call_target="tpu_custom_call" | custom-call | tf_op jit(solution)/shard_map/right_terms/pallas_call | solution.py:174
  29.2 2.6 %collective-permute-start.11 = (f32[136,128]{1,0:T(8,128)S(1)}, f32[136,128]{1,0:T(8,128)S(1)}, u32[]{:S(2)}, u32[]{:S(2)}) collective-permute-start(f32[136,128]{1,0:T(8,128)S(1)} %get-tuple-element.75), channel_id=1, source_target_pairs={{0,6},{2,4},{4,2},{6,0},{1,7},{3,5},{5,3},{7,1},{8,14},{10,12},{12... | collective-permute-start | bytes 208904 | tf_op jit(solution)/shard_map/ppermute | solution.py:382
  32.5 1.1 %collective-permute-done.11 = f32[136,128]{1,0:T(8,128)S(1)} collective-permute-done((f32[136,128]{1,0:T(8,128)S(1)}, f32[136,128]{1,0:T(8,128)S(1)}, u32[]{:S(2)}, u32[]{:S(2)}) %collective-permute-start.11) | collective-permute-done | bytes 69664 | tf_op jit(solution)/shard_map/ppermute | solution.py:382
  33.6 2.8 %collective-permute-done.10 = f32[136,128]{1,0:T(8,128)S(1)} collective-permute-done((f32[136,128]{1,0:T(8,128)S(1)}, f32[136,128]{1,0:T(8,128)S(1)}, u32[]{:S(2)}, u32[]{:S(2)}) %collective-permute-start.10) | collective-permute-done | bytes 69664 | tf_op jit(solution)/shard_map/ppermute | solution.py:382
  36.4 2.0 %collective-permute-start.13 = (f32[128,128]{1,0:T(8,128)S(1)}, f32[128,128]{1,0:T(8,128)S(1)}, u32[]{:S(2)}, u32[]{:S(2)}) collective-permute-start(f32[128,128]{1,0:T(8,128)S(1)} %slice.24), channel_id=1, source_target_pairs={{0,16},{8,24},{16,0},{24,8},{1,17},{9,25},{17,1},{25,9},{2,18},{10... | collective-permute-start | bytes 196616 | tf_op jit(solution)/shard_map/ppermute | solution.py:382
  39.2 2.8 %inverse_factor.1.inverse_ref = f32[8,128]{1,0:T(8,128)S(1)} custom-call(f32[136,128]{1,0:T(8,128)S(1)} %fusion.1.sum_ref), custom_call_target="tpu_custom_call" | custom-call | flops 4000000 | bytes 4000000 | tf_op jit(solution)/shard_map/inverse_factor/pallas_call | solution.py:203
  42.8 1.7 %collective-permute-start.17 = (f32[128,128]{1,0:T(8,128)S(1)}, f32[128,128]{1,0:T(8,128)S(1)}, u32[]{:S(2)}, u32[]{:S(2)}) collective-permute-start(f32[128,128]{1,0:T(8,128)S(1)} %add_add_fusion.1), channel_id=1, source_target_pairs={{0,96},{32,64},{64,32},{96,0},{128,224},{160,192},{192,160},{224,1... | collective-permute-start | bytes 196616 | tf_op jit(solution)/shard_map/ppermute | solution.py:382
  44.5 1.8 %collective-permute-start.16 = (f32[128,128]{1,0:T(8,128)S(1)}, f32[128,128]{1,0:T(8,128)S(1)}, u32[]{:S(2)}, u32[]{:S(2)}) collective-permute-start(f32[128,128]{1,0:T(8,128)S(1)} %add_add_fusion.1), channel_id=1, source_target_pairs={{0,64},{32,96},{64,0},{96,32},{128,192},{160,224},{192,128},{224,1... | collective-permute-start | bytes 196616 | tf_op jit(solution)/shard_map/ppermute | solution.py:382
  46.9 7.2 %collective-permute-start.18 = (f32[56,128]{1,0:T(8,128)S(1)}, f32[56,128]{1,0:T(8,128)S(1)}, u32[]{:S(2)}, u32[]{:S(2)}) collective-permute-start(f32[56,128]{1,0:T(8,128)S(1)} %get-tuple-element.57), channel_id=1, source_target_pairs={{0,1},{1,0},{2,3},{3,2},{4,5},{5,4},{6,7},{7,6},{8,9},{9,8},{10,11... | collective-permute-start | bytes 86024 | tf_op jit(solution)/shard_map/ppermute | solution.py:382
  54.1 0.8 %collective-permute-done.18.other_ref = f32[56,128]{1,0:T(8,128)S(1)} collective-permute-done((f32[56,128]{1,0:T(8,128)S(1)}, f32[56,128]{1,0:T(8,128)S(1)}, u32[]{:S(2)}, u32[]{:S(2)}) %collective-permute-start.18) | collective-permute-done | bytes 28704 | tf_op jit(solution)/shard_map/ppermute | solution.py:382
  54.9 3.4 %collective-permute-start.19 = (f32[128,128]{1,0:T(8,128)S(1)}, f32[128,128]{1,0:T(8,128)S(1)}, u32[]{:S(2)}, u32[]{:S(2)}) collective-permute-start(f32[128,128]{1,0:T(8,128)S(1)} %add_add_fusion.a_ref), channel_id=1, source_target_pairs={{0,192},{32,224},{64,128},{96,160},{128,64},{160,96},{192,0},{224,... | collective-permute-start | bytes 196616 | tf_op jit(solution)/shard_map/ppermute | solution.py:382
  58.8 1.5 %collective-permute-done.19.b_ref = f32[128,128]{1,0:T(8,128)S(1)} collective-permute-done((f32[128,128]{1,0:T(8,128)S(1)}, f32[128,128]{1,0:T(8,128)S(1)}, u32[]{:S(2)}, u32[]{:S(2)}) %collective-permute-start.19) | collective-permute-done | bytes 65568 | tf_op jit(solution)/shard_map/ppermute | solution.py:382
  60.5 1.1 %collective-permute-start.22 = (f32[1,128,128]{2,1,0:T(8,128)S(1)}, f32[1,128,128]{2,1,0:T(8,128)S(1)}, u32[]{:S(2)}, u32[]{:S(2)}) collective-permute-start(f32[1,128,128]{2,1,0:T(8,128)S(1)} %bitcast.13), channel_id=1, source_target_pairs={{0,6},{2,4},{4,2},{6,0},{1,7},{3,5},{5,3},{7,1},{8,14},{10,12},{12... | collective-permute-start | bytes 196616 | tf_op jit(solution)/shard_map/ppermute | solution.py:382
  61.6 3.4 %collective-permute-start.24 = (f32[1,128,128]{2,1,0:T(8,128)S(1)}, f32[1,128,128]{2,1,0:T(8,128)S(1)}, u32[]{:S(2)}, u32[]{:S(2)}) collective-permute-start(f32[1,128,128]{2,1,0:T(8,128)S(1)} %bitcast.14), channel_id=1, source_target_pairs={{0,1},{1,0},{2,3},{3,2},{4,5},{5,4},{6,7},{7,6},{8,9},{9,8},{10,11... | collective-permute-start | bytes 196616 | tf_op jit(solution)/shard_map/ppermute | solution.py:382
  65.6 1.5 %collective-permute-start.20 = (f32[1,128,128]{2,1,0:T(8,128)S(1)}, f32[1,128,128]{2,1,0:T(8,128)S(1)}, u32[]{:S(2)}, u32[]{:S(2)}) collective-permute-start(f32[1,128,128]{2,1,0:T(8,128)S(1)} %bitcast.16), channel_id=1, source_target_pairs={{0,2},{2,0},{4,6},{6,4},{1,3},{3,1},{5,7},{7,5},{8,10},{10,8},{12,... | collective-permute-start | bytes 196616 | tf_op jit(solution)/shard_map/ppermute | solution.py:382
  67.1 1.9 %collective-permute-start.23 = (f32[1,128,128]{2,1,0:T(8,128)S(1)}, f32[1,128,128]{2,1,0:T(8,128)S(1)}, u32[]{:S(2)}, u32[]{:S(2)}) collective-permute-start(f32[1,128,128]{2,1,0:T(8,128)S(1)} %collective-permute-done.22.refs_0_.refs_4_), channel_id=1, source_target_pairs={{0,1},{1,0},{2,3},{3,2},{4,5},{5,4},{6,7},{7,6},{8,9},{9,8},{10,11... | collective-permute-start | bytes 196616 | tf_op jit(solution)/shard_map/ppermute | solution.py:382
  69.1 1.1 %update_first.1.refs_5_ = f32[1,2,224,2048]{3,2,1,0:T(8,128)} custom-call(f32[1,128,128]{2,1,0:T(8,128)S(1)} %bitcast.17, f32[1,128,128]{2,1,0:T(8,128)S(1)} %collective-permute-done.24.refs_1_, bf16[2,224,96]{2,1,0:T(8,128)(2,1)S(1)} %get-tuple-element.64.refs_2_.refs_1_.refs_5_.refs_3_, ...), custom_call_target="tpu_custom_call" | custom-call | flops 40000000 | bytes 2000000 | tf_op jit(solution)/shard_map/update_first/pallas_call | solution.py:368
  70.3 1.0 %update_second.1.refs_11_ = f32[1,2,224,2048]{3,2,1,0:T(8,128)} custom-call(f32[1,128,128]{2,1,0:T(8,128)S(1)} %collective-permute-done.22.refs_0_.refs_4_, bf16[2,224,96]{2,1,0:T(8,128)(2,1)S(1)} %get-tuple-element.64.refs_2_.refs_1_.refs_5_.refs_3_, ...), custom_call_target="tpu_custom_call", output_to_operand_aliasing={{}: (5, {})} | custom-call | flops 20000000 | bytes 1000000 | tf_op jit(solution)/shard_map/update_second/pallas_call | solution.py:368
  71.7 1.5 %update_third.1 = (f32[1,2,224,2048]{3,2,1,0:T(8,128)}, f32[2,112,128]{2,1,0:T(8,128)}, f32[2,112,128]{2,1,0:T(8,128)}, bf16[2,112,128]{2,1,0:T(8,128)(2,1)}, f32[2,32,2048]{2,1,0:T(8,128)}) custom-call(f32[1,128,128]{2,1,0:T(8,128)S(1)} %collective-permute-done.20.refs_0_, ...), custom_call_target="tpu_custom_call", output_to_operand_aliasing={{0}: (11, {})} | custom-call | flops 60000000 | bytes 3000000 | tf_op jit(solution)/shard_map/update_third/pallas_call | solution.py:368
  73.2 1.3 %update_fourth.1 = (f32[1,2,224,2048]{3,2,1,0:T(8,128)}, f32[2,112,128]{2,1,0:T(8,128)}, f32[2,112,128]{2,1,0:T(8,128)}, bf16[2,112,128]{2,1,0:T(8,128)(2,1)}, f32[2,32,2048]{2,1,0:T(8,128)}) custom-call(f32[2,128,128]{2,1,0:T(8,128)S(1)} %collective-permute-done.25.refs_0_, ...), custom_call_target="tpu_custom_call", output_to_operand_aliasing={{0}: (9, {}), {1}: (10, {}), {2}: (11, {}), {3}: (12, {}), ... | custom-call | flops 40000000 | bytes 2000000 | tf_op jit(solution)/shard_map/update_fourth/pallas_call | solution.py:368
  (46 shorter events, 6.5 us)
Async XLA Ops:
  3.5 4.2 %collective-permute-start = (f32[56,128]{1,0:T(8,128)S(1)}, f32[56,128]{1,0:T(8,128)S(1)}, u32[]{:S(2)}, u32[]{:S(2)}) collective-permute-start(f32[56,128]{1,0:T(8,128)S(1)} %get-tuple-element.44), channel_id=1, source_target_pairs={{0,1},{1,0},{2,3},{3,2},{4,5},{5,4},{6,7},{7,6},{8,9},{9,8},{10,11... | collective-permute-start | bytes 86024 | tf_op jit(solution)/shard_map/ppermute | solution.py:382
  7.7 18.5 %collective-permute-start.8 = (f32[224,2048]{1,0:T(8,128)S(1)}, f32[224,2048]{1,0:T(8,128)S(1)}, u32[]{:S(2)}, u32[]{:S(2)}) collective-permute-start(f32[224,2048]{1,0:T(8,128)S(1)} %get-tuple-element.48.refs_5_.refs_4_.refs_8_.refs_6_), channel_id=1, source_target_pairs={{0,1},{1,0},{2,3},{3,2},{4,5},{5,4},{6,7},{7,6},{8,9},{9,8},{10,11... | collective-permute-start | bytes 5505032 | tf_op jit(solution)/shard_map/ppermute | solution.py:382
  8.0 4.2 %collective-permute-start.3 = (f32[112,128]{1,0:T(8,128)S(1)}, f32[112,128]{1,0:T(8,128)S(1)}, u32[]{:S(2)}, u32[]{:S(2)}) collective-permute-start(f32[112,128]{1,0:T(8,128)S(1)} %pad_maximum_fusion.1), channel_id=1, source_target_pairs={{0,24},{8,16},{16,8},{24,0},{1,25},{9,17},{17,9},{25,1},{2,26},{10... | collective-permute-start | bytes 172040 | tf_op jit(solution)/shard_map/ppermute | solution.py:382
  9.0 4.5 %collective-permute-start.2 = (f32[112,128]{1,0:T(8,128)S(1)}, f32[112,128]{1,0:T(8,128)S(1)}, u32[]{:S(2)}, u32[]{:S(2)}) collective-permute-start(f32[112,128]{1,0:T(8,128)S(1)} %pad_maximum_fusion.1), channel_id=1, source_target_pairs={{0,16},{8,24},{16,0},{24,8},{1,17},{9,25},{17,1},{25,9},{2,18},{10... | collective-permute-start | bytes 172040 | tf_op jit(solution)/shard_map/ppermute | solution.py:382
  9.4 4.3 %collective-permute-start.1 = (f32[112,128]{1,0:T(8,128)S(1)}, f32[112,128]{1,0:T(8,128)S(1)}, u32[]{:S(2)}, u32[]{:S(2)}) collective-permute-start(f32[112,128]{1,0:T(8,128)S(1)} %pad_maximum_fusion.1), channel_id=1, source_target_pairs={{0,8},{8,0},{16,24},{24,16},{1,9},{9,1},{17,25},{25,17},{2,10},{10... | collective-permute-start | bytes 172040 | tf_op jit(solution)/shard_map/ppermute | solution.py:382
  13.7 5.8 %collective-permute-start.6 = (f32[112,128]{1,0:T(8,128)S(1)}, f32[112,128]{1,0:T(8,128)S(1)}, u32[]{:S(2)}, u32[]{:S(2)}) collective-permute-start(f32[112,128]{1,0:T(8,128)S(1)} %add_add_fusion.3), channel_id=1, source_target_pairs={{0,96},{32,64},{64,32},{96,0},{128,224},{160,192},{192,160},{224,1... | collective-permute-start | bytes 172040 | tf_op jit(solution)/shard_map/ppermute | solution.py:382
  18.0 4.3 %collective-permute-start.5 = (f32[112,128]{1,0:T(8,128)S(1)}, f32[112,128]{1,0:T(8,128)S(1)}, u32[]{:S(2)}, u32[]{:S(2)}) collective-permute-start(f32[112,128]{1,0:T(8,128)S(1)} %add_add_fusion.3), channel_id=1, source_target_pairs={{0,64},{32,96},{64,0},{96,32},{128,192},{160,224},{192,128},{224,1... | collective-permute-start | bytes 172040 | tf_op jit(solution)/shard_map/ppermute | solution.py:382
  18.0 4.3 %collective-permute-start.4 = (f32[112,128]{1,0:T(8,128)S(1)}, f32[112,128]{1,0:T(8,128)S(1)}, u32[]{:S(2)}, u32[]{:S(2)}) collective-permute-start(f32[112,128]{1,0:T(8,128)S(1)} %add_add_fusion.3), channel_id=1, source_target_pairs={{0,32},{32,0},{64,96},{96,64},{128,160},{160,128},{192,224},{224,1... | collective-permute-start | bytes 172040 | tf_op jit(solution)/shard_map/ppermute | solution.py:382
  22.3 5.9 %collective-permute-start.7 = (f32[112,128]{1,0:T(8,128)S(1)}, f32[112,128]{1,0:T(8,128)S(1)}, u32[]{:S(2)}, u32[]{:S(2)}) collective-permute-start(f32[112,128]{1,0:T(8,128)S(1)} %add_add_fusion.2), channel_id=1, source_target_pairs={{0,192},{32,224},{64,128},{96,160},{128,64},{160,96},{192,0},{224,... | collective-permute-start | bytes 172040 | tf_op jit(solution)/shard_map/ppermute | solution.py:382
  29.2 4.5 %collective-permute-start.11 = (f32[136,128]{1,0:T(8,128)S(1)}, f32[136,128]{1,0:T(8,128)S(1)}, u32[]{:S(2)}, u32[]{:S(2)}) collective-permute-start(f32[136,128]{1,0:T(8,128)S(1)} %get-tuple-element.75), channel_id=1, source_target_pairs={{0,6},{2,4},{4,2},{6,0},{1,7},{3,5},{5,3},{7,1},{8,14},{10,12},{12... | collective-permute-start | bytes 208904 | tf_op jit(solution)/shard_map/ppermute | solution.py:382
  31.7 4.7 %collective-permute-start.10 = (f32[136,128]{1,0:T(8,128)S(1)}, f32[136,128]{1,0:T(8,128)S(1)}, u32[]{:S(2)}, u32[]{:S(2)}) collective-permute-start(f32[136,128]{1,0:T(8,128)S(1)} %get-tuple-element.76), channel_id=1, source_target_pairs={{0,4},{2,6},{4,0},{6,2},{1,5},{3,7},{5,1},{7,3},{8,12},{10,14},{12... | collective-permute-start | bytes 208904 | tf_op jit(solution)/shard_map/ppermute | solution.py:382
  32.3 4.1 %collective-permute-start.9 = (f32[136,128]{1,0:T(8,128)S(1)}, f32[136,128]{1,0:T(8,128)S(1)}, u32[]{:S(2)}, u32[]{:S(2)}) collective-permute-start(f32[136,128]{1,0:T(8,128)S(1)} %get-tuple-element.77), channel_id=1, source_target_pairs={{0,2},{2,0},{4,6},{6,4},{1,3},{3,1},{5,7},{7,5},{8,10},{10,8},{12,... | collective-permute-start | bytes 208904 | tf_op jit(solution)/shard_map/ppermute | solution.py:382
  36.4 5.6 %collective-permute-start.13 = (f32[128,128]{1,0:T(8,128)S(1)}, f32[128,128]{1,0:T(8,128)S(1)}, u32[]{:S(2)}, u32[]{:S(2)}) collective-permute-start(f32[128,128]{1,0:T(8,128)S(1)} %slice.24), channel_id=1, source_target_pairs={{0,16},{8,24},{16,0},{24,8},{1,17},{9,25},{17,1},{25,9},{2,18},{10... | collective-permute-start | bytes 196616 | tf_op jit(solution)/shard_map/ppermute | solution.py:382
  38.4 4.3 %collective-permute-start.14 = (f32[128,128]{1,0:T(8,128)S(1)}, f32[128,128]{1,0:T(8,128)S(1)}, u32[]{:S(2)}, u32[]{:S(2)}) collective-permute-start(f32[128,128]{1,0:T(8,128)S(1)} %slice.24), channel_id=1, source_target_pairs={{0,24},{8,16},{16,8},{24,0},{1,25},{9,17},{17,9},{25,1},{2,26},{10... | collective-permute-start | bytes 196616 | tf_op jit(solution)/shard_map/ppermute | solution.py:382
  38.9 3.8 %collective-permute-start.12 = (f32[128,128]{1,0:T(8,128)S(1)}, f32[128,128]{1,0:T(8,128)S(1)}, u32[]{:S(2)}, u32[]{:S(2)}) collective-permute-start(f32[128,128]{1,0:T(8,128)S(1)} %slice.24), channel_id=1, source_target_pairs={{0,8},{8,0},{16,24},{24,16},{1,9},{9,1},{17,25},{25,17},{2,10},{10... | collective-permute-start | bytes 196616 | tf_op jit(solution)/shard_map/ppermute | solution.py:382
  42.8 11.3 %collective-permute-start.17 = (f32[128,128]{1,0:T(8,128)S(1)}, f32[128,128]{1,0:T(8,128)S(1)}, u32[]{:S(2)}, u32[]{:S(2)}) collective-permute-start(f32[128,128]{1,0:T(8,128)S(1)} %add_add_fusion.1), channel_id=1, source_target_pairs={{0,96},{32,64},{64,32},{96,0},{128,224},{160,192},{192,160},{224,1... | collective-permute-start | bytes 196616 | tf_op jit(solution)/shard_map/ppermute | solution.py:382
  44.5 9.6 %collective-permute-start.16 = (f32[128,128]{1,0:T(8,128)S(1)}, f32[128,128]{1,0:T(8,128)S(1)}, u32[]{:S(2)}, u32[]{:S(2)}) collective-permute-start(f32[128,128]{1,0:T(8,128)S(1)} %add_add_fusion.1), channel_id=1, source_target_pairs={{0,64},{32,96},{64,0},{96,32},{128,192},{160,224},{192,128},{224,1... | collective-permute-start | bytes 196616 | tf_op jit(solution)/shard_map/ppermute | solution.py:382
  46.3 7.8 %collective-permute-start.15 = (f32[128,128]{1,0:T(8,128)S(1)}, f32[128,128]{1,0:T(8,128)S(1)}, u32[]{:S(2)}, u32[]{:S(2)}) collective-permute-start(f32[128,128]{1,0:T(8,128)S(1)} %add_add_fusion.1), channel_id=1, source_target_pairs={{0,32},{32,0},{64,96},{96,64},{128,160},{160,128},{192,224},{224,1... | collective-permute-start | bytes 196616 | tf_op jit(solution)/shard_map/ppermute | solution.py:382
  46.9 8.0 %collective-permute-start.18 = (f32[56,128]{1,0:T(8,128)S(1)}, f32[56,128]{1,0:T(8,128)S(1)}, u32[]{:S(2)}, u32[]{:S(2)}) collective-permute-start(f32[56,128]{1,0:T(8,128)S(1)} %get-tuple-element.57), channel_id=1, source_target_pairs={{0,1},{1,0},{2,3},{3,2},{4,5},{5,4},{6,7},{7,6},{8,9},{9,8},{10,11... | collective-permute-start | bytes 86024 | tf_op jit(solution)/shard_map/ppermute | solution.py:382
  54.9 5.3 %collective-permute-start.19 = (f32[128,128]{1,0:T(8,128)S(1)}, f32[128,128]{1,0:T(8,128)S(1)}, u32[]{:S(2)}, u32[]{:S(2)}) collective-permute-start(f32[128,128]{1,0:T(8,128)S(1)} %add_add_fusion.a_ref), channel_id=1, source_target_pairs={{0,192},{32,224},{64,128},{96,160},{128,64},{160,96},{192,0},{224,... | collective-permute-start | bytes 196616 | tf_op jit(solution)/shard_map/ppermute | solution.py:382
  60.5 6.6 %collective-permute-start.22 = (f32[1,128,128]{2,1,0:T(8,128)S(1)}, f32[1,128,128]{2,1,0:T(8,128)S(1)}, u32[]{:S(2)}, u32[]{:S(2)}) collective-permute-start(f32[1,128,128]{2,1,0:T(8,128)S(1)} %bitcast.13), channel_id=1, source_target_pairs={{0,6},{2,4},{4,2},{6,0},{1,7},{3,5},{5,3},{7,1},{8,14},{10,12},{12... | collective-permute-start | bytes 196616 | tf_op jit(solution)/shard_map/ppermute | solution.py:382
  61.6 7.5 %collective-permute-start.24 = (f32[1,128,128]{2,1,0:T(8,128)S(1)}, f32[1,128,128]{2,1,0:T(8,128)S(1)}, u32[]{:S(2)}, u32[]{:S(2)}) collective-permute-start(f32[1,128,128]{2,1,0:T(8,128)S(1)} %bitcast.14), channel_id=1, source_target_pairs={{0,1},{1,0},{2,3},{3,2},{4,5},{5,4},{6,7},{7,6},{8,9},{9,8},{10,11... | collective-permute-start | bytes 196616 | tf_op jit(solution)/shard_map/ppermute | solution.py:382
  65.0 6.3 %collective-permute-start.21 = (f32[1,128,128]{2,1,0:T(8,128)S(1)}, f32[1,128,128]{2,1,0:T(8,128)S(1)}, u32[]{:S(2)}, u32[]{:S(2)}) collective-permute-start(f32[1,128,128]{2,1,0:T(8,128)S(1)} %bitcast.15), channel_id=1, source_target_pairs={{0,4},{2,6},{4,0},{6,2},{1,5},{3,7},{5,1},{7,3},{8,12},{10,14},{12... | collective-permute-start | bytes 196616 | tf_op jit(solution)/shard_map/ppermute | solution.py:382
  65.6 5.7 %collective-permute-start.20 = (f32[1,128,128]{2,1,0:T(8,128)S(1)}, f32[1,128,128]{2,1,0:T(8,128)S(1)}, u32[]{:S(2)}, u32[]{:S(2)}) collective-permute-start(f32[1,128,128]{2,1,0:T(8,128)S(1)} %bitcast.16), channel_id=1, source_target_pairs={{0,2},{2,0},{4,6},{6,4},{1,3},{3,1},{5,7},{7,5},{8,10},{10,8},{12,... | collective-permute-start | bytes 196616 | tf_op jit(solution)/shard_map/ppermute | solution.py:382
  67.1 4.1 %collective-permute-start.23 = (f32[1,128,128]{2,1,0:T(8,128)S(1)}, f32[1,128,128]{2,1,0:T(8,128)S(1)}, u32[]{:S(2)}, u32[]{:S(2)}) collective-permute-start(f32[1,128,128]{2,1,0:T(8,128)S(1)} %collective-permute-done.22.refs_0_.refs_4_), channel_id=1, source_target_pairs={{0,1},{1,0},{2,3},{3,2},{4,5},{5,4},{6,7},{7,6},{8,9},{9,8},{10,11... | collective-permute-start | bytes 196616 | tf_op jit(solution)/shard_map/ppermute | solution.py:382
  70.2 1.5 %copy-start = (f32[2,112,128]{2,1,0:T(8,128)S(1)}, f32[2,112,128]{2,1,0:T(8,128)}, u32[]{:S(2)}) copy-start(f32[2,112,128]{2,1,0:T(8,128)} %refs_7_.1) | copy-start | bytes 344068
  70.2 1.4 %copy-start.1 = (f32[2,112,128]{2,1,0:T(8,128)S(1)}, f32[2,112,128]{2,1,0:T(8,128)}, u32[]{:S(2)}) copy-start(f32[2,112,128]{2,1,0:T(8,128)} %refs_8_.1) | copy-start | bytes 344068
  71.3 1.9 %collective-permute-start.25 = (f32[2,128,128]{2,1,0:T(8,128)S(1)}, f32[2,128,128]{2,1,0:T(8,128)S(1)}, u32[]{:S(2)}, u32[]{:S(2)}) collective-permute-start(f32[2,128,128]{2,1,0:T(8,128)S(1)} %pad_maximum_fusion), channel_id=1, source_target_pairs={{0,1},{1,0},{2,3},{3,2},{4,5},{5,4},{6,7},{7,6},{8,9},{9,8},{10,11... | collective-permute-start | bytes 393224 | tf_op jit(solution)/shard_map/ppermute | solution.py:382

commit v10 on v8

--- a/solution.py
+++ b/solution.py
@@ -149,8 +149,8 @@
     )(own, gift)
 
 
-def right_kernel(replicas, p_ref, hi_ref, lo_ref, out_ref):
-    slots, height, _ = out_ref.shape
+def right_kernel(replicas, slots, p_ref, hi_ref, lo_ref, out_ref):
+    height = out_ref.shape[1]
     tiles = (height - 8) // RANK
     width = tiles * LANES
     x = lax.axis_index("x")
@@ -160,24 +160,25 @@
     p_hi, p_lo = split(p)
     both = jnp.concatenate([p_hi, p_lo], axis=0)
     gram = pack(dot(p, p, 1, 1, lax.Precision.HIGHEST))
-    for slot in range(slots):
+    for k, slot in enumerate(slots):
         here = pl.ds(pl.multiple_of((x ^ slot) * width, width), width)
         wide = dot(both, hi_ref[:, here], 1, 0)
         q = wide[:RANK] + wide[RANK:] + dot(p_hi, lo_ref[:, here], 1, 0)
         for j in range(tiles):
-            out_ref[slot, j * RANK : (j + 1) * RANK, :] = q[:, j * LANES : (j + 1) * LANES]
-        out_ref[slot, tiles * RANK :, :] = gram
-
-
-def right_terms(p_sum, hi, lo, replicas, slots):
-    height = hi.shape[1] // slots // LANES * RANK + 8
-    return pl.pallas_call(
-        functools.partial(right_kernel, replicas),
+            out_ref[k, j * RANK : (j + 1) * RANK, :] = q[:, j * LANES : (j + 1) * LANES]
+        out_ref[k, tiles * RANK :, :] = gram
+
+
+def right_terms(p_sum, hi, lo, replicas, slots, total):
+    height = hi.shape[1] // total // LANES * RANK + 8
+    return pl.pallas_call(
+        functools.partial(right_kernel, replicas, slots),
         in_specs=[WHOLE] * 3,
         out_specs=WHOLE,
-        out_shape=jax.ShapeDtypeStruct((slots, height, LANES), F32),
-        compiler_params=PARAMS,
-        name="right_terms",
+        out_shape=jax.ShapeDtypeStruct((len(slots), height, LANES), F32),
+        compiler_params=PARAMS,
+        cost_estimate=pl.CostEstimate(flops=200_000_000, bytes_accessed=2_000_000, transcendentals=0),
+        name="right_terms_kept" if slots == (0,) else "right_terms_sent",
     )(p_sum, hi, lo)
 
 
@@ -357,16 +358,17 @@
     replicas, slots = lax.axis_size(("z", "y")), lax.axis_size("x")
     other_full, p_other, own_grads, own_errors, own_q = load(grads, errors, q_prev)
     own_full, p_own = left_own(own_grads, own_errors, own_q)
+    p_own, gift = lax.optimization_barrier((p_own, other_full))
     p = jnp.concatenate([p_own, swap(p_other, "c", 1)])
-    p, gift = lax.optimization_barrier((p, other_full))
     gift = swap(gift, "c", 1)
     p = four([p] * 4, "y")
     p = four([p] * 4, "z")
     far, hi, lo = lax.optimization_barrier((swap(p, "z", 6), *halves(own_full, gift)))
     p = p + far
 
-    terms = right_terms(p, hi, lo, replicas, slots)
-    total = four([terms[i] for i in range(slots)], "x")
+    sent = right_terms(p, hi, lo, replicas, tuple(range(1, slots)), slots)
+    kept = right_terms(p, hi, lo, replicas, (0,), slots)
+    total = four([kept[0], *(sent[i - 1] for i in range(1, slots))], "x")
     inverse = inverse_factor(total)
     q = four([total[:-8]] * 4, "y")
     q, inverse = lax.optimization_barrier((q, inverse))

time: 74.4 us -> 77.6 us (1.043)
  waiting for transfers between devices: 17.4 us -> 20.3 us
    ppermute x24, waiting for transfers between devices: 17.4 us -> 20.3 us  [swap(): lax.ppermute(value, axis, [(i, i ^ bit) for i in range(lax.axis_size(axis...]
  transfers between devices with their start and end apart: 24 -> 24, of which waited for: 13 -> 14; matrix products, arithmetic and copies ran while one was open for 0% -> 0% of each run, Pallas kernels for 9% -> 8%
where the time goes in v10:
time: 77.6 us; the launch traced here: 77.5 us
  starting transfers between devices  43.4 us (56%)
  waiting for transfers between devices  20.3 us (26%)
  Pallas kernels  12.6 us (16%)
  between operations  0.93 us (1%)
    ppermute x24, starting transfers between devices, swap(): lax.ppermute(value, axis, [(i, i ^ bit) for i in range(lax.axis_size(axis...  43.4 us
    ppermute x24, waiting for transfers between devices, swap(): lax.ppermute(value, axis, [(i, i ^ bit) for i in range(lax.axis_size(axis...  20.3 us
    pallas_call x2, Pallas kernels, update(): pl.pallas_call(functools.partial(update_kernel, mine), in_specs=[WHOLE] *...  3.3 us
    pallas_call x1, Pallas kernels, inverse_factor(): pl.pallas_call(factor_kernel, in_specs=[WHOLE], out_specs=WHOLE, out_shap...  2.85 us
    pallas_call x1, Pallas kernels, load(): pl.pallas_call(load_kernel, in_specs=[AWAY] * 3, out_specs=[WHOLE] * 5, o...  2.84 us
  transfers between devices with their start and end apart: 24, of which 14 were waited for; matrix products, arithmetic and copies ran while one was open for 0% of the time, Pallas kernels for 8%

profile of v10, /device:TPU:1, one launch (start us, length us, event | category | flops | bytes accessed | tf_op | source)
XLA Modules:
  0.0 77.5 jit_solution(18236285675678111260)
XLA Ops:
  0.6 2.8 %load.1 = (f32[224,2048]{1,0:T(8,128)S(1)}, f32[56,128]{1,0:T(8,128)S(1)}, bf16[224,2048]{1,0:T(8,128)(2,1)S(1)}, f32[224,2048]{1,0:T(8,128)S(1)}, f32[32,2048]{1,0:T(8,128)S(1)}) custom-call(bf16[1,2,224,2048]{3,2,1,0:T(8,128)(2,1)} %grads_hbm.1, f32[1,2,224,2048]{3,2,1,0:T(8,128)} %errors_hbm.1, f32[2,32,2048]{2,1,0:T(8,128)} %q_hbm.1), custom_call_target="tpu_custom_call" | custom-call | tf_op jit(solution)/shard_map/load/pallas_call | solution.py:89
  3.5 0.8 %left_own.1 = (f32[224,2048]{1,0:T(8,128)S(1)}, f32[56,128]{1,0:T(8,128)S(1)}) custom-call(bf16[224,2048]{1,0:T(8,128)(2,1)S(1)} %get-tuple-element.36.grads_ref, f32[224,2048]{1,0:T(8,128)S(1)} %get-tuple-element.37.errors_ref, f32[32,2048]{1,0:T(8,128)S(1)} %get-tuple-element.38.q_ref), custom_call_target="tpu_custom_call" | custom-call | flops 100000000 | bytes 3000000 | tf_op jit(solution)/shard_map/left_own/pallas_call | solution.py:120
  4.3 3.3 %collective-permute-start.8 = (f32[224,2048]{1,0:T(8,128)S(1)}, f32[224,2048]{1,0:T(8,128)S(1)}, u32[]{:S(2)}, u32[]{:S(2)}) collective-permute-start(f32[224,2048]{1,0:T(8,128)S(1)} %get-tuple-element.44.full_ref), channel_id=1, source_target_pairs={{0,1},{1,0},{2,3},{3,2},{4,5},{5,4},{6,7},{7,6},{8,9},{9,8},{10,11... | collective-permute-start | bytes 5505032 | tf_op jit(solution)/shard_map/ppermute | solution.py:350
  7.7 3.3 %collective-permute-done = f32[56,128]{1,0:T(8,128)S(1)} collective-permute-done((f32[56,128]{1,0:T(8,128)S(1)}, f32[56,128]{1,0:T(8,128)S(1)}, u32[]{:S(2)}, u32[]{:S(2)}) %collective-permute-start) | collective-permute-done | bytes 28704 | tf_op jit(solution)/shard_map/ppermute | solution.py:350
  11.1 1.0 %collective-permute-start.3 = (f32[112,128]{1,0:T(8,128)S(1)}, f32[112,128]{1,0:T(8,128)S(1)}, u32[]{:S(2)}, u32[]{:S(2)}) collective-permute-start(f32[112,128]{1,0:T(8,128)S(1)} %constant_dynamic-update-slice_fusion), channel_id=1, source_target_pairs={{0,24},{8,16},{16,8},{24,0},{1,25},{9,17},{17,9},{25,1},{2,26},{10... | collective-permute-start | bytes 172040 | tf_op jit(solution)/shard_map/ppermute | solution.py:350
  12.4 1.9 %collective-permute-start.1 = (f32[112,128]{1,0:T(8,128)S(1)}, f32[112,128]{1,0:T(8,128)S(1)}, u32[]{:S(2)}, u32[]{:S(2)}) collective-permute-start(f32[112,128]{1,0:T(8,128)S(1)} %constant_dynamic-update-slice_fusion), channel_id=1, source_target_pairs={{0,8},{8,0},{16,24},{24,16},{1,9},{9,1},{17,25},{25,17},{2,10},{10... | collective-permute-start | bytes 172040 | tf_op jit(solution)/shard_map/ppermute | solution.py:350
  14.3 1.0 %collective-permute-done.3 = f32[112,128]{1,0:T(8,128)S(1)} collective-permute-done((f32[112,128]{1,0:T(8,128)S(1)}, f32[112,128]{1,0:T(8,128)S(1)}, u32[]{:S(2)}, u32[]{:S(2)}) %collective-permute-start.3) | collective-permute-done | bytes 57376 | tf_op jit(solution)/shard_map/ppermute | solution.py:350
  15.3 1.4 %collective-permute-done.2 = f32[112,128]{1,0:T(8,128)S(1)} collective-permute-done((f32[112,128]{1,0:T(8,128)S(1)}, f32[112,128]{1,0:T(8,128)S(1)}, u32[]{:S(2)}, u32[]{:S(2)}) %collective-permute-start.2) | collective-permute-done | bytes 57376 | tf_op jit(solution)/shard_map/ppermute | solution.py:350
  16.9 4.1 %collective-permute-start.6 = (f32[112,128]{1,0:T(8,128)S(1)}, f32[112,128]{1,0:T(8,128)S(1)}, u32[]{:S(2)}, u32[]{:S(2)}) collective-permute-start(f32[112,128]{1,0:T(8,128)S(1)} %add_add_fusion.3), channel_id=1, source_target_pairs={{0,96},{32,64},{64,32},{96,0},{128,224},{160,192},{192,160},{224,1... | collective-permute-start | bytes 172040 | tf_op jit(solution)/shard_map/ppermute | solution.py:350
  21.4 1.2 %collective-permute-done.6 = f32[112,128]{1,0:T(8,128)S(1)} collective-permute-done((f32[112,128]{1,0:T(8,128)S(1)}, f32[112,128]{1,0:T(8,128)S(1)}, u32[]{:S(2)}, u32[]{:S(2)}) %collective-permute-start.6) | collective-permute-done | bytes 57376 | tf_op jit(solution)/shard_map/ppermute | solution.py:350
  22.6 2.7 %collective-permute-done.5 = f32[112,128]{1,0:T(8,128)S(1)} collective-permute-done((f32[112,128]{1,0:T(8,128)S(1)}, f32[112,128]{1,0:T(8,128)S(1)}, u32[]{:S(2)}, u32[]{:S(2)}) %collective-permute-start.5) | collective-permute-done | bytes 57376 | tf_op jit(solution)/shard_map/ppermute | solution.py:350
  25.4 3.9 %collective-permute-start.7 = (f32[112,128]{1,0:T(8,128)S(1)}, f32[112,128]{1,0:T(8,128)S(1)}, u32[]{:S(2)}, u32[]{:S(2)}) collective-permute-start(f32[112,128]{1,0:T(8,128)S(1)} %add_add_fusion.2), channel_id=1, source_target_pairs={{0,192},{32,224},{64,128},{96,160},{128,64},{160,96},{192,0},{224,... | collective-permute-start | bytes 172040 | tf_op jit(solution)/shard_map/ppermute | solution.py:350
  29.7 1.6 %collective-permute-done.7 = f32[112,128]{1,0:T(8,128)S(1)} collective-permute-done((f32[112,128]{1,0:T(8,128)S(1)}, f32[112,128]{1,0:T(8,128)S(1)}, u32[]{:S(2)}, u32[]{:S(2)}) %collective-permute-start.7) | collective-permute-done | bytes 57376 | tf_op jit(solution)/shard_map/ppermute | solution.py:350
  31.3 0.7 right_terms_sent.1
  32.1 2.6 %collective-permute-start.11 = (f32[136,128]{1,0:T(8,128)S(1)}, f32[136,128]{1,0:T(8,128)S(1)}, u32[]{:S(2)}, u32[]{:S(2)}) collective-permute-start(f32[136,128]{1,0:T(8,128)S(1)} %get-tuple-element.67), channel_id=1, source_target_pairs={{0,6},{2,4},{4,2},{6,0},{1,7},{3,5},{5,3},{7,1},{8,14},{10,12},{12... | collective-permute-start | bytes 208904 | tf_op jit(solution)/shard_map/ppermute | solution.py:350
  36.5 2.8 %collective-permute-done.10 = f32[136,128]{1,0:T(8,128)S(1)} collective-permute-done((f32[136,128]{1,0:T(8,128)S(1)}, f32[136,128]{1,0:T(8,128)S(1)}, u32[]{:S(2)}, u32[]{:S(2)}) %collective-permute-start.10) | collective-permute-done | bytes 69664 | tf_op jit(solution)/shard_map/ppermute | solution.py:350
  39.3 2.0 %collective-permute-start.13 = (f32[128,128]{1,0:T(8,128)S(1)}, f32[128,128]{1,0:T(8,128)S(1)}, u32[]{:S(2)}, u32[]{:S(2)}) collective-permute-start(f32[128,128]{1,0:T(8,128)S(1)} %slice.19), channel_id=1, source_target_pairs={{0,16},{8,24},{16,0},{24,8},{1,17},{9,25},{17,1},{25,9},{2,18},{10... | collective-permute-start | bytes 196616 | tf_op jit(solution)/shard_map/ppermute | solution.py:350
  42.1 2.8 %inverse_factor.1.inverse_ref = f32[8,128]{1,0:T(8,128)S(1)} custom-call(f32[136,128]{1,0:T(8,128)S(1)} %fusion.sum_ref), custom_call_target="tpu_custom_call" | custom-call | flops 4000000 | bytes 4000000 | tf_op jit(solution)/shard_map/inverse_factor/pallas_call | solution.py:204
  44.9 0.7 collective-permute-done.14
  45.7 1.9 %collective-permute-start.17 = (f32[128,128]{1,0:T(8,128)S(1)}, f32[128,128]{1,0:T(8,128)S(1)}, u32[]{:S(2)}, u32[]{:S(2)}) collective-permute-start(f32[128,128]{1,0:T(8,128)S(1)} %add_add_fusion.1), channel_id=1, source_target_pairs={{0,96},{32,64},{64,32},{96,0},{128,224},{160,192},{192,160},{224,1... | collective-permute-start | bytes 196616 | tf_op jit(solution)/shard_map/ppermute | solution.py:350
  47.6 1.3 %collective-permute-start.16 = (f32[128,128]{1,0:T(8,128)S(1)}, f32[128,128]{1,0:T(8,128)S(1)}, u32[]{:S(2)}, u32[]{:S(2)}) collective-permute-start(f32[128,128]{1,0:T(8,128)S(1)} %add_add_fusion.1), channel_id=1, source_target_pairs={{0,64},{32,96},{64,0},{96,32},{128,192},{160,224},{192,128},{224,1... | collective-permute-start | bytes 196616 | tf_op jit(solution)/shard_map/ppermute | solution.py:350
  50.0 7.2 %collective-permute-start.18 = (f32[56,128]{1,0:T(8,128)S(1)}, f32[56,128]{1,0:T(8,128)S(1)}, u32[]{:S(2)}, u32[]{:S(2)}) collective-permute-start(f32[56,128]{1,0:T(8,128)S(1)} %get-tuple-element.53), channel_id=1, source_target_pairs={{0,1},{1,0},{2,3},{3,2},{4,5},{5,4},{6,7},{7,6},{8,9},{9,8},{10,11... | collective-permute-start | bytes 86024 | tf_op jit(solution)/shard_map/ppermute | solution.py:350
  57.2 0.8 %collective-permute-done.18.other_ref = f32[56,128]{1,0:T(8,128)S(1)} collective-permute-done((f32[56,128]{1,0:T(8,128)S(1)}, f32[56,128]{1,0:T(8,128)S(1)}, u32[]{:S(2)}, u32[]{:S(2)}) %collective-permute-start.18) | collective-permute-done | bytes 28704 | tf_op jit(solution)/shard_map/ppermute | solution.py:350
  58.1 3.4 %collective-permute-start.19 = (f32[128,128]{1,0:T(8,128)S(1)}, f32[128,128]{1,0:T(8,128)S(1)}, u32[]{:S(2)}, u32[]{:S(2)}) collective-permute-start(f32[128,128]{1,0:T(8,128)S(1)} %add_add_fusion.a_ref), channel_id=1, source_target_pairs={{0,192},{32,224},{64,128},{96,160},{128,64},{160,96},{192,0},{224,... | collective-permute-start | bytes 196616 | tf_op jit(solution)/shard_map/ppermute | solution.py:350
  61.9 1.5 %collective-permute-done.19.b_ref = f32[128,128]{1,0:T(8,128)S(1)} collective-permute-done((f32[128,128]{1,0:T(8,128)S(1)}, f32[128,128]{1,0:T(8,128)S(1)}, u32[]{:S(2)}, u32[]{:S(2)}) %collective-permute-start.19) | collective-permute-done | bytes 65568 | tf_op jit(solution)/shard_map/ppermute | solution.py:350
  63.6 1.1 %collective-permute-start.22 = (f32[128,128]{1,0:T(8,128)S(1)}, f32[128,128]{1,0:T(8,128)S(1)}, u32[]{:S(2)}, u32[]{:S(2)}) collective-permute-start(f32[128,128]{1,0:T(8,128)S(1)} %finished_piece.1), channel_id=1, source_target_pairs={{0,6},{2,4},{4,2},{6,0},{1,7},{3,5},{5,3},{7,1},{8,14},{10,12},{12... | collective-permute-start | bytes 196616 | tf_op jit(solution)/shard_map/ppermute | solution.py:350
  65.5 1.4 %collective-permute-start.20 = (f32[128,128]{1,0:T(8,128)S(1)}, f32[128,128]{1,0:T(8,128)S(1)}, u32[]{:S(2)}, u32[]{:S(2)}) collective-permute-start(f32[128,128]{1,0:T(8,128)S(1)} %finished_piece.1), channel_id=1, source_target_pairs={{0,2},{2,0},{4,6},{6,4},{1,3},{3,1},{5,7},{7,5},{8,10},{10,8},{12,... | collective-permute-start | bytes 196616 | tf_op jit(solution)/shard_map/ppermute | solution.py:350
  66.9 1.1 %collective-permute-done.22 = f32[128,128]{1,0:T(8,128)S(1)} collective-permute-done((f32[128,128]{1,0:T(8,128)S(1)}, f32[128,128]{1,0:T(8,128)S(1)}, u32[]{:S(2)}, u32[]{:S(2)}) %collective-permute-start.22) | collective-permute-done | bytes 65568 | tf_op jit(solution)/shard_map/ppermute | solution.py:350
  68.0 1.4 %collective-permute-done.21 = f32[128,128]{1,0:T(8,128)S(1)} collective-permute-done((f32[128,128]{1,0:T(8,128)S(1)}, f32[128,128]{1,0:T(8,128)S(1)}, u32[]{:S(2)}, u32[]{:S(2)}) %collective-permute-start.21) | collective-permute-done | bytes 65568 | tf_op jit(solution)/shard_map/ppermute | solution.py:350
  69.4 4.6 %collective-permute-start.23 = (f32[4,128,128]{2,1,0:T(8,128)S(1)}, f32[4,128,128]{2,1,0:T(8,128)S(1)}, u32[]{:S(2)}, u32[]{:S(2)}) collective-permute-start(f32[4,128,128]{2,1,0:T(8,128)S(1)} %pad_maximum_fusion.pieces_ref), channel_id=1, source_target_pairs={{0,1},{1,0},{2,3},{3,2},{4,5},{5,4},{6,7},{7,6},{8,9},{9,8},{10,11... | collective-permute-start | bytes 786440 | tf_op jit(solution)/shard_map/ppermute | solution.py:350
  74.0 1.6 %update_own.1 = (f32[1,2,224,2048]{3,2,1,0:T(8,128)}, f32[2,112,128]{2,1,0:T(8,128)}, f32[2,112,128]{2,1,0:T(8,128)}, bf16[2,112,128]{2,1,0:T(8,128)(2,1)}, f32[2,32,2048]{2,1,0:T(8,128)}) custom-call(f32[4,128,128]{2,1,0:T(8,128)S(1)} %pad_maximum_fusion.pieces_ref, bf16[2,224,96]{2,1,0:T(8,128)(2,1)S(1)} %get-tuple-element.60.hat_ref, ...), custom_call_target="tpu_custom_call" | custom-call | flops 100000000 | bytes 4000000 | tf_op jit(solution)/shard_map/update_own/pallas_call | solution.py:320
  75.7 1.6 %update_other.1 = (f32[1,2,224,2048]{3,2,1,0:T(8,128)}, f32[2,112,128]{2,1,0:T(8,128)}, f32[2,112,128]{2,1,0:T(8,128)}, bf16[2,112,128]{2,1,0:T(8,128)(2,1)}, f32[2,32,2048]{2,1,0:T(8,128)}) custom-call(f32[4,128,128]{2,1,0:T(8,128)S(1)} %collective-permute-done.23.pieces_ref, ...), custom_call_target="tpu_custom_call", output_to_operand_aliasing={{0}: (6, {}), {1}: (7, {}), {2}: (8, {}), {3}: (9, {}), {4}... | custom-call | flops 100000000 | bytes 4000000 | tf_op jit(solution)/shard_map/update_other/pallas_call | solution.py:320
  (42 shorter events, 6.8 us)
Async XLA Ops:
  4.3 24.9 %collective-permute-start.8 = (f32[224,2048]{1,0:T(8,128)S(1)}, f32[224,2048]{1,0:T(8,128)S(1)}, u32[]{:S(2)}, u32[]{:S(2)}) collective-permute-start(f32[224,2048]{1,0:T(8,128)S(1)} %get-tuple-element.44.full_ref), channel_id=1, source_target_pairs={{0,1},{1,0},{2,3},{3,2},{4,5},{5,4},{6,7},{7,6},{8,9},{9,8},{10,11... | collective-permute-start | bytes 5505032 | tf_op jit(solution)/shard_map/ppermute | solution.py:350
  7.6 3.5 %collective-permute-start = (f32[56,128]{1,0:T(8,128)S(1)}, f32[56,128]{1,0:T(8,128)S(1)}, u32[]{:S(2)}, u32[]{:S(2)}) collective-permute-start(f32[56,128]{1,0:T(8,128)S(1)} %get-tuple-element.42), channel_id=1, source_target_pairs={{0,1},{1,0},{2,3},{3,2},{4,5},{5,4},{6,7},{7,6},{8,9},{9,8},{10,11... | collective-permute-start | bytes 86024 | tf_op jit(solution)/shard_map/ppermute | solution.py:350
  11.1 4.2 %collective-permute-start.3 = (f32[112,128]{1,0:T(8,128)S(1)}, f32[112,128]{1,0:T(8,128)S(1)}, u32[]{:S(2)}, u32[]{:S(2)}) collective-permute-start(f32[112,128]{1,0:T(8,128)S(1)} %constant_dynamic-update-slice_fusion), channel_id=1, source_target_pairs={{0,24},{8,16},{16,8},{24,0},{1,25},{9,17},{17,9},{25,1},{2,26},{10... | collective-permute-start | bytes 172040 | tf_op jit(solution)/shard_map/ppermute | solution.py:350
  12.1 4.6 %collective-permute-start.2 = (f32[112,128]{1,0:T(8,128)S(1)}, f32[112,128]{1,0:T(8,128)S(1)}, u32[]{:S(2)}, u32[]{:S(2)}) collective-permute-start(f32[112,128]{1,0:T(8,128)S(1)} %constant_dynamic-update-slice_fusion), channel_id=1, source_target_pairs={{0,16},{8,24},{16,0},{24,8},{1,17},{9,25},{17,1},{25,9},{2,18},{10... | collective-permute-start | bytes 172040 | tf_op jit(solution)/shard_map/ppermute | solution.py:350
  12.4 4.5 %collective-permute-start.1 = (f32[112,128]{1,0:T(8,128)S(1)}, f32[112,128]{1,0:T(8,128)S(1)}, u32[]{:S(2)}, u32[]{:S(2)}) collective-permute-start(f32[112,128]{1,0:T(8,128)S(1)} %constant_dynamic-update-slice_fusion), channel_id=1, source_target_pairs={{0,8},{8,0},{16,24},{24,16},{1,9},{9,1},{17,25},{25,17},{2,10},{10... | collective-permute-start | bytes 172040 | tf_op jit(solution)/shard_map/ppermute | solution.py:350
  16.9 5.7 %collective-permute-start.6 = (f32[112,128]{1,0:T(8,128)S(1)}, f32[112,128]{1,0:T(8,128)S(1)}, u32[]{:S(2)}, u32[]{:S(2)}) collective-permute-start(f32[112,128]{1,0:T(8,128)S(1)} %add_add_fusion.3), channel_id=1, source_target_pairs={{0,96},{32,64},{64,32},{96,0},{128,224},{160,192},{192,160},{224,1... | collective-permute-start | bytes 172040 | tf_op jit(solution)/shard_map/ppermute | solution.py:350
  21.1 4.3 %collective-permute-start.5 = (f32[112,128]{1,0:T(8,128)S(1)}, f32[112,128]{1,0:T(8,128)S(1)}, u32[]{:S(2)}, u32[]{:S(2)}) collective-permute-start(f32[112,128]{1,0:T(8,128)S(1)} %add_add_fusion.3), channel_id=1, source_target_pairs={{0,64},{32,96},{64,0},{96,32},{128,192},{160,224},{192,128},{224,1... | collective-permute-start | bytes 172040 | tf_op jit(solution)/shard_map/ppermute | solution.py:350
  21.1 4.3 %collective-permute-start.4 = (f32[112,128]{1,0:T(8,128)S(1)}, f32[112,128]{1,0:T(8,128)S(1)}, u32[]{:S(2)}, u32[]{:S(2)}) collective-permute-start(f32[112,128]{1,0:T(8,128)S(1)} %add_add_fusion.3), channel_id=1, source_target_pairs={{0,32},{32,0},{64,96},{96,64},{128,160},{160,128},{192,224},{224,1... | collective-permute-start | bytes 172040 | tf_op jit(solution)/shard_map/ppermute | solution.py:350
  25.4 5.9 %collective-permute-start.7 = (f32[112,128]{1,0:T(8,128)S(1)}, f32[112,128]{1,0:T(8,128)S(1)}, u32[]{:S(2)}, u32[]{:S(2)}) collective-permute-start(f32[112,128]{1,0:T(8,128)S(1)} %add_add_fusion.2), channel_id=1, source_target_pairs={{0,192},{32,224},{64,128},{96,160},{128,64},{160,96},{192,0},{224,... | collective-permute-start | bytes 172040 | tf_op jit(solution)/shard_map/ppermute | solution.py:350
  32.1 4.5 %collective-permute-start.11 = (f32[136,128]{1,0:T(8,128)S(1)}, f32[136,128]{1,0:T(8,128)S(1)}, u32[]{:S(2)}, u32[]{:S(2)}) collective-permute-start(f32[136,128]{1,0:T(8,128)S(1)} %get-tuple-element.67), channel_id=1, source_target_pairs={{0,6},{2,4},{4,2},{6,0},{1,7},{3,5},{5,3},{7,1},{8,14},{10,12},{12... | collective-permute-start | bytes 208904 | tf_op jit(solution)/shard_map/ppermute | solution.py:350
  34.6 4.7 %collective-permute-start.10 = (f32[136,128]{1,0:T(8,128)S(1)}, f32[136,128]{1,0:T(8,128)S(1)}, u32[]{:S(2)}, u32[]{:S(2)}) collective-permute-start(f32[136,128]{1,0:T(8,128)S(1)} %get-tuple-element.68), channel_id=1, source_target_pairs={{0,4},{2,6},{4,0},{6,2},{1,5},{3,7},{5,1},{7,3},{8,12},{10,14},{12... | collective-permute-start | bytes 208904 | tf_op jit(solution)/shard_map/ppermute | solution.py:350
  35.2 4.2 %collective-permute-start.9 = (f32[136,128]{1,0:T(8,128)S(1)}, f32[136,128]{1,0:T(8,128)S(1)}, u32[]{:S(2)}, u32[]{:S(2)}) collective-permute-start(f32[136,128]{1,0:T(8,128)S(1)} %get-tuple-element.69), channel_id=1, source_target_pairs={{0,2},{2,0},{4,6},{6,4},{1,3},{3,1},{5,7},{7,5},{8,10},{10,8},{12,... | collective-permute-start | bytes 208904 | tf_op jit(solution)/shard_map/ppermute | solution.py:350
  35.9 38.1 %copy-start = (f32[2,112,128]{2,1,0:T(8,128)S(1)}, f32[2,112,128]{2,1,0:T(8,128)}, u32[]{:S(2)}) copy-start(f32[2,112,128]{2,1,0:T(8,128)} %m1_ref.3) | copy-start | bytes 344068
  35.9 38.1 %copy-start.1 = (f32[2,112,128]{2,1,0:T(8,128)S(1)}, f32[2,112,128]{2,1,0:T(8,128)}, u32[]{:S(2)}) copy-start(f32[2,112,128]{2,1,0:T(8,128)} %m2_ref.3) | copy-start | bytes 344068
  39.3 5.6 %collective-permute-start.13 = (f32[128,128]{1,0:T(8,128)S(1)}, f32[128,128]{1,0:T(8,128)S(1)}, u32[]{:S(2)}, u32[]{:S(2)}) collective-permute-start(f32[128,128]{1,0:T(8,128)S(1)} %slice.19), channel_id=1, source_target_pairs={{0,16},{8,24},{16,0},{24,8},{1,17},{9,25},{17,1},{25,9},{2,18},{10... | collective-permute-start | bytes 196616 | tf_op jit(solution)/shard_map/ppermute | solution.py:350
  41.3 4.3 %collective-permute-start.14 = (f32[128,128]{1,0:T(8,128)S(1)}, f32[128,128]{1,0:T(8,128)S(1)}, u32[]{:S(2)}, u32[]{:S(2)}) collective-permute-start(f32[128,128]{1,0:T(8,128)S(1)} %slice.19), channel_id=1, source_target_pairs={{0,24},{8,16},{16,8},{24,0},{1,25},{9,17},{17,9},{25,1},{2,26},{10... | collective-permute-start | bytes 196616 | tf_op jit(solution)/shard_map/ppermute | solution.py:350
  41.9 3.8 %collective-permute-start.12 = (f32[128,128]{1,0:T(8,128)S(1)}, f32[128,128]{1,0:T(8,128)S(1)}, u32[]{:S(2)}, u32[]{:S(2)}) collective-permute-start(f32[128,128]{1,0:T(8,128)S(1)} %slice.19), channel_id=1, source_target_pairs={{0,8},{8,0},{16,24},{24,16},{1,9},{9,1},{17,25},{25,17},{2,10},{10... | collective-permute-start | bytes 196616 | tf_op jit(solution)/shard_map/ppermute | solution.py:350
  45.7 11.5 %collective-permute-start.17 = (f32[128,128]{1,0:T(8,128)S(1)}, f32[128,128]{1,0:T(8,128)S(1)}, u32[]{:S(2)}, u32[]{:S(2)}) collective-permute-start(f32[128,128]{1,0:T(8,128)S(1)} %add_add_fusion.1), channel_id=1, source_target_pairs={{0,96},{32,64},{64,32},{96,0},{128,224},{160,192},{192,160},{224,1... | collective-permute-start | bytes 196616 | tf_op jit(solution)/shard_map/ppermute | solution.py:350
  47.6 9.6 %collective-permute-start.16 = (f32[128,128]{1,0:T(8,128)S(1)}, f32[128,128]{1,0:T(8,128)S(1)}, u32[]{:S(2)}, u32[]{:S(2)}) collective-permute-start(f32[128,128]{1,0:T(8,128)S(1)} %add_add_fusion.1), channel_id=1, source_target_pairs={{0,64},{32,96},{64,0},{96,32},{128,192},{160,224},{192,128},{224,1... | collective-permute-start | bytes 196616 | tf_op jit(solution)/shard_map/ppermute | solution.py:350
  48.9 8.3 %collective-permute-start.15 = (f32[128,128]{1,0:T(8,128)S(1)}, f32[128,128]{1,0:T(8,128)S(1)}, u32[]{:S(2)}, u32[]{:S(2)}) collective-permute-start(f32[128,128]{1,0:T(8,128)S(1)} %add_add_fusion.1), channel_id=1, source_target_pairs={{0,32},{32,0},{64,96},{96,64},{128,160},{160,128},{192,224},{224,1... | collective-permute-start | bytes 196616 | tf_op jit(solution)/shard_map/ppermute | solution.py:350
  50.0 8.1 %collective-permute-start.18 = (f32[56,128]{1,0:T(8,128)S(1)}, f32[56,128]{1,0:T(8,128)S(1)}, u32[]{:S(2)}, u32[]{:S(2)}) collective-permute-start(f32[56,128]{1,0:T(8,128)S(1)} %get-tuple-element.53), channel_id=1, source_target_pairs={{0,1},{1,0},{2,3},{3,2},{4,5},{5,4},{6,7},{7,6},{8,9},{9,8},{10,11... | collective-permute-start | bytes 86024 | tf_op jit(solution)/shard_map/ppermute | solution.py:350
  58.1 5.3 %collective-permute-start.19 = (f32[128,128]{1,0:T(8,128)S(1)}, f32[128,128]{1,0:T(8,128)S(1)}, u32[]{:S(2)}, u32[]{:S(2)}) collective-permute-start(f32[128,128]{1,0:T(8,128)S(1)} %add_add_fusion.a_ref), channel_id=1, source_target_pairs={{0,192},{32,224},{64,128},{96,160},{128,64},{160,96},{192,0},{224,... | collective-permute-start | bytes 196616 | tf_op jit(solution)/shard_map/ppermute | solution.py:350
  63.6 4.3 %collective-permute-start.22 = (f32[128,128]{1,0:T(8,128)S(1)}, f32[128,128]{1,0:T(8,128)S(1)}, u32[]{:S(2)}, u32[]{:S(2)}) collective-permute-start(f32[128,128]{1,0:T(8,128)S(1)} %finished_piece.1), channel_id=1, source_target_pairs={{0,6},{2,4},{4,2},{6,0},{1,7},{3,5},{5,3},{7,1},{8,14},{10,12},{12... | collective-permute-start | bytes 196616 | tf_op jit(solution)/shard_map/ppermute | solution.py:350
  64.8 4.6 %collective-permute-start.21 = (f32[128,128]{1,0:T(8,128)S(1)}, f32[128,128]{1,0:T(8,128)S(1)}, u32[]{:S(2)}, u32[]{:S(2)}) collective-permute-start(f32[128,128]{1,0:T(8,128)S(1)} %finished_piece.1), channel_id=1, source_target_pairs={{0,4},{2,6},{4,0},{6,2},{1,5},{3,7},{5,1},{7,3},{8,12},{10,14},{12... | collective-permute-start | bytes 196616 | tf_op jit(solution)/shard_map/ppermute | solution.py:350
  65.5 3.9 %collective-permute-start.20 = (f32[128,128]{1,0:T(8,128)S(1)}, f32[128,128]{1,0:T(8,128)S(1)}, u32[]{:S(2)}, u32[]{:S(2)}) collective-permute-start(f32[128,128]{1,0:T(8,128)S(1)} %finished_piece.1), channel_id=1, source_target_pairs={{0,2},{2,0},{4,6},{6,4},{1,3},{3,1},{5,7},{7,5},{8,10},{10,8},{12,... | collective-permute-start | bytes 196616 | tf_op jit(solution)/shard_map/ppermute | solution.py:350
  69.4 6.3 %collective-permute-start.23 = (f32[4,128,128]{2,1,0:T(8,128)S(1)}, f32[4,128,128]{2,1,0:T(8,128)S(1)}, u32[]{:S(2)}, u32[]{:S(2)}) collective-permute-start(f32[4,128,128]{2,1,0:T(8,128)S(1)} %pad_maximum_fusion.pieces_ref), channel_id=1, source_target_pairs={{0,1},{1,0},{2,3},{3,2},{4,5},{5,4},{6,7},{7,6},{8,9},{9,8},{10,11... | collective-permute-start | bytes 786440 | tf_op jit(solution)/shard_map/ppermute | solution.py:350

commit v11 on v9

--- a/solution.py
+++ b/solution.py
@@ -412,17 +412,15 @@
     piece = finished_piece(q, far, inverse, replicas)
     side = (hat, rows, (own_full, other_full), (moment1, moment2))
     own0 = piece[None]
-    other0 = swap(own0, "c", 1)
     own3, own2, own1 = (swap(own0, "x", i) for i in (3, 2, 1))
-    other3 = swap(own3, "c", 1)
-    err = update([(0, 0, own0, 0), (1, 0, other0, 0)], None, *side, "update_first")
-    err = update([(0, 3, own3, 0)], None, *side, "update_second", err)
-    own1, own2, other3, err = lax.optimization_barrier((own1, own2, other3, err))
-    last = swap(jnp.concatenate([own1, own2]), "c", 1)
+    err = update([(0, 0, own0, 0), (0, 3, own3, 0)], None, *side, "update_first")
+    own1, own2, err = lax.optimization_barrier((own1, own2, err))
+    last = swap(jnp.concatenate([own0, own1, own2, own3]), "c", 1)
     sources = [(own0, 0), (own1, 0), (own2, 0), (own3, 0)]
-    done = update([(0, 1, own1, 0), (0, 2, own2, 0), (1, 3, other3, 0)], (0, sources), *side, "update_third", err)
-    sources = [(other0, 0), (last, 0), (last, 1), (other3, 0)]
-    return tuple(update([(1, 1, last, 0), (1, 2, last, 1)], (1, sources), *side, "update_fourth", done))
+    done = update([(0, 1, own1, 0), (0, 2, own2, 0)], (0, sources), *side, "update_second", err)
+    sources = [(last, i) for i in range(4)]
+    blocks = [(1, i, last, i) for i in range(4)]
+    return tuple(update(blocks, (1, sources), *side, "update_third", done))
 
 
 def solution(mesh):

time: 74.7 us -> 74.2 us (level)
  waiting for transfers between devices: 14.9 us -> 16.2 us
  starting transfers between devices: 44.7 us -> 43.6 us
  Pallas kernels: 14 us -> 13.2 us
    ppermute x26 -> x24, waiting for transfers between devices: 14.9 us -> 16.2 us  [swap(): lax.ppermute(value, axis, [(i, i ^ bit) for i in range(lax.axis_size(axis...]
    ppermute x26 -> x24, starting transfers between devices: 44.7 us -> 43.6 us  [swap(): lax.ppermute(value, axis, [(i, i ^ bit) for i in range(lax.axis_size(axis...]
    pallas_call x4 -> x3, Pallas kernels: 4.92 us -> 4.09 us  [update(): pl.pallas_call(functools.partial(update_kernel, counts, blocks, adam), in...]
  transfers between devices with their start and end apart: 26 -> 24, of which waited for: 11 -> 13; matrix products, arithmetic and copies ran while one was open for 0% -> 0% of each run, Pallas kernels for 12% -> 10%
where the time goes in v11:
time: 74.2 us; the launch traced here: 74.1 us
  starting transfers between devices  43.6 us (59%)
  waiting for transfers between devices  16.2 us (22%)
  Pallas kernels  13.2 us (18%)
  between operations  0.92 us (1%)
    ppermute x24, starting transfers between devices, swap(): lax.ppermute(value, axis, [(i, i ^ bit) for i in range(lax.axis_size(axis...  43.6 us
    ppermute x24, waiting for transfers between devices, swap(): lax.ppermute(value, axis, [(i, i ^ bit) for i in range(lax.axis_size(axis...  16.2 us
    pallas_call x3, Pallas kernels, update(): pl.pallas_call(functools.partial(update_kernel, counts, blocks, adam), in...  4.09 us
    pallas_call x1, Pallas kernels, inverse_factor(): pl.pallas_call(factor_kernel, in_specs=[WHOLE], out_specs=WHOLE, out_shap...  2.85 us
    pallas_call x1, Pallas kernels, load(): pl.pallas_call(load_kernel, in_specs=[AWAY] * 3, out_specs=[WHOLE] * 5, o...  2.84 us
  transfers between devices with their start and end apart: 24, of which 13 were waited for; matrix products, arithmetic and copies ran while one was open for 0% of the time, Pallas kernels for 10%

profile of v11, /device:TPU:1, one launch (start us, length us, event | category | flops | bytes accessed | tf_op | source)
XLA Modules:
  0.0 74.1 jit_solution(18189305481457156007)
XLA Ops:
  0.6 2.8 %load.1 = (f32[224,2048]{1,0:T(8,128)S(1)}, f32[56,128]{1,0:T(8,128)S(1)}, bf16[224,2048]{1,0:T(8,128)(2,1)S(1)}, f32[224,2048]{1,0:T(8,128)S(1)}, f32[32,2048]{1,0:T(8,128)S(1)}) custom-call(bf16[1,2,224,2048]{3,2,1,0:T(8,128)(2,1)} %grads_hbm.1, f32[1,2,224,2048]{3,2,1,0:T(8,128)} %errors_hbm.1, f32[2,32,2048]{2,1,0:T(8,128)} %q_hbm.1), custom_call_target="tpu_custom_call" | custom-call | tf_op jit(solution)/shard_map/load/pallas_call | solution.py:89
  3.5 3.3 %collective-permute-start = (f32[56,128]{1,0:T(8,128)S(1)}, f32[56,128]{1,0:T(8,128)S(1)}, u32[]{:S(2)}, u32[]{:S(2)}) collective-permute-start(f32[56,128]{1,0:T(8,128)S(1)} %get-tuple-element.43), channel_id=1, source_target_pairs={{0,1},{1,0},{2,3},{3,2},{4,5},{5,4},{6,7},{7,6},{8,9},{9,8},{10,11... | collective-permute-start | bytes 86024 | tf_op jit(solution)/shard_map/ppermute | solution.py:382
  6.8 0.8 %left_own.1 = (f32[224,2048]{1,0:T(8,128)S(1)}, f32[56,128]{1,0:T(8,128)S(1)}) custom-call(bf16[224,2048]{1,0:T(8,128)(2,1)S(1)} %get-tuple-element.39.grads_ref, f32[224,2048]{1,0:T(8,128)S(1)} %get-tuple-element.40.errors_ref, f32[32,2048]{1,0:T(8,128)S(1)} %get-tuple-element.41.q_ref), custom_call_target="tpu_custom_call" | custom-call | flops 100000000 | bytes 3000000 | tf_op jit(solution)/shard_map/left_own/pallas_call | solution.py:120
  8.0 1.0 %collective-permute-start.3 = (f32[112,128]{1,0:T(8,128)S(1)}, f32[112,128]{1,0:T(8,128)S(1)}, u32[]{:S(2)}, u32[]{:S(2)}) collective-permute-start(f32[112,128]{1,0:T(8,128)S(1)} %pad_maximum_fusion.1), channel_id=1, source_target_pairs={{0,24},{8,16},{16,8},{24,0},{1,25},{9,17},{17,9},{25,1},{2,26},{10... | collective-permute-start | bytes 172040 | tf_op jit(solution)/shard_map/ppermute | solution.py:382
  9.4 1.9 %collective-permute-start.1 = (f32[112,128]{1,0:T(8,128)S(1)}, f32[112,128]{1,0:T(8,128)S(1)}, u32[]{:S(2)}, u32[]{:S(2)}) collective-permute-start(f32[112,128]{1,0:T(8,128)S(1)} %pad_maximum_fusion.1), channel_id=1, source_target_pairs={{0,8},{8,0},{16,24},{24,16},{1,9},{9,1},{17,25},{25,17},{2,10},{10... | collective-permute-start | bytes 172040 | tf_op jit(solution)/shard_map/ppermute | solution.py:382
  11.3 1.0 %collective-permute-done.3 = f32[112,128]{1,0:T(8,128)S(1)} collective-permute-done((f32[112,128]{1,0:T(8,128)S(1)}, f32[112,128]{1,0:T(8,128)S(1)}, u32[]{:S(2)}, u32[]{:S(2)}) %collective-permute-start.3) | collective-permute-done | bytes 57376 | tf_op jit(solution)/shard_map/ppermute | solution.py:382
  12.3 1.3 %collective-permute-done.2 = f32[112,128]{1,0:T(8,128)S(1)} collective-permute-done((f32[112,128]{1,0:T(8,128)S(1)}, f32[112,128]{1,0:T(8,128)S(1)}, u32[]{:S(2)}, u32[]{:S(2)}) %collective-permute-start.2) | collective-permute-done | bytes 57376 | tf_op jit(solution)/shard_map/ppermute | solution.py:382
  13.7 4.3 %collective-permute-start.6 = (f32[112,128]{1,0:T(8,128)S(1)}, f32[112,128]{1,0:T(8,128)S(1)}, u32[]{:S(2)}, u32[]{:S(2)}) collective-permute-start(f32[112,128]{1,0:T(8,128)S(1)} %add_add_fusion.3), channel_id=1, source_target_pairs={{0,96},{32,64},{64,32},{96,0},{128,224},{160,192},{192,160},{224,1... | collective-permute-start | bytes 172040 | tf_op jit(solution)/shard_map/ppermute | solution.py:382
  18.4 1.2 %collective-permute-done.6 = f32[112,128]{1,0:T(8,128)S(1)} collective-permute-done((f32[112,128]{1,0:T(8,128)S(1)}, f32[112,128]{1,0:T(8,128)S(1)}, u32[]{:S(2)}, u32[]{:S(2)}) %collective-permute-start.6) | collective-permute-done | bytes 57376 | tf_op jit(solution)/shard_map/ppermute | solution.py:382
  19.6 2.7 %collective-permute-done.5 = f32[112,128]{1,0:T(8,128)S(1)} collective-permute-done((f32[112,128]{1,0:T(8,128)S(1)}, f32[112,128]{1,0:T(8,128)S(1)}, u32[]{:S(2)}, u32[]{:S(2)}) %collective-permute-start.5) | collective-permute-done | bytes 57376 | tf_op jit(solution)/shard_map/ppermute | solution.py:382
  22.3 3.9 %collective-permute-start.7 = (f32[112,128]{1,0:T(8,128)S(1)}, f32[112,128]{1,0:T(8,128)S(1)}, u32[]{:S(2)}, u32[]{:S(2)}) collective-permute-start(f32[112,128]{1,0:T(8,128)S(1)} %add_add_fusion.2), channel_id=1, source_target_pairs={{0,192},{32,224},{64,128},{96,160},{128,64},{160,96},{192,0},{224,... | collective-permute-start | bytes 172040 | tf_op jit(solution)/shard_map/ppermute | solution.py:382
  26.7 1.6 %collective-permute-done.7 = f32[112,128]{1,0:T(8,128)S(1)} collective-permute-done((f32[112,128]{1,0:T(8,128)S(1)}, f32[112,128]{1,0:T(8,128)S(1)}, u32[]{:S(2)}, u32[]{:S(2)}) %collective-permute-start.7) | collective-permute-done | bytes 57376 | tf_op jit(solution)/shard_map/ppermute | solution.py:382
  28.2 0.9 %right_terms.1 = f32[4,136,128]{2,1,0:T(8,128)S(1)} custom-call(f32[112,128]{1,0:T(8,128)S(1)} %add.54.p_ref, bf16[448,2048]{1,0:T(8,128)(2,1)S(1)} %get-tuple-element.51.hi_ref, bf16[448,2048]{1,0:T(8,128)(2,1)S(1)} %get-tuple-element.52.lo_ref), custom_call_target="tpu_custom_call" | custom-call | tf_op jit(solution)/shard_map/right_terms/pallas_call | solution.py:174
  29.2 2.6 %collective-permute-start.11 = (f32[136,128]{1,0:T(8,128)S(1)}, f32[136,128]{1,0:T(8,128)S(1)}, u32[]{:S(2)}, u32[]{:S(2)}) collective-permute-start(f32[136,128]{1,0:T(8,128)S(1)} %get-tuple-element.73), channel_id=1, source_target_pairs={{0,6},{2,4},{4,2},{6,0},{1,7},{3,5},{5,3},{7,1},{8,14},{10,12},{12... | collective-permute-start | bytes 208904 | tf_op jit(solution)/shard_map/ppermute | solution.py:382
  32.5 1.1 %collective-permute-done.11 = f32[136,128]{1,0:T(8,128)S(1)} collective-permute-done((f32[136,128]{1,0:T(8,128)S(1)}, f32[136,128]{1,0:T(8,128)S(1)}, u32[]{:S(2)}, u32[]{:S(2)}) %collective-permute-start.11) | collective-permute-done | bytes 69664 | tf_op jit(solution)/shard_map/ppermute | solution.py:382
  33.6 2.8 %collective-permute-done.10 = f32[136,128]{1,0:T(8,128)S(1)} collective-permute-done((f32[136,128]{1,0:T(8,128)S(1)}, f32[136,128]{1,0:T(8,128)S(1)}, u32[]{:S(2)}, u32[]{:S(2)}) %collective-permute-start.10) | collective-permute-done | bytes 69664 | tf_op jit(solution)/shard_map/ppermute | solution.py:382
  36.4 2.0 %collective-permute-start.13 = (f32[128,128]{1,0:T(8,128)S(1)}, f32[128,128]{1,0:T(8,128)S(1)}, u32[]{:S(2)}, u32[]{:S(2)}) collective-permute-start(f32[128,128]{1,0:T(8,128)S(1)} %slice.24), channel_id=1, source_target_pairs={{0,16},{8,24},{16,0},{24,8},{1,17},{9,25},{17,1},{25,9},{2,18},{10... | collective-permute-start | bytes 196616 | tf_op jit(solution)/shard_map/ppermute | solution.py:382
  39.2 2.8 %inverse_factor.1.inverse_ref = f32[8,128]{1,0:T(8,128)S(1)} custom-call(f32[136,128]{1,0:T(8,128)S(1)} %fusion.1.sum_ref), custom_call_target="tpu_custom_call" | custom-call | flops 4000000 | bytes 4000000 | tf_op jit(solution)/shard_map/inverse_factor/pallas_call | solution.py:203
  42.0 0.7 collective-permute-done.14
  42.8 1.7 %collective-permute-start.17 = (f32[128,128]{1,0:T(8,128)S(1)}, f32[128,128]{1,0:T(8,128)S(1)}, u32[]{:S(2)}, u32[]{:S(2)}) collective-permute-start(f32[128,128]{1,0:T(8,128)S(1)} %add_add_fusion.1), channel_id=1, source_target_pairs={{0,96},{32,64},{64,32},{96,0},{128,224},{160,192},{192,160},{224,1... | collective-permute-start | bytes 196616 | tf_op jit(solution)/shard_map/ppermute | solution.py:382
  44.5 1.8 %collective-permute-start.16 = (f32[128,128]{1,0:T(8,128)S(1)}, f32[128,128]{1,0:T(8,128)S(1)}, u32[]{:S(2)}, u32[]{:S(2)}) collective-permute-start(f32[128,128]{1,0:T(8,128)S(1)} %add_add_fusion.1), channel_id=1, source_target_pairs={{0,64},{32,96},{64,0},{96,32},{128,192},{160,224},{192,128},{224,1... | collective-permute-start | bytes 196616 | tf_op jit(solution)/shard_map/ppermute | solution.py:382
  46.9 7.2 %collective-permute-start.18 = (f32[56,128]{1,0:T(8,128)S(1)}, f32[56,128]{1,0:T(8,128)S(1)}, u32[]{:S(2)}, u32[]{:S(2)}) collective-permute-start(f32[56,128]{1,0:T(8,128)S(1)} %get-tuple-element.56), channel_id=1, source_target_pairs={{0,1},{1,0},{2,3},{3,2},{4,5},{5,4},{6,7},{7,6},{8,9},{9,8},{10,11... | collective-permute-start | bytes 86024 | tf_op jit(solution)/shard_map/ppermute | solution.py:382
  54.1 0.8 %collective-permute-done.18.other_ref = f32[56,128]{1,0:T(8,128)S(1)} collective-permute-done((f32[56,128]{1,0:T(8,128)S(1)}, f32[56,128]{1,0:T(8,128)S(1)}, u32[]{:S(2)}, u32[]{:S(2)}) %collective-permute-start.18) | collective-permute-done | bytes 28704 | tf_op jit(solution)/shard_map/ppermute | solution.py:382
  54.9 3.4 %collective-permute-start.19 = (f32[128,128]{1,0:T(8,128)S(1)}, f32[128,128]{1,0:T(8,128)S(1)}, u32[]{:S(2)}, u32[]{:S(2)}) collective-permute-start(f32[128,128]{1,0:T(8,128)S(1)} %add_add_fusion.a_ref), channel_id=1, source_target_pairs={{0,192},{32,224},{64,128},{96,160},{128,64},{160,96},{192,0},{224,... | collective-permute-start | bytes 196616 | tf_op jit(solution)/shard_map/ppermute | solution.py:382
  58.8 1.5 %collective-permute-done.19.b_ref = f32[128,128]{1,0:T(8,128)S(1)} collective-permute-done((f32[128,128]{1,0:T(8,128)S(1)}, f32[128,128]{1,0:T(8,128)S(1)}, u32[]{:S(2)}, u32[]{:S(2)}) %collective-permute-start.19) | collective-permute-done | bytes 65568 | tf_op jit(solution)/shard_map/ppermute | solution.py:382
  60.5 1.2 %collective-permute-start.22 = (f32[1,128,128]{2,1,0:T(8,128)S(1)}, f32[1,128,128]{2,1,0:T(8,128)S(1)}, u32[]{:S(2)}, u32[]{:S(2)}) collective-permute-start(f32[1,128,128]{2,1,0:T(8,128)S(1)} %bitcast.13), channel_id=1, source_target_pairs={{0,6},{2,4},{4,2},{6,0},{1,7},{3,5},{5,3},{7,1},{8,14},{10,12},{12... | collective-permute-start | bytes 196616 | tf_op jit(solution)/shard_map/ppermute | solution.py:382
  62.4 1.4 %collective-permute-start.20 = (f32[1,128,128]{2,1,0:T(8,128)S(1)}, f32[1,128,128]{2,1,0:T(8,128)S(1)}, u32[]{:S(2)}, u32[]{:S(2)}) collective-permute-start(f32[1,128,128]{2,1,0:T(8,128)S(1)} %bitcast.15), channel_id=1, source_target_pairs={{0,2},{2,0},{4,6},{6,4},{1,3},{3,1},{5,7},{7,5},{8,10},{10,8},{12,... | collective-permute-start | bytes 196616 | tf_op jit(solution)/shard_map/ppermute | solution.py:382
  63.9 1.1 %collective-permute-done.22.refs_1_.refs_3_ = f32[1,128,128]{2,1,0:T(8,128)S(1)} collective-permute-done((f32[1,128,128]{2,1,0:T(8,128)S(1)}, f32[1,128,128]{2,1,0:T(8,128)S(1)}, u32[]{:S(2)}, u32[]{:S(2)}) %collective-permute-start.22) | collective-permute-done | bytes 65568 | tf_op jit(solution)/shard_map/ppermute | solution.py:382
  64.9 1.1 %update_first.1.refs_10_ = f32[1,2,224,2048]{3,2,1,0:T(8,128)} custom-call(f32[1,128,128]{2,1,0:T(8,128)S(1)} %bitcast.16, f32[1,128,128]{2,1,0:T(8,128)S(1)} %collective-permute-done.22.refs_1_.refs_3_, bf16[2,224,96]{2,1,0:T(8,128)(2,1)S(1)} %get-tuple-element.63.refs_2_.refs_4_.refs_1_, bf16[2,16,96]{2,1,0:T(8,128)(2,1)S(1)} %get-tuple-element.64.refs_3_.refs_5_.refs_2_, ...), custom_call_target="tpu_custom_call" | custom-call | flops 40000000 | bytes 2000000 | tf_op jit(solution)/shard_map/update_first/pallas_call | solution.py:368
  66.4 4.6 %collective-permute-start.23 = (f32[4,128,128]{2,1,0:T(8,128)S(1)}, f32[4,128,128]{2,1,0:T(8,128)S(1)}, u32[]{:S(2)}, u32[]{:S(2)}) collective-permute-start(f32[4,128,128]{2,1,0:T(8,128)S(1)} %pad_maximum_fusion), channel_id=1, source_target_pairs={{0,1},{1,0},{2,3},{3,2},{4,5},{5,4},{6,7},{7,6},{8,9},{9,8},{10,11... | collective-permute-start | bytes 786440 | tf_op jit(solution)/shard_map/ppermute | solution.py:382
  71.0 1.3 %update_second.1 = (f32[1,2,224,2048]{3,2,1,0:T(8,128)}, f32[2,112,128]{2,1,0:T(8,128)}, f32[2,112,128]{2,1,0:T(8,128)}, bf16[2,112,128]{2,1,0:T(8,128)(2,1)}, f32[2,32,2048]{2,1,0:T(8,128)}) custom-call(f32[1,128,128]{2,1,0:T(8,128)S(1)} %collective-permute-done.20.refs_0_, ...), custom_call_target="tpu_custom_call", output_to_operand_aliasing={{0}: (10, {})} | custom-call | flops 40000000 | bytes 2000000 | tf_op jit(solution)/shard_map/update_second/pallas_call | solution.py:368
  72.3 1.6 %update_third.1 = (f32[1,2,224,2048]{3,2,1,0:T(8,128)}, f32[2,112,128]{2,1,0:T(8,128)}, f32[2,112,128]{2,1,0:T(8,128)}, bf16[2,112,128]{2,1,0:T(8,128)(2,1)}, f32[2,32,2048]{2,1,0:T(8,128)}) custom-call(f32[4,128,128]{2,1,0:T(8,128)S(1)} %collective-permute-done.23.refs_0_, ...), custom_call_target="tpu_custom_call", output_to_operand_aliasing={{0}: (7, {}), {1}: (8, {}), {2}: (9, {}), {3}: (10, {}), {4... | custom-call | flops 80000000 | bytes 4000000 | tf_op jit(solution)/shard_map/update_third/pallas_call | solution.py:368
  (41 shorter events, 5.7 us)
Async XLA Ops:
  3.5 4.2 %collective-permute-start = (f32[56,128]{1,0:T(8,128)S(1)}, f32[56,128]{1,0:T(8,128)S(1)}, u32[]{:S(2)}, u32[]{:S(2)}) collective-permute-start(f32[56,128]{1,0:T(8,128)S(1)} %get-tuple-element.43), channel_id=1, source_target_pairs={{0,1},{1,0},{2,3},{3,2},{4,5},{5,4},{6,7},{7,6},{8,9},{9,8},{10,11... | collective-permute-start | bytes 86024 | tf_op jit(solution)/shard_map/ppermute | solution.py:382
  7.7 18.5 %collective-permute-start.8 = (f32[224,2048]{1,0:T(8,128)S(1)}, f32[224,2048]{1,0:T(8,128)S(1)}, u32[]{:S(2)}, u32[]{:S(2)}) collective-permute-start(f32[224,2048]{1,0:T(8,128)S(1)} %get-tuple-element.47.refs_5_.refs_7_.refs_4_), channel_id=1, source_target_pairs={{0,1},{1,0},{2,3},{3,2},{4,5},{5,4},{6,7},{7,6},{8,9},{9,8},{10,11... | collective-permute-start | bytes 5505032 | tf_op jit(solution)/shard_map/ppermute | solution.py:382
  8.0 4.2 %collective-permute-start.3 = (f32[112,128]{1,0:T(8,128)S(1)}, f32[112,128]{1,0:T(8,128)S(1)}, u32[]{:S(2)}, u32[]{:S(2)}) collective-permute-start(f32[112,128]{1,0:T(8,128)S(1)} %pad_maximum_fusion.1), channel_id=1, source_target_pairs={{0,24},{8,16},{16,8},{24,0},{1,25},{9,17},{17,9},{25,1},{2,26},{10... | collective-permute-start | bytes 172040 | tf_op jit(solution)/shard_map/ppermute | solution.py:382
  9.0 4.5 %collective-permute-start.2 = (f32[112,128]{1,0:T(8,128)S(1)}, f32[112,128]{1,0:T(8,128)S(1)}, u32[]{:S(2)}, u32[]{:S(2)}) collective-permute-start(f32[112,128]{1,0:T(8,128)S(1)} %pad_maximum_fusion.1), channel_id=1, source_target_pairs={{0,16},{8,24},{16,0},{24,8},{1,17},{9,25},{17,1},{25,9},{2,18},{10... | collective-permute-start | bytes 172040 | tf_op jit(solution)/shard_map/ppermute | solution.py:382
  9.4 4.3 %collective-permute-start.1 = (f32[112,128]{1,0:T(8,128)S(1)}, f32[112,128]{1,0:T(8,128)S(1)}, u32[]{:S(2)}, u32[]{:S(2)}) collective-permute-start(f32[112,128]{1,0:T(8,128)S(1)} %pad_maximum_fusion.1), channel_id=1, source_target_pairs={{0,8},{8,0},{16,24},{24,16},{1,9},{9,1},{17,25},{25,17},{2,10},{10... | collective-permute-start | bytes 172040 | tf_op jit(solution)/shard_map/ppermute | solution.py:382
  13.7 5.8 %collective-permute-start.6 = (f32[112,128]{1,0:T(8,128)S(1)}, f32[112,128]{1,0:T(8,128)S(1)}, u32[]{:S(2)}, u32[]{:S(2)}) collective-permute-start(f32[112,128]{1,0:T(8,128)S(1)} %add_add_fusion.3), channel_id=1, source_target_pairs={{0,96},{32,64},{64,32},{96,0},{128,224},{160,192},{192,160},{224,1... | collective-permute-start | bytes 172040 | tf_op jit(solution)/shard_map/ppermute | solution.py:382
  18.0 4.3 %collective-permute-start.5 = (f32[112,128]{1,0:T(8,128)S(1)}, f32[112,128]{1,0:T(8,128)S(1)}, u32[]{:S(2)}, u32[]{:S(2)}) collective-permute-start(f32[112,128]{1,0:T(8,128)S(1)} %add_add_fusion.3), channel_id=1, source_target_pairs={{0,64},{32,96},{64,0},{96,32},{128,192},{160,224},{192,128},{224,1... | collective-permute-start | bytes 172040 | tf_op jit(solution)/shard_map/ppermute | solution.py:382
  18.0 4.3 %collective-permute-start.4 = (f32[112,128]{1,0:T(8,128)S(1)}, f32[112,128]{1,0:T(8,128)S(1)}, u32[]{:S(2)}, u32[]{:S(2)}) collective-permute-start(f32[112,128]{1,0:T(8,128)S(1)} %add_add_fusion.3), channel_id=1, source_target_pairs={{0,32},{32,0},{64,96},{96,64},{128,160},{160,128},{192,224},{224,1... | collective-permute-start | bytes 172040 | tf_op jit(solution)/shard_map/ppermute | solution.py:382
  22.3 5.9 %collective-permute-start.7 = (f32[112,128]{1,0:T(8,128)S(1)}, f32[112,128]{1,0:T(8,128)S(1)}, u32[]{:S(2)}, u32[]{:S(2)}) collective-permute-start(f32[112,128]{1,0:T(8,128)S(1)} %add_add_fusion.2), channel_id=1, source_target_pairs={{0,192},{32,224},{64,128},{96,160},{128,64},{160,96},{192,0},{224,... | collective-permute-start | bytes 172040 | tf_op jit(solution)/shard_map/ppermute | solution.py:382
  29.2 4.5 %collective-permute-start.11 = (f32[136,128]{1,0:T(8,128)S(1)}, f32[136,128]{1,0:T(8,128)S(1)}, u32[]{:S(2)}, u32[]{:S(2)}) collective-permute-start(f32[136,128]{1,0:T(8,128)S(1)} %get-tuple-element.73), channel_id=1, source_target_pairs={{0,6},{2,4},{4,2},{6,0},{1,7},{3,5},{5,3},{7,1},{8,14},{10,12},{12... | collective-permute-start | bytes 208904 | tf_op jit(solution)/shard_map/ppermute | solution.py:382
  31.7 4.7 %collective-permute-start.10 = (f32[136,128]{1,0:T(8,128)S(1)}, f32[136,128]{1,0:T(8,128)S(1)}, u32[]{:S(2)}, u32[]{:S(2)}) collective-permute-start(f32[136,128]{1,0:T(8,128)S(1)} %get-tuple-element.74), channel_id=1, source_target_pairs={{0,4},{2,6},{4,0},{6,2},{1,5},{3,7},{5,1},{7,3},{8,12},{10,14},{12... | collective-permute-start | bytes 208904 | tf_op jit(solution)/shard_map/ppermute | solution.py:382
  32.3 4.1 %collective-permute-start.9 = (f32[136,128]{1,0:T(8,128)S(1)}, f32[136,128]{1,0:T(8,128)S(1)}, u32[]{:S(2)}, u32[]{:S(2)}) collective-permute-start(f32[136,128]{1,0:T(8,128)S(1)} %get-tuple-element.75), channel_id=1, source_target_pairs={{0,2},{2,0},{4,6},{6,4},{1,3},{3,1},{5,7},{7,5},{8,10},{10,8},{12,... | collective-permute-start | bytes 208904 | tf_op jit(solution)/shard_map/ppermute | solution.py:382
  36.4 5.6 %collective-permute-start.13 = (f32[128,128]{1,0:T(8,128)S(1)}, f32[128,128]{1,0:T(8,128)S(1)}, u32[]{:S(2)}, u32[]{:S(2)}) collective-permute-start(f32[128,128]{1,0:T(8,128)S(1)} %slice.24), channel_id=1, source_target_pairs={{0,16},{8,24},{16,0},{24,8},{1,17},{9,25},{17,1},{25,9},{2,18},{10... | collective-permute-start | bytes 196616 | tf_op jit(solution)/shard_map/ppermute | solution.py:382
  38.4 4.3 %collective-permute-start.14 = (f32[128,128]{1,0:T(8,128)S(1)}, f32[128,128]{1,0:T(8,128)S(1)}, u32[]{:S(2)}, u32[]{:S(2)}) collective-permute-start(f32[128,128]{1,0:T(8,128)S(1)} %slice.24), channel_id=1, source_target_pairs={{0,24},{8,16},{16,8},{24,0},{1,25},{9,17},{17,9},{25,1},{2,26},{10... | collective-permute-start | bytes 196616 | tf_op jit(solution)/shard_map/ppermute | solution.py:382
  38.9 3.8 %collective-permute-start.12 = (f32[128,128]{1,0:T(8,128)S(1)}, f32[128,128]{1,0:T(8,128)S(1)}, u32[]{:S(2)}, u32[]{:S(2)}) collective-permute-start(f32[128,128]{1,0:T(8,128)S(1)} %slice.24), channel_id=1, source_target_pairs={{0,8},{8,0},{16,24},{24,16},{1,9},{9,1},{17,25},{25,17},{2,10},{10... | collective-permute-start | bytes 196616 | tf_op jit(solution)/shard_map/ppermute | solution.py:382
  42.8 11.3 %collective-permute-start.17 = (f32[128,128]{1,0:T(8,128)S(1)}, f32[128,128]{1,0:T(8,128)S(1)}, u32[]{:S(2)}, u32[]{:S(2)}) collective-permute-start(f32[128,128]{1,0:T(8,128)S(1)} %add_add_fusion.1), channel_id=1, source_target_pairs={{0,96},{32,64},{64,32},{96,0},{128,224},{160,192},{192,160},{224,1... | collective-permute-start | bytes 196616 | tf_op jit(solution)/shard_map/ppermute | solution.py:382
  44.5 9.6 %collective-permute-start.16 = (f32[128,128]{1,0:T(8,128)S(1)}, f32[128,128]{1,0:T(8,128)S(1)}, u32[]{:S(2)}, u32[]{:S(2)}) collective-permute-start(f32[128,128]{1,0:T(8,128)S(1)} %add_add_fusion.1), channel_id=1, source_target_pairs={{0,64},{32,96},{64,0},{96,32},{128,192},{160,224},{192,128},{224,1... | collective-permute-start | bytes 196616 | tf_op jit(solution)/shard_map/ppermute | solution.py:382
  46.3 7.8 %collective-permute-start.15 = (f32[128,128]{1,0:T(8,128)S(1)}, f32[128,128]{1,0:T(8,128)S(1)}, u32[]{:S(2)}, u32[]{:S(2)}) collective-permute-start(f32[128,128]{1,0:T(8,128)S(1)} %add_add_fusion.1), channel_id=1, source_target_pairs={{0,32},{32,0},{64,96},{96,64},{128,160},{160,128},{192,224},{224,1... | collective-permute-start | bytes 196616 | tf_op jit(solution)/shard_map/ppermute | solution.py:382
  46.9 8.0 %collective-permute-start.18 = (f32[56,128]{1,0:T(8,128)S(1)}, f32[56,128]{1,0:T(8,128)S(1)}, u32[]{:S(2)}, u32[]{:S(2)}) collective-permute-start(f32[56,128]{1,0:T(8,128)S(1)} %get-tuple-element.56), channel_id=1, source_target_pairs={{0,1},{1,0},{2,3},{3,2},{4,5},{5,4},{6,7},{7,6},{8,9},{9,8},{10,11... | collective-permute-start | bytes 86024 | tf_op jit(solution)/shard_map/ppermute | solution.py:382
  54.9 5.3 %collective-permute-start.19 = (f32[128,128]{1,0:T(8,128)S(1)}, f32[128,128]{1,0:T(8,128)S(1)}, u32[]{:S(2)}, u32[]{:S(2)}) collective-permute-start(f32[128,128]{1,0:T(8,128)S(1)} %add_add_fusion.a_ref), channel_id=1, source_target_pairs={{0,192},{32,224},{64,128},{96,160},{128,64},{160,96},{192,0},{224,... | collective-permute-start | bytes 196616 | tf_op jit(solution)/shard_map/ppermute | solution.py:382
  60.5 10.5 %copy-start = (f32[2,112,128]{2,1,0:T(8,128)S(1)}, f32[2,112,128]{2,1,0:T(8,128)}, u32[]{:S(2)}) copy-start(f32[2,112,128]{2,1,0:T(8,128)} %refs_5_.1) | copy-start | bytes 344068
  60.5 10.5 %copy-start.1 = (f32[2,112,128]{2,1,0:T(8,128)S(1)}, f32[2,112,128]{2,1,0:T(8,128)}, u32[]{:S(2)}) copy-start(f32[2,112,128]{2,1,0:T(8,128)} %refs_6_.1) | copy-start | bytes 344068
  60.5 4.4 %collective-permute-start.22 = (f32[1,128,128]{2,1,0:T(8,128)S(1)}, f32[1,128,128]{2,1,0:T(8,128)S(1)}, u32[]{:S(2)}, u32[]{:S(2)}) collective-permute-start(f32[1,128,128]{2,1,0:T(8,128)S(1)} %bitcast.13), channel_id=1, source_target_pairs={{0,6},{2,4},{4,2},{6,0},{1,7},{3,5},{5,3},{7,1},{8,14},{10,12},{12... | collective-permute-start | bytes 196616 | tf_op jit(solution)/shard_map/ppermute | solution.py:382
  61.7 4.6 %collective-permute-start.21 = (f32[1,128,128]{2,1,0:T(8,128)S(1)}, f32[1,128,128]{2,1,0:T(8,128)S(1)}, u32[]{:S(2)}, u32[]{:S(2)}) collective-permute-start(f32[1,128,128]{2,1,0:T(8,128)S(1)} %bitcast.14), channel_id=1, source_target_pairs={{0,4},{2,6},{4,0},{6,2},{1,5},{3,7},{5,1},{7,3},{8,12},{10,14},{12... | collective-permute-start | bytes 196616 | tf_op jit(solution)/shard_map/ppermute | solution.py:382
  62.4 3.9 %collective-permute-start.20 = (f32[1,128,128]{2,1,0:T(8,128)S(1)}, f32[1,128,128]{2,1,0:T(8,128)S(1)}, u32[]{:S(2)}, u32[]{:S(2)}) collective-permute-start(f32[1,128,128]{2,1,0:T(8,128)S(1)} %bitcast.15), channel_id=1, source_target_pairs={{0,2},{2,0},{4,6},{6,4},{1,3},{3,1},{5,7},{7,5},{8,10},{10,8},{12,... | collective-permute-start | bytes 196616 | tf_op jit(solution)/shard_map/ppermute | solution.py:382
  66.4 5.9 %collective-permute-start.23 = (f32[4,128,128]{2,1,0:T(8,128)S(1)}, f32[4,128,128]{2,1,0:T(8,128)S(1)}, u32[]{:S(2)}, u32[]{:S(2)}) collective-permute-start(f32[4,128,128]{2,1,0:T(8,128)S(1)} %pad_maximum_fusion), channel_id=1, source_target_pairs={{0,1},{1,0},{2,3},{3,2},{4,5},{5,4},{6,7},{7,6},{8,9},{9,8},{10,11... | collective-permute-start | bytes 786440 | tf_op jit(solution)/shard_map/ppermute | solution.py:382

commit v12 on v8

--- a/solution.py
+++ b/solution.py
@@ -232,14 +232,14 @@
     )(p_sum, inverse)
 
 
-def side_kernel(replicas, own_ref, other_ref, hat_ref, rows_ref):
-    rows = hat_ref.shape[1]
+def side_kernel(replicas, own_ref, other_ref, hat_ref):
+    rows = hat_ref.shape[1] - 16
     at = lax.broadcasted_iota(jnp.int32, (16, rows), 0) + lax.axis_index(("z", "y")) * (rows // replicas)
     chosen = (lax.broadcasted_iota(jnp.int32, (16, rows), 1) == at).astype(F32)
     for i, ref in enumerate((own_ref, other_ref)):
         hat = unpack_rows(ref[...])
-        hat_ref[i] = left_three(hat)
-        rows_ref[i] = left_three(dot(chosen, hat, 1, 0, lax.Precision.HIGHEST))
+        hat_ref[i, :rows] = left_three(hat)
+        hat_ref[i, rows:] = left_three(dot(chosen, hat, 1, 0, lax.Precision.HIGHEST))
 
 
 def left_sides(own, other, replicas):
@@ -247,8 +247,8 @@
     return pl.pallas_call(
         functools.partial(side_kernel, replicas),
         in_specs=[WHOLE] * 2,
-        out_specs=[WHOLE] * 2,
-        out_shape=[jax.ShapeDtypeStruct((2, rows, 3 * RANK), BF16), jax.ShapeDtypeStruct((2, 16, 3 * RANK), BF16)],
+        out_specs=WHOLE,
+        out_shape=jax.ShapeDtypeStruct((2, rows + 16, 3 * RANK), BF16),
         compiler_params=PARAMS,
         cost_estimate=pl.CostEstimate(flops=4_000_000, bytes_accessed=1_000_000, transcendentals=64),
         name="left_sides",
@@ -276,7 +276,7 @@
     )(a, b, inverse)
 
 
-def update_kernel(mine, pieces_ref, hat_ref, rows_ref, full_ref, m1_ref, m2_ref, *refs):
+def update_kernel(mine, pieces_ref, hat_ref, full_ref, m1_ref, m2_ref, *refs):
     err_hbm, n1_hbm, n2_hbm, up_hbm, q_hbm, err_ref, n1_ref, n2_ref, up_ref, q_ref, tile_ref, flat_ref, err_sem, sem = refs[-14:]
     slots, height, _ = pieces_ref.shape
     tiles = height // RANK
@@ -289,11 +289,12 @@
         here = pl.ds(pl.multiple_of(block * width, width), width)
         q = jnp.concatenate([pieces_ref[slot, j * RANK : (j + 1) * RANK, :] for j in range(tiles)], axis=1)
         right = right_three(q)
-        err_ref[slot] = full_ref[:, here] - dot(hat_ref[i], right, 1, 0)
+        approx = dot(hat_ref[i], right, 1, 0)
+        err_ref[slot] = full_ref[:, here] - approx[: full_ref.shape[0]]
         copies.append(pltpu.make_async_copy(err_ref.at[slot], err_hbm.at[0, m, :, here], err_sem.at[slot]))
         copies[-1].start()
         q_ref[:, here] = q
-        state = dot(rows_ref[i], right, 1, 0)
+        state = approx[full_ref.shape[0] :]
         for j in range(tiles):
             tile_ref[block * tiles + j] = state[:8, j * LANES : (j + 1) * LANES]
     share = flat_ref.shape[0]
@@ -312,13 +313,13 @@
         copy.wait()
 
 
-def update(pieces, hat, rows, full, moment1, moment2, mine, before=()):
+def update(pieces, hat, full, moment1, moment2, mine, before=()):
     depth, columns = full.shape
     projections, slots = hat.shape[0], pieces.shape[0]
     state, tiles = moment1.shape[1], columns // LANES
     return pl.pallas_call(
         functools.partial(update_kernel, mine),
-        in_specs=[WHOLE] * 6 + [AWAY] * len(before),
+        in_specs=[WHOLE] * 5 + [AWAY] * len(before),
         out_specs=[AWAY] * 5,
         out_shape=[
             pltpu.HBM((1, projections, depth, columns), F32),
@@ -338,11 +339,11 @@
             pltpu.SemaphoreType.DMA((slots,)),
             pltpu.SemaphoreType.DMA((4,)),
         ],
-        input_output_aliases={6 + k: k for k in range(len(before))},
+        input_output_aliases={5 + k: k for k in range(len(before))},
         compiler_params=PARAMS,
         cost_estimate=pl.CostEstimate(flops=100_000_000, bytes_accessed=4_000_000, transcendentals=30_000),
         name="update_own" if mine else "update_other",
-    )(pieces, hat, rows, full, moment1, moment2, *before)
+    )(pieces, hat, full, moment1, moment2, *before)
 
 
 def swap(value, axis, bit):
@@ -374,13 +375,13 @@
     hat_gift = swap(hat_other, "c", 1)
     q = four([q] * 4, "z")
     q, hat_own, hat_gift = lax.optimization_barrier((q, hat_own, hat_gift))
-    hat, rows = left_sides(hat_own, hat_gift, replicas)
-    far, hat, rows = lax.optimization_barrier((swap(q, "z", 6), hat, rows))
+    hat = left_sides(hat_own, hat_gift, replicas)
+    far, hat = lax.optimization_barrier((swap(q, "z", 6), hat))
     piece = finished_piece(q, far, inverse, replicas)
     own = jnp.stack([piece] + [swap(piece, "x", i) for i in range(1, slots)])
     other = swap(own, "c", 1)
-    done = update(own, hat, rows, own_full, moment1, moment2, True)
-    return tuple(update(other, hat, rows, other_full, moment1, moment2, False, done))
+    done = update(own, hat, own_full, moment1, moment2, True)
+    return tuple(update(other, hat, other_full, moment1, moment2, False, done))
 
 
 def solution(mesh):

time: 74.4 us -> 74.4 us (level)
  no operation moved by 1% of the time
where the time goes in v12:
time: 74.4 us; the launch traced here: 74.3 us
  starting transfers between devices  43.6 us (59%)
  waiting for transfers between devices  17.4 us (23%)
  Pallas kernels  12.3 us (17%)
  between operations  0.91 us (1%)
    ppermute x24, starting transfers between devices, swap(): lax.ppermute(value, axis, [(i, i ^ bit) for i in range(lax.axis_size(axis...  43.6 us
    ppermute x24, waiting for transfers between devices, swap(): lax.ppermute(value, axis, [(i, i ^ bit) for i in range(lax.axis_size(axis...  17.4 us
    pallas_call x2, Pallas kernels, update(): pl.pallas_call(functools.partial(update_kernel, mine), in_specs=[WHOLE] *...  3.27 us
    pallas_call x1, Pallas kernels, inverse_factor(): pl.pallas_call(factor_kernel, in_specs=[WHOLE], out_specs=WHOLE, out_shap...  2.85 us
    pallas_call x1, Pallas kernels, load(): pl.pallas_call(load_kernel, in_specs=[AWAY] * 3, out_specs=[WHOLE] * 5, o...  2.84 us
  transfers between devices with their start and end apart: 24, of which 13 were waited for; matrix products, arithmetic and copies ran while one was open for 0% of the time, Pallas kernels for 9%

profile of v12, /device:TPU:1, one launch (start us, length us, event | category | flops | bytes accessed | tf_op | source)
XLA Modules:
  0.0 74.3 jit_solution(1705498184033099653)
XLA Ops:
  0.6 2.8 %load.1 = (f32[224,2048]{1,0:T(8,128)S(1)}, f32[56,128]{1,0:T(8,128)S(1)}, bf16[224,2048]{1,0:T(8,128)(2,1)S(1)}, f32[224,2048]{1,0:T(8,128)S(1)}, f32[32,2048]{1,0:T(8,128)S(1)}) custom-call(bf16[1,2,224,2048]{3,2,1,0:T(8,128)(2,1)} %grads_hbm.1, f32[1,2,224,2048]{3,2,1,0:T(8,128)} %errors_hbm.1, f32[2,32,2048]{2,1,0:T(8,128)} %q_hbm.1), custom_call_target="tpu_custom_call" | custom-call | tf_op jit(solution)/shard_map/load/pallas_call | solution.py:89
  3.5 3.3 %collective-permute-start = (f32[56,128]{1,0:T(8,128)S(1)}, f32[56,128]{1,0:T(8,128)S(1)}, u32[]{:S(2)}, u32[]{:S(2)}) collective-permute-start(f32[56,128]{1,0:T(8,128)S(1)} %get-tuple-element.37), channel_id=1, source_target_pairs={{0,1},{1,0},{2,3},{3,2},{4,5},{5,4},{6,7},{7,6},{8,9},{9,8},{10,11... | collective-permute-start | bytes 86024 | tf_op jit(solution)/shard_map/ppermute | solution.py:350
  6.8 0.8 %left_own.1 = (f32[224,2048]{1,0:T(8,128)S(1)}, f32[56,128]{1,0:T(8,128)S(1)}) custom-call(bf16[224,2048]{1,0:T(8,128)(2,1)S(1)} %get-tuple-element.33.grads_ref, f32[224,2048]{1,0:T(8,128)S(1)} %get-tuple-element.34.errors_ref, f32[32,2048]{1,0:T(8,128)S(1)} %get-tuple-element.35.q_ref), custom_call_target="tpu_custom_call" | custom-call | flops 100000000 | bytes 3000000 | tf_op jit(solution)/shard_map/left_own/pallas_call | solution.py:120
  8.0 1.0 %collective-permute-start.3 = (f32[112,128]{1,0:T(8,128)S(1)}, f32[112,128]{1,0:T(8,128)S(1)}, u32[]{:S(2)}, u32[]{:S(2)}) collective-permute-start(f32[112,128]{1,0:T(8,128)S(1)} %pad_maximum_fusion.1), channel_id=1, source_target_pairs={{0,24},{8,16},{16,8},{24,0},{1,25},{9,17},{17,9},{25,1},{2,26},{10... | collective-permute-start | bytes 172040 | tf_op jit(solution)/shard_map/ppermute | solution.py:350
  9.4 1.9 %collective-permute-start.1 = (f32[112,128]{1,0:T(8,128)S(1)}, f32[112,128]{1,0:T(8,128)S(1)}, u32[]{:S(2)}, u32[]{:S(2)}) collective-permute-start(f32[112,128]{1,0:T(8,128)S(1)} %pad_maximum_fusion.1), channel_id=1, source_target_pairs={{0,8},{8,0},{16,24},{24,16},{1,9},{9,1},{17,25},{25,17},{2,10},{10... | collective-permute-start | bytes 172040 | tf_op jit(solution)/shard_map/ppermute | solution.py:350
  11.3 1.0 %collective-permute-done.3 = f32[112,128]{1,0:T(8,128)S(1)} collective-permute-done((f32[112,128]{1,0:T(8,128)S(1)}, f32[112,128]{1,0:T(8,128)S(1)}, u32[]{:S(2)}, u32[]{:S(2)}) %collective-permute-start.3) | collective-permute-done | bytes 57376 | tf_op jit(solution)/shard_map/ppermute | solution.py:350
  12.3 1.3 %collective-permute-done.2 = f32[112,128]{1,0:T(8,128)S(1)} collective-permute-done((f32[112,128]{1,0:T(8,128)S(1)}, f32[112,128]{1,0:T(8,128)S(1)}, u32[]{:S(2)}, u32[]{:S(2)}) %collective-permute-start.2) | collective-permute-done | bytes 57376 | tf_op jit(solution)/shard_map/ppermute | solution.py:350
  13.7 4.3 %collective-permute-start.6 = (f32[112,128]{1,0:T(8,128)S(1)}, f32[112,128]{1,0:T(8,128)S(1)}, u32[]{:S(2)}, u32[]{:S(2)}) collective-permute-start(f32[112,128]{1,0:T(8,128)S(1)} %add_add_fusion.3), channel_id=1, source_target_pairs={{0,96},{32,64},{64,32},{96,0},{128,224},{160,192},{192,160},{224,1... | collective-permute-start | bytes 172040 | tf_op jit(solution)/shard_map/ppermute | solution.py:350
  18.4 1.2 %collective-permute-done.6 = f32[112,128]{1,0:T(8,128)S(1)} collective-permute-done((f32[112,128]{1,0:T(8,128)S(1)}, f32[112,128]{1,0:T(8,128)S(1)}, u32[]{:S(2)}, u32[]{:S(2)}) %collective-permute-start.6) | collective-permute-done | bytes 57376 | tf_op jit(solution)/shard_map/ppermute | solution.py:350
  19.6 2.7 %collective-permute-done.5 = f32[112,128]{1,0:T(8,128)S(1)} collective-permute-done((f32[112,128]{1,0:T(8,128)S(1)}, f32[112,128]{1,0:T(8,128)S(1)}, u32[]{:S(2)}, u32[]{:S(2)}) %collective-permute-start.5) | collective-permute-done | bytes 57376 | tf_op jit(solution)/shard_map/ppermute | solution.py:350
  22.3 3.9 %collective-permute-start.7 = (f32[112,128]{1,0:T(8,128)S(1)}, f32[112,128]{1,0:T(8,128)S(1)}, u32[]{:S(2)}, u32[]{:S(2)}) collective-permute-start(f32[112,128]{1,0:T(8,128)S(1)} %add_add_fusion.2), channel_id=1, source_target_pairs={{0,192},{32,224},{64,128},{96,160},{128,64},{160,96},{192,0},{224,... | collective-permute-start | bytes 172040 | tf_op jit(solution)/shard_map/ppermute | solution.py:350
  26.7 1.6 %collective-permute-done.7 = f32[112,128]{1,0:T(8,128)S(1)} collective-permute-done((f32[112,128]{1,0:T(8,128)S(1)}, f32[112,128]{1,0:T(8,128)S(1)}, u32[]{:S(2)}, u32[]{:S(2)}) %collective-permute-start.7) | collective-permute-done | bytes 57376 | tf_op jit(solution)/shard_map/ppermute | solution.py:350
  28.2 0.9 %right_terms.1 = f32[4,136,128]{2,1,0:T(8,128)S(1)} custom-call(f32[112,128]{1,0:T(8,128)S(1)} %add.54.p_ref, bf16[448,2048]{1,0:T(8,128)(2,1)S(1)} %get-tuple-element.45.hi_ref, bf16[448,2048]{1,0:T(8,128)(2,1)S(1)} %get-tuple-element.46.lo_ref), custom_call_target="tpu_custom_call" | custom-call | tf_op jit(solution)/shard_map/right_terms/pallas_call | solution.py:174
  29.2 2.6 %collective-permute-start.11 = (f32[136,128]{1,0:T(8,128)S(1)}, f32[136,128]{1,0:T(8,128)S(1)}, u32[]{:S(2)}, u32[]{:S(2)}) collective-permute-start(f32[136,128]{1,0:T(8,128)S(1)} %get-tuple-element.61), channel_id=1, source_target_pairs={{0,6},{2,4},{4,2},{6,0},{1,7},{3,5},{5,3},{7,1},{8,14},{10,12},{12... | collective-permute-start | bytes 208904 | tf_op jit(solution)/shard_map/ppermute | solution.py:350
  32.5 1.1 %collective-permute-done.11 = f32[136,128]{1,0:T(8,128)S(1)} collective-permute-done((f32[136,128]{1,0:T(8,128)S(1)}, f32[136,128]{1,0:T(8,128)S(1)}, u32[]{:S(2)}, u32[]{:S(2)}) %collective-permute-start.11) | collective-permute-done | bytes 69664 | tf_op jit(solution)/shard_map/ppermute | solution.py:350
  33.7 2.8 %collective-permute-done.10 = f32[136,128]{1,0:T(8,128)S(1)} collective-permute-done((f32[136,128]{1,0:T(8,128)S(1)}, f32[136,128]{1,0:T(8,128)S(1)}, u32[]{:S(2)}, u32[]{:S(2)}) %collective-permute-start.10) | collective-permute-done | bytes 69664 | tf_op jit(solution)/shard_map/ppermute | solution.py:350
  36.5 2.0 %collective-permute-start.13 = (f32[128,128]{1,0:T(8,128)S(1)}, f32[128,128]{1,0:T(8,128)S(1)}, u32[]{:S(2)}, u32[]{:S(2)}) collective-permute-start(f32[128,128]{1,0:T(8,128)S(1)} %slice.24), channel_id=1, source_target_pairs={{0,16},{8,24},{16,0},{24,8},{1,17},{9,25},{17,1},{25,9},{2,18},{10... | collective-permute-start | bytes 196616 | tf_op jit(solution)/shard_map/ppermute | solution.py:350
  39.2 2.8 %inverse_factor.1.inverse_ref = f32[8,128]{1,0:T(8,128)S(1)} custom-call(f32[136,128]{1,0:T(8,128)S(1)} %fusion.1.sum_ref), custom_call_target="tpu_custom_call" | custom-call | flops 4000000 | bytes 4000000 | tf_op jit(solution)/shard_map/inverse_factor/pallas_call | solution.py:203
  42.0 0.7 collective-permute-done.14
  42.8 1.7 %collective-permute-start.17 = (f32[128,128]{1,0:T(8,128)S(1)}, f32[128,128]{1,0:T(8,128)S(1)}, u32[]{:S(2)}, u32[]{:S(2)}) collective-permute-start(f32[128,128]{1,0:T(8,128)S(1)} %add_add_fusion.1), channel_id=1, source_target_pairs={{0,96},{32,64},{64,32},{96,0},{128,224},{160,192},{192,160},{224,1... | collective-permute-start | bytes 196616 | tf_op jit(solution)/shard_map/ppermute | solution.py:350
  44.5 1.8 %collective-permute-start.16 = (f32[128,128]{1,0:T(8,128)S(1)}, f32[128,128]{1,0:T(8,128)S(1)}, u32[]{:S(2)}, u32[]{:S(2)}) collective-permute-start(f32[128,128]{1,0:T(8,128)S(1)} %add_add_fusion.1), channel_id=1, source_target_pairs={{0,64},{32,96},{64,0},{96,32},{128,192},{160,224},{192,128},{224,1... | collective-permute-start | bytes 196616 | tf_op jit(solution)/shard_map/ppermute | solution.py:350
  46.9 7.2 %collective-permute-start.18 = (f32[56,128]{1,0:T(8,128)S(1)}, f32[56,128]{1,0:T(8,128)S(1)}, u32[]{:S(2)}, u32[]{:S(2)}) collective-permute-start(f32[56,128]{1,0:T(8,128)S(1)} %get-tuple-element.50), channel_id=1, source_target_pairs={{0,1},{1,0},{2,3},{3,2},{4,5},{5,4},{6,7},{7,6},{8,9},{9,8},{10,11... | collective-permute-start | bytes 86024 | tf_op jit(solution)/shard_map/ppermute | solution.py:350
  54.1 0.8 %collective-permute-done.18.other_ref = f32[56,128]{1,0:T(8,128)S(1)} collective-permute-done((f32[56,128]{1,0:T(8,128)S(1)}, f32[56,128]{1,0:T(8,128)S(1)}, u32[]{:S(2)}, u32[]{:S(2)}) %collective-permute-start.18) | collective-permute-done | bytes 28704 | tf_op jit(solution)/shard_map/ppermute | solution.py:350
  54.9 3.4 %collective-permute-start.19 = (f32[128,128]{1,0:T(8,128)S(1)}, f32[128,128]{1,0:T(8,128)S(1)}, u32[]{:S(2)}, u32[]{:S(2)}) collective-permute-start(f32[128,128]{1,0:T(8,128)S(1)} %add_add_fusion.a_ref), channel_id=1, source_target_pairs={{0,192},{32,224},{64,128},{96,160},{128,64},{160,96},{192,0},{224,... | collective-permute-start | bytes 196616 | tf_op jit(solution)/shard_map/ppermute | solution.py:350
  58.8 1.5 %collective-permute-done.19.b_ref = f32[128,128]{1,0:T(8,128)S(1)} collective-permute-done((f32[128,128]{1,0:T(8,128)S(1)}, f32[128,128]{1,0:T(8,128)S(1)}, u32[]{:S(2)}, u32[]{:S(2)}) %collective-permute-start.19) | collective-permute-done | bytes 65568 | tf_op jit(solution)/shard_map/ppermute | solution.py:350
  60.5 1.1 %collective-permute-start.22 = (f32[128,128]{1,0:T(8,128)S(1)}, f32[128,128]{1,0:T(8,128)S(1)}, u32[]{:S(2)}, u32[]{:S(2)}) collective-permute-start(f32[128,128]{1,0:T(8,128)S(1)} %finished_piece.1), channel_id=1, source_target_pairs={{0,6},{2,4},{4,2},{6,0},{1,7},{3,5},{5,3},{7,1},{8,14},{10,12},{12... | collective-permute-start | bytes 196616 | tf_op jit(solution)/shard_map/ppermute | solution.py:350
  62.4 1.4 %collective-permute-start.20 = (f32[128,128]{1,0:T(8,128)S(1)}, f32[128,128]{1,0:T(8,128)S(1)}, u32[]{:S(2)}, u32[]{:S(2)}) collective-permute-start(f32[128,128]{1,0:T(8,128)S(1)} %finished_piece.1), channel_id=1, source_target_pairs={{0,2},{2,0},{4,6},{6,4},{1,3},{3,1},{5,7},{7,5},{8,10},{10,8},{12,... | collective-permute-start | bytes 196616 | tf_op jit(solution)/shard_map/ppermute | solution.py:350
  63.8 1.1 %collective-permute-done.22 = f32[128,128]{1,0:T(8,128)S(1)} collective-permute-done((f32[128,128]{1,0:T(8,128)S(1)}, f32[128,128]{1,0:T(8,128)S(1)}, u32[]{:S(2)}, u32[]{:S(2)}) %collective-permute-start.22) | collective-permute-done | bytes 65568 | tf_op jit(solution)/shard_map/ppermute | solution.py:350
  64.9 1.4 %collective-permute-done.21 = f32[128,128]{1,0:T(8,128)S(1)} collective-permute-done((f32[128,128]{1,0:T(8,128)S(1)}, f32[128,128]{1,0:T(8,128)S(1)}, u32[]{:S(2)}, u32[]{:S(2)}) %collective-permute-start.21) | collective-permute-done | bytes 65568 | tf_op jit(solution)/shard_map/ppermute | solution.py:350
  66.3 4.6 %collective-permute-start.23 = (f32[4,128,128]{2,1,0:T(8,128)S(1)}, f32[4,128,128]{2,1,0:T(8,128)S(1)}, u32[]{:S(2)}, u32[]{:S(2)}) collective-permute-start(f32[4,128,128]{2,1,0:T(8,128)S(1)} %pad_maximum_fusion.pieces_ref), channel_id=1, source_target_pairs={{0,1},{1,0},{2,3},{3,2},{4,5},{5,4},{6,7},{7,6},{8,9},{9,8},{10,11... | collective-permute-start | bytes 786440 | tf_op jit(solution)/shard_map/ppermute | solution.py:350
  70.9 1.6 %update_own.1 = (f32[1,2,224,2048]{3,2,1,0:T(8,128)}, f32[2,112,128]{2,1,0:T(8,128)}, f32[2,112,128]{2,1,0:T(8,128)}, bf16[2,112,128]{2,1,0:T(8,128)(2,1)}, f32[2,32,2048]{2,1,0:T(8,128)}) custom-call(f32[4,128,128]{2,1,0:T(8,128)S(1)} %pad_maximum_fusion.pieces_ref, bf16[2,240,96]{2,1,0:T(8,128)(2,1)S(1)} %left_sides.1.hat_ref, ...), custom_call_target="tpu_custom_call" | custom-call | flops 100000000 | bytes 4000000 | tf_op jit(solution)/shard_map/update_own/pallas_call | solution.py:320
  72.5 1.6 %update_other.1 = (f32[1,2,224,2048]{3,2,1,0:T(8,128)}, f32[2,112,128]{2,1,0:T(8,128)}, f32[2,112,128]{2,1,0:T(8,128)}, bf16[2,112,128]{2,1,0:T(8,128)(2,1)}, f32[2,32,2048]{2,1,0:T(8,128)}) custom-call(f32[4,128,128]{2,1,0:T(8,128)S(1)} %collective-permute-done.23.pieces_ref, ...), custom_call_target="tpu_custom_call", output_to_operand_aliasing={{0}: (5, {}), {1}: (6, {}), {2}: (7, {}), {3}: (8, {}), {4}... | custom-call | flops 100000000 | bytes 4000000 | tf_op jit(solution)/shard_map/update_other/pallas_call | solution.py:320
  (40 shorter events, 5.5 us)
Async XLA Ops:
  3.5 4.2 %collective-permute-start = (f32[56,128]{1,0:T(8,128)S(1)}, f32[56,128]{1,0:T(8,128)S(1)}, u32[]{:S(2)}, u32[]{:S(2)}) collective-permute-start(f32[56,128]{1,0:T(8,128)S(1)} %get-tuple-element.37), channel_id=1, source_target_pairs={{0,1},{1,0},{2,3},{3,2},{4,5},{5,4},{6,7},{7,6},{8,9},{9,8},{10,11... | collective-permute-start | bytes 86024 | tf_op jit(solution)/shard_map/ppermute | solution.py:350
  7.7 18.5 %collective-permute-start.8 = (f32[224,2048]{1,0:T(8,128)S(1)}, f32[224,2048]{1,0:T(8,128)S(1)}, u32[]{:S(2)}, u32[]{:S(2)}) collective-permute-start(f32[224,2048]{1,0:T(8,128)S(1)} %get-tuple-element.41.full_ref), channel_id=1, source_target_pairs={{0,1},{1,0},{2,3},{3,2},{4,5},{5,4},{6,7},{7,6},{8,9},{9,8},{10,11... | collective-permute-start | bytes 5505032 | tf_op jit(solution)/shard_map/ppermute | solution.py:350
  8.0 4.2 %collective-permute-start.3 = (f32[112,128]{1,0:T(8,128)S(1)}, f32[112,128]{1,0:T(8,128)S(1)}, u32[]{:S(2)}, u32[]{:S(2)}) collective-permute-start(f32[112,128]{1,0:T(8,128)S(1)} %pad_maximum_fusion.1), channel_id=1, source_target_pairs={{0,24},{8,16},{16,8},{24,0},{1,25},{9,17},{17,9},{25,1},{2,26},{10... | collective-permute-start | bytes 172040 | tf_op jit(solution)/shard_map/ppermute | solution.py:350
  9.0 4.5 %collective-permute-start.2 = (f32[112,128]{1,0:T(8,128)S(1)}, f32[112,128]{1,0:T(8,128)S(1)}, u32[]{:S(2)}, u32[]{:S(2)}) collective-permute-start(f32[112,128]{1,0:T(8,128)S(1)} %pad_maximum_fusion.1), channel_id=1, source_target_pairs={{0,16},{8,24},{16,0},{24,8},{1,17},{9,25},{17,1},{25,9},{2,18},{10... | collective-permute-start | bytes 172040 | tf_op jit(solution)/shard_map/ppermute | solution.py:350
  9.4 4.3 %collective-permute-start.1 = (f32[112,128]{1,0:T(8,128)S(1)}, f32[112,128]{1,0:T(8,128)S(1)}, u32[]{:S(2)}, u32[]{:S(2)}) collective-permute-start(f32[112,128]{1,0:T(8,128)S(1)} %pad_maximum_fusion.1), channel_id=1, source_target_pairs={{0,8},{8,0},{16,24},{24,16},{1,9},{9,1},{17,25},{25,17},{2,10},{10... | collective-permute-start | bytes 172040 | tf_op jit(solution)/shard_map/ppermute | solution.py:350
  13.7 5.8 %collective-permute-start.6 = (f32[112,128]{1,0:T(8,128)S(1)}, f32[112,128]{1,0:T(8,128)S(1)}, u32[]{:S(2)}, u32[]{:S(2)}) collective-permute-start(f32[112,128]{1,0:T(8,128)S(1)} %add_add_fusion.3), channel_id=1, source_target_pairs={{0,96},{32,64},{64,32},{96,0},{128,224},{160,192},{192,160},{224,1... | collective-permute-start | bytes 172040 | tf_op jit(solution)/shard_map/ppermute | solution.py:350
  18.0 4.3 %collective-permute-start.5 = (f32[112,128]{1,0:T(8,128)S(1)}, f32[112,128]{1,0:T(8,128)S(1)}, u32[]{:S(2)}, u32[]{:S(2)}) collective-permute-start(f32[112,128]{1,0:T(8,128)S(1)} %add_add_fusion.3), channel_id=1, source_target_pairs={{0,64},{32,96},{64,0},{96,32},{128,192},{160,224},{192,128},{224,1... | collective-permute-start | bytes 172040 | tf_op jit(solution)/shard_map/ppermute | solution.py:350
  18.0 4.3 %collective-permute-start.4 = (f32[112,128]{1,0:T(8,128)S(1)}, f32[112,128]{1,0:T(8,128)S(1)}, u32[]{:S(2)}, u32[]{:S(2)}) collective-permute-start(f32[112,128]{1,0:T(8,128)S(1)} %add_add_fusion.3), channel_id=1, source_target_pairs={{0,32},{32,0},{64,96},{96,64},{128,160},{160,128},{192,224},{224,1... | collective-permute-start | bytes 172040 | tf_op jit(solution)/shard_map/ppermute | solution.py:350
  22.3 5.9 %collective-permute-start.7 = (f32[112,128]{1,0:T(8,128)S(1)}, f32[112,128]{1,0:T(8,128)S(1)}, u32[]{:S(2)}, u32[]{:S(2)}) collective-permute-start(f32[112,128]{1,0:T(8,128)S(1)} %add_add_fusion.2), channel_id=1, source_target_pairs={{0,192},{32,224},{64,128},{96,160},{128,64},{160,96},{192,0},{224,... | collective-permute-start | bytes 172040 | tf_op jit(solution)/shard_map/ppermute | solution.py:350
  29.2 41.7 %copy-start = (f32[2,112,128]{2,1,0:T(8,128)S(1)}, f32[2,112,128]{2,1,0:T(8,128)}, u32[]{:S(2)}) copy-start(f32[2,112,128]{2,1,0:T(8,128)} %m1_ref.3) | copy-start | bytes 344068
  29.2 41.7 %copy-start.1 = (f32[2,112,128]{2,1,0:T(8,128)S(1)}, f32[2,112,128]{2,1,0:T(8,128)}, u32[]{:S(2)}) copy-start(f32[2,112,128]{2,1,0:T(8,128)} %m2_ref.3) | copy-start | bytes 344068
  29.2 4.5 %collective-permute-start.11 = (f32[136,128]{1,0:T(8,128)S(1)}, f32[136,128]{1,0:T(8,128)S(1)}, u32[]{:S(2)}, u32[]{:S(2)}) collective-permute-start(f32[136,128]{1,0:T(8,128)S(1)} %get-tuple-element.61), channel_id=1, source_target_pairs={{0,6},{2,4},{4,2},{6,0},{1,7},{3,5},{5,3},{7,1},{8,14},{10,12},{12... | collective-permute-start | bytes 208904 | tf_op jit(solution)/shard_map/ppermute | solution.py:350
  31.8 4.7 %collective-permute-start.10 = (f32[136,128]{1,0:T(8,128)S(1)}, f32[136,128]{1,0:T(8,128)S(1)}, u32[]{:S(2)}, u32[]{:S(2)}) collective-permute-start(f32[136,128]{1,0:T(8,128)S(1)} %get-tuple-element.62), channel_id=1, source_target_pairs={{0,4},{2,6},{4,0},{6,2},{1,5},{3,7},{5,1},{7,3},{8,12},{10,14},{12... | collective-permute-start | bytes 208904 | tf_op jit(solution)/shard_map/ppermute | solution.py:350
  32.3 4.1 %collective-permute-start.9 = (f32[136,128]{1,0:T(8,128)S(1)}, f32[136,128]{1,0:T(8,128)S(1)}, u32[]{:S(2)}, u32[]{:S(2)}) collective-permute-start(f32[136,128]{1,0:T(8,128)S(1)} %get-tuple-element.63), channel_id=1, source_target_pairs={{0,2},{2,0},{4,6},{6,4},{1,3},{3,1},{5,7},{7,5},{8,10},{10,8},{12,... | collective-permute-start | bytes 208904 | tf_op jit(solution)/shard_map/ppermute | solution.py:350
  36.5 5.6 %collective-permute-start.13 = (f32[128,128]{1,0:T(8,128)S(1)}, f32[128,128]{1,0:T(8,128)S(1)}, u32[]{:S(2)}, u32[]{:S(2)}) collective-permute-start(f32[128,128]{1,0:T(8,128)S(1)} %slice.24), channel_id=1, source_target_pairs={{0,16},{8,24},{16,0},{24,8},{1,17},{9,25},{17,1},{25,9},{2,18},{10... | collective-permute-start | bytes 196616 | tf_op jit(solution)/shard_map/ppermute | solution.py:350
  38.5 4.3 %collective-permute-start.14 = (f32[128,128]{1,0:T(8,128)S(1)}, f32[128,128]{1,0:T(8,128)S(1)}, u32[]{:S(2)}, u32[]{:S(2)}) collective-permute-start(f32[128,128]{1,0:T(8,128)S(1)} %slice.24), channel_id=1, source_target_pairs={{0,24},{8,16},{16,8},{24,0},{1,25},{9,17},{17,9},{25,1},{2,26},{10... | collective-permute-start | bytes 196616 | tf_op jit(solution)/shard_map/ppermute | solution.py:350
  38.9 3.8 %collective-permute-start.12 = (f32[128,128]{1,0:T(8,128)S(1)}, f32[128,128]{1,0:T(8,128)S(1)}, u32[]{:S(2)}, u32[]{:S(2)}) collective-permute-start(f32[128,128]{1,0:T(8,128)S(1)} %slice.24), channel_id=1, source_target_pairs={{0,8},{8,0},{16,24},{24,16},{1,9},{9,1},{17,25},{25,17},{2,10},{10... | collective-permute-start | bytes 196616 | tf_op jit(solution)/shard_map/ppermute | solution.py:350
  42.8 11.3 %collective-permute-start.17 = (f32[128,128]{1,0:T(8,128)S(1)}, f32[128,128]{1,0:T(8,128)S(1)}, u32[]{:S(2)}, u32[]{:S(2)}) collective-permute-start(f32[128,128]{1,0:T(8,128)S(1)} %add_add_fusion.1), channel_id=1, source_target_pairs={{0,96},{32,64},{64,32},{96,0},{128,224},{160,192},{192,160},{224,1... | collective-permute-start | bytes 196616 | tf_op jit(solution)/shard_map/ppermute | solution.py:350
  44.5 9.6 %collective-permute-start.16 = (f32[128,128]{1,0:T(8,128)S(1)}, f32[128,128]{1,0:T(8,128)S(1)}, u32[]{:S(2)}, u32[]{:S(2)}) collective-permute-start(f32[128,128]{1,0:T(8,128)S(1)} %add_add_fusion.1), channel_id=1, source_target_pairs={{0,64},{32,96},{64,0},{96,32},{128,192},{160,224},{192,128},{224,1... | collective-permute-start | bytes 196616 | tf_op jit(solution)/shard_map/ppermute | solution.py:350
  46.3 7.8 %collective-permute-start.15 = (f32[128,128]{1,0:T(8,128)S(1)}, f32[128,128]{1,0:T(8,128)S(1)}, u32[]{:S(2)}, u32[]{:S(2)}) collective-permute-start(f32[128,128]{1,0:T(8,128)S(1)} %add_add_fusion.1), channel_id=1, source_target_pairs={{0,32},{32,0},{64,96},{96,64},{128,160},{160,128},{192,224},{224,1... | collective-permute-start | bytes 196616 | tf_op jit(solution)/shard_map/ppermute | solution.py:350
  46.9 8.0 %collective-permute-start.18 = (f32[56,128]{1,0:T(8,128)S(1)}, f32[56,128]{1,0:T(8,128)S(1)}, u32[]{:S(2)}, u32[]{:S(2)}) collective-permute-start(f32[56,128]{1,0:T(8,128)S(1)} %get-tuple-element.50), channel_id=1, source_target_pairs={{0,1},{1,0},{2,3},{3,2},{4,5},{5,4},{6,7},{7,6},{8,9},{9,8},{10,11... | collective-permute-start | bytes 86024 | tf_op jit(solution)/shard_map/ppermute | solution.py:350
  54.9 5.3 %collective-permute-start.19 = (f32[128,128]{1,0:T(8,128)S(1)}, f32[128,128]{1,0:T(8,128)S(1)}, u32[]{:S(2)}, u32[]{:S(2)}) collective-permute-start(f32[128,128]{1,0:T(8,128)S(1)} %add_add_fusion.a_ref), channel_id=1, source_target_pairs={{0,192},{32,224},{64,128},{96,160},{128,64},{160,96},{192,0},{224,... | collective-permute-start | bytes 196616 | tf_op jit(solution)/shard_map/ppermute | solution.py:350
  60.5 4.3 %collective-permute-start.22 = (f32[128,128]{1,0:T(8,128)S(1)}, f32[128,128]{1,0:T(8,128)S(1)}, u32[]{:S(2)}, u32[]{:S(2)}) collective-permute-start(f32[128,128]{1,0:T(8,128)S(1)} %finished_piece.1), channel_id=1, source_target_pairs={{0,6},{2,4},{4,2},{6,0},{1,7},{3,5},{5,3},{7,1},{8,14},{10,12},{12... | collective-permute-start | bytes 196616 | tf_op jit(solution)/shard_map/ppermute | solution.py:350
  61.6 4.6 %collective-permute-start.21 = (f32[128,128]{1,0:T(8,128)S(1)}, f32[128,128]{1,0:T(8,128)S(1)}, u32[]{:S(2)}, u32[]{:S(2)}) collective-permute-start(f32[128,128]{1,0:T(8,128)S(1)} %finished_piece.1), channel_id=1, source_target_pairs={{0,4},{2,6},{4,0},{6,2},{1,5},{3,7},{5,1},{7,3},{8,12},{10,14},{12... | collective-permute-start | bytes 196616 | tf_op jit(solution)/shard_map/ppermute | solution.py:350
  62.4 3.9 %collective-permute-start.20 = (f32[128,128]{1,0:T(8,128)S(1)}, f32[128,128]{1,0:T(8,128)S(1)}, u32[]{:S(2)}, u32[]{:S(2)}) collective-permute-start(f32[128,128]{1,0:T(8,128)S(1)} %finished_piece.1), channel_id=1, source_target_pairs={{0,2},{2,0},{4,6},{6,4},{1,3},{3,1},{5,7},{7,5},{8,10},{10,8},{12,... | collective-permute-start | bytes 196616 | tf_op jit(solution)/shard_map/ppermute | solution.py:350
  66.3 6.2 %collective-permute-start.23 = (f32[4,128,128]{2,1,0:T(8,128)S(1)}, f32[4,128,128]{2,1,0:T(8,128)S(1)}, u32[]{:S(2)}, u32[]{:S(2)}) collective-permute-start(f32[4,128,128]{2,1,0:T(8,128)S(1)} %pad_maximum_fusion.pieces_ref), channel_id=1, source_target_pairs={{0,1},{1,0},{2,3},{3,2},{4,5},{5,4},{6,7},{7,6},{8,9},{9,8},{10,11... | collective-permute-start | bytes 786440 | tf_op jit(solution)/shard_map/ppermute | solution.py:350
